TPU v7x, 32 devices: a whole 2x2x4 slice. The times are simulated.
32 devices in a mesh: ctx: 16 (over z, y, x), head: 2 (over core).
Axes of the slice: x: 2, y: 2, z: 4, core: 2. Of those that a mesh axis runs over, the one named last changes fastest.
Arguments:
- queries: bfloat16 [2048, 64, 128], P('ctx', 'head'), may hold values from -90 to 90
- key_heads: bfloat16 [2048, 8, 128], P('ctx', 'head'), may hold values from -4 to 4
- value_head_rows: bfloat16 [2048, 8, 128], P('ctx', 'head'), may hold values from -6 to 6
- doc_lengths: int32 [8], replicated, may hold values from 1 to 512, 2048 in all
Outputs:
- attended: bfloat16 [2048, 64, 128], P(('ctx', 'head'))
Inputs may be any that keep to these rules, and one draw needn't show every extreme that they name: `doc_lengths`: lengths of 8 documents in order, summing to 2048; the longest is exactly 512.
All inputs are finite; a program needn't handle non-finite values.
Results may differ from a plain program's by a relative error of at most 0.0055.
Values may be sent and summed in bfloat16 or wider, within the bound.
No kernel may reach another device: no remote copies, remote signals or barrier semaphores. Data moves between devices by JAX's collectives and lax.ppermute only.
A program may use at most 128 MiB of HBM per device.

v0:
```python
import functools
import math

import jax
import jax.numpy as jnp
from jax import lax
from jax.experimental import pallas as pl
from jax.experimental.pallas import tpu as pltpu
from jax.sharding import PartitionSpec as P

REACH_LOG = 3
MASKED_SCORE = -1e30


def query_bounds(first_place, lanes, group, doc_lengths):
    place = first_place + lax.broadcasted_iota(jnp.int32, (1, lanes), 1) // group
    begin = jnp.zeros((1, lanes), jnp.int32)
    end = jnp.int32(0)
    for j in range(doc_lengths.shape[0]):
        end = end + doc_lengths[j]
        begin = jnp.where(place >= end, end, begin)
    return place, begin


def attention_kernel(
    devices, doc_lengths, index, queries, gathered, out, window, bias, sems, *, group
):
    kv_count, block = window.shape[2], gathered.shape[4]
    reach = 2**REACH_LOG
    span = (reach + 1) * block
    lanes = block * group
    device = index[0]
    factor = math.log2(math.e) / math.sqrt(queries.shape[2])
    stretches = (device, 2 * devices - 1 - device)

    def copy(half, step):
        source = jnp.maximum(stretches[half] - reach + step, 0)
        folded = source >= devices
        row = jnp.where(folded, 2 * devices - 1 - source, source)
        return pltpu.make_async_copy(
            gathered.at[row, :, :, folded.astype(jnp.int32)],
            window.at[half, :, :, pl.ds(step * block, block)],
            sems.at[half, step],
        )

    for half in range(2):
        for step in range(reach + 1):
            copy(half, step).start()
    for half in range(2):
        first = stretches[half] * block
        place, begin = query_bounds(first, lanes, group, doc_lengths)
        key_place = first - reach * block + lax.broadcasted_iota(jnp.int32, (span, lanes), 0)
        allowed = (key_place >= begin) & (key_place <= place)
        bias[...] = jnp.where(allowed, 0.0, MASKED_SCORE)
        for step in range(reach + 1):
            copy(half, step).wait()
        rows = slice(half * block, (half + 1) * block)
        for pair in range(kv_count // 2):
            heads = slice(2 * pair * group, 2 * (pair + 1) * group)
            both = queries[rows, heads, :].astype(jnp.float32)
            done = []
            for part in range(2):
                head = 2 * pair + part
                q = both[:, part * group : (part + 1) * group, :]
                q = q.reshape(lanes, q.shape[2]).astype(jnp.bfloat16)
                scores = lax.dot_general(
                    window[half, 0, head],
                    q,
                    (((1,), (1,)), ((), ())),
                    preferred_element_type=jnp.float32,
                )
                scores = scores * factor + bias[...]
                weights = jnp.exp2(scores - jnp.max(scores, axis=0, keepdims=True))
                total = jnp.sum(weights, axis=0, keepdims=True)
                mixed = lax.dot_general(
                    window[half, 1, head],
                    weights.astype(jnp.bfloat16),
                    (((0,), (0,)), ((), ())),
                    preferred_element_type=jnp.float32,
                )
                mixed = (mixed / total).T
                done.append(mixed.reshape(block, group, mixed.shape[1]))
            out[rows, heads, :] = jnp.concatenate(done, axis=1).astype(out.dtype)


def shards(queries, key_heads, value_head_rows, doc_lengths):
    stride, heads, width = queries.shape
    kv_count = key_heads.shape[1]
    block = stride // 2
    group = heads // kv_count
    devices = lax.axis_size("ctx")
    index = lax.axis_index("ctx").astype(jnp.int32)[None]
    span = (2**REACH_LOG + 1) * block

    packed = jnp.stack([key_heads, value_head_rows])
    packed = packed.reshape(2, 2, block, kv_count, width).transpose(0, 3, 1, 2, 4)
    gathered = lax.all_gather(packed, "ctx")

    attended = pl.pallas_call(
        functools.partial(attention_kernel, devices, group=group),
        out_shape=jax.ShapeDtypeStruct(queries.shape, jnp.bfloat16),
        in_specs=[
            pl.BlockSpec(memory_space=pltpu.SMEM),
            pl.BlockSpec(memory_space=pltpu.SMEM),
            pl.BlockSpec(memory_space=pltpu.VMEM),
            pl.BlockSpec(memory_space=pl.ANY),
        ],
        out_specs=pl.BlockSpec(memory_space=pltpu.VMEM),
        scratch_shapes=[
            pltpu.VMEM((2, 2, kv_count, span, width), jnp.bfloat16),
            pltpu.VMEM((span, block * group), jnp.float32),
            pltpu.SemaphoreType.DMA((2, 2**REACH_LOG + 1)),
        ],
        compiler_params=pltpu.CompilerParams(vmem_limit_bytes=48 * 2**20),
        name="attention",
    )(doc_lengths, index, queries, gathered)
    return lax.all_to_all(attended, "head", split_axis=0, concat_axis=1, tiled=True)


def solution(mesh):
    in_specs = (P("ctx", "head", None), P("ctx", "head", None), P("ctx", "head", None), P())
    out_specs = P(("ctx", "head"), None, None)
    return jax.shard_map(shards, mesh=mesh, in_specs=in_specs, out_specs=out_specs, check_vma=False)
```

profile of v0, /device:TPU:0, one launch (start us, length us, event | category | flops | bytes accessed | tf_op | source)
XLA Modules:
  0.0 110.8 jit_solution(7705719300442147824)
XLA Ops:
  6.5 0.0 all-gather.3.cloned.1.call-start
  6.5 0.9 copy.8
  7.5 0.9 copy.9
  8.4 0.7 maximum_bitcast_fusion
  9.1 0.0 all-gather.3.cloned.1.call-update
  9.1 79.8 %all-gather.3.cloned.1.call-done = bf16[32,4,2,64,128]{4,3,2,1,0:T(8,128)(2,1)} async-done(((bf16[2,4,2,64,128]{4,3,2,1,0:T(8,128)(2,1)}), bf16[32,4,2,64,128]{4,3,2,1,0:T(8,128)(2,1)}) %all-gather.3.cloned.1.call-update) | async-done | bytes 4194320 | tf_op jit(solution)/shard_map/all_gather | solution.py:97
  88.9 0.0 copy-start
  88.9 1.2 %copy-done = bf16[128,32,128]{2,1,0:T(8,128)(2,1)S(1)} copy-done((bf16[128,32,128]{2,1,0:T(8,128)(2,1)S(1)}, bf16[128,32,128]{2,1,0:T(8,128)(2,1)}, u32[]{:S(2)}) %copy-start) | copy-done | bytes 1048600
  90.2 0.0 copy-start.1
  90.2 0.7 copy-done.1
  90.8 7.5 %attention.1 = bf16[128,32,128]{2,1,0:T(8,128)(2,1)S(1)} custom-call(s32[8]{0:T(128)S(1)} %copy-done.1, s32[1]{0:T(128)} %bitcast.index, bf16[128,32,128]{2,1,0:T(8,128)(2,1)S(1)} %copy-done, bf16[16,2,4,2,64,128]{5,4,3,2,1,0:T(8,128)(2,1)} %bitcast.10), custom_call_target="tpu_custom_call" | custom-call | tf_op jit(solution)/shard_map/attention/pallas_call | solution.py:99
  98.3 4.6 %all_to_all.18 = bf16[128,32,128]{2,1,0:T(8,128)(2,1)S(1)} all-to-all(bf16[128,32,128]{2,1,0:T(8,128)(2,1)S(1)} %attention.1), channel_id=1, replica_groups=mesh['ctx'=16,'head'=2] {'head'}, dimensions={0} | all-to-all | bytes 2097152 | tf_op jit(solution)/shard_map/all_to_all | solution.py:117
  102.9 1.1 %copy.10 = bf16[64,2,32,128]{3,2,1,0:T(8,128)(2,1)} copy(bf16[64,2,32,128]{3,2,0,1:T(8,128)(2,1)S(1)} %bitcast.11) | data formatting | bytes 2097152 | tf_op jit(solution)/shard_map/all_to_all | solution.py:117
Async XLA Ops:
  6.5 82.4 %all-gather.3.cloned.1.call-start = ((), (), s32[]{:S(2)}) async-start(), calls=%async_computation.1 | async-start | bytes 4456448 | tf_op jit(solution)/shard_map/all_gather | solution.py:97
  88.9 1.2 %copy-start = (bf16[128,32,128]{2,1,0:T(8,128)(2,1)S(1)}, bf16[128,32,128]{2,1,0:T(8,128)(2,1)}, u32[]{:S(2)}) copy-start(bf16[128,32,128]{2,1,0:T(8,128)(2,1)} %queries.1) | copy-start | bytes 3145732
  90.2 0.7 copy-start.1
Sparse Core Ops, SparseCore 0:
  10.1 78.7 all-gather.2
where the time goes:
time: 111 us
  waiting for transfers between devices  79.8 us (72%)
  between operations  13.4 us (12%)
  Pallas kernels  7.47 us (7%)
  local copies, waits for them, and re-layouts  4.85 us (4%)
  blocking collectives  4.58 us (4%)
    all_gather x1, waiting for transfers between devices, shards(): gathered = lax.all_gather(packed, 'ctx')  79.8 us
    pallas_call x1, Pallas kernels, shards(): pl.pallas_call(functools.partial(attention_kernel, devices, group=group),...  7.47 us
    all_to_all x1, blocking collectives, shards(): lax.all_to_all(attended, 'head', split_axis=0, concat_axis=1, tiled=True)  4.58 us
    unnamed x6, local copies, waits for them, and re-layouts  3.73 us
  transfers between devices with their start and end apart: 1, of which 1 were waited for; matrix products, arithmetic and copies ran while one was open for 0% of the time, Pallas kernels for 0%

commit v1 on v0

v1 whole, which is shorter than its diff:
```python
import functools
import math

import jax
import jax.numpy as jnp
from jax import lax
from jax.experimental import pallas as pl
from jax.experimental.pallas import tpu as pltpu
from jax.sharding import PartitionSpec as P

REACH_LOG = 3
MASKED_SCORE = -1e30


def query_bounds(first_place, lanes, group, doc_lengths):
    place = first_place + lax.broadcasted_iota(jnp.int32, (1, lanes), 1) // group
    begin = jnp.zeros((1, lanes), jnp.int32)
    end = jnp.int32(0)
    for j in range(doc_lengths.shape[0]):
        end = end + doc_lengths[j]
        begin = jnp.where(place >= end, end, begin)
    return place, begin


def attention_kernel(doc_lengths, position, queries, partner_queries, *refs, group):
    reach = 2**REACH_LOG
    blocks, (out, all_queries, window, bias, sems) = refs[: reach + 1], refs[reach + 1 :]
    stretch, core = position[0], position[1]
    kv_count, block, width = blocks[0].shape[1:]
    span = (reach + 1) * block
    lanes = block * group
    half_heads = kv_count * group // 2
    factor = math.log2(math.e) / math.sqrt(width)

    copies = [
        pltpu.make_async_copy(
            queries.at[pl.ds(core * block, block)],
            all_queries.at[:, pl.ds(core * half_heads, half_heads)],
            sems.at[reach + 1],
        ),
        pltpu.make_async_copy(
            partner_queries,
            all_queries.at[:, pl.ds((1 - core) * half_heads, half_heads)],
            sems.at[reach + 2],
        ),
    ]
    for distance in range(reach + 1):
        rows = slice((reach - distance) * block, (reach - distance + 1) * block)
        copies.append(
            pltpu.make_async_copy(blocks[distance], window.at[:, :, rows], sems.at[distance])
        )
    for copy in copies:
        copy.start()
    first = stretch * block
    place, begin = query_bounds(first, lanes, group, doc_lengths)
    key_place = first - reach * block + lax.broadcasted_iota(jnp.int32, (span, lanes), 0)
    allowed = (key_place >= begin) & (key_place <= place)
    bias[...] = jnp.where(allowed, 0.0, MASKED_SCORE)
    for copy in copies:
        copy.wait()
    for pair in range(kv_count // 2):
        heads = slice(2 * pair * group, 2 * (pair + 1) * group)
        both = all_queries[:, heads, :].astype(jnp.float32)
        done = []
        for part in range(2):
            head = 2 * pair + part
            q = both[:, part * group : (part + 1) * group, :]
            q = q.reshape(lanes, width).astype(jnp.bfloat16)
            scores = lax.dot_general(
                window[0, head],
                q,
                (((1,), (1,)), ((), ())),
                preferred_element_type=jnp.float32,
            )
            scores = scores * factor + bias[...]
            weights = jnp.exp2(scores - jnp.max(scores, axis=0, keepdims=True))
            total = jnp.sum(weights, axis=0, keepdims=True)
            mixed = lax.dot_general(
                window[1, head],
                weights.astype(jnp.bfloat16),
                (((0,), (0,)), ((), ())),
                preferred_element_type=jnp.float32,
            )
            mixed = (mixed / total).T
            done.append(mixed.reshape(block, group, width))
        out[:, heads, :] = jnp.concatenate(done, axis=1).astype(out.dtype)


def shards(queries, key_heads, value_head_rows, doc_lengths):
    stride, heads, width = queries.shape
    kv_count = key_heads.shape[1]
    block = stride // 2
    group = heads // kv_count
    devices = lax.axis_size("ctx")
    device = lax.axis_index("ctx").astype(jnp.int32)
    core = lax.axis_index("head").astype(jnp.int32)
    stretch = jnp.where(core == 0, device, 2 * devices - 1 - device)
    reach = 2**REACH_LOG
    stretches = 2 * devices
    span = (reach + 1) * block

    def owner(place):
        return 2 * place if place < devices else 2 * (stretches - 1 - place) + 1

    def swap(array):
        return lax.ppermute(array, "head", [(0, 1), (1, 0)])

    packed = jnp.stack([key_heads, value_head_rows])
    packed = packed.reshape(2, 2, block, kv_count, width).transpose(1, 0, 3, 2, 4)
    keep = lax.dynamic_index_in_dim(packed, core, 0, keepdims=False)
    given = swap(lax.dynamic_index_in_dim(packed, 1 - core, 0, keepdims=False))
    own = jnp.concatenate(
        [jnp.where(core == 0, keep, given), jnp.where(core == 0, given, keep)], axis=1
    )
    partner_queries = swap(lax.dynamic_slice_in_dim(queries, (1 - core) * block, block, 0))
    blocks = [own]
    for distance in range(1, reach + 1):
        pairs = [(owner(at), owner(at + distance)) for at in range(stretches - distance)]
        blocks.append(lax.ppermute(own, ("ctx", "head"), pairs))

    return pl.pallas_call(
        functools.partial(attention_kernel, group=group),
        out_shape=jax.ShapeDtypeStruct((block, 2 * heads, width), jnp.bfloat16),
        in_specs=[pl.BlockSpec(memory_space=pltpu.SMEM)] * 2
        + [pl.BlockSpec(memory_space=pl.ANY)] * (reach + 3),
        out_specs=pl.BlockSpec(memory_space=pltpu.VMEM),
        scratch_shapes=[
            pltpu.VMEM((block, 2 * heads, width), jnp.bfloat16),
            pltpu.VMEM((2, 2 * kv_count, span, width), jnp.bfloat16),
            pltpu.VMEM((span, block * group), jnp.float32),
            pltpu.SemaphoreType.DMA((reach + 3,)),
        ],
        compiler_params=pltpu.CompilerParams(vmem_limit_bytes=48 * 2**20),
        name="attention",
    )(doc_lengths, jnp.stack([stretch, core]), queries, partner_queries, *blocks)


def solution(mesh):
    in_specs = (P("ctx", "head", None), P("ctx", "head", None), P("ctx", "head", None), P())
    out_specs = P(("ctx", "head"), None, None)
    return jax.shard_map(shards, mesh=mesh, in_specs=in_specs, out_specs=out_specs, check_vma=False)
```

time: 111 us -> 55.6 us (0.50)
  the two profiles are of different devices: /device:TPU:0 before, /device:TPU:16 now
where the time goes in v1:
time: 55.6 us; the launch traced here: 55.2 us
  starting transfers between devices  32.8 us (59%)
  waiting for transfers between devices  12.1 us (22%)
  Pallas kernels  7.31 us (13%)
  local copies, waits for them, and re-layouts  2.82 us (5%)
    ppermute x8, starting transfers between devices, shards(): blocks.append(lax.ppermute(own, ('ctx', 'head'), pairs))  32.7 us
    ppermute x8, waiting for transfers between devices, shards(): blocks.append(lax.ppermute(own, ('ctx', 'head'), pairs))  10.7 us
    pallas_call x1, Pallas kernels, shards(): pl.pallas_call(functools.partial(attention_kernel, group=group), out_shap...  7.31 us
    ppermute x2, waiting for transfers between devices, swap(): return lax.ppermute(array, 'head', [(0, 1), (1, 0)])  1.33 us
  transfers between devices with their start and end apart: 10, of which 4 were waited for; matrix products, arithmetic and copies ran while one was open for 2% of the time, Pallas kernels for 0%

profile of v1, /device:TPU:16, one launch (start us, length us, event | category | flops | bytes accessed | tf_op | source)
XLA Modules:
  0.0 55.2 jit_solution(5076220064644384066)
XLA Ops:
  0.0 0.0 copy-start
  0.0 1.0 %copy_dynamic-update-slice_fusion.1 = bf16[2,2,64,4,128]{4,2,3,0,1:T(8,128)(2,1)S(1)} fusion(bf16[1,2,64,4,128]{4,3,2,1,0:T(4,128)(2,1)} %bitcast.13), kind=kLoop, calls=%fused_computation.4 | loop fusion | bytes 262144
  1.0 0.9 %copy_dynamic-update-slice_fusion = bf16[2,2,64,4,128]{4,2,3,0,1:T(8,128)(2,1)S(1)} fusion(bf16[2,2,64,4,128]{4,2,3,0,1:T(8,128)(2,1)S(1)} %copy_dynamic-update-slice_fusion.1, bf16[1,2,64,4,128]{4,3,2,1,0:T(4,128)(2,1)} %bitcast.14), kind=kLoop, calls=%fused_computation.3 | loop fusion | bytes 262144 | tf_op jit(solution)/shard_map/stack | solution.py:108
  2.0 0.1 collective-permute-start.1
  2.1 1.3 %collective-permute-done.1 = bf16[2,4,64,128]{3,2,1,0:T(8,128)(2,1)S(1)} collective-permute-done((bf16[2,4,64,128]{3,2,1,0:T(8,128)(2,1)S(1)}, bf16[2,4,64,128]{3,2,1,0:T(8,128)(2,1)S(1)}, u32[]{:S(2)}, u32[]{:S(2)}) %collective-permute-start.1) | collective-permute-done | bytes 131104 | tf_op jit(solution)/shard_map/ppermute | solution.py:106
  3.5 5.1 %collective-permute-start.9 = (bf16[2,8,64,128]{3,2,1,0:T(8,128)(2,1)S(1)}, bf16[2,8,64,128]{3,2,1,0:T(8,128)(2,1)S(1)}, u32[]{:S(2)}, u32[]{:S(2)}) collective-permute-start(bf16[2,8,64,128]{3,2,1,0:T(8,128)(2,1)S(1)} %pad_maximum_fusion.refs_0_), channel_id=1, source_target_pairs={{0,16},{2,18},{4,20},{6,22},{8,24},{10,26},{12,28},{14,30},{16,31}... | collective-permute-start | bytes 786440 | tf_op jit(solution)/shard_map/ppermute | solution.py:119
  8.6 2.3 %collective-permute-start.8 = (bf16[2,8,64,128]{3,2,1,0:T(8,128)(2,1)S(1)}, bf16[2,8,64,128]{3,2,1,0:T(8,128)(2,1)S(1)}, u32[]{:S(2)}, u32[]{:S(2)}) collective-permute-start(bf16[2,8,64,128]{3,2,1,0:T(8,128)(2,1)S(1)} %pad_maximum_fusion.refs_0_), channel_id=1, source_target_pairs={{0,14},{2,16},{4,18},{6,20},{8,22},{10,24},{12,26},{14,28},{16,30}... | collective-permute-start | bytes 786440 | tf_op jit(solution)/shard_map/ppermute | solution.py:119
  10.9 1.9 %collective-permute-start.7 = (bf16[2,8,64,128]{3,2,1,0:T(8,128)(2,1)S(1)}, bf16[2,8,64,128]{3,2,1,0:T(8,128)(2,1)S(1)}, u32[]{:S(2)}, u32[]{:S(2)}) collective-permute-start(bf16[2,8,64,128]{3,2,1,0:T(8,128)(2,1)S(1)} %pad_maximum_fusion.refs_0_), channel_id=1, source_target_pairs={{0,12},{2,14},{4,16},{6,18},{8,20},{10,22},{12,24},{14,26},{16,28}... | collective-permute-start | bytes 786440 | tf_op jit(solution)/shard_map/ppermute | solution.py:119
  12.8 2.0 %collective-permute-start.6 = (bf16[2,8,64,128]{3,2,1,0:T(8,128)(2,1)S(1)}, bf16[2,8,64,128]{3,2,1,0:T(8,128)(2,1)S(1)}, u32[]{:S(2)}, u32[]{:S(2)}) collective-permute-start(bf16[2,8,64,128]{3,2,1,0:T(8,128)(2,1)S(1)} %pad_maximum_fusion.refs_0_), channel_id=1, source_target_pairs={{0,10},{2,12},{4,14},{6,16},{8,18},{10,20},{12,22},{14,24},{16,26}... | collective-permute-start | bytes 786440 | tf_op jit(solution)/shard_map/ppermute | solution.py:119
  14.9 0.0 copy-done
  14.9 0.8 %constant_dynamic-slice_fusion = bf16[64,32,128]{2,1,0:T(8,128)(2,1)} fusion(bf16[128,32,128]{2,1,0:T(8,128)(2,1)S(1)} %copy-done, s32[]{:T(128)S(6)} %select_n.27), kind=kLoop, calls=%fused_computation.6 | loop fusion | bytes 1048580 | tf_op jit(solution)/shard_map/dynamic_slice | solution.py:115
  15.7 0.0 collective-permute-start
  15.7 0.0 collective-permute-done.9.refs_8_
  15.7 3.2 %collective-permute-start.5 = (bf16[2,8,64,128]{3,2,1,0:T(8,128)(2,1)S(1)}, bf16[2,8,64,128]{3,2,1,0:T(8,128)(2,1)S(1)}, u32[]{:S(2)}, u32[]{:S(2)}) collective-permute-start(bf16[2,8,64,128]{3,2,1,0:T(8,128)(2,1)S(1)} %pad_maximum_fusion.refs_0_), channel_id=1, source_target_pairs={{0,8},{2,10},{4,12},{6,14},{8,16},{10,18},{12,20},{14,22},{16,24},... | collective-permute-start | bytes 786440 | tf_op jit(solution)/shard_map/ppermute | solution.py:119
  18.9 0.5 collective-permute-done.8.refs_7_
  19.4 7.7 %collective-permute-start.4 = (bf16[2,8,64,128]{3,2,1,0:T(8,128)(2,1)S(1)}, bf16[2,8,64,128]{3,2,1,0:T(8,128)(2,1)S(1)}, u32[]{:S(2)}, u32[]{:S(2)}) collective-permute-start(bf16[2,8,64,128]{3,2,1,0:T(8,128)(2,1)S(1)} %pad_maximum_fusion.refs_0_), channel_id=1, source_target_pairs={{0,6},{2,8},{4,10},{6,12},{8,14},{10,16},{12,18},{14,20},{16,22},{... | collective-permute-start | bytes 786440 | tf_op jit(solution)/shard_map/ppermute | solution.py:119
  27.1 0.0 collective-permute-done.7.refs_6_
  27.1 5.5 %collective-permute-start.3 = (bf16[2,8,64,128]{3,2,1,0:T(8,128)(2,1)S(1)}, bf16[2,8,64,128]{3,2,1,0:T(8,128)(2,1)}, u32[]{:S(2)}, u32[]{:S(2)}) collective-permute-start(bf16[2,8,64,128]{3,2,1,0:T(8,128)(2,1)S(1)} %pad_maximum_fusion.refs_0_), channel_id=1, source_target_pairs={{0,4},{2,6},{4,8},{6,10},{8,12},{10,14},{12,16},{14,18},{16,20},{1... | collective-permute-start | bytes 786440 | tf_op jit(solution)/shard_map/ppermute | solution.py:119
  32.6 0.0 collective-permute-done.6.refs_5_
  32.6 5.0 %collective-permute-start.2 = (bf16[2,8,64,128]{3,2,1,0:T(8,128)(2,1)S(1)}, bf16[2,8,64,128]{3,2,1,0:T(8,128)(2,1)}, u32[]{:S(2)}, u32[]{:S(2)}) collective-permute-start(bf16[2,8,64,128]{3,2,1,0:T(8,128)(2,1)S(1)} %pad_maximum_fusion.refs_0_), channel_id=1, source_target_pairs={{0,2},{2,4},{4,6},{6,8},{8,10},{10,12},{12,14},{14,16},{16,18},{18... | collective-permute-start | bytes 786440 | tf_op jit(solution)/shard_map/ppermute | solution.py:119
  37.6 0.0 copy-start.1
  37.6 0.1 pad_add_fusion.position
  37.7 0.0 collective-permute-done.5.refs_4_
  37.7 0.0 collective-permute-done.4.refs_3_
  37.7 4.4 %collective-permute-done.3.refs_2_ = bf16[2,8,64,128]{3,2,1,0:T(8,128)(2,1)} collective-permute-done((bf16[2,8,64,128]{3,2,1,0:T(8,128)(2,1)S(1)}, bf16[2,8,64,128]{3,2,1,0:T(8,128)(2,1)}, u32[]{:S(2)}, u32[]{:S(2)}) %collective-permute-start.3) | collective-permute-done | bytes 262176 | tf_op jit(solution)/shard_map/ppermute | solution.py:119
  42.1 5.9 %collective-permute-done.2.refs_1_ = bf16[2,8,64,128]{3,2,1,0:T(8,128)(2,1)} collective-permute-done((bf16[2,8,64,128]{3,2,1,0:T(8,128)(2,1)S(1)}, bf16[2,8,64,128]{3,2,1,0:T(8,128)(2,1)}, u32[]{:S(2)}, u32[]{:S(2)}) %collective-permute-start.2) | collective-permute-done | bytes 262176 | tf_op jit(solution)/shard_map/ppermute | solution.py:119
  47.9 0.0 collective-permute-done.partner_queries
  47.9 0.0 copy-done.1
  47.9 7.3 %attention.1 = bf16[64,64,128]{2,1,0:T(8,128)(2,1)} custom-call(s32[8]{0:T(128)S(1)} %copy-done.1, s32[2]{0:T(128)S(1)} %pad_add_fusion.position, bf16[128,32,128]{2,1,0:T(8,128)(2,1)S(1)} %copy-done, bf16[64,32,128]{2,1,0:T(8,128)(2,1)S(1)} %collective-permute-done.partner_queries, bf16[2,8,64,128]{3,2,1,0:T(8,128)(2,1)S(1)} %pad_maximum_fusion.refs_0_, ...), custom_call_target="tpu_custom_call" | custom-call | tf_op jit(solution)/shard_map/attention/pallas_call | solution.py:121
  (3 shorter events, 0.1 us)
Async XLA Ops:
  0.0 14.9 %copy-start = (bf16[128,32,128]{2,1,0:T(8,128)(2,1)S(1)}, bf16[128,32,128]{2,1,0:T(8,128)(2,1)}, u32[]{:S(2)}) copy-start(bf16[128,32,128]{2,1,0:T(8,128)(2,1)} %queries.1) | copy-start | bytes 3145732
  2.0 1.4 %collective-permute-start.1 = (bf16[2,4,64,128]{3,2,1,0:T(8,128)(2,1)S(1)}, bf16[2,4,64,128]{3,2,1,0:T(8,128)(2,1)S(1)}, u32[]{:S(2)}, u32[]{:S(2)}) collective-permute-start(bf16[2,4,64,128]{3,2,1,0:T(8,128)(2,1)S(1)} %dynamic-slice_bitcast_fusion), channel_id=1, source_target_pairs={{0,1},{1,0},{2,3},{3,2},{4,5},{5,4},{6,7},{7,6},{8,9},{9,8},{10,11... | collective-permute-start | bytes 393224 | tf_op jit(solution)/shard_map/ppermute | solution.py:106
  3.5 12.2 %collective-permute-start.9 = (bf16[2,8,64,128]{3,2,1,0:T(8,128)(2,1)S(1)}, bf16[2,8,64,128]{3,2,1,0:T(8,128)(2,1)S(1)}, u32[]{:S(2)}, u32[]{:S(2)}) collective-permute-start(bf16[2,8,64,128]{3,2,1,0:T(8,128)(2,1)S(1)} %pad_maximum_fusion.refs_0_), channel_id=1, source_target_pairs={{0,16},{2,18},{4,20},{6,22},{8,24},{10,26},{12,28},{14,30},{16,31}... | collective-permute-start | bytes 786440 | tf_op jit(solution)/shard_map/ppermute | solution.py:119
  8.6 10.8 %collective-permute-start.8 = (bf16[2,8,64,128]{3,2,1,0:T(8,128)(2,1)S(1)}, bf16[2,8,64,128]{3,2,1,0:T(8,128)(2,1)S(1)}, u32[]{:S(2)}, u32[]{:S(2)}) collective-permute-start(bf16[2,8,64,128]{3,2,1,0:T(8,128)(2,1)S(1)} %pad_maximum_fusion.refs_0_), channel_id=1, source_target_pairs={{0,14},{2,16},{4,18},{6,20},{8,22},{10,24},{12,26},{14,28},{16,30}... | collective-permute-start | bytes 786440 | tf_op jit(solution)/shard_map/ppermute | solution.py:119
  10.9 16.2 %collective-permute-start.7 = (bf16[2,8,64,128]{3,2,1,0:T(8,128)(2,1)S(1)}, bf16[2,8,64,128]{3,2,1,0:T(8,128)(2,1)S(1)}, u32[]{:S(2)}, u32[]{:S(2)}) collective-permute-start(bf16[2,8,64,128]{3,2,1,0:T(8,128)(2,1)S(1)} %pad_maximum_fusion.refs_0_), channel_id=1, source_target_pairs={{0,12},{2,14},{4,16},{6,18},{8,20},{10,22},{12,24},{14,26},{16,28}... | collective-permute-start | bytes 786440 | tf_op jit(solution)/shard_map/ppermute | solution.py:119
  12.8 19.8 %collective-permute-start.6 = (bf16[2,8,64,128]{3,2,1,0:T(8,128)(2,1)S(1)}, bf16[2,8,64,128]{3,2,1,0:T(8,128)(2,1)S(1)}, u32[]{:S(2)}, u32[]{:S(2)}) collective-permute-start(bf16[2,8,64,128]{3,2,1,0:T(8,128)(2,1)S(1)} %pad_maximum_fusion.refs_0_), channel_id=1, source_target_pairs={{0,10},{2,12},{4,14},{6,16},{8,18},{10,20},{12,22},{14,24},{16,26}... | collective-permute-start | bytes 786440 | tf_op jit(solution)/shard_map/ppermute | solution.py:119
  15.7 32.2 %collective-permute-start = (bf16[64,32,128]{2,1,0:T(8,128)(2,1)}, bf16[64,32,128]{2,1,0:T(8,128)(2,1)S(1)}, u32[]{:S(2)}, u32[]{:S(2)}) collective-permute-start(bf16[64,32,128]{2,1,0:T(8,128)(2,1)} %constant_dynamic-slice_fusion), channel_id=1, source_target_pairs={{0,1},{1,0},{2,3},{3,2},{4,5},{5,4},{6,7},{7,6},{8,9},{9,8},{10,11... | collective-permute-start | bytes 1572872 | tf_op jit(solution)/shard_map/ppermute | solution.py:106
  15.7 22.0 %collective-permute-start.5 = (bf16[2,8,64,128]{3,2,1,0:T(8,128)(2,1)S(1)}, bf16[2,8,64,128]{3,2,1,0:T(8,128)(2,1)S(1)}, u32[]{:S(2)}, u32[]{:S(2)}) collective-permute-start(bf16[2,8,64,128]{3,2,1,0:T(8,128)(2,1)S(1)} %pad_maximum_fusion.refs_0_), channel_id=1, source_target_pairs={{0,8},{2,10},{4,12},{6,14},{8,16},{10,18},{12,20},{14,22},{16,24},... | collective-permute-start | bytes 786440 | tf_op jit(solution)/shard_map/ppermute | solution.py:119
  19.4 18.3 %collective-permute-start.4 = (bf16[2,8,64,128]{3,2,1,0:T(8,128)(2,1)S(1)}, bf16[2,8,64,128]{3,2,1,0:T(8,128)(2,1)S(1)}, u32[]{:S(2)}, u32[]{:S(2)}) collective-permute-start(bf16[2,8,64,128]{3,2,1,0:T(8,128)(2,1)S(1)} %pad_maximum_fusion.refs_0_), channel_id=1, source_target_pairs={{0,6},{2,8},{4,10},{6,12},{8,14},{10,16},{12,18},{14,20},{16,22},{... | collective-permute-start | bytes 786440 | tf_op jit(solution)/shard_map/ppermute | solution.py:119
  27.1 15.0 %collective-permute-start.3 = (bf16[2,8,64,128]{3,2,1,0:T(8,128)(2,1)S(1)}, bf16[2,8,64,128]{3,2,1,0:T(8,128)(2,1)}, u32[]{:S(2)}, u32[]{:S(2)}) collective-permute-start(bf16[2,8,64,128]{3,2,1,0:T(8,128)(2,1)S(1)} %pad_maximum_fusion.refs_0_), channel_id=1, source_target_pairs={{0,4},{2,6},{4,8},{6,10},{8,12},{10,14},{12,16},{14,18},{16,20},{1... | collective-permute-start | bytes 786440 | tf_op jit(solution)/shard_map/ppermute | solution.py:119
  32.6 15.3 %collective-permute-start.2 = (bf16[2,8,64,128]{3,2,1,0:T(8,128)(2,1)S(1)}, bf16[2,8,64,128]{3,2,1,0:T(8,128)(2,1)}, u32[]{:S(2)}, u32[]{:S(2)}) collective-permute-start(bf16[2,8,64,128]{3,2,1,0:T(8,128)(2,1)S(1)} %pad_maximum_fusion.refs_0_), channel_id=1, source_target_pairs={{0,2},{2,4},{4,6},{6,8},{8,10},{10,12},{12,14},{14,16},{16,18},{18... | collective-permute-start | bytes 786440 | tf_op jit(solution)/shard_map/ppermute | solution.py:119
  37.6 10.4 %copy-start.1 = (s32[8]{0:T(128)S(1)}, s32[8]{0:T(128)}, u32[]{:S(2)}) copy-start(s32[8]{0:T(128)} %doc_lengths.1) | copy-start | bytes 100

commit v2 on v1

v2 whole, which is shorter than its diff:
```python
import functools
import math

import jax
import jax.numpy as jnp
from jax import lax
from jax.experimental import pallas as pl
from jax.experimental.pallas import tpu as pltpu
from jax.sharding import PartitionSpec as P

REACH_LOG = 3
MASKED_SCORE = -1e30


def query_bounds(first_place, lanes, group, doc_lengths):
    place = first_place + lax.broadcasted_iota(jnp.int32, (1, lanes), 1) // group
    begin = jnp.zeros((1, lanes), jnp.int32)
    end = jnp.int32(0)
    for j in range(doc_lengths.shape[0]):
        end = end + doc_lengths[j]
        begin = jnp.where(place >= end, end, begin)
    return place, begin


def block_bias(stretch, nearest, count, block, group, doc_lengths):
    lanes = block * group
    first = stretch * block
    place, begin = query_bounds(first, lanes, group, doc_lengths)
    lowest = first - (nearest + count - 1) * block
    key_place = lowest + lax.broadcasted_iota(jnp.int32, (count * block, lanes), 0)
    allowed = (key_place >= begin) & (key_place <= place)
    return jnp.where(allowed, 0.0, MASKED_SCORE)


def load_queries(queries, partner_queries, core, block, group, slot, half):
    heads = slice(2 * slot * group, 2 * (slot + 1) * group)
    rows = pl.ds(core * block, block)
    both = (queries[rows, heads, :] if half == 0 else partner_queries[:, heads, :]).astype(
        jnp.float32
    )
    width = both.shape[2]
    return [
        both[:, part * group : (part + 1) * group, :]
        .reshape(block * group, width)
        .astype(jnp.bfloat16)
        for part in range(2)
    ]


def weigh(q, keys, values, bias, floor):
    factor = math.log2(math.e) / math.sqrt(q.shape[1])
    scores = lax.dot_general(
        keys, q, (((1,), (1,)), ((), ())), preferred_element_type=jnp.float32
    )
    scores = scores * factor + bias
    largest = jnp.max(scores, axis=0, keepdims=True)
    if floor is not None:
        largest = jnp.maximum(largest, floor)
    weights = jnp.exp2(scores - largest)
    total = jnp.sum(weights, axis=0, keepdims=True)
    mixed = lax.dot_general(
        values,
        weights.astype(jnp.bfloat16),
        (((0,), (0,)), ((), ())),
        preferred_element_type=jnp.float32,
    )
    return largest, total, mixed


def near_kernel(doc_lengths, position, queries, partner_queries, *refs, group):
    blocks, (peak, sums, mixes, bias) = refs[:-4], refs[-4:]
    stretch, core = position[0], position[1]
    kv_count, block = blocks[0].shape[1:3]
    bias[...] = block_bias(stretch, 0, len(blocks), block, group, doc_lengths)
    for half in range(2):
        base = (core if half == 0 else 1 - core) * (kv_count // 2)
        for pair in range(kv_count // 4):
            both = load_queries(queries, partner_queries, core, block, group, pair, half)
            for part in range(2):
                head = base + 2 * pair + part
                slot = half * (kv_count // 2) + 2 * pair + part
                keys = jnp.concatenate([ref[0, head] for ref in blocks[::-1]], axis=0)
                values = jnp.concatenate([ref[1, head] for ref in blocks[::-1]], axis=0)
                largest, total, mixed = weigh(both[part], keys, values, bias[...], None)
                peak[slot] = largest
                sums[slot] = total
                mixes[slot] = mixed


def far_kernel(
    doc_lengths, position, queries, partner_queries, far, peak, sums, mixes, out, bias, *, group
):
    stretch, core = position[0], position[1]
    count, _, kv_count, block, width = far.shape
    half_heads = kv_count * group // 2
    bias[...] = block_bias(stretch, count + 1, count, block, group, doc_lengths)
    for half in range(2):
        side = core if half == 0 else 1 - core
        base = side * (kv_count // 2)
        for pair in range(kv_count // 4):
            both = load_queries(queries, partner_queries, core, block, group, pair, half)
            done = []
            for part in range(2):
                head = base + 2 * pair + part
                slot = half * (kv_count // 2) + 2 * pair + part
                keys = far[:, 0, head].reshape(count * block, width)
                values = far[:, 1, head].reshape(count * block, width)
                earlier = peak[slot]
                largest, total, mixed = weigh(both[part], keys, values, bias[...], earlier)
                shrink = jnp.exp2(earlier - largest)
                total = total + sums[slot] * shrink
                mixed = (mixed + mixes[slot] * shrink) / total
                done.append(mixed.T.reshape(block, group, width))
            begin = pl.multiple_of(side * half_heads + 2 * pair * group, 2 * group)
            out[:, pl.ds(begin, 2 * group), :] = jnp.concatenate(done, axis=1).astype(out.dtype)


def shards(queries, key_heads, value_head_rows, doc_lengths):
    stride, heads, width = queries.shape
    kv_half = key_heads.shape[1]
    kv_count = 2 * kv_half
    block = stride // 2
    group = heads // kv_half
    lanes = block * group
    devices = lax.axis_size("ctx")
    device = lax.axis_index("ctx").astype(jnp.int32)
    core = lax.axis_index("head").astype(jnp.int32)
    stretch = jnp.where(core == 0, device, 2 * devices - 1 - device)
    stretches = 2 * devices
    jump = 2**REACH_LOG // 2

    def owner(place):
        return 2 * place if place < devices else 2 * (stretches - 1 - place) + 1

    def swap(array):
        return lax.ppermute(array, "head", [(0, 1), (1, 0)])

    def from_below(array, distance):
        pairs = [(owner(at), owner(at + distance)) for at in range(stretches - distance)]
        return lax.ppermute(array, ("ctx", "head"), pairs)

    packed = jnp.stack([key_heads, value_head_rows])
    packed = packed.reshape(2, 2, block, kv_half, width).transpose(1, 0, 3, 2, 4)
    keep = lax.dynamic_index_in_dim(packed, core, 0, keepdims=False)
    given = swap(lax.dynamic_index_in_dim(packed, 1 - core, 0, keepdims=False))
    own = jnp.concatenate(
        [jnp.where(core == 0, keep, given), jnp.where(core == 0, given, keep)], axis=1
    )
    partner_queries = swap(lax.dynamic_slice_in_dim(queries, (1 - core) * block, block, 0))
    blocks = [own] + [from_below(own, distance) for distance in range(1, jump + 1)]
    far = from_below(jnp.stack(blocks[:0:-1]), jump)

    position = jnp.stack([stretch, core])
    smem = pl.BlockSpec(memory_space=pltpu.SMEM)
    vmem = pl.BlockSpec(memory_space=pltpu.VMEM)
    params = pltpu.CompilerParams(vmem_limit_bytes=40 * 2**20)

    def cost(keys):
        work = kv_count * keys * lanes
        return pl.CostEstimate(
            flops=4 * work * width, bytes_accessed=4 * 2**20, transcendentals=work
        )

    state = pl.pallas_call(
        functools.partial(near_kernel, group=group),
        out_shape=[
            jax.ShapeDtypeStruct((kv_count, 1, lanes), jnp.float32),
            jax.ShapeDtypeStruct((kv_count, 1, lanes), jnp.float32),
            jax.ShapeDtypeStruct((kv_count, width, lanes), jnp.float32),
        ],
        in_specs=[smem] * 2 + [vmem] * (jump + 3),
        out_specs=[vmem] * 3,
        scratch_shapes=[pltpu.VMEM(((jump + 1) * block, lanes), jnp.float32)],
        compiler_params=params,
        cost_estimate=cost((jump + 1) * block),
        name="near",
    )(doc_lengths, position, queries, partner_queries, *blocks)
    return pl.pallas_call(
        functools.partial(far_kernel, group=group),
        out_shape=jax.ShapeDtypeStruct((block, 2 * heads, width), jnp.bfloat16),
        in_specs=[smem] * 2 + [vmem] * 6,
        out_specs=vmem,
        scratch_shapes=[pltpu.VMEM((jump * block, lanes), jnp.float32)],
        compiler_params=params,
        cost_estimate=cost(jump * block),
        name="far",
    )(doc_lengths, position, queries, partner_queries, far, *state)


def solution(mesh):
    in_specs = (P("ctx", "head", None), P("ctx", "head", None), P("ctx", "head", None), P())
    out_specs = P(("ctx", "head"), None, None)
    return jax.shard_map(shards, mesh=mesh, in_specs=in_specs, out_specs=out_specs, check_vma=False)
```

time: 55.6 us -> 49.4 us (0.89)
  the two profiles are of different devices: /device:TPU:16 before, /device:TPU:27 now
where the time goes in v2:
time: 49.4 us; the launch traced here: 49.1 us
  waiting for transfers between devices  21.4 us (43%)
  starting transfers between devices  13.5 us (27%)
  Pallas kernels  8.13 us (16%)
  local copies, waits for them, and re-layouts  4.72 us (10%)
  other arithmetic  1.26 us (3%)
    ppermute x5, waiting for transfers between devices, from_below(): return lax.ppermute(array, ('ctx', 'head'), pairs)  18.7 us
    ppermute x5, starting transfers between devices, from_below(): return lax.ppermute(array, ('ctx', 'head'), pairs)  12.2 us
    pallas_call x1, Pallas kernels, shards(): pl.pallas_call(functools.partial(far_kernel, group=group), out_shape=jax....  4.35 us
    pallas_call x1, Pallas kernels, shards(): pl.pallas_call(functools.partial(near_kernel, group=group), out_shape=[ja...  3.78 us
    unnamed x13, local copies, waits for them, and re-layouts  2.93 us
    ppermute x2, waiting for transfers between devices, swap(): return lax.ppermute(array, 'head', [(0, 1), (1, 0)])  2.66 us
    ppermute x2, starting transfers between devices, swap(): return lax.ppermute(array, 'head', [(0, 1), (1, 0)])  1.34 us
    another operation x1, other arithmetic, shards(): far = from_below(jnp.stack(blocks[:0:-1]), jump)  1.13 us
  transfers between devices with their start and end apart: 7, of which 5 were waited for; matrix products, arithmetic and copies ran while one was open for 2% of the time, Pallas kernels for 8%

profile of v2, /device:TPU:27, one launch (start us, length us, event | category | flops | bytes accessed | tf_op | source)
XLA Modules:
  0.0 49.1 jit_solution(12721350542983454290)
XLA Ops:
  0.0 0.0 copy-start
  0.0 1.0 %copy_dynamic-update-slice_fusion.1 = bf16[2,2,64,4,128]{4,2,3,0,1:T(8,128)(2,1)S(1)} fusion(bf16[1,2,64,4,128]{4,3,2,1,0:T(4,128)(2,1)} %bitcast.21), kind=kLoop, calls=%fused_computation.5 | loop fusion | bytes 262144
  1.0 0.9 %copy_dynamic-update-slice_fusion = bf16[2,2,64,4,128]{4,2,3,0,1:T(8,128)(2,1)S(1)} fusion(bf16[2,2,64,4,128]{4,2,3,0,1:T(8,128)(2,1)S(1)} %copy_dynamic-update-slice_fusion.1, bf16[1,2,64,4,128]{4,3,2,1,0:T(4,128)(2,1)} %bitcast.22), kind=kLoop, calls=%fused_computation.4 | loop fusion | bytes 262144 | tf_op jit(solution)/shard_map/stack | solution.py:142
  2.0 0.7 %collective-permute-start.1 = (bf16[2,4,64,128]{3,2,1,0:T(8,128)(2,1)S(1)}, bf16[2,4,64,128]{3,2,1,0:T(8,128)(2,1)S(1)}, u32[]{:S(2)}, u32[]{:S(2)}) collective-permute-start(bf16[2,4,64,128]{3,2,1,0:T(8,128)(2,1)S(1)} %dynamic-slice_bitcast_fusion), channel_id=1, source_target_pairs={{0,1},{1,0},{2,3},{3,2},{4,5},{5,4},{6,7},{7,6},{8,9},{9,8},{10,11... | collective-permute-start | bytes 393224 | tf_op jit(solution)/shard_map/ppermute | solution.py:136
  2.7 0.0 copy-start.5
  2.7 1.0 %collective-permute-done.1 = bf16[2,4,64,128]{3,2,1,0:T(8,128)(2,1)S(1)} collective-permute-done((bf16[2,4,64,128]{3,2,1,0:T(8,128)(2,1)S(1)}, bf16[2,4,64,128]{3,2,1,0:T(8,128)(2,1)S(1)}, u32[]{:S(2)}, u32[]{:S(2)}) %collective-permute-start.1) | collective-permute-done | bytes 131104 | tf_op jit(solution)/shard_map/ppermute | solution.py:136
  3.8 2.1 %collective-permute-start.2 = (bf16[2,8,64,128]{3,2,1,0:T(8,128)(2,1)S(1)}, bf16[2,8,64,128]{3,2,1,0:T(8,128)(2,1)S(1)}, u32[]{:S(2)}, u32[]{:S(2)}) collective-permute-start(bf16[2,8,64,128]{3,2,1,0:T(8,128)(2,1)S(1)} %pad_maximum_fusion.1.refs_0_), channel_id=1, source_target_pairs={{0,8},{2,10},{4,12},{6,14},{8,16},{10,18},{12,20},{14,22},{16,24},... | collective-permute-start | bytes 786440 | tf_op jit(solution)/shard_map/ppermute | solution.py:140
  5.9 3.0 %collective-permute-start.3 = (bf16[2,8,64,128]{3,2,1,0:T(8,128)(2,1)S(1)}, bf16[2,8,64,128]{3,2,1,0:T(8,128)(2,1)S(1)}, u32[]{:S(2)}, u32[]{:S(2)}) collective-permute-start(bf16[2,8,64,128]{3,2,1,0:T(8,128)(2,1)S(1)} %pad_maximum_fusion.1.refs_0_), channel_id=1, source_target_pairs={{0,6},{2,8},{4,10},{6,12},{8,14},{10,16},{12,18},{14,20},{16,22},{... | collective-permute-start | bytes 786440 | tf_op jit(solution)/shard_map/ppermute | solution.py:140
  8.9 2.1 %collective-permute-start.4 = (bf16[2,8,64,128]{3,2,1,0:T(8,128)(2,1)S(1)}, bf16[2,8,64,128]{3,2,1,0:T(8,128)(2,1)S(1)}, u32[]{:S(2)}, u32[]{:S(2)}) collective-permute-start(bf16[2,8,64,128]{3,2,1,0:T(8,128)(2,1)S(1)} %pad_maximum_fusion.1.refs_0_), channel_id=1, source_target_pairs={{0,4},{2,6},{4,8},{6,10},{8,12},{10,14},{12,16},{14,18},{16,20},{1... | collective-permute-start | bytes 786440 | tf_op jit(solution)/shard_map/ppermute | solution.py:140
  11.0 3.1 %collective-permute-start.5 = (bf16[2,8,64,128]{3,2,1,0:T(8,128)(2,1)S(1)}, bf16[2,8,64,128]{3,2,1,0:T(8,128)(2,1)S(1)}, u32[]{:S(2)}, u32[]{:S(2)}) collective-permute-start(bf16[2,8,64,128]{3,2,1,0:T(8,128)(2,1)S(1)} %pad_maximum_fusion.1.refs_0_), channel_id=1, source_target_pairs={{0,2},{2,4},{4,6},{6,8},{8,10},{10,12},{12,14},{14,16},{16,18},{18... | collective-permute-start | bytes 786440 | tf_op jit(solution)/shard_map/ppermute | solution.py:140
  14.1 0.0 collective-permute-done.2.refs_4_
  14.1 11.4 %collective-permute-done.3.refs_3_ = bf16[2,8,64,128]{3,2,1,0:T(8,128)(2,1)S(1)} collective-permute-done((bf16[2,8,64,128]{3,2,1,0:T(8,128)(2,1)S(1)}, bf16[2,8,64,128]{3,2,1,0:T(8,128)(2,1)S(1)}, u32[]{:S(2)}, u32[]{:S(2)}) %collective-permute-start.3) | collective-permute-done | bytes 262176 | tf_op jit(solution)/shard_map/ppermute | solution.py:140
  25.5 0.9 %collective-permute-done.4.refs_2_ = bf16[2,8,64,128]{3,2,1,0:T(8,128)(2,1)S(1)} collective-permute-done((bf16[2,8,64,128]{3,2,1,0:T(8,128)(2,1)S(1)}, bf16[2,8,64,128]{3,2,1,0:T(8,128)(2,1)S(1)}, u32[]{:S(2)}, u32[]{:S(2)}) %collective-permute-start.4) | collective-permute-done | bytes 262176 | tf_op jit(solution)/shard_map/ppermute | solution.py:140
  26.4 0.0 copy-start.1
  26.4 0.0 collective-permute-done.5.refs_1_
  26.4 0.0 copy-start.3
  26.4 1.1 %pad_maximum_fusion = bf16[4,2,8,64,128]{4,3,2,1,0:T(8,128)(2,1)} fusion(bf16[1,2,8,64,128]{4,3,2,1,0:T(8,128)(2,1)S(1)} %bitcast.20, bf16[1,2,8,64,128]{4,3,2,1,0:T(8,128)(2,1)S(1)} %bitcast.19, bf16[1,2,8,64,128]{4,3,2,1,0:T(8,128)(2,1)S(1)} %bitcast.18, bf16[1,2,8,64,128]{4,3,2,1,0:T(8,128)(2,1)S(1)} %bitcast.17), kind=kLoop, calls=%fused_computation | loop fusion | flops 1572864 | bytes 2097152 | tf_op jit(solution)/shard_map/stack | solution.py:151
  27.6 1.9 %collective-permute-start.6 = (bf16[4,2,8,64,128]{4,3,2,1,0:T(8,128)(2,1)}, bf16[4,2,8,64,128]{4,3,2,1,0:T(8,128)(2,1)S(1)}, u32[]{:S(2)}, u32[]{:S(2)}) collective-permute-start(bf16[4,2,8,64,128]{4,3,2,1,0:T(8,128)(2,1)} %pad_maximum_fusion), channel_id=1, source_target_pairs={{0,8},{2,10},{4,12},{6,14},{8,16},{10,18},{12,20},{14,22},{16,24},... | collective-permute-start | bytes 3145736 | tf_op jit(solution)/shard_map/ppermute | solution.py:140
  29.5 0.0 copy-done.1
  29.5 0.0 copy-done.3
  29.5 0.0 copy-done
  29.5 0.8 %constant_dynamic-slice_fusion = bf16[64,32,128]{2,1,0:T(8,128)(2,1)} fusion(bf16[128,32,128]{2,1,0:T(8,128)(2,1)S(1)} %copy-done, s32[]{:T(128)S(6)} %select_n.27), kind=kLoop, calls=%fused_computation.7 | loop fusion | bytes 1048580 | tf_op jit(solution)/shard_map/dynamic_slice | solution.py:149
  30.3 0.6 %collective-permute-start = (bf16[64,32,128]{2,1,0:T(8,128)(2,1)}, bf16[64,32,128]{2,1,0:T(8,128)(2,1)S(1)}, u32[]{:S(2)}, u32[]{:S(2)}) collective-permute-start(bf16[64,32,128]{2,1,0:T(8,128)(2,1)} %constant_dynamic-slice_fusion), channel_id=1, source_target_pairs={{0,1},{1,0},{2,3},{3,2},{4,5},{5,4},{6,7},{7,6},{8,9},{9,8},{10,11... | collective-permute-start | bytes 1572872 | tf_op jit(solution)/shard_map/ppermute | solution.py:136
  30.9 0.1 pad_add_fusion.position
  31.0 1.7 %collective-permute-done.partner_queries = bf16[64,32,128]{2,1,0:T(8,128)(2,1)S(1)} collective-permute-done((bf16[64,32,128]{2,1,0:T(8,128)(2,1)}, bf16[64,32,128]{2,1,0:T(8,128)(2,1)S(1)}, u32[]{:S(2)}, u32[]{:S(2)}) %collective-permute-start) | collective-permute-done | bytes 524320 | tf_op jit(solution)/shard_map/ppermute | solution.py:136
  32.7 0.0 copy-done.5
  32.7 0.0 copy-start.2
  32.7 0.9 %copy-done.2 = bf16[2,8,64,128]{3,2,1,0:T(8,128)(2,1)S(1)} copy-done((bf16[2,8,64,128]{3,2,1,0:T(8,128)(2,1)S(1)}, bf16[2,8,64,128]{3,2,1,0:T(8,128)(2,1)}, u32[]{:S(2)}) %copy-start.2) | copy-done | bytes 262168
  33.6 0.0 copy-start.4
  33.6 0.9 %copy-done.4 = bf16[2,8,64,128]{3,2,1,0:T(8,128)(2,1)S(1)} copy-done((bf16[2,8,64,128]{3,2,1,0:T(8,128)(2,1)S(1)}, bf16[2,8,64,128]{3,2,1,0:T(8,128)(2,1)}, u32[]{:S(2)}) %copy-start.4) | copy-done | bytes 262168
  34.6 3.8 %near.1 = (f32[8,1,512]{2,1,0:T(1,128)S(1)}, f32[8,1,512]{2,1,0:T(1,128)S(1)}, f32[8,128,512]{2,1,0:T(8,128)S(1)}) custom-call(s32[8]{0:T(128)S(1)} %copy-done.5, s32[2]{0:T(128)S(1)} %pad_add_fusion.position, bf16[128,32,128]{2,1,0:T(8,128)(2,1)S(1)} %copy-done, bf16[64,32,128]{2,1,0:T(8,128)(2,1)S(1)} %collective-permute-done.partner_queries, ...), custom_call_target="tpu_custom_call" | custom-call | flops 671088640 | bytes 4194304 | tf_op jit(solution)/shard_map/near/pallas_call | solution.py:164
  38.4 6.4 %collective-permute-done.6.far = bf16[4,2,8,64,128]{4,3,2,1,0:T(8,128)(2,1)S(1)} collective-permute-done((bf16[4,2,8,64,128]{4,3,2,1,0:T(8,128)(2,1)}, bf16[4,2,8,64,128]{4,3,2,1,0:T(8,128)(2,1)S(1)}, u32[]{:S(2)}, u32[]{:S(2)}) %collective-permute-start.6) | collective-permute-done | bytes 1048608 | tf_op jit(solution)/shard_map/ppermute | solution.py:140
  44.8 4.4 %far.1 = bf16[64,64,128]{2,1,0:T(8,128)(2,1)} custom-call(s32[8]{0:T(128)S(1)} %copy-done.5, s32[2]{0:T(128)S(1)} %pad_add_fusion.position, bf16[128,32,128]{2,1,0:T(8,128)(2,1)S(1)} %copy-done, bf16[64,32,128]{2,1,0:T(8,128)(2,1)S(1)} %collective-permute-done.partner_queries, bf16[4,2,8,64,128]{4,3,2,1,0:T(8,128)(2,1)S(1)} %collective-permute-done.6.far, ...), custom_call_target="tpu_custom_call" | custom-call | flops 536870912 | bytes 4194304 | tf_op jit(solution)/shard_map/far/pallas_call | solution.py:178
  (3 shorter events, 0.1 us)
Async XLA Ops:
  0.0 29.5 %copy-start = (bf16[128,32,128]{2,1,0:T(8,128)(2,1)S(1)}, bf16[128,32,128]{2,1,0:T(8,128)(2,1)}, u32[]{:S(2)}) copy-start(bf16[128,32,128]{2,1,0:T(8,128)(2,1)} %queries.3) | copy-start | bytes 3145732
  2.0 1.7 %collective-permute-start.1 = (bf16[2,4,64,128]{3,2,1,0:T(8,128)(2,1)S(1)}, bf16[2,4,64,128]{3,2,1,0:T(8,128)(2,1)S(1)}, u32[]{:S(2)}, u32[]{:S(2)}) collective-permute-start(bf16[2,4,64,128]{3,2,1,0:T(8,128)(2,1)S(1)} %dynamic-slice_bitcast_fusion), channel_id=1, source_target_pairs={{0,1},{1,0},{2,3},{3,2},{4,5},{5,4},{6,7},{7,6},{8,9},{9,8},{10,11... | collective-permute-start | bytes 393224 | tf_op jit(solution)/shard_map/ppermute | solution.py:136
  2.7 30.0 %copy-start.5 = (s32[8]{0:T(128)S(1)}, s32[8]{0:T(128)}, u32[]{:S(2)}) copy-start(s32[8]{0:T(128)} %doc_lengths.3) | copy-start | bytes 100
  3.8 10.3 %collective-permute-start.2 = (bf16[2,8,64,128]{3,2,1,0:T(8,128)(2,1)S(1)}, bf16[2,8,64,128]{3,2,1,0:T(8,128)(2,1)S(1)}, u32[]{:S(2)}, u32[]{:S(2)}) collective-permute-start(bf16[2,8,64,128]{3,2,1,0:T(8,128)(2,1)S(1)} %pad_maximum_fusion.1.refs_0_), channel_id=1, source_target_pairs={{0,8},{2,10},{4,12},{6,14},{8,16},{10,18},{12,20},{14,22},{16,24},... | collective-permute-start | bytes 786440 | tf_op jit(solution)/shard_map/ppermute | solution.py:140
  5.9 19.7 %collective-permute-start.3 = (bf16[2,8,64,128]{3,2,1,0:T(8,128)(2,1)S(1)}, bf16[2,8,64,128]{3,2,1,0:T(8,128)(2,1)S(1)}, u32[]{:S(2)}, u32[]{:S(2)}) collective-permute-start(bf16[2,8,64,128]{3,2,1,0:T(8,128)(2,1)S(1)} %pad_maximum_fusion.1.refs_0_), channel_id=1, source_target_pairs={{0,6},{2,8},{4,10},{6,12},{8,14},{10,16},{12,18},{14,20},{16,22},{... | collective-permute-start | bytes 786440 | tf_op jit(solution)/shard_map/ppermute | solution.py:140
  8.9 17.5 %collective-permute-start.4 = (bf16[2,8,64,128]{3,2,1,0:T(8,128)(2,1)S(1)}, bf16[2,8,64,128]{3,2,1,0:T(8,128)(2,1)S(1)}, u32[]{:S(2)}, u32[]{:S(2)}) collective-permute-start(bf16[2,8,64,128]{3,2,1,0:T(8,128)(2,1)S(1)} %pad_maximum_fusion.1.refs_0_), channel_id=1, source_target_pairs={{0,4},{2,6},{4,8},{6,10},{8,12},{10,14},{12,16},{14,18},{16,20},{1... | collective-permute-start | bytes 786440 | tf_op jit(solution)/shard_map/ppermute | solution.py:140
  11.0 15.4 %collective-permute-start.5 = (bf16[2,8,64,128]{3,2,1,0:T(8,128)(2,1)S(1)}, bf16[2,8,64,128]{3,2,1,0:T(8,128)(2,1)S(1)}, u32[]{:S(2)}, u32[]{:S(2)}) collective-permute-start(bf16[2,8,64,128]{3,2,1,0:T(8,128)(2,1)S(1)} %pad_maximum_fusion.1.refs_0_), channel_id=1, source_target_pairs={{0,2},{2,4},{4,6},{6,8},{8,10},{10,12},{12,14},{14,16},{16,18},{18... | collective-permute-start | bytes 786440 | tf_op jit(solution)/shard_map/ppermute | solution.py:140
  26.4 3.1 %copy-start.1 = (bf16[2,8,64,128]{3,2,1,0:T(8,128)(2,1)}, bf16[2,8,64,128]{3,2,1,0:T(8,128)(2,1)S(1)}, u32[]{:S(2)}) copy-start(bf16[2,8,64,128]{3,2,1,0:T(8,128)(2,1)S(1)} %collective-permute-done.4.refs_2_) | copy-start | bytes 786436
  26.4 3.1 %copy-start.3 = (bf16[2,8,64,128]{3,2,1,0:T(8,128)(2,1)}, bf16[2,8,64,128]{3,2,1,0:T(8,128)(2,1)S(1)}, u32[]{:S(2)}) copy-start(bf16[2,8,64,128]{3,2,1,0:T(8,128)(2,1)S(1)} %collective-permute-done.5.refs_1_) | copy-start | bytes 786436
  27.6 17.2 %collective-permute-start.6 = (bf16[4,2,8,64,128]{4,3,2,1,0:T(8,128)(2,1)}, bf16[4,2,8,64,128]{4,3,2,1,0:T(8,128)(2,1)S(1)}, u32[]{:S(2)}, u32[]{:S(2)}) collective-permute-start(bf16[4,2,8,64,128]{4,3,2,1,0:T(8,128)(2,1)} %pad_maximum_fusion), channel_id=1, source_target_pairs={{0,8},{2,10},{4,12},{6,14},{8,16},{10,18},{12,20},{14,22},{16,24},... | collective-permute-start | bytes 3145736 | tf_op jit(solution)/shard_map/ppermute | solution.py:140
  30.3 2.3 %collective-permute-start = (bf16[64,32,128]{2,1,0:T(8,128)(2,1)}, bf16[64,32,128]{2,1,0:T(8,128)(2,1)S(1)}, u32[]{:S(2)}, u32[]{:S(2)}) collective-permute-start(bf16[64,32,128]{2,1,0:T(8,128)(2,1)} %constant_dynamic-slice_fusion), channel_id=1, source_target_pairs={{0,1},{1,0},{2,3},{3,2},{4,5},{5,4},{6,7},{7,6},{8,9},{9,8},{10,11... | collective-permute-start | bytes 1572872 | tf_op jit(solution)/shard_map/ppermute | solution.py:136
  32.7 1.0 %copy-start.2 = (bf16[2,8,64,128]{3,2,1,0:T(8,128)(2,1)S(1)}, bf16[2,8,64,128]{3,2,1,0:T(8,128)(2,1)}, u32[]{:S(2)}) copy-start(bf16[2,8,64,128]{3,2,1,0:T(8,128)(2,1)} %copy-done.1) | copy-start | bytes 786436
  33.6 0.9 %copy-start.4 = (bf16[2,8,64,128]{3,2,1,0:T(8,128)(2,1)S(1)}, bf16[2,8,64,128]{3,2,1,0:T(8,128)(2,1)}, u32[]{:S(2)}) copy-start(bf16[2,8,64,128]{3,2,1,0:T(8,128)(2,1)} %copy-done.3) | copy-start | bytes 786436

commit v3 on v2

v3 whole, which is shorter than its diff:
```python
import functools
import math

import jax
import jax.numpy as jnp
from jax import lax
from jax.experimental import pallas as pl
from jax.experimental.pallas import tpu as pltpu
from jax.sharding import PartitionSpec as P

REACH_LOG = 3
MASKED_SCORE = -1e30


def query_bounds(first_place, lanes, group, doc_lengths):
    place = first_place + lax.broadcasted_iota(jnp.int32, (1, lanes), 1) // group
    begin = jnp.zeros((1, lanes), jnp.int32)
    end = jnp.int32(0)
    for j in range(doc_lengths.shape[0]):
        end = end + doc_lengths[j]
        begin = jnp.where(place >= end, end, begin)
    return place, begin


def block_bias(stretch, distance, block, group, doc_lengths):
    lanes = block * group
    first = stretch * block
    place, begin = query_bounds(first, lanes, group, doc_lengths)
    key_place = first - distance * block + lax.broadcasted_iota(jnp.int32, (block, lanes), 0)
    allowed = (key_place >= begin) & (key_place <= place)
    return jnp.where(allowed, 0.0, MASKED_SCORE)


def weigh(q, keys, values, bias, floor):
    factor = math.log2(math.e) / math.sqrt(q.shape[1])
    scores = lax.dot_general(
        keys, q, (((1,), (1,)), ((), ())), preferred_element_type=jnp.float32
    )
    scores = scores * factor + bias
    largest = jnp.max(scores, axis=0, keepdims=True)
    if floor is not None:
        largest = jnp.maximum(largest, floor)
    weights = jnp.exp2(scores - largest)
    total = jnp.sum(weights, axis=0, keepdims=True)
    mixed = lax.dot_general(
        values,
        weights.astype(jnp.bfloat16),
        (((0,), (0,)), ((), ())),
        preferred_element_type=jnp.float32,
    )
    return largest, total, mixed


def stage_kernel(doc_lengths, position, *refs, group, arrays, pieces, begins, ends):
    stretch, core = position[0], position[1]
    refs = list(refs)

    def take(count):
        taken = refs[:count]
        del refs[:count]
        return taken

    if begins:
        own_queries, partner_queries = take(2)
    else:
        (folded,) = take(1)
    blocks = take(arrays)
    earlier = None if begins else take(3)
    if ends:
        (out,) = take(1)
    else:
        if begins:
            (folded,) = take(1)
        later = take(3)
    (bias,) = take(1)
    if ends:
        staged, sems = take(2)
    kv_count, lanes, width = folded.shape
    block = lanes // group
    half_heads = kv_count * group // 2

    def gather(kind, head):
        parts = [
            blocks[at][kind, head] if index is None else blocks[at][index, kind, head]
            for at, index, _ in pieces
        ]
        return jnp.concatenate(parts, axis=0)

    for row, (_, _, distance) in enumerate(pieces):
        bias[row * block : (row + 1) * block, :] = block_bias(
            stretch, distance, block, group, doc_lengths
        )
    copies = []
    for half in range(2):
        side = core if half == 0 else 1 - core
        for pair in range(kv_count // 4):
            if begins:
                heads = slice(2 * pair * group, 2 * (pair + 1) * group)
                if half == 0:
                    both = own_queries[pl.ds(core * block, block), heads, :]
                else:
                    both = partner_queries[:, heads, :]
                both = both.astype(jnp.float32)
            done = []
            for part in range(2):
                head = side * (kv_count // 2) + 2 * pair + part
                slot = half * (kv_count // 2) + 2 * pair + part
                if begins:
                    q = both[:, part * group : (part + 1) * group, :]
                    q = q.reshape(lanes, width).astype(jnp.bfloat16)
                    folded[slot] = q
                else:
                    q = folded[slot]
                floor = None if begins else earlier[0][slot]
                largest, total, mixed = weigh(
                    q, gather(0, head), gather(1, head), bias[...], floor
                )
                if not begins:
                    shrink = jnp.exp2(floor - largest)
                    total = total + earlier[1][slot] * shrink
                    mixed = mixed + earlier[2][slot] * shrink
                if ends:
                    done.append((mixed / total).T.reshape(block, group, width))
                else:
                    later[0][slot] = largest
                    later[1][slot] = total
                    later[2][slot] = mixed
            if ends:
                number = half * (kv_count // 4) + pair
                staged[number] = jnp.concatenate(done, axis=1).astype(staged.dtype)
                begin = pl.multiple_of(side * half_heads + 2 * pair * group, 2 * group)
                copies.append(
                    pltpu.make_async_copy(
                        staged.at[number], out.at[:, pl.ds(begin, 2 * group)], sems.at[number]
                    )
                )
                copies[-1].start()
    for copy in copies:
        copy.wait()


def run_stage(name, scalars, queries, blocks, pieces, state, shape):
    block, kv_count, group, width = shape
    lanes = block * group
    begins, ends = state is None, name == "finish"
    smem = pl.BlockSpec(memory_space=pltpu.SMEM)
    vmem = pl.BlockSpec(memory_space=pltpu.VMEM)
    rows = len(pieces) * block
    scratch = [pltpu.VMEM((rows, lanes), jnp.float32)]
    if ends:
        out_shape = jax.ShapeDtypeStruct((block, kv_count * group, width), jnp.bfloat16)
        out_specs = pl.BlockSpec(memory_space=pl.ANY)
        scratch += [
            pltpu.VMEM((kv_count // 2, block, 2 * group, width), jnp.bfloat16),
            pltpu.SemaphoreType.DMA((kv_count // 2,)),
        ]
    else:
        out_shape = [
            jax.ShapeDtypeStruct((kv_count, 1, lanes), jnp.float32),
            jax.ShapeDtypeStruct((kv_count, 1, lanes), jnp.float32),
            jax.ShapeDtypeStruct((kv_count, width, lanes), jnp.float32),
        ]
        if begins:
            out_shape.insert(0, jax.ShapeDtypeStruct((kv_count, lanes, width), jnp.bfloat16))
        out_specs = [vmem] * len(out_shape)
    operands = [*queries, *blocks, *([] if begins else state)]
    work = kv_count * rows * lanes
    return pl.pallas_call(
        functools.partial(
            stage_kernel,
            group=group,
            arrays=len(blocks),
            pieces=pieces,
            begins=begins,
            ends=ends,
        ),
        out_shape=out_shape,
        in_specs=[smem] * 2 + [vmem] * len(operands),
        out_specs=out_specs,
        scratch_shapes=scratch,
        compiler_params=pltpu.CompilerParams(vmem_limit_bytes=32 * 2**20),
        cost_estimate=pl.CostEstimate(
            flops=4 * work * width, bytes_accessed=4 * 2**20, transcendentals=work
        ),
        name=name,
    )(*scalars, *operands)


def shards(queries, key_heads, value_head_rows, doc_lengths):
    stride, heads, width = queries.shape
    kv_half = key_heads.shape[1]
    block = stride // 2
    group = heads // kv_half
    devices = lax.axis_size("ctx")
    device = lax.axis_index("ctx").astype(jnp.int32)
    core = lax.axis_index("head").astype(jnp.int32)
    stretch = jnp.where(core == 0, device, 2 * devices - 1 - device)
    stretches = 2 * devices

    def owner(place):
        return 2 * place if place < devices else 2 * (stretches - 1 - place) + 1

    def swap(array):
        return lax.ppermute(array, "head", [(0, 1), (1, 0)])

    def from_below(array, distance):
        pairs = [(owner(at), owner(at + distance)) for at in range(stretches - distance)]
        return lax.ppermute(array, ("ctx", "head"), pairs)

    packed = jnp.stack([key_heads, value_head_rows])
    packed = packed.reshape(2, 2, block, kv_half, width).transpose(1, 0, 3, 2, 4)
    keep = lax.dynamic_index_in_dim(packed, core, 0, keepdims=False)
    given = swap(lax.dynamic_index_in_dim(packed, 1 - core, 0, keepdims=False))
    own = jnp.concatenate(
        [jnp.where(core == 0, keep, given), jnp.where(core == 0, given, keep)], axis=1
    )
    partner_queries = swap(lax.dynamic_slice_in_dim(queries, (1 - core) * block, block, 0))
    by_four = from_below(own, 4)
    by_one = from_below(own, 1)
    own, partner_queries = lax.optimization_barrier((own, partner_queries))
    by_two = from_below(own, 2)
    by_three = from_below(own, 3)
    outer = from_below(jnp.stack([by_four, by_one]), 4)
    inner = from_below(jnp.stack([by_three, by_two]), 4)

    scalars = (doc_lengths, jnp.stack([stretch, core]))
    shape = (block, 2 * kv_half, group, width)
    near = tuple((at, None, 4 - at) for at in range(5))
    folded, *state = run_stage(
        "near",
        scalars,
        (queries, partner_queries),
        (by_four, by_three, by_two, by_one, own),
        near,
        None,
        shape,
    )
    state = run_stage("outer", scalars, (folded,), (outer,), ((0, 0, 8), (0, 1, 5)), state, shape)
    return run_stage("finish", scalars, (folded,), (inner,), ((0, 0, 7), (0, 1, 6)), state, shape)


def solution(mesh):
    in_specs = (P("ctx", "head", None), P("ctx", "head", None), P("ctx", "head", None), P())
    out_specs = P(("ctx", "head"), None, None)
    return jax.shard_map(shards, mesh=mesh, in_specs=in_specs, out_specs=out_specs, check_vma=False)
```

time: 49.4 us -> 49.9 us (1.010)
  waiting for transfers between devices: 21.4 us -> 17.9 us
  Pallas kernels: 8.13 us -> 10.7 us
  starting transfers between devices: 13.5 us -> 15.8 us
  local copies, waits for them, and re-layouts: 4.72 us -> 3.06 us
  other arithmetic: 1.26 us -> 1.81 us
    ppermute x5 -> x6, starting transfers between devices: 12.2 us -> 15 us  [from_below(): return lax.ppermute(array, ('ctx', 'head'), pairs)]
    ppermute x2, waiting for transfers between devices: 2.66 us -> 0.01 us  [swap(): return lax.ppermute(array, 'head', [(0, 1), (1, 0)])]
    pallas_call x2 -> x3, Pallas kernels: 8.13 us -> 10.7 us  [run_stage(): pl.pallas_call(functools.partial(stage_kernel, group=group, arrays=len(bl...]
    unnamed x13 -> x5, local copies, waits for them, and re-layouts: 2.93 us -> 0.93 us
    ppermute x5 -> x6, waiting for transfers between devices: 18.7 us -> 17.9 us  [from_below(): return lax.ppermute(array, ('ctx', 'head'), pairs)]
    another operation x2 -> x3, other arithmetic: 1.21 us -> 1.76 us  [the longest x1 0.84 us: shards(): outer = from_below(jnp.stack([by_four, by_one]), 4)]
  transfers between devices with their start and end apart: 7 -> 8, of which waited for: 5 -> 4; matrix products, arithmetic and copies ran while one was open for 2% -> 6% of each run, Pallas kernels for 8% -> 13%
where the time goes in v3:
time: 49.9 us; the launch traced here: 49.5 us
  waiting for transfers between devices  17.9 us (36%)
  starting transfers between devices  15.8 us (32%)
  Pallas kernels  10.7 us (21%)
  local copies, waits for them, and re-layouts  3.06 us (6%)
  other arithmetic  1.81 us (4%)
    ppermute x6, waiting for transfers between devices, from_below(): return lax.ppermute(array, ('ctx', 'head'), pairs)  17.9 us
    ppermute x6, starting transfers between devices, from_below(): return lax.ppermute(array, ('ctx', 'head'), pairs)  15 us
    pallas_call x3, Pallas kernels, run_stage(): pl.pallas_call(functools.partial(stage_kernel, group=group, arrays=len(bl...  10.7 us
    dynamic_slice x1, local copies, waits for them, and re-layouts, shards(): lax.dynamic_slice_in_dim(queries, (1 - core) * block, block, 0)  1.16 us
  transfers between devices with their start and end apart: 8, of which 4 were waited for; matrix products, arithmetic and copies ran while one was open for 6% of the time, Pallas kernels for 13%

profile of v3, /device:TPU:27, one launch (start us, length us, event | category | flops | bytes accessed | tf_op | source)
XLA Modules:
  0.0 49.5 jit_solution(10693037161437619879)
XLA Ops:
  0.0 0.9 %copy_dynamic-update-slice_fusion.1 = bf16[2,2,64,4,128]{4,2,3,0,1:T(8,128)(2,1)S(1)} fusion(bf16[1,2,64,4,128]{4,3,2,1,0:T(4,128)(2,1)} %bitcast.21), kind=kLoop, calls=%fused_computation.6 | loop fusion | bytes 262144
  0.9 0.9 %copy_dynamic-update-slice_fusion = bf16[2,2,64,4,128]{4,2,3,0,1:T(8,128)(2,1)S(1)} fusion(bf16[2,2,64,4,128]{4,2,3,0,1:T(8,128)(2,1)S(1)} %copy_dynamic-update-slice_fusion.1, bf16[1,2,64,4,128]{4,3,2,1,0:T(4,128)(2,1)} %bitcast.22), kind=kLoop, calls=%fused_computation.5 | loop fusion | bytes 262144 | tf_op jit(solution)/shard_map/stack | solution.py:210
  1.9 0.7 %collective-permute-start = (bf16[2,4,64,128]{3,2,1,0:T(8,128)(2,1)S(1)}, bf16[2,4,64,128]{3,2,1,0:T(8,128)(2,1)S(1)}, u32[]{:S(2)}, u32[]{:S(2)}) collective-permute-start(bf16[2,4,64,128]{3,2,1,0:T(8,128)(2,1)S(1)} %dynamic-slice_bitcast_fusion), channel_id=1, source_target_pairs={{0,1},{1,0},{2,3},{3,2},{4,5},{5,4},{6,7},{7,6},{8,9},{9,8},{10,11... | collective-permute-start | bytes 393224 | tf_op jit(solution)/shard_map/ppermute | solution.py:204
  2.6 0.0 copy-start
  2.6 0.0 copy-start.1
  2.6 1.2 %constant_dynamic-slice_fusion = bf16[64,32,128]{2,1,0:T(8,128)(2,1)S(1)} fusion(bf16[128,32,128]{2,1,0:T(8,128)(2,1)} %refs_0_.1, s32[]{:T(128)S(6)} %select_n.32), kind=kLoop, calls=%fused_computation.8 | loop fusion | bytes 1048580 | tf_op jit(solution)/shard_map/dynamic_slice | solution.py:217
  3.8 0.1 collective-permute-start.1
  3.9 0.0 collective-permute-done
  4.0 2.2 %collective-permute-start.5 = (bf16[2,8,64,128]{3,2,1,0:T(8,128)(2,1)S(1)}, bf16[2,8,64,128]{3,2,1,0:T(8,128)(2,1)S(1)}, u32[]{:S(2)}, u32[]{:S(2)}) collective-permute-start(bf16[2,8,64,128]{3,2,1,0:T(8,128)(2,1)S(1)} %pad_maximum_fusion.2.refs_6_), channel_id=1, source_target_pairs={{0,2},{2,4},{4,6},{6,8},{8,10},{10,12},{12,14},{14,16},{16,18},{18... | collective-permute-start | bytes 786440 | tf_op jit(solution)/shard_map/ppermute | solution.py:208
  6.1 2.1 %collective-permute-start.2 = (bf16[2,8,64,128]{3,2,1,0:T(8,128)(2,1)S(1)}, bf16[2,8,64,128]{3,2,1,0:T(8,128)(2,1)S(1)}, u32[]{:S(2)}, u32[]{:S(2)}) collective-permute-start(bf16[2,8,64,128]{3,2,1,0:T(8,128)(2,1)S(1)} %pad_maximum_fusion.2.refs_6_), channel_id=1, source_target_pairs={{0,8},{2,10},{4,12},{6,14},{8,16},{10,18},{12,20},{14,22},{16,24},... | collective-permute-start | bytes 786440 | tf_op jit(solution)/shard_map/ppermute | solution.py:208
  8.2 0.0 collective-permute-done.1.refs_1_
  8.2 3.0 %collective-permute-start.4 = (bf16[2,8,64,128]{3,2,1,0:T(8,128)(2,1)S(1)}, bf16[2,8,64,128]{3,2,1,0:T(8,128)(2,1)S(1)}, u32[]{:S(2)}, u32[]{:S(2)}) collective-permute-start(bf16[2,8,64,128]{3,2,1,0:T(8,128)(2,1)S(1)} %pad_maximum_fusion.2.refs_6_), channel_id=1, source_target_pairs={{0,4},{2,6},{4,8},{6,10},{8,12},{10,14},{12,16},{14,18},{16,20},{1... | collective-permute-start | bytes 786440 | tf_op jit(solution)/shard_map/ppermute | solution.py:208
  11.3 3.9 %collective-permute-start.3 = (bf16[2,8,64,128]{3,2,1,0:T(8,128)(2,1)S(1)}, bf16[2,8,64,128]{3,2,1,0:T(8,128)(2,1)S(1)}, u32[]{:S(2)}, u32[]{:S(2)}) collective-permute-start(bf16[2,8,64,128]{3,2,1,0:T(8,128)(2,1)S(1)} %pad_maximum_fusion.2.refs_6_), channel_id=1, source_target_pairs={{0,6},{2,8},{4,10},{6,12},{8,14},{10,16},{12,18},{14,20},{16,22},{... | collective-permute-start | bytes 786440 | tf_op jit(solution)/shard_map/ppermute | solution.py:208
  15.2 0.0 collective-permute-done.5.refs_5_
  15.2 3.9 %collective-permute-done.2.refs_2_ = bf16[2,8,64,128]{3,2,1,0:T(8,128)(2,1)S(1)} collective-permute-done((bf16[2,8,64,128]{3,2,1,0:T(8,128)(2,1)S(1)}, bf16[2,8,64,128]{3,2,1,0:T(8,128)(2,1)S(1)}, u32[]{:S(2)}, u32[]{:S(2)}) %collective-permute-start.2) | collective-permute-done | bytes 262176 | tf_op jit(solution)/shard_map/ppermute | solution.py:208
  19.1 0.8 %pad_maximum_fusion.1 = bf16[2,2,8,64,128]{4,3,2,1,0:T(8,128)(2,1)} fusion(bf16[1,2,8,64,128]{4,3,2,1,0:T(8,128)(2,1)S(1)} %bitcast.17, bf16[1,2,8,64,128]{4,3,2,1,0:T(8,128)(2,1)S(1)} %bitcast.18), kind=kLoop, calls=%fused_computation.1 | loop fusion | flops 262144 | bytes 1048576 | tf_op jit(solution)/shard_map/stack | solution.py:223
  20.0 1.9 %collective-permute-start.7 = (bf16[2,2,8,64,128]{4,3,2,1,0:T(8,128)(2,1)}, bf16[2,2,8,64,128]{4,3,2,1,0:T(8,128)(2,1)S(1)}, u32[]{:S(2)}, u32[]{:S(2)}) collective-permute-start(bf16[2,2,8,64,128]{4,3,2,1,0:T(8,128)(2,1)} %pad_maximum_fusion.1), channel_id=1, source_target_pairs={{0,8},{2,10},{4,12},{6,14},{8,16},{10,18},{12,20},{14,22},{16,24},... | collective-permute-start | bytes 1572872 | tf_op jit(solution)/shard_map/ppermute | solution.py:208
  21.9 3.9 %collective-permute-done.4.refs_4_ = bf16[2,8,64,128]{3,2,1,0:T(8,128)(2,1)S(1)} collective-permute-done((bf16[2,8,64,128]{3,2,1,0:T(8,128)(2,1)S(1)}, bf16[2,8,64,128]{3,2,1,0:T(8,128)(2,1)S(1)}, u32[]{:S(2)}, u32[]{:S(2)}) %collective-permute-start.4) | collective-permute-done | bytes 262176 | tf_op jit(solution)/shard_map/ppermute | solution.py:208
  25.7 7.1 %collective-permute-done.3.refs_3_ = bf16[2,8,64,128]{3,2,1,0:T(8,128)(2,1)S(1)} collective-permute-done((bf16[2,8,64,128]{3,2,1,0:T(8,128)(2,1)S(1)}, bf16[2,8,64,128]{3,2,1,0:T(8,128)(2,1)S(1)}, u32[]{:S(2)}, u32[]{:S(2)}) %collective-permute-start.3) | collective-permute-done | bytes 262176 | tf_op jit(solution)/shard_map/ppermute | solution.py:208
  32.8 0.8 %pad_maximum_fusion = bf16[2,2,8,64,128]{4,3,2,1,0:T(8,128)(2,1)} fusion(bf16[1,2,8,64,128]{4,3,2,1,0:T(8,128)(2,1)S(1)} %bitcast.19, bf16[1,2,8,64,128]{4,3,2,1,0:T(8,128)(2,1)S(1)} %bitcast.20), kind=kLoop, calls=%fused_computation | loop fusion | flops 262144 | bytes 1048576 | tf_op jit(solution)/shard_map/stack | solution.py:224
  33.7 1.9 %collective-permute-start.6 = (bf16[2,2,8,64,128]{4,3,2,1,0:T(8,128)(2,1)}, bf16[2,2,8,64,128]{4,3,2,1,0:T(8,128)(2,1)}, u32[]{:S(2)}, u32[]{:S(2)}) collective-permute-start(bf16[2,2,8,64,128]{4,3,2,1,0:T(8,128)(2,1)} %pad_maximum_fusion), channel_id=1, source_target_pairs={{0,8},{2,10},{4,12},{6,14},{8,16},{10,18},{12,20},{14,22},{16,24},... | collective-permute-start | bytes 1572872 | tf_op jit(solution)/shard_map/ppermute | solution.py:208
  35.6 0.1 pad_add_fusion.position
  35.7 0.0 copy-done
  35.7 0.0 copy-done.1
  35.7 3.8 %near.1 = (bf16[8,512,128]{2,1,0:T(8,128)(2,1)S(1)}, f32[8,1,512]{2,1,0:T(1,128)S(1)}, f32[8,1,512]{2,1,0:T(1,128)S(1)}, f32[8,128,512]{2,1,0:T(8,128)S(1)}) custom-call(s32[8]{0:T(128)S(1)} %copy-done.1, s32[2]{0:T(128)S(1)} %pad_add_fusion.position, bf16[128,32,128]{2,1,0:T(8,128)(2,1)S(1)} %copy-done, ...), custom_call_target="tpu_custom_call" | custom-call | flops 671088640 | bytes 4194304 | tf_op jit(solution)/shard_map/near/pallas_call | solution.py:168
  39.5 0.0 collective-permute-done.7.refs_1_
  39.5 2.8 %outer.1 = (f32[8,1,512]{2,1,0:T(1,128)S(1)}, f32[8,1,512]{2,1,0:T(1,128)S(1)}, f32[8,128,512]{2,1,0:T(8,128)S(1)}) custom-call(s32[8]{0:T(128)S(1)} %copy-done.1, s32[2]{0:T(128)S(1)} %pad_add_fusion.position, bf16[8,512,128]{2,1,0:T(8,128)(2,1)S(1)} %get-tuple-element.16.refs_0_, bf16[2,2,8,64,128]{4,3,2,1,0:T(8,128)(2,1)S(1)} %collective-permute-done.7.refs_1_, ...), custom_call_target="tpu_custom_call" | custom-call | flops 268435456 | bytes 4194304 | tf_op jit(solution)/shard_map/outer/pallas_call | solution.py:168
  42.3 3.1 %collective-permute-done.6.refs_1_ = bf16[2,2,8,64,128]{4,3,2,1,0:T(8,128)(2,1)} collective-permute-done((bf16[2,2,8,64,128]{4,3,2,1,0:T(8,128)(2,1)}, bf16[2,2,8,64,128]{4,3,2,1,0:T(8,128)(2,1)}, u32[]{:S(2)}, u32[]{:S(2)}) %collective-permute-start.6) | collective-permute-done | bytes 524320 | tf_op jit(solution)/shard_map/ppermute | solution.py:208
  45.4 4.1 %finish.1 = bf16[64,64,128]{2,1,0:T(8,128)(2,1)} custom-call(s32[8]{0:T(128)S(1)} %copy-done.1, s32[2]{0:T(128)S(1)} %pad_add_fusion.position, bf16[8,512,128]{2,1,0:T(8,128)(2,1)S(1)} %get-tuple-element.16.refs_0_, bf16[2,2,8,64,128]{4,3,2,1,0:T(8,128)(2,1)} %collective-permute-done.6.refs_1_, f32[8,1,512]{2,1,0:T(1,128)S(1)} %get-tuple-element.20.refs_2_, ...), custom_call_target="tpu_custom_call" | custom-call | flops 268435456 | bytes 4194304 | tf_op jit(solution)/shard_map/finish/pallas_call | solution.py:168
  (3 shorter events, 0.1 us)
Async XLA Ops:
  1.9 2.0 %collective-permute-start = (bf16[2,4,64,128]{3,2,1,0:T(8,128)(2,1)S(1)}, bf16[2,4,64,128]{3,2,1,0:T(8,128)(2,1)S(1)}, u32[]{:S(2)}, u32[]{:S(2)}) collective-permute-start(bf16[2,4,64,128]{3,2,1,0:T(8,128)(2,1)S(1)} %dynamic-slice_bitcast_fusion), channel_id=1, source_target_pairs={{0,1},{1,0},{2,3},{3,2},{4,5},{5,4},{6,7},{7,6},{8,9},{9,8},{10,11... | collective-permute-start | bytes 393224 | tf_op jit(solution)/shard_map/ppermute | solution.py:204
  2.6 33.1 %copy-start = (bf16[128,32,128]{2,1,0:T(8,128)(2,1)S(1)}, bf16[128,32,128]{2,1,0:T(8,128)(2,1)}, u32[]{:S(2)}) copy-start(bf16[128,32,128]{2,1,0:T(8,128)(2,1)} %refs_0_.1) | copy-start | bytes 3145732
  2.6 33.1 %copy-start.1 = (s32[8]{0:T(128)S(1)}, s32[8]{0:T(128)}, u32[]{:S(2)}) copy-start(s32[8]{0:T(128)} %doc_lengths.5) | copy-start | bytes 100
  3.8 4.4 %collective-permute-start.1 = (bf16[64,32,128]{2,1,0:T(8,128)(2,1)S(1)}, bf16[64,32,128]{2,1,0:T(8,128)(2,1)S(1)}, u32[]{:S(2)}, u32[]{:S(2)}) collective-permute-start(bf16[64,32,128]{2,1,0:T(8,128)(2,1)S(1)} %constant_dynamic-slice_fusion), channel_id=1, source_target_pairs={{0,1},{1,0},{2,3},{3,2},{4,5},{5,4},{6,7},{7,6},{8,9},{9,8},{10,11... | collective-permute-start | bytes 1572872 | tf_op jit(solution)/shard_map/ppermute | solution.py:204
  4.0 11.2 %collective-permute-start.5 = (bf16[2,8,64,128]{3,2,1,0:T(8,128)(2,1)S(1)}, bf16[2,8,64,128]{3,2,1,0:T(8,128)(2,1)S(1)}, u32[]{:S(2)}, u32[]{:S(2)}) collective-permute-start(bf16[2,8,64,128]{3,2,1,0:T(8,128)(2,1)S(1)} %pad_maximum_fusion.2.refs_6_), channel_id=1, source_target_pairs={{0,2},{2,4},{4,6},{6,8},{8,10},{10,12},{12,14},{14,16},{16,18},{18... | collective-permute-start | bytes 786440 | tf_op jit(solution)/shard_map/ppermute | solution.py:208
  6.1 13.0 %collective-permute-start.2 = (bf16[2,8,64,128]{3,2,1,0:T(8,128)(2,1)S(1)}, bf16[2,8,64,128]{3,2,1,0:T(8,128)(2,1)S(1)}, u32[]{:S(2)}, u32[]{:S(2)}) collective-permute-start(bf16[2,8,64,128]{3,2,1,0:T(8,128)(2,1)S(1)} %pad_maximum_fusion.2.refs_6_), channel_id=1, source_target_pairs={{0,8},{2,10},{4,12},{6,14},{8,16},{10,18},{12,20},{14,22},{16,24},... | collective-permute-start | bytes 786440 | tf_op jit(solution)/shard_map/ppermute | solution.py:208
  8.2 17.5 %collective-permute-start.4 = (bf16[2,8,64,128]{3,2,1,0:T(8,128)(2,1)S(1)}, bf16[2,8,64,128]{3,2,1,0:T(8,128)(2,1)S(1)}, u32[]{:S(2)}, u32[]{:S(2)}) collective-permute-start(bf16[2,8,64,128]{3,2,1,0:T(8,128)(2,1)S(1)} %pad_maximum_fusion.2.refs_6_), channel_id=1, source_target_pairs={{0,4},{2,6},{4,8},{6,10},{8,12},{10,14},{12,16},{14,18},{16,20},{1... | collective-permute-start | bytes 786440 | tf_op jit(solution)/shard_map/ppermute | solution.py:208
  11.3 21.6 %collective-permute-start.3 = (bf16[2,8,64,128]{3,2,1,0:T(8,128)(2,1)S(1)}, bf16[2,8,64,128]{3,2,1,0:T(8,128)(2,1)S(1)}, u32[]{:S(2)}, u32[]{:S(2)}) collective-permute-start(bf16[2,8,64,128]{3,2,1,0:T(8,128)(2,1)S(1)} %pad_maximum_fusion.2.refs_6_), channel_id=1, source_target_pairs={{0,6},{2,8},{4,10},{6,12},{8,14},{10,16},{12,18},{14,20},{16,22},{... | collective-permute-start | bytes 786440 | tf_op jit(solution)/shard_map/ppermute | solution.py:208
  20.0 19.6 %collective-permute-start.7 = (bf16[2,2,8,64,128]{4,3,2,1,0:T(8,128)(2,1)}, bf16[2,2,8,64,128]{4,3,2,1,0:T(8,128)(2,1)S(1)}, u32[]{:S(2)}, u32[]{:S(2)}) collective-permute-start(bf16[2,2,8,64,128]{4,3,2,1,0:T(8,128)(2,1)} %pad_maximum_fusion.1), channel_id=1, source_target_pairs={{0,8},{2,10},{4,12},{6,14},{8,16},{10,18},{12,20},{14,22},{16,24},... | collective-permute-start | bytes 1572872 | tf_op jit(solution)/shard_map/ppermute | solution.py:208
  33.7 11.7 %collective-permute-start.6 = (bf16[2,2,8,64,128]{4,3,2,1,0:T(8,128)(2,1)}, bf16[2,2,8,64,128]{4,3,2,1,0:T(8,128)(2,1)}, u32[]{:S(2)}, u32[]{:S(2)}) collective-permute-start(bf16[2,2,8,64,128]{4,3,2,1,0:T(8,128)(2,1)} %pad_maximum_fusion), channel_id=1, source_target_pairs={{0,8},{2,10},{4,12},{6,14},{8,16},{10,18},{12,20},{14,22},{16,24},... | collective-permute-start | bytes 1572872 | tf_op jit(solution)/shard_map/ppermute | solution.py:208

commit v4 on v2

v4 whole, which is shorter than its diff:
```python
import functools
import math

import jax
import jax.numpy as jnp
from jax import lax
from jax.experimental import pallas as pl
from jax.experimental.pallas import tpu as pltpu
from jax.sharding import PartitionSpec as P

REACH_LOG = 3
MASKED_SCORE = -1e30

EARLY_CHOICES = ((2, (2, 0, 2, 2)), (1, (3, 1, 1, 1)))
LATE_CHOICES = ((3, (2, 2, 3, 2)), (0, (1, 1, 2, 0)))
FAR_DISTANCES = (7, 6, 8, 5)
EARLY_TARGETS = (0, 3, 1, 2)
LATE_TARGETS = (1, 2, 0, 3)
TURN_DISTANCES = ((7, 8, 6, 5), (6, 5, 8, 7), (6, 5, 8, 7), (6, 8, 7, 5))


def query_bounds(first_place, lanes, group, doc_lengths):
    place = first_place + lax.broadcasted_iota(jnp.int32, (1, lanes), 1) // group
    begin = jnp.zeros((1, lanes), jnp.int32)
    end = jnp.int32(0)
    for j in range(doc_lengths.shape[0]):
        end = end + doc_lengths[j]
        begin = jnp.where(place >= end, end, begin)
    return place, begin


def block_bias(stretch, distance, block, group, doc_lengths):
    lanes = block * group
    first = stretch * block
    place, begin = query_bounds(first, lanes, group, doc_lengths)
    key_place = first - distance * block + lax.broadcasted_iota(jnp.int32, (block, lanes), 0)
    allowed = (key_place >= begin) & (key_place <= place)
    return jnp.where(allowed, 0.0, MASKED_SCORE)


def score(q, keys, bias):
    factor = math.log2(math.e) / math.sqrt(q.shape[1])
    scores = lax.dot_general(
        keys, q, (((1,), (1,)), ((), ())), preferred_element_type=jnp.float32
    )
    return scores * factor + bias


def mix(values, weights):
    return lax.dot_general(
        values,
        weights.astype(jnp.bfloat16),
        (((0,), (0,)), ((), ())),
        preferred_element_type=jnp.float32,
    )


def stage_setup(position, bias, distances, block, group, doc_lengths):
    for row, distance in enumerate(distances):
        bias[row * block : (row + 1) * block, :] = block_bias(
            position[0], distance, block, group, doc_lengths
        )


def bundle_kernel(position, *refs, devices, choices):
    candidates, out = refs[:-1], refs[-1]
    source = position[0] - (devices - 4)
    for slot, (usual, special) in enumerate(choices):
        for candidate, ref in enumerate(candidates):
            chosen = jnp.bool_(candidate == usual)
            for row, number in enumerate(special):
                chosen = jnp.where(source == row, number == candidate, chosen)

            @pl.when(chosen)
            def _(slot=slot, ref=ref):
                out[slot] = ref[...]


def near_kernel(doc_lengths, position, queries, partner_queries, *refs, group):
    blocks, (folded, peak, sums, mixes, bias) = refs[:-5], refs[-5:]
    core = position[1]
    kv_count, block, width = blocks[0].shape[1:]
    lanes = block * group
    stage_setup(position, bias, range(len(blocks)), block, group, doc_lengths)

    def gather(kind, head):
        return jnp.concatenate([ref[kind, head] for ref in blocks], axis=0)

    for half in range(2):
        side = core if half == 0 else 1 - core
        for pair in range(kv_count // 4):
            heads = slice(2 * pair * group, 2 * (pair + 1) * group)
            if half == 0:
                both = queries[pl.ds(core * block, block), heads, :]
            else:
                both = partner_queries[:, heads, :]
            both = both.astype(jnp.float32)
            qs = [
                both[:, part * group : (part + 1) * group, :]
                .reshape(lanes, width)
                .astype(jnp.bfloat16)
                for part in range(2)
            ]
            first_head = side * (kv_count // 2) + 2 * pair
            slots = [half * (kv_count // 2) + 2 * pair + part for part in range(2)]
            scores = [
                score(q, gather(0, first_head + part), bias[...]) for part, q in enumerate(qs)
            ]
            largest = [jnp.max(each, axis=0, keepdims=True) for each in scores]
            weights = [jnp.exp2(each - top) for each, top in zip(scores, largest)]
            for part, slot in enumerate(slots):
                folded[slot] = qs[part]
                peak[slot] = largest[part]
                sums[slot] = jnp.sum(weights[part], axis=0, keepdims=True)
                mixes[slot] = mix(gather(1, first_head + part), weights[part])


def far_kernel(
    doc_lengths,
    position,
    folded,
    peak,
    sums,
    mixes,
    early,
    late,
    out,
    bias,
    staged,
    sems,
    *,
    devices,
    group,
):
    core = position[1]
    _, _, kv_count, block, width = early.shape
    lanes = block * group
    half_heads = kv_count * group // 2
    turn = position[0] - devices
    distances = []
    for column, distance in enumerate(FAR_DISTANCES):
        for row, special in enumerate(TURN_DISTANCES):
            distance = jnp.where(turn == row, special[column], distance)
        distances.append(distance)
    stage_setup(position, bias, distances, block, group, doc_lengths)

    def gather(kind, head):
        return jnp.concatenate(
            [ref[index, kind, head] for ref in (early, late) for index in range(2)], axis=0
        )

    copies = []
    for half in range(2):
        side = core if half == 0 else 1 - core
        for pair in range(kv_count // 4):
            first_head = side * (kv_count // 2) + 2 * pair
            slots = [half * (kv_count // 2) + 2 * pair + part for part in range(2)]
            scores = [
                score(folded[slot], gather(0, first_head + part), bias[...])
                for part, slot in enumerate(slots)
            ]
            largest = [
                jnp.maximum(jnp.max(each, axis=0, keepdims=True), peak[slot])
                for each, slot in zip(scores, slots)
            ]
            weights = [jnp.exp2(each - top) for each, top in zip(scores, largest)]
            shrinks = [jnp.exp2(peak[slot] - top) for slot, top in zip(slots, largest)]
            scales = [
                1.0 / (jnp.sum(each, axis=0, keepdims=True) + sums[slot] * shrink)
                for each, slot, shrink in zip(weights, slots, shrinks)
            ]
            mixed = [
                mix(gather(1, first_head + part), each) for part, each in enumerate(weights)
            ]
            done = [
                (each * scale + mixes[slot] * (shrink * scale)).T.reshape(block, group, width)
                for each, slot, shrink, scale in zip(mixed, slots, shrinks, scales)
            ]
            number = half * (kv_count // 4) + pair
            staged[number] = jnp.concatenate(done, axis=1).astype(staged.dtype)
            begin = pl.multiple_of(side * half_heads + 2 * pair * group, 2 * group)
            copy = pltpu.make_async_copy(
                staged.at[number], out.at[:, pl.ds(begin, 2 * group)], sems.at[number]
            )
            copy.start()
            copies.append(copy)
    for copy in copies:
        copy.wait()


def shards(queries, key_heads, value_head_rows, doc_lengths):
    stride, heads, width = queries.shape
    kv_half = key_heads.shape[1]
    kv_count = 2 * kv_half
    block = stride // 2
    group = heads // kv_half
    lanes = block * group
    devices = lax.axis_size("ctx")
    device = lax.axis_index("ctx").astype(jnp.int32)
    core = lax.axis_index("head").astype(jnp.int32)
    stretch = jnp.where(core == 0, device, 2 * devices - 1 - device)
    stretches = 2 * devices

    def owner(place):
        return 2 * place if place < devices else 2 * (stretches - 1 - place) + 1

    def swap(array):
        return lax.ppermute(array, "head", [(0, 1), (1, 0)])

    def from_below(array, distance, turned=()):
        target = {at: at + distance for at in range(stretches - distance)}
        for number, to in enumerate(turned):
            target[devices - 4 + number] = devices + to
        pairs = [(owner(at), owner(to)) for at, to in target.items()]
        return lax.ppermute(array, ("ctx", "head"), pairs)

    packed = jnp.stack([key_heads, value_head_rows])
    packed = packed.reshape(2, 2, block, kv_half, width).transpose(1, 0, 3, 2, 4)
    keep = lax.dynamic_index_in_dim(packed, core, 0, keepdims=False)
    given = swap(lax.dynamic_index_in_dim(packed, 1 - core, 0, keepdims=False))
    own = jnp.concatenate(
        [jnp.where(core == 0, keep, given), jnp.where(core == 0, given, keep)], axis=1
    )
    partner_queries = swap(lax.dynamic_slice_in_dim(queries, (1 - core) * block, block, 0))
    by_three = from_below(own, 3)
    own, partner_queries = lax.optimization_barrier((own, partner_queries))
    by_two = from_below(own, 2)
    by_four = from_below(own, 4)
    own, by_three = lax.optimization_barrier((own, by_three))
    by_one = from_below(own, 1)

    scalars = (doc_lengths, jnp.stack([stretch, core]))
    vmem = pl.BlockSpec(memory_space=pltpu.VMEM)

    def bundle(name, candidates, choices):
        return pl.pallas_call(
            functools.partial(bundle_kernel, devices=devices, choices=choices),
            out_shape=jax.ShapeDtypeStruct((2, *own.shape), own.dtype),
            in_specs=[pl.BlockSpec(memory_space=pltpu.SMEM)] + [vmem] * len(candidates),
            out_specs=vmem,
            compiler_params=pltpu.CompilerParams(vmem_limit_bytes=6 * 2**20),
            name=name,
        )(scalars[1], *candidates)

    early = from_below(
        bundle("early", (own, by_two, by_three, by_four), EARLY_CHOICES), 4, EARLY_TARGETS
    )
    late = from_below(
        bundle("late", (by_one, by_two, by_three, by_four), LATE_CHOICES), 4, LATE_TARGETS
    )

    blocks = (own, by_one, by_two, by_three, by_four)
    smem = pl.BlockSpec(memory_space=pltpu.SMEM)
    params = pltpu.CompilerParams(vmem_limit_bytes=14 * 2**20)

    def cost(count):
        work = kv_count * count * block * lanes
        return pl.CostEstimate(
            flops=4 * work * width, bytes_accessed=4 * 2**20, transcendentals=work
        )

    state = pl.pallas_call(
        functools.partial(near_kernel, group=group),
        out_shape=[
            jax.ShapeDtypeStruct((kv_count, lanes, width), jnp.bfloat16),
            jax.ShapeDtypeStruct((kv_count, 1, lanes), jnp.float32),
            jax.ShapeDtypeStruct((kv_count, 1, lanes), jnp.float32),
            jax.ShapeDtypeStruct((kv_count, width, lanes), jnp.float32),
        ],
        in_specs=[smem] * 2 + [vmem] * (2 + len(blocks)),
        out_specs=[vmem] * 4,
        scratch_shapes=[pltpu.VMEM((len(blocks) * block, lanes), jnp.float32)],
        compiler_params=params,
        cost_estimate=cost(len(blocks)),
        name="near",
    )(*scalars, queries, partner_queries, *blocks)
    return pl.pallas_call(
        functools.partial(far_kernel, devices=devices, group=group),
        out_shape=jax.ShapeDtypeStruct((block, 2 * heads, width), jnp.bfloat16),
        in_specs=[smem] * 2 + [vmem] * 6,
        out_specs=pl.BlockSpec(memory_space=pl.ANY),
        scratch_shapes=[
            pltpu.VMEM((4 * block, lanes), jnp.float32),
            pltpu.VMEM((kv_count // 2, block, 2 * group, width), jnp.bfloat16),
            pltpu.SemaphoreType.DMA((kv_count // 2,)),
        ],
        compiler_params=params,
        cost_estimate=cost(4),
        name="far",
    )(*scalars, *state, early, late)


def solution(mesh):
    in_specs = (P("ctx", "head", None), P("ctx", "head", None), P("ctx", "head", None), P())
    out_specs = P(("ctx", "head"), None, None)
    return jax.shard_map(shards, mesh=mesh, in_specs=in_specs, out_specs=out_specs, check_vma=False)
```

time: 49.4 us -> 45 us (0.911)
  the two profiles are of different devices: /device:TPU:27 before, /device:TPU:19 now
where the time goes in v4:
time: 45 us; the launch traced here: 44.7 us
  starting transfers between devices  17 us (38%)
  waiting for transfers between devices  16.6 us (37%)
  Pallas kernels  7.87 us (17%)
  local copies, waits for them, and re-layouts  2.97 us (7%)
    ppermute x6, waiting for transfers between devices, from_below(): return lax.ppermute(array, ('ctx', 'head'), pairs)  16.6 us
    ppermute x6, starting transfers between devices, from_below(): return lax.ppermute(array, ('ctx', 'head'), pairs)  16.1 us
    pallas_call x1, Pallas kernels, shards(): pl.pallas_call(functools.partial(far_kernel, devices=devices, group=group...  3.53 us
    pallas_call x1, Pallas kernels, shards(): pl.pallas_call(functools.partial(near_kernel, group=group), out_shape=[ja...  3.11 us
    pallas_call x2, Pallas kernels, bundle(): pl.pallas_call(functools.partial(bundle_kernel, devices=devices, choices=...  1.22 us
    dynamic_slice x1, local copies, waits for them, and re-layouts, shards(): lax.dynamic_slice_in_dim(queries, (1 - core) * block, block, 0)  1.08 us
    another operation x1, local copies, waits for them, and re-layouts, shards(): packed = jnp.stack([key_heads, value_head_rows])  0.94 us
    unnamed x5, local copies, waits for them, and re-layouts  0.93 us
  transfers between devices with their start and end apart: 8, of which 6 were waited for; matrix products, arithmetic and copies ran while one was open for 3% of the time, Pallas kernels for 10%

profile of v4, /device:TPU:19, one launch (start us, length us, event | category | flops | bytes accessed | tf_op | source)
XLA Modules:
  0.0 44.7 jit_solution(4577694495052765492)
XLA Ops:
  0.0 0.9 %copy_dynamic-update-slice_fusion.1 = bf16[2,2,64,4,128]{4,2,3,0,1:T(8,128)(2,1)S(1)} fusion(bf16[1,2,64,4,128]{4,3,2,1,0:T(4,128)(2,1)} %bitcast.13), kind=kLoop, calls=%fused_computation.4 | loop fusion | bytes 262144
  0.9 0.9 %copy_dynamic-update-slice_fusion = bf16[2,2,64,4,128]{4,2,3,0,1:T(8,128)(2,1)S(1)} fusion(bf16[2,2,64,4,128]{4,2,3,0,1:T(8,128)(2,1)S(1)} %copy_dynamic-update-slice_fusion.1, bf16[1,2,64,4,128]{4,3,2,1,0:T(4,128)(2,1)} %bitcast.14), kind=kLoop, calls=%fused_computation.3 | loop fusion | bytes 262144 | tf_op jit(solution)/shard_map/stack | solution.py:217
  1.9 0.7 %collective-permute-start = (bf16[2,4,64,128]{3,2,1,0:T(8,128)(2,1)S(1)}, bf16[2,4,64,128]{3,2,1,0:T(8,128)(2,1)S(1)}, u32[]{:S(2)}, u32[]{:S(2)}) collective-permute-start(bf16[2,4,64,128]{3,2,1,0:T(8,128)(2,1)S(1)} %dynamic-slice_bitcast_fusion), channel_id=1, source_target_pairs={{0,1},{1,0},{2,3},{3,2},{4,5},{5,4},{6,7},{7,6},{8,9},{9,8},{10,11... | collective-permute-start | bytes 393224 | tf_op jit(solution)/shard_map/ppermute | solution.py:208
  2.6 1.1 %constant_dynamic-slice_fusion = bf16[64,32,128]{2,1,0:T(8,128)(2,1)S(1)} fusion(bf16[128,32,128]{2,1,0:T(8,128)(2,1)} %queries.1, s32[]{:T(128)S(6)} %select_n.32), kind=kLoop, calls=%fused_computation.6 | loop fusion | bytes 1048580 | tf_op jit(solution)/shard_map/dynamic_slice | solution.py:224
  3.7 0.1 collective-permute-start.1
  3.8 0.0 copy-start
  3.8 0.0 copy-start.1
  3.8 0.0 collective-permute-done
  3.9 3.1 %collective-permute-start.2 = (bf16[2,8,64,128]{3,2,1,0:T(8,128)(2,1)S(1)}, bf16[2,8,64,128]{3,2,1,0:T(8,128)(2,1)S(1)}, u32[]{:S(2)}, u32[]{:S(2)}) collective-permute-start(bf16[2,8,64,128]{3,2,1,0:T(8,128)(2,1)S(1)} %pad_maximum_fusion.refs_0_), channel_id=1, source_target_pairs={{0,6},{2,8},{4,10},{6,12},{8,14},{10,16},{12,18},{14,20},{16,22},{... | collective-permute-start | bytes 786440 | tf_op jit(solution)/shard_map/ppermute | solution.py:215
  7.0 0.0 collective-permute-done.1.partner_queries
  7.1 2.1 %collective-permute-start.4 = (bf16[2,8,64,128]{3,2,1,0:T(8,128)(2,1)S(1)}, bf16[2,8,64,128]{3,2,1,0:T(8,128)(2,1)S(1)}, u32[]{:S(2)}, u32[]{:S(2)}) collective-permute-start(bf16[2,8,64,128]{3,2,1,0:T(8,128)(2,1)S(1)} %pad_maximum_fusion.refs_0_), channel_id=1, source_target_pairs={{0,4},{2,6},{4,8},{6,10},{8,12},{10,14},{12,16},{14,18},{16,20},{1... | collective-permute-start | bytes 786440 | tf_op jit(solution)/shard_map/ppermute | solution.py:215
  9.2 1.9 %collective-permute-start.5 = (bf16[2,8,64,128]{3,2,1,0:T(8,128)(2,1)S(1)}, bf16[2,8,64,128]{3,2,1,0:T(8,128)(2,1)S(1)}, u32[]{:S(2)}, u32[]{:S(2)}) collective-permute-start(bf16[2,8,64,128]{3,2,1,0:T(8,128)(2,1)S(1)} %pad_maximum_fusion.refs_0_), channel_id=1, source_target_pairs={{0,8},{2,10},{4,12},{6,14},{8,16},{10,18},{12,20},{14,22},{16,24},... | collective-permute-start | bytes 786440 | tf_op jit(solution)/shard_map/ppermute | solution.py:215
  11.1 1.3 %collective-permute-done.2.refs_3_.refs_2_ = bf16[2,8,64,128]{3,2,1,0:T(8,128)(2,1)S(1)} collective-permute-done((bf16[2,8,64,128]{3,2,1,0:T(8,128)(2,1)S(1)}, bf16[2,8,64,128]{3,2,1,0:T(8,128)(2,1)S(1)}, u32[]{:S(2)}, u32[]{:S(2)}) %collective-permute-start.2) | collective-permute-done | bytes 262176 | tf_op jit(solution)/shard_map/ppermute | solution.py:215
  12.4 4.8 %collective-permute-start.3 = (bf16[2,8,64,128]{3,2,1,0:T(8,128)(2,1)S(1)}, bf16[2,8,64,128]{3,2,1,0:T(8,128)(2,1)S(1)}, u32[]{:S(2)}, u32[]{:S(2)}) collective-permute-start(bf16[2,8,64,128]{3,2,1,0:T(8,128)(2,1)S(1)} %pad_maximum_fusion.refs_0_), channel_id=1, source_target_pairs={{0,2},{2,4},{4,6},{6,8},{8,10},{10,12},{12,14},{14,16},{16,18},{18... | collective-permute-start | bytes 786440 | tf_op jit(solution)/shard_map/ppermute | solution.py:215
  17.2 0.1 pad_add_fusion.position
  17.3 2.4 %collective-permute-done.4.refs_2_.refs_1_ = bf16[2,8,64,128]{3,2,1,0:T(8,128)(2,1)S(1)} collective-permute-done((bf16[2,8,64,128]{3,2,1,0:T(8,128)(2,1)S(1)}, bf16[2,8,64,128]{3,2,1,0:T(8,128)(2,1)S(1)}, u32[]{:S(2)}, u32[]{:S(2)}) %collective-permute-start.4) | collective-permute-done | bytes 262176 | tf_op jit(solution)/shard_map/ppermute | solution.py:215
  19.6 0.9 %collective-permute-done.5.refs_4_.refs_3_ = bf16[2,8,64,128]{3,2,1,0:T(8,128)(2,1)S(1)} collective-permute-done((bf16[2,8,64,128]{3,2,1,0:T(8,128)(2,1)S(1)}, bf16[2,8,64,128]{3,2,1,0:T(8,128)(2,1)S(1)}, u32[]{:S(2)}, u32[]{:S(2)}) %collective-permute-start.5) | collective-permute-done | bytes 262176 | tf_op jit(solution)/shard_map/ppermute | solution.py:215
  20.5 0.6 %early.1 = bf16[2,2,8,64,128]{4,3,2,1,0:T(8,128)(2,1)S(1)} custom-call(s32[2]{0:T(128)S(1)} %pad_add_fusion.position, bf16[2,8,64,128]{3,2,1,0:T(8,128)(2,1)S(1)} %pad_maximum_fusion.refs_0_, bf16[2,8,64,128]{3,2,1,0:T(8,128)(2,1)S(1)} %collective-permute-done.4.refs_2_.refs_1_, bf16[2,8,64,128]{3,2,1,0:T(8,128)(2,1)S(1)} %collective-permute-done.2.refs_3_.refs_2_, ...), custom_call_target="tpu_custom_call" | custom-call | tf_op jit(solution)/shard_map/early/pallas_call | solution.py:236
  21.1 2.1 %collective-permute-start.6 = (bf16[2,2,8,64,128]{4,3,2,1,0:T(8,128)(2,1)S(1)}, bf16[2,2,8,64,128]{4,3,2,1,0:T(8,128)(2,1)S(1)}, u32[]{:S(2)}, u32[]{:S(2)}) collective-permute-start(bf16[2,2,8,64,128]{4,3,2,1,0:T(8,128)(2,1)S(1)} %early.1), channel_id=1, source_target_pairs={{0,8},{2,10},{4,12},{6,14},{8,16},{10,18},{12,20},{14,22},{16,24},... | collective-permute-start | bytes 1572872 | tf_op jit(solution)/shard_map/ppermute | solution.py:215
  23.2 0.5 %collective-permute-done.3.refs_1_.refs_0_ = bf16[2,8,64,128]{3,2,1,0:T(8,128)(2,1)S(1)} collective-permute-done((bf16[2,8,64,128]{3,2,1,0:T(8,128)(2,1)S(1)}, bf16[2,8,64,128]{3,2,1,0:T(8,128)(2,1)S(1)}, u32[]{:S(2)}, u32[]{:S(2)}) %collective-permute-start.3) | collective-permute-done | bytes 262176 | tf_op jit(solution)/shard_map/ppermute | solution.py:215
  23.7 0.6 %late.1 = bf16[2,2,8,64,128]{4,3,2,1,0:T(8,128)(2,1)S(1)} custom-call(s32[2]{0:T(128)S(1)} %pad_add_fusion.position, bf16[2,8,64,128]{3,2,1,0:T(8,128)(2,1)S(1)} %collective-permute-done.3.refs_1_.refs_0_, bf16[2,8,64,128]{3,2,1,0:T(8,128)(2,1)S(1)} %collective-permute-done.4.refs_2_.refs_1_, ...), custom_call_target="tpu_custom_call" | custom-call | tf_op jit(solution)/shard_map/late/pallas_call | solution.py:236
  24.4 2.1 %collective-permute-start.7 = (bf16[2,2,8,64,128]{4,3,2,1,0:T(8,128)(2,1)S(1)}, bf16[2,2,8,64,128]{4,3,2,1,0:T(8,128)(2,1)S(1)}, u32[]{:S(2)}, u32[]{:S(2)}) collective-permute-start(bf16[2,2,8,64,128]{4,3,2,1,0:T(8,128)(2,1)S(1)} %late.1), channel_id=1, source_target_pairs={{0,8},{2,10},{4,12},{6,14},{8,16},{10,18},{12,20},{14,22},{16,24},... | collective-permute-start | bytes 1572872 | tf_op jit(solution)/shard_map/ppermute | solution.py:215
  26.5 0.0 copy-done
  26.5 0.0 copy-done.1
  26.5 3.1 %near.1 = (bf16[8,512,128]{2,1,0:T(8,128)(2,1)S(1)}, f32[8,1,512]{2,1,0:T(1,128)S(1)}, f32[8,1,512]{2,1,0:T(1,128)S(1)}, f32[8,128,512]{2,1,0:T(8,128)S(1)}) custom-call(s32[8]{0:T(128)S(1)} %copy-done.1, s32[2]{0:T(128)S(1)} %pad_add_fusion.position, bf16[128,32,128]{2,1,0:T(8,128)(2,1)S(1)} %copy-done, ...), custom_call_target="tpu_custom_call" | custom-call | flops 671088640 | bytes 4194304 | tf_op jit(solution)/shard_map/near/pallas_call | solution.py:262
  29.6 4.3 %collective-permute-done.6.early = bf16[2,2,8,64,128]{4,3,2,1,0:T(8,128)(2,1)S(1)} collective-permute-done((bf16[2,2,8,64,128]{4,3,2,1,0:T(8,128)(2,1)S(1)}, bf16[2,2,8,64,128]{4,3,2,1,0:T(8,128)(2,1)S(1)}, u32[]{:S(2)}, u32[]{:S(2)}) %collective-permute-start.6) | collective-permute-done | bytes 524320 | tf_op jit(solution)/shard_map/ppermute | solution.py:215
  33.9 7.3 %collective-permute-done.7.late = bf16[2,2,8,64,128]{4,3,2,1,0:T(8,128)(2,1)S(1)} collective-permute-done((bf16[2,2,8,64,128]{4,3,2,1,0:T(8,128)(2,1)S(1)}, bf16[2,2,8,64,128]{4,3,2,1,0:T(8,128)(2,1)S(1)}, u32[]{:S(2)}, u32[]{:S(2)}) %collective-permute-start.7) | collective-permute-done | bytes 524320 | tf_op jit(solution)/shard_map/ppermute | solution.py:215
  41.2 3.5 %far.1 = bf16[64,64,128]{2,1,0:T(8,128)(2,1)} custom-call(s32[8]{0:T(128)S(1)} %copy-done.1, s32[2]{0:T(128)S(1)} %pad_add_fusion.position, bf16[8,512,128]{2,1,0:T(8,128)(2,1)S(1)} %get-tuple-element.17.folded, f32[8,1,512]{2,1,0:T(1,128)S(1)} %get-tuple-element.18.peak, f32[8,1,512]{2,1,0:T(1,128)S(1)} %get-tuple-element.19.sums, ...), custom_call_target="tpu_custom_call" | custom-call | flops 536870912 | bytes 4194304 | tf_op jit(solution)/shard_map/far/pallas_call | solution.py:277
  (3 shorter events, 0.1 us)
Async XLA Ops:
  1.9 1.9 %collective-permute-start = (bf16[2,4,64,128]{3,2,1,0:T(8,128)(2,1)S(1)}, bf16[2,4,64,128]{3,2,1,0:T(8,128)(2,1)S(1)}, u32[]{:S(2)}, u32[]{:S(2)}) collective-permute-start(bf16[2,4,64,128]{3,2,1,0:T(8,128)(2,1)S(1)} %dynamic-slice_bitcast_fusion), channel_id=1, source_target_pairs={{0,1},{1,0},{2,3},{3,2},{4,5},{5,4},{6,7},{7,6},{8,9},{9,8},{10,11... | collective-permute-start | bytes 393224 | tf_op jit(solution)/shard_map/ppermute | solution.py:208
  3.7 3.3 %collective-permute-start.1 = (bf16[64,32,128]{2,1,0:T(8,128)(2,1)S(1)}, bf16[64,32,128]{2,1,0:T(8,128)(2,1)S(1)}, u32[]{:S(2)}, u32[]{:S(2)}) collective-permute-start(bf16[64,32,128]{2,1,0:T(8,128)(2,1)S(1)} %constant_dynamic-slice_fusion), channel_id=1, source_target_pairs={{0,1},{1,0},{2,3},{3,2},{4,5},{5,4},{6,7},{7,6},{8,9},{9,8},{10,11... | collective-permute-start | bytes 1572872 | tf_op jit(solution)/shard_map/ppermute | solution.py:208
  3.8 22.6 %copy-start = (bf16[128,32,128]{2,1,0:T(8,128)(2,1)S(1)}, bf16[128,32,128]{2,1,0:T(8,128)(2,1)}, u32[]{:S(2)}) copy-start(bf16[128,32,128]{2,1,0:T(8,128)(2,1)} %queries.1) | copy-start | bytes 3145732
  3.8 22.7 %copy-start.1 = (s32[8]{0:T(128)S(1)}, s32[8]{0:T(128)}, u32[]{:S(2)}) copy-start(s32[8]{0:T(128)} %doc_lengths.3) | copy-start | bytes 100
  3.9 8.5 %collective-permute-start.2 = (bf16[2,8,64,128]{3,2,1,0:T(8,128)(2,1)S(1)}, bf16[2,8,64,128]{3,2,1,0:T(8,128)(2,1)S(1)}, u32[]{:S(2)}, u32[]{:S(2)}) collective-permute-start(bf16[2,8,64,128]{3,2,1,0:T(8,128)(2,1)S(1)} %pad_maximum_fusion.refs_0_), channel_id=1, source_target_pairs={{0,6},{2,8},{4,10},{6,12},{8,14},{10,16},{12,18},{14,20},{16,22},{... | collective-permute-start | bytes 786440 | tf_op jit(solution)/shard_map/ppermute | solution.py:215
  7.1 12.6 %collective-permute-start.4 = (bf16[2,8,64,128]{3,2,1,0:T(8,128)(2,1)S(1)}, bf16[2,8,64,128]{3,2,1,0:T(8,128)(2,1)S(1)}, u32[]{:S(2)}, u32[]{:S(2)}) collective-permute-start(bf16[2,8,64,128]{3,2,1,0:T(8,128)(2,1)S(1)} %pad_maximum_fusion.refs_0_), channel_id=1, source_target_pairs={{0,4},{2,6},{4,8},{6,10},{8,12},{10,14},{12,16},{14,18},{16,20},{1... | collective-permute-start | bytes 786440 | tf_op jit(solution)/shard_map/ppermute | solution.py:215
  9.2 11.3 %collective-permute-start.5 = (bf16[2,8,64,128]{3,2,1,0:T(8,128)(2,1)S(1)}, bf16[2,8,64,128]{3,2,1,0:T(8,128)(2,1)S(1)}, u32[]{:S(2)}, u32[]{:S(2)}) collective-permute-start(bf16[2,8,64,128]{3,2,1,0:T(8,128)(2,1)S(1)} %pad_maximum_fusion.refs_0_), channel_id=1, source_target_pairs={{0,8},{2,10},{4,12},{6,14},{8,16},{10,18},{12,20},{14,22},{16,24},... | collective-permute-start | bytes 786440 | tf_op jit(solution)/shard_map/ppermute | solution.py:215
  12.4 11.4 %collective-permute-start.3 = (bf16[2,8,64,128]{3,2,1,0:T(8,128)(2,1)S(1)}, bf16[2,8,64,128]{3,2,1,0:T(8,128)(2,1)S(1)}, u32[]{:S(2)}, u32[]{:S(2)}) collective-permute-start(bf16[2,8,64,128]{3,2,1,0:T(8,128)(2,1)S(1)} %pad_maximum_fusion.refs_0_), channel_id=1, source_target_pairs={{0,2},{2,4},{4,6},{6,8},{8,10},{10,12},{12,14},{14,16},{16,18},{18... | collective-permute-start | bytes 786440 | tf_op jit(solution)/shard_map/ppermute | solution.py:215
  21.1 12.8 %collective-permute-start.6 = (bf16[2,2,8,64,128]{4,3,2,1,0:T(8,128)(2,1)S(1)}, bf16[2,2,8,64,128]{4,3,2,1,0:T(8,128)(2,1)S(1)}, u32[]{:S(2)}, u32[]{:S(2)}) collective-permute-start(bf16[2,2,8,64,128]{4,3,2,1,0:T(8,128)(2,1)S(1)} %early.1), channel_id=1, source_target_pairs={{0,8},{2,10},{4,12},{6,14},{8,16},{10,18},{12,20},{14,22},{16,24},... | collective-permute-start | bytes 1572872 | tf_op jit(solution)/shard_map/ppermute | solution.py:215
  24.4 16.8 %collective-permute-start.7 = (bf16[2,2,8,64,128]{4,3,2,1,0:T(8,128)(2,1)S(1)}, bf16[2,2,8,64,128]{4,3,2,1,0:T(8,128)(2,1)S(1)}, u32[]{:S(2)}, u32[]{:S(2)}) collective-permute-start(bf16[2,2,8,64,128]{4,3,2,1,0:T(8,128)(2,1)S(1)} %late.1), channel_id=1, source_target_pairs={{0,8},{2,10},{4,12},{6,14},{8,16},{10,18},{12,20},{14,22},{16,24},... | collective-permute-start | bytes 1572872 | tf_op jit(solution)/shard_map/ppermute | solution.py:215

commit v5 on v4

--- a/solution.py
+++ b/solution.py
@@ -226,7 +226,6 @@
     own, partner_queries = lax.optimization_barrier((own, partner_queries))
     by_two = from_below(own, 2)
     by_four = from_below(own, 4)
-    own, by_three = lax.optimization_barrier((own, by_three))
     by_one = from_below(own, 1)
 
     scalars = (doc_lengths, jnp.stack([stretch, core]))

time: 45 us -> 47.1 us (1.047)
  waiting for transfers between devices: 16.6 us -> 20.4 us
  starting transfers between devices: 17 us -> 14.9 us
    ppermute x6, waiting for transfers between devices: 16.6 us -> 19.1 us  [from_below(): return lax.ppermute(array, ('ctx', 'head'), pairs)]
    ppermute x6, starting transfers between devices: 16.1 us -> 14.1 us  [from_below(): return lax.ppermute(array, ('ctx', 'head'), pairs)]
    ppermute x2, waiting for transfers between devices: 0.01 us -> 1.31 us  [swap(): return lax.ppermute(array, 'head', [(0, 1), (1, 0)])]
  transfers between devices with their start and end apart: 8 -> 8, of which waited for: 6 -> 4; matrix products, arithmetic and copies ran while one was open for 3% -> 4% of each run, Pallas kernels for 10% -> 9%
where the time goes in v5:
time: 47.1 us; the launch traced here: 46.5 us
  waiting for transfers between devices  20.4 us (43%)
  starting transfers between devices  14.9 us (32%)
  Pallas kernels  7.87 us (17%)
  local copies, waits for them, and re-layouts  2.97 us (6%)
    ppermute x6, waiting for transfers between devices, from_below(): return lax.ppermute(array, ('ctx', 'head'), pairs)  19.1 us
    ppermute x6, starting transfers between devices, from_below(): return lax.ppermute(array, ('ctx', 'head'), pairs)  14.1 us
    pallas_call x1, Pallas kernels, shards(): pl.pallas_call(functools.partial(far_kernel, devices=devices, group=group...  3.53 us
    pallas_call x1, Pallas kernels, shards(): pl.pallas_call(functools.partial(near_kernel, group=group), out_shape=[ja...  3.11 us
    ppermute x2, waiting for transfers between devices, swap(): return lax.ppermute(array, 'head', [(0, 1), (1, 0)])  1.31 us
    pallas_call x2, Pallas kernels, bundle(): pl.pallas_call(functools.partial(bundle_kernel, devices=devices, choices=...  1.22 us
    dynamic_slice x1, local copies, waits for them, and re-layouts, shards(): lax.dynamic_slice_in_dim(queries, (1 - core) * block, block, 0)  1.08 us
    another operation x1, local copies, waits for them, and re-layouts, shards(): packed = jnp.stack([key_heads, value_head_rows])  0.94 us
  transfers between devices with their start and end apart: 8, of which 4 were waited for; matrix products, arithmetic and copies ran while one was open for 4% of the time, Pallas kernels for 9%

profile of v5, /device:TPU:19, one launch (start us, length us, event | category | flops | bytes accessed | tf_op | source)
XLA Modules:
  0.0 46.5 jit_solution(1957855927242556825)
XLA Ops:
  0.0 1.1 %constant_dynamic-slice_fusion = bf16[64,32,128]{2,1,0:T(8,128)(2,1)S(1)} fusion(bf16[128,32,128]{2,1,0:T(8,128)(2,1)} %queries.1, s32[]{:T(128)S(6)} %select_n.32), kind=kLoop, calls=%fused_computation.6 | loop fusion | bytes 1048580 | tf_op jit(solution)/shard_map/dynamic_slice | solution.py:224
  1.1 0.7 %collective-permute-start.1 = (bf16[64,32,128]{2,1,0:T(8,128)(2,1)S(1)}, bf16[64,32,128]{2,1,0:T(8,128)(2,1)S(1)}, u32[]{:S(2)}, u32[]{:S(2)}) collective-permute-start(bf16[64,32,128]{2,1,0:T(8,128)(2,1)S(1)} %constant_dynamic-slice_fusion), channel_id=1, source_target_pairs={{0,1},{1,0},{2,3},{3,2},{4,5},{5,4},{6,7},{7,6},{8,9},{9,8},{10,11... | collective-permute-start | bytes 1572872 | tf_op jit(solution)/shard_map/ppermute | solution.py:208
  1.8 0.9 %copy_dynamic-update-slice_fusion.1 = bf16[2,2,64,4,128]{4,2,3,0,1:T(8,128)(2,1)S(1)} fusion(bf16[1,2,64,4,128]{4,3,2,1,0:T(4,128)(2,1)} %bitcast.13), kind=kLoop, calls=%fused_computation.4 | loop fusion | bytes 262144
  2.7 0.9 %copy_dynamic-update-slice_fusion = bf16[2,2,64,4,128]{4,2,3,0,1:T(8,128)(2,1)S(1)} fusion(bf16[2,2,64,4,128]{4,2,3,0,1:T(8,128)(2,1)S(1)} %copy_dynamic-update-slice_fusion.1, bf16[1,2,64,4,128]{4,3,2,1,0:T(4,128)(2,1)} %bitcast.14), kind=kLoop, calls=%fused_computation.3 | loop fusion | bytes 262144 | tf_op jit(solution)/shard_map/stack | solution.py:217
  3.7 0.1 collective-permute-start
  3.8 0.0 copy-start
  3.8 0.0 copy-start.1
  3.8 1.3 %collective-permute-done = bf16[2,4,64,128]{3,2,1,0:T(8,128)(2,1)S(1)} collective-permute-done((bf16[2,4,64,128]{3,2,1,0:T(8,128)(2,1)S(1)}, bf16[2,4,64,128]{3,2,1,0:T(8,128)(2,1)S(1)}, u32[]{:S(2)}, u32[]{:S(2)}) %collective-permute-start) | collective-permute-done | bytes 131104 | tf_op jit(solution)/shard_map/ppermute | solution.py:208
  5.2 3.0 %collective-permute-start.4 = (bf16[2,8,64,128]{3,2,1,0:T(8,128)(2,1)S(1)}, bf16[2,8,64,128]{3,2,1,0:T(8,128)(2,1)S(1)}, u32[]{:S(2)}, u32[]{:S(2)}) collective-permute-start(bf16[2,8,64,128]{3,2,1,0:T(8,128)(2,1)S(1)} %pad_maximum_fusion.refs_0_), channel_id=1, source_target_pairs={{0,6},{2,8},{4,10},{6,12},{8,14},{10,16},{12,18},{14,20},{16,22},{... | collective-permute-start | bytes 786440 | tf_op jit(solution)/shard_map/ppermute | solution.py:215
  8.2 0.0 collective-permute-done.1.partner_queries
  8.2 2.1 %collective-permute-start.3 = (bf16[2,8,64,128]{3,2,1,0:T(8,128)(2,1)S(1)}, bf16[2,8,64,128]{3,2,1,0:T(8,128)(2,1)S(1)}, u32[]{:S(2)}, u32[]{:S(2)}) collective-permute-start(bf16[2,8,64,128]{3,2,1,0:T(8,128)(2,1)S(1)} %pad_maximum_fusion.refs_0_), channel_id=1, source_target_pairs={{0,4},{2,6},{4,8},{6,10},{8,12},{10,14},{12,16},{14,18},{16,20},{1... | collective-permute-start | bytes 786440 | tf_op jit(solution)/shard_map/ppermute | solution.py:215
  10.4 1.9 %collective-permute-start.5 = (bf16[2,8,64,128]{3,2,1,0:T(8,128)(2,1)S(1)}, bf16[2,8,64,128]{3,2,1,0:T(8,128)(2,1)S(1)}, u32[]{:S(2)}, u32[]{:S(2)}) collective-permute-start(bf16[2,8,64,128]{3,2,1,0:T(8,128)(2,1)S(1)} %pad_maximum_fusion.refs_0_), channel_id=1, source_target_pairs={{0,8},{2,10},{4,12},{6,14},{8,16},{10,18},{12,20},{14,22},{16,24},... | collective-permute-start | bytes 786440 | tf_op jit(solution)/shard_map/ppermute | solution.py:215
  12.3 3.1 %collective-permute-start.2 = (bf16[2,8,64,128]{3,2,1,0:T(8,128)(2,1)S(1)}, bf16[2,8,64,128]{3,2,1,0:T(8,128)(2,1)S(1)}, u32[]{:S(2)}, u32[]{:S(2)}) collective-permute-start(bf16[2,8,64,128]{3,2,1,0:T(8,128)(2,1)S(1)} %pad_maximum_fusion.refs_0_), channel_id=1, source_target_pairs={{0,2},{2,4},{4,6},{6,8},{8,10},{10,12},{12,14},{14,16},{16,18},{18... | collective-permute-start | bytes 786440 | tf_op jit(solution)/shard_map/ppermute | solution.py:215
  15.4 0.1 pad_add_fusion.position
  15.4 0.0 collective-permute-done.4.refs_3_.refs_2_
  15.4 8.3 %collective-permute-done.3.refs_2_.refs_1_ = bf16[2,8,64,128]{3,2,1,0:T(8,128)(2,1)S(1)} collective-permute-done((bf16[2,8,64,128]{3,2,1,0:T(8,128)(2,1)S(1)}, bf16[2,8,64,128]{3,2,1,0:T(8,128)(2,1)S(1)}, u32[]{:S(2)}, u32[]{:S(2)}) %collective-permute-start.3) | collective-permute-done | bytes 262176 | tf_op jit(solution)/shard_map/ppermute | solution.py:215
  23.7 0.0 collective-permute-done.5.refs_4_.refs_3_
  23.8 0.6 %early.1 = bf16[2,2,8,64,128]{4,3,2,1,0:T(8,128)(2,1)S(1)} custom-call(s32[2]{0:T(128)S(1)} %pad_add_fusion.position, bf16[2,8,64,128]{3,2,1,0:T(8,128)(2,1)S(1)} %pad_maximum_fusion.refs_0_, bf16[2,8,64,128]{3,2,1,0:T(8,128)(2,1)S(1)} %collective-permute-done.3.refs_2_.refs_1_, bf16[2,8,64,128]{3,2,1,0:T(8,128)(2,1)S(1)} %collective-permute-done.4.refs_3_.refs_2_, ...), custom_call_target="tpu_custom_call" | custom-call | tf_op jit(solution)/shard_map/early/pallas_call | solution.py:235
  24.4 2.1 %collective-permute-start.6 = (bf16[2,2,8,64,128]{4,3,2,1,0:T(8,128)(2,1)S(1)}, bf16[2,2,8,64,128]{4,3,2,1,0:T(8,128)(2,1)S(1)}, u32[]{:S(2)}, u32[]{:S(2)}) collective-permute-start(bf16[2,2,8,64,128]{4,3,2,1,0:T(8,128)(2,1)S(1)} %early.1), channel_id=1, source_target_pairs={{0,8},{2,10},{4,12},{6,14},{8,16},{10,18},{12,20},{14,22},{16,24},... | collective-permute-start | bytes 1572872 | tf_op jit(solution)/shard_map/ppermute | solution.py:215
  26.5 0.0 collective-permute-done.2.refs_1_.refs_0_
  26.5 0.6 %late.1 = bf16[2,2,8,64,128]{4,3,2,1,0:T(8,128)(2,1)S(1)} custom-call(s32[2]{0:T(128)S(1)} %pad_add_fusion.position, bf16[2,8,64,128]{3,2,1,0:T(8,128)(2,1)S(1)} %collective-permute-done.2.refs_1_.refs_0_, bf16[2,8,64,128]{3,2,1,0:T(8,128)(2,1)S(1)} %collective-permute-done.3.refs_2_.refs_1_, ...), custom_call_target="tpu_custom_call" | custom-call | tf_op jit(solution)/shard_map/late/pallas_call | solution.py:235
  27.1 1.9 %collective-permute-start.7 = (bf16[2,2,8,64,128]{4,3,2,1,0:T(8,128)(2,1)S(1)}, bf16[2,2,8,64,128]{4,3,2,1,0:T(8,128)(2,1)S(1)}, u32[]{:S(2)}, u32[]{:S(2)}) collective-permute-start(bf16[2,2,8,64,128]{4,3,2,1,0:T(8,128)(2,1)S(1)} %late.1), channel_id=1, source_target_pairs={{0,8},{2,10},{4,12},{6,14},{8,16},{10,18},{12,20},{14,22},{16,24},... | collective-permute-start | bytes 1572872 | tf_op jit(solution)/shard_map/ppermute | solution.py:215
  29.0 0.0 copy-done
  29.0 0.0 copy-done.1
  29.0 3.1 %near.1 = (bf16[8,512,128]{2,1,0:T(8,128)(2,1)S(1)}, f32[8,1,512]{2,1,0:T(1,128)S(1)}, f32[8,1,512]{2,1,0:T(1,128)S(1)}, f32[8,128,512]{2,1,0:T(8,128)S(1)}) custom-call(s32[8]{0:T(128)S(1)} %copy-done.1, s32[2]{0:T(128)S(1)} %pad_add_fusion.position, bf16[128,32,128]{2,1,0:T(8,128)(2,1)S(1)} %copy-done, ...), custom_call_target="tpu_custom_call" | custom-call | flops 671088640 | bytes 4194304 | tf_op jit(solution)/shard_map/near/pallas_call | solution.py:261
  32.2 5.5 %collective-permute-done.6.early = bf16[2,2,8,64,128]{4,3,2,1,0:T(8,128)(2,1)S(1)} collective-permute-done((bf16[2,2,8,64,128]{4,3,2,1,0:T(8,128)(2,1)S(1)}, bf16[2,2,8,64,128]{4,3,2,1,0:T(8,128)(2,1)S(1)}, u32[]{:S(2)}, u32[]{:S(2)}) %collective-permute-start.6) | collective-permute-done | bytes 524320 | tf_op jit(solution)/shard_map/ppermute | solution.py:215
  37.6 5.3 %collective-permute-done.7.late = bf16[2,2,8,64,128]{4,3,2,1,0:T(8,128)(2,1)S(1)} collective-permute-done((bf16[2,2,8,64,128]{4,3,2,1,0:T(8,128)(2,1)S(1)}, bf16[2,2,8,64,128]{4,3,2,1,0:T(8,128)(2,1)S(1)}, u32[]{:S(2)}, u32[]{:S(2)}) %collective-permute-start.7) | collective-permute-done | bytes 524320 | tf_op jit(solution)/shard_map/ppermute | solution.py:215
  42.9 3.5 %far.1 = bf16[64,64,128]{2,1,0:T(8,128)(2,1)} custom-call(s32[8]{0:T(128)S(1)} %copy-done.1, s32[2]{0:T(128)S(1)} %pad_add_fusion.position, bf16[8,512,128]{2,1,0:T(8,128)(2,1)S(1)} %get-tuple-element.13.folded, f32[8,1,512]{2,1,0:T(1,128)S(1)} %get-tuple-element.14.peak, f32[8,1,512]{2,1,0:T(1,128)S(1)} %get-tuple-element.15.sums, ...), custom_call_target="tpu_custom_call" | custom-call | flops 536870912 | bytes 4194304 | tf_op jit(solution)/shard_map/far/pallas_call | solution.py:276
  (3 shorter events, 0.1 us)
Async XLA Ops:
  1.1 7.1 %collective-permute-start.1 = (bf16[64,32,128]{2,1,0:T(8,128)(2,1)S(1)}, bf16[64,32,128]{2,1,0:T(8,128)(2,1)S(1)}, u32[]{:S(2)}, u32[]{:S(2)}) collective-permute-start(bf16[64,32,128]{2,1,0:T(8,128)(2,1)S(1)} %constant_dynamic-slice_fusion), channel_id=1, source_target_pairs={{0,1},{1,0},{2,3},{3,2},{4,5},{5,4},{6,7},{7,6},{8,9},{9,8},{10,11... | collective-permute-start | bytes 1572872 | tf_op jit(solution)/shard_map/ppermute | solution.py:208
  3.7 1.4 %collective-permute-start = (bf16[2,4,64,128]{3,2,1,0:T(8,128)(2,1)S(1)}, bf16[2,4,64,128]{3,2,1,0:T(8,128)(2,1)S(1)}, u32[]{:S(2)}, u32[]{:S(2)}) collective-permute-start(bf16[2,4,64,128]{3,2,1,0:T(8,128)(2,1)S(1)} %dynamic-slice_bitcast_fusion), channel_id=1, source_target_pairs={{0,1},{1,0},{2,3},{3,2},{4,5},{5,4},{6,7},{7,6},{8,9},{9,8},{10,11... | collective-permute-start | bytes 393224 | tf_op jit(solution)/shard_map/ppermute | solution.py:208
  3.8 25.2 %copy-start = (bf16[128,32,128]{2,1,0:T(8,128)(2,1)S(1)}, bf16[128,32,128]{2,1,0:T(8,128)(2,1)}, u32[]{:S(2)}) copy-start(bf16[128,32,128]{2,1,0:T(8,128)(2,1)} %queries.1) | copy-start | bytes 3145732
  3.8 25.2 %copy-start.1 = (s32[8]{0:T(128)S(1)}, s32[8]{0:T(128)}, u32[]{:S(2)}) copy-start(s32[8]{0:T(128)} %doc_lengths.3) | copy-start | bytes 100
  5.2 10.3 %collective-permute-start.4 = (bf16[2,8,64,128]{3,2,1,0:T(8,128)(2,1)S(1)}, bf16[2,8,64,128]{3,2,1,0:T(8,128)(2,1)S(1)}, u32[]{:S(2)}, u32[]{:S(2)}) collective-permute-start(bf16[2,8,64,128]{3,2,1,0:T(8,128)(2,1)S(1)} %pad_maximum_fusion.refs_0_), channel_id=1, source_target_pairs={{0,6},{2,8},{4,10},{6,12},{8,14},{10,16},{12,18},{14,20},{16,22},{... | collective-permute-start | bytes 786440 | tf_op jit(solution)/shard_map/ppermute | solution.py:215
  8.2 15.5 %collective-permute-start.3 = (bf16[2,8,64,128]{3,2,1,0:T(8,128)(2,1)S(1)}, bf16[2,8,64,128]{3,2,1,0:T(8,128)(2,1)S(1)}, u32[]{:S(2)}, u32[]{:S(2)}) collective-permute-start(bf16[2,8,64,128]{3,2,1,0:T(8,128)(2,1)S(1)} %pad_maximum_fusion.refs_0_), channel_id=1, source_target_pairs={{0,4},{2,6},{4,8},{6,10},{8,12},{10,14},{12,16},{14,18},{16,20},{1... | collective-permute-start | bytes 786440 | tf_op jit(solution)/shard_map/ppermute | solution.py:215
  10.4 13.4 %collective-permute-start.5 = (bf16[2,8,64,128]{3,2,1,0:T(8,128)(2,1)S(1)}, bf16[2,8,64,128]{3,2,1,0:T(8,128)(2,1)S(1)}, u32[]{:S(2)}, u32[]{:S(2)}) collective-permute-start(bf16[2,8,64,128]{3,2,1,0:T(8,128)(2,1)S(1)} %pad_maximum_fusion.refs_0_), channel_id=1, source_target_pairs={{0,8},{2,10},{4,12},{6,14},{8,16},{10,18},{12,20},{14,22},{16,24},... | collective-permute-start | bytes 786440 | tf_op jit(solution)/shard_map/ppermute | solution.py:215
  12.3 14.2 %collective-permute-start.2 = (bf16[2,8,64,128]{3,2,1,0:T(8,128)(2,1)S(1)}, bf16[2,8,64,128]{3,2,1,0:T(8,128)(2,1)S(1)}, u32[]{:S(2)}, u32[]{:S(2)}) collective-permute-start(bf16[2,8,64,128]{3,2,1,0:T(8,128)(2,1)S(1)} %pad_maximum_fusion.refs_0_), channel_id=1, source_target_pairs={{0,2},{2,4},{4,6},{6,8},{8,10},{10,12},{12,14},{14,16},{16,18},{18... | collective-permute-start | bytes 786440 | tf_op jit(solution)/shard_map/ppermute | solution.py:215
  24.4 13.2 %collective-permute-start.6 = (bf16[2,2,8,64,128]{4,3,2,1,0:T(8,128)(2,1)S(1)}, bf16[2,2,8,64,128]{4,3,2,1,0:T(8,128)(2,1)S(1)}, u32[]{:S(2)}, u32[]{:S(2)}) collective-permute-start(bf16[2,2,8,64,128]{4,3,2,1,0:T(8,128)(2,1)S(1)} %early.1), channel_id=1, source_target_pairs={{0,8},{2,10},{4,12},{6,14},{8,16},{10,18},{12,20},{14,22},{16,24},... | collective-permute-start | bytes 1572872 | tf_op jit(solution)/shard_map/ppermute | solution.py:215
  27.1 15.9 %collective-permute-start.7 = (bf16[2,2,8,64,128]{4,3,2,1,0:T(8,128)(2,1)S(1)}, bf16[2,2,8,64,128]{4,3,2,1,0:T(8,128)(2,1)S(1)}, u32[]{:S(2)}, u32[]{:S(2)}) collective-permute-start(bf16[2,2,8,64,128]{4,3,2,1,0:T(8,128)(2,1)S(1)} %late.1), channel_id=1, source_target_pairs={{0,8},{2,10},{4,12},{6,14},{8,16},{10,18},{12,20},{14,22},{16,24},... | collective-permute-start | bytes 1572872 | tf_op jit(solution)/shard_map/ppermute | solution.py:215

commit v6 on v3

--- a/solution.py
+++ b/solution.py
@@ -31,24 +31,21 @@
     return jnp.where(allowed, 0.0, MASKED_SCORE)
 
 
-def weigh(q, keys, values, bias, floor):
+def score(q, keys, bias):
     factor = math.log2(math.e) / math.sqrt(q.shape[1])
     scores = lax.dot_general(
         keys, q, (((1,), (1,)), ((), ())), preferred_element_type=jnp.float32
     )
-    scores = scores * factor + bias
-    largest = jnp.max(scores, axis=0, keepdims=True)
-    if floor is not None:
-        largest = jnp.maximum(largest, floor)
-    weights = jnp.exp2(scores - largest)
-    total = jnp.sum(weights, axis=0, keepdims=True)
-    mixed = lax.dot_general(
+    return scores * factor + bias
+
+
+def mix(values, weights):
+    return lax.dot_general(
         values,
         weights.astype(jnp.bfloat16),
         (((0,), (0,)), ((), ())),
         preferred_element_type=jnp.float32,
     )
-    return largest, total, mixed
 
 
 def stage_kernel(doc_lengths, position, *refs, group, arrays, pieces, begins, ends):
@@ -64,14 +61,14 @@
         own_queries, partner_queries = take(2)
     else:
         (folded,) = take(1)
+        peak, sums, mixes = take(3)
     blocks = take(arrays)
-    earlier = None if begins else take(3)
     if ends:
         (out,) = take(1)
     else:
         if begins:
             (folded,) = take(1)
-        later = take(3)
+        new_peak, new_sums, new_mixes = take(3)
     (bias,) = take(1)
     if ends:
         staged, sems = take(2)
@@ -94,6 +91,8 @@
     for half in range(2):
         side = core if half == 0 else 1 - core
         for pair in range(kv_count // 4):
+            first_head = side * (kv_count // 2) + 2 * pair
+            slots = [half * (kv_count // 2) + 2 * pair + part for part in range(2)]
             if begins:
                 heads = slice(2 * pair * group, 2 * (pair + 1) * group)
                 if half == 0:
@@ -101,48 +100,63 @@
                 else:
                     both = partner_queries[:, heads, :]
                 both = both.astype(jnp.float32)
-            done = []
-            for part in range(2):
-                head = side * (kv_count // 2) + 2 * pair + part
-                slot = half * (kv_count // 2) + 2 * pair + part
-                if begins:
-                    q = both[:, part * group : (part + 1) * group, :]
-                    q = q.reshape(lanes, width).astype(jnp.bfloat16)
+                qs = [
+                    both[:, part * group : (part + 1) * group, :]
+                    .reshape(lanes, width)
+                    .astype(jnp.bfloat16)
+                    for part in range(2)
+                ]
+                for slot, q in zip(slots, qs):
                     folded[slot] = q
-                else:
-                    q = folded[slot]
-                floor = None if begins else earlier[0][slot]
-                largest, total, mixed = weigh(
-                    q, gather(0, head), gather(1, head), bias[...], floor
-                )
-                if not begins:
-                    shrink = jnp.exp2(floor - largest)
-                    total = total + earlier[1][slot] * shrink
-                    mixed = mixed + earlier[2][slot] * shrink
-                if ends:
-                    done.append((mixed / total).T.reshape(block, group, width))
-                else:
-                    later[0][slot] = largest
-                    later[1][slot] = total
-                    later[2][slot] = mixed
-            if ends:
-                number = half * (kv_count // 4) + pair
-                staged[number] = jnp.concatenate(done, axis=1).astype(staged.dtype)
-                begin = pl.multiple_of(side * half_heads + 2 * pair * group, 2 * group)
-                copies.append(
-                    pltpu.make_async_copy(
-                        staged.at[number], out.at[:, pl.ds(begin, 2 * group)], sems.at[number]
-                    )
-                )
-                copies[-1].start()
+            else:
+                qs = [folded[slot] for slot in slots]
+            scores = [
+                score(q, gather(0, first_head + part), bias[...]) for part, q in enumerate(qs)
+            ]
+            largest = [jnp.max(each, axis=0, keepdims=True) for each in scores]
+            if not begins:
+                largest = [jnp.maximum(top, peak[slot]) for top, slot in zip(largest, slots)]
+            weights = [jnp.exp2(each - top) for each, top in zip(scores, largest)]
+            totals = [jnp.sum(each, axis=0, keepdims=True) for each in weights]
+            mixed = [
+                mix(gather(1, first_head + part), each) for part, each in enumerate(weights)
+            ]
+            if not begins:
+                shrinks = [jnp.exp2(peak[slot] - top) for slot, top in zip(slots, largest)]
+                totals = [
+                    total + sums[slot] * shrink
+                    for total, slot, shrink in zip(totals, slots, shrinks)
+                ]
+            if not ends:
+                for part, slot in enumerate(slots):
+                    new_peak[slot] = largest[part]
+                    new_sums[slot] = totals[part]
+                    if begins:
+                        new_mixes[slot] = mixed[part]
+                    else:
+                        new_mixes[slot] = mixed[part] + mixes[slot] * shrinks[part]
+                continue
+            scales = [1.0 / total for total in totals]
+            done = [
+                (each * scale + mixes[slot] * (shrink * scale)).T.reshape(block, group, width)
+                for each, slot, shrink, scale in zip(mixed, slots, shrinks, scales)
+            ]
+            number = half * (kv_count // 4) + pair
+            staged[number] = jnp.concatenate(done, axis=1).astype(staged.dtype)
+            begin = pl.multiple_of(side * half_heads + 2 * pair * group, 2 * group)
+            copy = pltpu.make_async_copy(
+                staged.at[number], out.at[:, pl.ds(begin, 2 * group)], sems.at[number]
+            )
+            copy.start()
+            copies.append(copy)
     for copy in copies:
         copy.wait()
 
 
-def run_stage(name, scalars, queries, blocks, pieces, state, shape):
+def run_stage(name, scalars, queries, state, blocks, pieces, shape, ends=False):
     block, kv_count, group, width = shape
     lanes = block * group
-    begins, ends = state is None, name == "finish"
+    begins = state is None
     smem = pl.BlockSpec(memory_space=pltpu.SMEM)
     vmem = pl.BlockSpec(memory_space=pltpu.VMEM)
     rows = len(pieces) * block
@@ -163,7 +177,7 @@
         if begins:
             out_shape.insert(0, jax.ShapeDtypeStruct((kv_count, lanes, width), jnp.bfloat16))
         out_specs = [vmem] * len(out_shape)
-    operands = [*queries, *blocks, *([] if begins else state)]
+    operands = [*queries, *([] if begins else state), *blocks]
     work = kv_count * rows * lanes
     return pl.pallas_call(
         functools.partial(
@@ -178,7 +192,7 @@
         in_specs=[smem] * 2 + [vmem] * len(operands),
         out_specs=out_specs,
         scratch_shapes=scratch,
-        compiler_params=pltpu.CompilerParams(vmem_limit_bytes=32 * 2**20),
+        compiler_params=pltpu.CompilerParams(vmem_limit_bytes=14 * 2**20),
         cost_estimate=pl.CostEstimate(
             flops=4 * work * width, bytes_accessed=4 * 2**20, transcendentals=work
         ),
@@ -215,28 +229,32 @@
         [jnp.where(core == 0, keep, given), jnp.where(core == 0, given, keep)], axis=1
     )
     partner_queries = swap(lax.dynamic_slice_in_dim(queries, (1 - core) * block, block, 0))
+    by_three = from_below(own, 3)
+    own, partner_queries = lax.optimization_barrier((own, partner_queries))
     by_four = from_below(own, 4)
     by_one = from_below(own, 1)
-    own, partner_queries = lax.optimization_barrier((own, partner_queries))
     by_two = from_below(own, 2)
-    by_three = from_below(own, 3)
-    outer = from_below(jnp.stack([by_four, by_one]), 4)
-    inner = from_below(jnp.stack([by_three, by_two]), 4)
+    early = from_below(jnp.stack([by_three, by_four]), 4)
+    late = from_below(jnp.stack([by_one, by_two]), 4)
 
     scalars = (doc_lengths, jnp.stack([stretch, core]))
     shape = (block, 2 * kv_half, group, width)
-    near = tuple((at, None, 4 - at) for at in range(5))
+    near = tuple((at, None, at) for at in range(5))
     folded, *state = run_stage(
         "near",
         scalars,
         (queries, partner_queries),
-        (by_four, by_three, by_two, by_one, own),
+        None,
+        (own, by_one, by_two, by_three, by_four),
         near,
-        None,
         shape,
     )
-    state = run_stage("outer", scalars, (folded,), (outer,), ((0, 0, 8), (0, 1, 5)), state, shape)
-    return run_stage("finish", scalars, (folded,), (inner,), ((0, 0, 7), (0, 1, 6)), state, shape)
+    state = run_stage(
+        "middle", scalars, (folded,), state, (early,), ((0, 0, 7), (0, 1, 8)), shape
+    )
+    return run_stage(
+        "finish", scalars, (folded,), state, (late,), ((0, 0, 5), (0, 1, 6)), shape, ends=True
+    )
 
 
 def solution(mesh):

time: 49.9 us -> 47.1 us (0.944)
  Pallas kernels: 10.7 us -> 8.44 us
  starting transfers between devices: 15.8 us -> 15 us
  waiting for transfers between devices: 17.9 us -> 18.4 us
    pallas_call x3, Pallas kernels: 10.7 us -> 8.44 us  [run_stage(): pl.pallas_call(functools.partial(stage_kernel, group=group, arrays=len(bl...]
    ppermute x2, waiting for transfers between devices: 0.01 us -> 1.26 us  [swap(): return lax.ppermute(array, 'head', [(0, 1), (1, 0)])]
    ppermute x6, starting transfers between devices: 15 us -> 14.1 us  [from_below(): return lax.ppermute(array, ('ctx', 'head'), pairs)]
    ppermute x6, waiting for transfers between devices: 17.9 us -> 17.1 us  [from_below(): return lax.ppermute(array, ('ctx', 'head'), pairs)]
  transfers between devices with their start and end apart: 8 -> 8, of which waited for: 4 -> 4; matrix products, arithmetic and copies ran while one was open for 6% -> 8% of each run, Pallas kernels for 13% -> 11%
where the time goes in v6:
time: 47.1 us; the launch traced here: 46.8 us
  waiting for transfers between devices  18.4 us (39%)
  starting transfers between devices  15 us (32%)
  Pallas kernels  8.44 us (18%)
  local copies, waits for them, and re-layouts  2.97 us (6%)
  other arithmetic  1.82 us (4%)
    ppermute x6, waiting for transfers between devices, from_below(): return lax.ppermute(array, ('ctx', 'head'), pairs)  17.1 us
    ppermute x6, starting transfers between devices, from_below(): return lax.ppermute(array, ('ctx', 'head'), pairs)  14.1 us
    pallas_call x3, Pallas kernels, run_stage(): pl.pallas_call(functools.partial(stage_kernel, group=group, arrays=len(bl...  8.44 us
    ppermute x2, waiting for transfers between devices, swap(): return lax.ppermute(array, 'head', [(0, 1), (1, 0)])  1.26 us
    dynamic_slice x1, local copies, waits for them, and re-layouts, shards(): lax.dynamic_slice_in_dim(queries, (1 - core) * block, block, 0)  1.08 us
    another operation x1, local copies, waits for them, and re-layouts, shards(): packed = jnp.stack([key_heads, value_head_rows])  0.94 us
  transfers between devices with their start and end apart: 8, of which 4 were waited for; matrix products, arithmetic and copies ran while one was open for 8% of the time, Pallas kernels for 11%

profile of v6, /device:TPU:27, one launch (start us, length us, event | category | flops | bytes accessed | tf_op | source)
XLA Modules:
  0.0 46.8 jit_solution(6652613628842475200)
XLA Ops:
  0.0 1.1 %constant_dynamic-slice_fusion = bf16[64,32,128]{2,1,0:T(8,128)(2,1)S(1)} fusion(bf16[128,32,128]{2,1,0:T(8,128)(2,1)} %refs_0_.1, s32[]{:T(128)S(6)} %select_n.32), kind=kLoop, calls=%fused_computation.8 | loop fusion | bytes 1048580 | tf_op jit(solution)/shard_map/dynamic_slice | solution.py:231
  1.1 0.0 copy-start
  1.1 0.0 copy-start.1
  1.1 0.7 %collective-permute-start.1 = (bf16[64,32,128]{2,1,0:T(8,128)(2,1)S(1)}, bf16[64,32,128]{2,1,0:T(8,128)(2,1)S(1)}, u32[]{:S(2)}, u32[]{:S(2)}) collective-permute-start(bf16[64,32,128]{2,1,0:T(8,128)(2,1)S(1)} %constant_dynamic-slice_fusion), channel_id=1, source_target_pairs={{0,1},{1,0},{2,3},{3,2},{4,5},{5,4},{6,7},{7,6},{8,9},{9,8},{10,11... | collective-permute-start | bytes 1572872 | tf_op jit(solution)/shard_map/ppermute | solution.py:218
  1.8 0.9 %copy_dynamic-update-slice_fusion.1 = bf16[2,2,64,4,128]{4,2,3,0,1:T(8,128)(2,1)S(1)} fusion(bf16[1,2,64,4,128]{4,3,2,1,0:T(4,128)(2,1)} %bitcast.21), kind=kLoop, calls=%fused_computation.6 | loop fusion | bytes 262144
  2.8 0.9 %copy_dynamic-update-slice_fusion = bf16[2,2,64,4,128]{4,2,3,0,1:T(8,128)(2,1)S(1)} fusion(bf16[2,2,64,4,128]{4,2,3,0,1:T(8,128)(2,1)S(1)} %copy_dynamic-update-slice_fusion.1, bf16[1,2,64,4,128]{4,3,2,1,0:T(4,128)(2,1)} %bitcast.22), kind=kLoop, calls=%fused_computation.5 | loop fusion | bytes 262144 | tf_op jit(solution)/shard_map/stack | solution.py:224
  3.7 0.2 collective-permute-start
  3.9 1.3 %collective-permute-done = bf16[2,4,64,128]{3,2,1,0:T(8,128)(2,1)S(1)} collective-permute-done((bf16[2,4,64,128]{3,2,1,0:T(8,128)(2,1)S(1)}, bf16[2,4,64,128]{3,2,1,0:T(8,128)(2,1)S(1)}, u32[]{:S(2)}, u32[]{:S(2)}) %collective-permute-start) | collective-permute-done | bytes 131104 | tf_op jit(solution)/shard_map/ppermute | solution.py:218
  5.2 3.0 %collective-permute-start.4 = (bf16[2,8,64,128]{3,2,1,0:T(8,128)(2,1)S(1)}, bf16[2,8,64,128]{3,2,1,0:T(8,128)(2,1)S(1)}, u32[]{:S(2)}, u32[]{:S(2)}) collective-permute-start(bf16[2,8,64,128]{3,2,1,0:T(8,128)(2,1)S(1)} %pad_maximum_fusion.2.refs_2_), channel_id=1, source_target_pairs={{0,6},{2,8},{4,10},{6,12},{8,14},{10,16},{12,18},{14,20},{16,22},{... | collective-permute-start | bytes 786440 | tf_op jit(solution)/shard_map/ppermute | solution.py:222
  8.2 0.0 collective-permute-done.1.refs_1_
  8.2 2.1 %collective-permute-start.5 = (bf16[2,8,64,128]{3,2,1,0:T(8,128)(2,1)S(1)}, bf16[2,8,64,128]{3,2,1,0:T(8,128)(2,1)S(1)}, u32[]{:S(2)}, u32[]{:S(2)}) collective-permute-start(bf16[2,8,64,128]{3,2,1,0:T(8,128)(2,1)S(1)} %pad_maximum_fusion.2.refs_2_), channel_id=1, source_target_pairs={{0,8},{2,10},{4,12},{6,14},{8,16},{10,18},{12,20},{14,22},{16,24},... | collective-permute-start | bytes 786440 | tf_op jit(solution)/shard_map/ppermute | solution.py:222
  10.3 2.1 %collective-permute-start.3 = (bf16[2,8,64,128]{3,2,1,0:T(8,128)(2,1)S(1)}, bf16[2,8,64,128]{3,2,1,0:T(8,128)(2,1)S(1)}, u32[]{:S(2)}, u32[]{:S(2)}) collective-permute-start(bf16[2,8,64,128]{3,2,1,0:T(8,128)(2,1)S(1)} %pad_maximum_fusion.2.refs_2_), channel_id=1, source_target_pairs={{0,4},{2,6},{4,8},{6,10},{8,12},{10,14},{12,16},{14,18},{16,20},{1... | collective-permute-start | bytes 786440 | tf_op jit(solution)/shard_map/ppermute | solution.py:222
  12.5 3.1 %collective-permute-start.2 = (bf16[2,8,64,128]{3,2,1,0:T(8,128)(2,1)S(1)}, bf16[2,8,64,128]{3,2,1,0:T(8,128)(2,1)S(1)}, u32[]{:S(2)}, u32[]{:S(2)}) collective-permute-start(bf16[2,8,64,128]{3,2,1,0:T(8,128)(2,1)S(1)} %pad_maximum_fusion.2.refs_2_), channel_id=1, source_target_pairs={{0,2},{2,4},{4,6},{6,8},{8,10},{10,12},{12,14},{14,16},{16,18},{18... | collective-permute-start | bytes 786440 | tf_op jit(solution)/shard_map/ppermute | solution.py:222
  15.5 9.7 %collective-permute-done.4.refs_5_ = bf16[2,8,64,128]{3,2,1,0:T(8,128)(2,1)S(1)} collective-permute-done((bf16[2,8,64,128]{3,2,1,0:T(8,128)(2,1)S(1)}, bf16[2,8,64,128]{3,2,1,0:T(8,128)(2,1)S(1)}, u32[]{:S(2)}, u32[]{:S(2)}) %collective-permute-start.4) | collective-permute-done | bytes 262176 | tf_op jit(solution)/shard_map/ppermute | solution.py:222
  25.3 0.0 collective-permute-done.5.refs_6_
  25.3 0.8 %pad_maximum_fusion = bf16[2,2,8,64,128]{4,3,2,1,0:T(8,128)(2,1)} fusion(bf16[1,2,8,64,128]{4,3,2,1,0:T(8,128)(2,1)S(1)} %bitcast.18, bf16[1,2,8,64,128]{4,3,2,1,0:T(8,128)(2,1)S(1)} %bitcast.17), kind=kLoop, calls=%fused_computation | loop fusion | flops 262144 | bytes 1048576 | tf_op jit(solution)/shard_map/stack | solution.py:237
  26.1 1.9 %collective-permute-start.6 = (bf16[2,2,8,64,128]{4,3,2,1,0:T(8,128)(2,1)}, bf16[2,2,8,64,128]{4,3,2,1,0:T(8,128)(2,1)S(1)}, u32[]{:S(2)}, u32[]{:S(2)}) collective-permute-start(bf16[2,2,8,64,128]{4,3,2,1,0:T(8,128)(2,1)} %pad_maximum_fusion), channel_id=1, source_target_pairs={{0,8},{2,10},{4,12},{6,14},{8,16},{10,18},{12,20},{14,22},{16,24},... | collective-permute-start | bytes 1572872 | tf_op jit(solution)/shard_map/ppermute | solution.py:222
  28.0 0.0 collective-permute-done.3.refs_4_
  28.0 0.0 collective-permute-done.2.refs_3_
  28.0 0.9 %pad_maximum_fusion.1 = bf16[2,2,8,64,128]{4,3,2,1,0:T(8,128)(2,1)} fusion(bf16[1,2,8,64,128]{4,3,2,1,0:T(8,128)(2,1)S(1)} %bitcast.19, bf16[1,2,8,64,128]{4,3,2,1,0:T(8,128)(2,1)S(1)} %bitcast.20), kind=kLoop, calls=%fused_computation.1 | loop fusion | flops 262144 | bytes 1048576 | tf_op jit(solution)/shard_map/stack | solution.py:238
  28.9 1.9 %collective-permute-start.7 = (bf16[2,2,8,64,128]{4,3,2,1,0:T(8,128)(2,1)}, bf16[2,2,8,64,128]{4,3,2,1,0:T(8,128)(2,1)}, u32[]{:S(2)}, u32[]{:S(2)}) collective-permute-start(bf16[2,2,8,64,128]{4,3,2,1,0:T(8,128)(2,1)} %pad_maximum_fusion.1), channel_id=1, source_target_pairs={{0,8},{2,10},{4,12},{6,14},{8,16},{10,18},{12,20},{14,22},{16,24},... | collective-permute-start | bytes 1572872 | tf_op jit(solution)/shard_map/ppermute | solution.py:222
  30.8 0.1 pad_add_fusion.position
  30.9 0.0 copy-done
  30.9 0.0 copy-done.1
  30.9 3.1 %near.1 = (bf16[8,512,128]{2,1,0:T(8,128)(2,1)S(1)}, f32[8,1,512]{2,1,0:T(1,128)S(1)}, f32[8,1,512]{2,1,0:T(1,128)S(1)}, f32[8,128,512]{2,1,0:T(8,128)S(1)}) custom-call(s32[8]{0:T(128)S(1)} %copy-done.1, s32[2]{0:T(128)S(1)} %pad_add_fusion.position, bf16[128,32,128]{2,1,0:T(8,128)(2,1)S(1)} %copy-done, ...), custom_call_target="tpu_custom_call" | custom-call | flops 671088640 | bytes 4194304 | tf_op jit(solution)/shard_map/near/pallas_call | solution.py:182
  34.0 3.7 %collective-permute-done.6.refs_4_ = bf16[2,2,8,64,128]{4,3,2,1,0:T(8,128)(2,1)S(1)} collective-permute-done((bf16[2,2,8,64,128]{4,3,2,1,0:T(8,128)(2,1)}, bf16[2,2,8,64,128]{4,3,2,1,0:T(8,128)(2,1)S(1)}, u32[]{:S(2)}, u32[]{:S(2)}) %collective-permute-start.6) | collective-permute-done | bytes 524320 | tf_op jit(solution)/shard_map/ppermute | solution.py:222
  37.7 2.0 %middle.1 = (f32[8,1,512]{2,1,0:T(1,128)S(1)}, f32[8,1,512]{2,1,0:T(1,128)S(1)}, f32[8,128,512]{2,1,0:T(8,128)S(1)}) custom-call(s32[8]{0:T(128)S(1)} %copy-done.1, s32[2]{0:T(128)S(1)} %pad_add_fusion.position, bf16[8,512,128]{2,1,0:T(8,128)(2,1)S(1)} %get-tuple-element.16.refs_0_, f32[8,1,512]{2,1,0:T(1,128)S(1)} %get-tuple-element.17.refs_1_, ...), custom_call_target="tpu_custom_call" | custom-call | flops 268435456 | bytes 4194304 | tf_op jit(solution)/shard_map/middle/pallas_call | solution.py:182
  39.7 3.7 %collective-permute-done.7.refs_4_ = bf16[2,2,8,64,128]{4,3,2,1,0:T(8,128)(2,1)} collective-permute-done((bf16[2,2,8,64,128]{4,3,2,1,0:T(8,128)(2,1)}, bf16[2,2,8,64,128]{4,3,2,1,0:T(8,128)(2,1)}, u32[]{:S(2)}, u32[]{:S(2)}) %collective-permute-start.7) | collective-permute-done | bytes 524320 | tf_op jit(solution)/shard_map/ppermute | solution.py:222
  43.4 3.4 %finish.1 = bf16[64,64,128]{2,1,0:T(8,128)(2,1)} custom-call(s32[8]{0:T(128)S(1)} %copy-done.1, s32[2]{0:T(128)S(1)} %pad_add_fusion.position, bf16[8,512,128]{2,1,0:T(8,128)(2,1)S(1)} %get-tuple-element.16.refs_0_, f32[8,1,512]{2,1,0:T(1,128)S(1)} %get-tuple-element.20.refs_1_, f32[8,1,512]{2,1,0:T(1,128)S(1)} %get-tuple-element.21.refs_2_, ...), custom_call_target="tpu_custom_call" | custom-call | flops 268435456 | bytes 4194304 | tf_op jit(solution)/shard_map/finish/pallas_call | solution.py:182
  (3 shorter events, 0.1 us)
Async XLA Ops:
  1.1 29.8 %copy-start = (bf16[128,32,128]{2,1,0:T(8,128)(2,1)S(1)}, bf16[128,32,128]{2,1,0:T(8,128)(2,1)}, u32[]{:S(2)}) copy-start(bf16[128,32,128]{2,1,0:T(8,128)(2,1)} %refs_0_.1) | copy-start | bytes 3145732
  1.1 29.8 %copy-start.1 = (s32[8]{0:T(128)S(1)}, s32[8]{0:T(128)}, u32[]{:S(2)}) copy-start(s32[8]{0:T(128)} %doc_lengths.5) | copy-start | bytes 100
  1.1 7.1 %collective-permute-start.1 = (bf16[64,32,128]{2,1,0:T(8,128)(2,1)S(1)}, bf16[64,32,128]{2,1,0:T(8,128)(2,1)S(1)}, u32[]{:S(2)}, u32[]{:S(2)}) collective-permute-start(bf16[64,32,128]{2,1,0:T(8,128)(2,1)S(1)} %constant_dynamic-slice_fusion), channel_id=1, source_target_pairs={{0,1},{1,0},{2,3},{3,2},{4,5},{5,4},{6,7},{7,6},{8,9},{9,8},{10,11... | collective-permute-start | bytes 1572872 | tf_op jit(solution)/shard_map/ppermute | solution.py:218
  3.7 1.4 %collective-permute-start = (bf16[2,4,64,128]{3,2,1,0:T(8,128)(2,1)S(1)}, bf16[2,4,64,128]{3,2,1,0:T(8,128)(2,1)S(1)}, u32[]{:S(2)}, u32[]{:S(2)}) collective-permute-start(bf16[2,4,64,128]{3,2,1,0:T(8,128)(2,1)S(1)} %dynamic-slice_bitcast_fusion), channel_id=1, source_target_pairs={{0,1},{1,0},{2,3},{3,2},{4,5},{5,4},{6,7},{7,6},{8,9},{9,8},{10,11... | collective-permute-start | bytes 393224 | tf_op jit(solution)/shard_map/ppermute | solution.py:218
  5.2 20.0 %collective-permute-start.4 = (bf16[2,8,64,128]{3,2,1,0:T(8,128)(2,1)S(1)}, bf16[2,8,64,128]{3,2,1,0:T(8,128)(2,1)S(1)}, u32[]{:S(2)}, u32[]{:S(2)}) collective-permute-start(bf16[2,8,64,128]{3,2,1,0:T(8,128)(2,1)S(1)} %pad_maximum_fusion.2.refs_2_), channel_id=1, source_target_pairs={{0,6},{2,8},{4,10},{6,12},{8,14},{10,16},{12,18},{14,20},{16,22},{... | collective-permute-start | bytes 786440 | tf_op jit(solution)/shard_map/ppermute | solution.py:222
  8.2 17.0 %collective-permute-start.5 = (bf16[2,8,64,128]{3,2,1,0:T(8,128)(2,1)S(1)}, bf16[2,8,64,128]{3,2,1,0:T(8,128)(2,1)S(1)}, u32[]{:S(2)}, u32[]{:S(2)}) collective-permute-start(bf16[2,8,64,128]{3,2,1,0:T(8,128)(2,1)S(1)} %pad_maximum_fusion.2.refs_2_), channel_id=1, source_target_pairs={{0,8},{2,10},{4,12},{6,14},{8,16},{10,18},{12,20},{14,22},{16,24},... | collective-permute-start | bytes 786440 | tf_op jit(solution)/shard_map/ppermute | solution.py:222
  10.3 17.7 %collective-permute-start.3 = (bf16[2,8,64,128]{3,2,1,0:T(8,128)(2,1)S(1)}, bf16[2,8,64,128]{3,2,1,0:T(8,128)(2,1)S(1)}, u32[]{:S(2)}, u32[]{:S(2)}) collective-permute-start(bf16[2,8,64,128]{3,2,1,0:T(8,128)(2,1)S(1)} %pad_maximum_fusion.2.refs_2_), channel_id=1, source_target_pairs={{0,4},{2,6},{4,8},{6,10},{8,12},{10,14},{12,16},{14,18},{16,20},{1... | collective-permute-start | bytes 786440 | tf_op jit(solution)/shard_map/ppermute | solution.py:222
  12.5 15.6 %collective-permute-start.2 = (bf16[2,8,64,128]{3,2,1,0:T(8,128)(2,1)S(1)}, bf16[2,8,64,128]{3,2,1,0:T(8,128)(2,1)S(1)}, u32[]{:S(2)}, u32[]{:S(2)}) collective-permute-start(bf16[2,8,64,128]{3,2,1,0:T(8,128)(2,1)S(1)} %pad_maximum_fusion.2.refs_2_), channel_id=1, source_target_pairs={{0,2},{2,4},{4,6},{6,8},{8,10},{10,12},{12,14},{14,16},{16,18},{18... | collective-permute-start | bytes 786440 | tf_op jit(solution)/shard_map/ppermute | solution.py:222
  26.1 11.6 %collective-permute-start.6 = (bf16[2,2,8,64,128]{4,3,2,1,0:T(8,128)(2,1)}, bf16[2,2,8,64,128]{4,3,2,1,0:T(8,128)(2,1)S(1)}, u32[]{:S(2)}, u32[]{:S(2)}) collective-permute-start(bf16[2,2,8,64,128]{4,3,2,1,0:T(8,128)(2,1)} %pad_maximum_fusion), channel_id=1, source_target_pairs={{0,8},{2,10},{4,12},{6,14},{8,16},{10,18},{12,20},{14,22},{16,24},... | collective-permute-start | bytes 1572872 | tf_op jit(solution)/shard_map/ppermute | solution.py:222
  28.9 14.5 %collective-permute-start.7 = (bf16[2,2,8,64,128]{4,3,2,1,0:T(8,128)(2,1)}, bf16[2,2,8,64,128]{4,3,2,1,0:T(8,128)(2,1)}, u32[]{:S(2)}, u32[]{:S(2)}) collective-permute-start(bf16[2,2,8,64,128]{4,3,2,1,0:T(8,128)(2,1)} %pad_maximum_fusion.1), channel_id=1, source_target_pairs={{0,8},{2,10},{4,12},{6,14},{8,16},{10,18},{12,20},{14,22},{16,24},... | collective-permute-start | bytes 1572872 | tf_op jit(solution)/shard_map/ppermute | solution.py:222

commit v7 on v6

--- a/solution.py
+++ b/solution.py
@@ -10,6 +10,13 @@
 
 REACH_LOG = 3
 MASKED_SCORE = -1e30
+
+EARLY_TARGETS = (0, 2, 3, 1)
+LATE_TARGETS = (1, 3, 0, 2)
+EARLY_CHOICES = ((1, (1, 1, 1, 1)), (2, (2, 0, 0, 2)))
+LATE_CHOICES = ((1, (3, 1, 3, 3)), (2, (2, 0, 4, 4)))
+EARLY_DISTANCES = ((7, (7, 5, 8, 8)), (8, (8, 6, 5, 5)))
+LATE_DISTANCES = ((5, (5, 8, 6, 7)), (6, (6, 7, 7, 6)))
 
 
 def query_bounds(first_place, lanes, group, doc_lengths):
@@ -48,7 +55,43 @@
     )
 
 
-def stage_kernel(doc_lengths, position, *refs, group, arrays, pieces, begins, ends):
+def pack_kernel(keys, values, queries, keep, given, given_queries, staged, sems):
+    core = lax.axis_index("head")
+    block = given_queries.shape[0]
+    kept_rows, given_rows = pl.ds(core * block, block), pl.ds((1 - core) * block, block)
+    copies = [
+        pltpu.make_async_copy(keys, staged.at[0], sems.at[0]),
+        pltpu.make_async_copy(values, staged.at[1], sems.at[1]),
+        pltpu.make_async_copy(queries.at[given_rows], given_queries, sems.at[2]),
+    ]
+    for copy in copies:
+        copy.start()
+    for kind in range(2):
+        copies[kind].wait()
+        for rows, out in ((given_rows, given), (kept_rows, keep)):
+            part = staged[kind, rows].astype(jnp.float32)
+            out[kind] = jnp.swapaxes(part, 0, 1).astype(out.dtype)
+    copies[2].wait()
+
+
+def bundle_kernel(position, *refs, devices, choices):
+    candidates, out = refs[:-1], refs[-1]
+    source = position[0] - (devices - 4)
+    for slot, (usual, special) in enumerate(choices):
+        for candidate, ref in enumerate(candidates):
+            if candidate != usual and candidate not in special:
+                continue
+            chosen = jnp.bool_(candidate == usual)
+            for row, number in enumerate(special):
+                chosen = jnp.where(source == row, number == candidate, chosen)
+
+            @pl.when(chosen)
+            def _(slot=slot, ref=ref):
+                out[slot] = ref[...]
+
+
+def stage_kernel(doc_lengths, position, *refs, devices, group, arrays, pieces, begins, ends):
+    step = 2 if begins else 4
     stretch, core = position[0], position[1]
     refs = list(refs)
 
@@ -74,7 +117,6 @@
         staged, sems = take(2)
     kv_count, lanes, width = folded.shape
     block = lanes // group
-    half_heads = kv_count * group // 2
 
     def gather(kind, head):
         parts = [
@@ -83,28 +125,31 @@
         ]
         return jnp.concatenate(parts, axis=0)
 
-    for row, (_, _, distance) in enumerate(pieces):
+    turn = stretch - devices
+    for row, (_, _, (distance, special)) in enumerate(pieces):
+        for number, other in enumerate(special):
+            distance = jnp.where(turn == number, other, distance)
         bias[row * block : (row + 1) * block, :] = block_bias(
             stretch, distance, block, group, doc_lengths
         )
     copies = []
     for half in range(2):
         side = core if half == 0 else 1 - core
-        for pair in range(kv_count // 4):
-            first_head = side * (kv_count // 2) + 2 * pair
-            slots = [half * (kv_count // 2) + 2 * pair + part for part in range(2)]
+        for begin in range(0, kv_count // 2, step):
+            first_head = side * (kv_count // 2) + begin
+            slots = [half * (kv_count // 2) + begin + part for part in range(step)]
             if begins:
-                heads = slice(2 * pair * group, 2 * (pair + 1) * group)
+                heads = slice(begin * group, (begin + step) * group)
                 if half == 0:
-                    both = own_queries[pl.ds(core * block, block), heads, :]
+                    some = own_queries[pl.ds(core * block, block), heads, :]
                 else:
-                    both = partner_queries[:, heads, :]
-                both = both.astype(jnp.float32)
+                    some = partner_queries[:, heads, :]
+                some = some.astype(jnp.float32)
                 qs = [
-                    both[:, part * group : (part + 1) * group, :]
+                    some[:, part * group : (part + 1) * group, :]
                     .reshape(lanes, width)
                     .astype(jnp.bfloat16)
-                    for part in range(2)
+                    for part in range(step)
                 ]
                 for slot, q in zip(slots, qs):
                     folded[slot] = q
@@ -141,20 +186,24 @@
                 (each * scale + mixes[slot] * (shrink * scale)).T.reshape(block, group, width)
                 for each, slot, shrink, scale in zip(mixed, slots, shrinks, scales)
             ]
-            number = half * (kv_count // 4) + pair
-            staged[number] = jnp.concatenate(done, axis=1).astype(staged.dtype)
-            begin = pl.multiple_of(side * half_heads + 2 * pair * group, 2 * group)
-            copy = pltpu.make_async_copy(
-                staged.at[number], out.at[:, pl.ds(begin, 2 * group)], sems.at[number]
-            )
-            copy.start()
-            copies.append(copy)
+            for part in range(0, step, 2):
+                number = slots[part] // 2
+                pair = jnp.concatenate(done[part : part + 2], axis=1)
+                staged[number] = pair.astype(staged.dtype)
+            for part in range(0, step, 2):
+                number = slots[part] // 2
+                first = pl.multiple_of((first_head + part) * group, 2 * group)
+                copy = pltpu.make_async_copy(
+                    staged.at[number], out.at[:, pl.ds(first, 2 * group)], sems.at[number]
+                )
+                copy.start()
+                copies.append(copy)
     for copy in copies:
         copy.wait()
 
 
 def run_stage(name, scalars, queries, state, blocks, pieces, shape, ends=False):
-    block, kv_count, group, width = shape
+    devices, block, kv_count, group, width = shape
     lanes = block * group
     begins = state is None
     smem = pl.BlockSpec(memory_space=pltpu.SMEM)
@@ -182,6 +231,7 @@
     return pl.pallas_call(
         functools.partial(
             stage_kernel,
+            devices=devices,
             group=group,
             arrays=len(blocks),
             pieces=pieces,
@@ -217,29 +267,62 @@
     def swap(array):
         return lax.ppermute(array, "head", [(0, 1), (1, 0)])
 
-    def from_below(array, distance):
-        pairs = [(owner(at), owner(at + distance)) for at in range(stretches - distance)]
+    def from_below(array, distance, turned=()):
+        target = {at: at + distance for at in range(stretches - distance)}
+        for number, to in enumerate(turned):
+            target[devices - 4 + number] = devices + to
+        pairs = [(owner(at), owner(to)) for at, to in target.items()]
         return lax.ppermute(array, ("ctx", "head"), pairs)
 
-    packed = jnp.stack([key_heads, value_head_rows])
-    packed = packed.reshape(2, 2, block, kv_half, width).transpose(1, 0, 3, 2, 4)
-    keep = lax.dynamic_index_in_dim(packed, core, 0, keepdims=False)
-    given = swap(lax.dynamic_index_in_dim(packed, 1 - core, 0, keepdims=False))
+    smem = pl.BlockSpec(memory_space=pltpu.SMEM)
+    vmem = pl.BlockSpec(memory_space=pltpu.VMEM)
+    inputs = (key_heads, value_head_rows, queries)
+    half = jax.ShapeDtypeStruct((2, kv_half, block, width), jnp.bfloat16)
+    keep, given, given_queries = pl.pallas_call(
+        pack_kernel,
+        out_shape=[half, half, jax.ShapeDtypeStruct((block, heads, width), jnp.bfloat16)],
+        in_specs=[pl.BlockSpec(memory_space=pltpu.HBM)] * 3,
+        out_specs=[vmem] * 3,
+        scratch_shapes=[
+            pltpu.VMEM((2, stride, kv_half, width), jnp.bfloat16),
+            pltpu.SemaphoreType.DMA((3,)),
+        ],
+        compiler_params=pltpu.CompilerParams(vmem_limit_bytes=6 * 2**20),
+        name="pack",
+    )(*[pltpu.with_memory_space_constraint(array, pltpu.HBM) for array in inputs])
+    given = swap(given)
     own = jnp.concatenate(
         [jnp.where(core == 0, keep, given), jnp.where(core == 0, given, keep)], axis=1
     )
-    partner_queries = swap(lax.dynamic_slice_in_dim(queries, (1 - core) * block, block, 0))
+    own, given_queries = lax.optimization_barrier((own, given_queries))
+    partner_queries = swap(given_queries)
     by_three = from_below(own, 3)
     own, partner_queries = lax.optimization_barrier((own, partner_queries))
     by_four = from_below(own, 4)
     by_one = from_below(own, 1)
     by_two = from_below(own, 2)
-    early = from_below(jnp.stack([by_three, by_four]), 4)
-    late = from_below(jnp.stack([by_one, by_two]), 4)
 
     scalars = (doc_lengths, jnp.stack([stretch, core]))
-    shape = (block, 2 * kv_half, group, width)
-    near = tuple((at, None, at) for at in range(5))
+
+    def bundle(name, candidates, choices):
+        return pl.pallas_call(
+            functools.partial(bundle_kernel, devices=devices, choices=choices),
+            out_shape=jax.ShapeDtypeStruct((2, *own.shape), own.dtype),
+            in_specs=[smem] + [vmem] * len(candidates),
+            out_specs=vmem,
+            compiler_params=pltpu.CompilerParams(vmem_limit_bytes=6 * 2**20),
+            name=name,
+        )(scalars[1], *candidates)
+
+    early = from_below(
+        bundle("early", (own, by_three, by_four), EARLY_CHOICES), 4, EARLY_TARGETS
+    )
+    late = from_below(
+        bundle("late", (own, by_one, by_two, by_three, by_four), LATE_CHOICES), 4, LATE_TARGETS
+    )
+
+    shape = (devices, block, 2 * kv_half, group, width)
+    near = tuple((at, None, (at, ())) for at in range(5))
     folded, *state = run_stage(
         "near",
         scalars,
@@ -249,11 +332,13 @@
         near,
         shape,
     )
-    state = run_stage(
-        "middle", scalars, (folded,), state, (early,), ((0, 0, 7), (0, 1, 8)), shape
-    )
+    pieces = [
+        tuple((0, index, distances) for index, distances in enumerate(table))
+        for table in (EARLY_DISTANCES, LATE_DISTANCES)
+    ]
+    state = run_stage("middle", scalars, (folded,), state, (early,), pieces[0], shape)
     return run_stage(
-        "finish", scalars, (folded,), state, (late,), ((0, 0, 5), (0, 1, 6)), shape, ends=True
+        "finish", scalars, (folded,), state, (late,), pieces[1], shape, ends=True
     )
 
 

time: 47.1 us -> 42.3 us (0.90)
  the two profiles are of different devices: /device:TPU:27 before, /device:TPU:19 now
where the time goes in v7:
time: 42.3 us; the launch traced here: 42.1 us
  waiting for transfers between devices  16.4 us (39%)
  starting transfers between devices  15.4 us (36%)
  Pallas kernels  9.99 us (24%)
    ppermute x6, waiting for transfers between devices, from_below(): return lax.ppermute(array, ('ctx', 'head'), pairs)  15.5 us
    ppermute x6, starting transfers between devices, from_below(): return lax.ppermute(array, ('ctx', 'head'), pairs)  14.2 us
    pallas_call x3, Pallas kernels, run_stage(): pl.pallas_call(functools.partial(stage_kernel, devices=devices, group=gro...  7.59 us
    pallas_call x1, Pallas kernels, shards(): pl.pallas_call(pack_kernel, out_shape=[half, half, jax.ShapeDtypeStruct((...  1.2 us
    pallas_call x2, Pallas kernels, bundle(): pl.pallas_call(functools.partial(bundle_kernel, devices=devices, choices=...  1.2 us
    ppermute x2, starting transfers between devices, swap(): return lax.ppermute(array, 'head', [(0, 1), (1, 0)])  1.17 us
    ppermute x2, waiting for transfers between devices, swap(): return lax.ppermute(array, 'head', [(0, 1), (1, 0)])  0.99 us
  transfers between devices with their start and end apart: 8, of which 5 were waited for; matrix products, arithmetic and copies ran while one was open for 0% of the time, Pallas kernels for 14%

profile of v7, /device:TPU:19, one launch (start us, length us, event | category | flops | bytes accessed | tf_op | source)
XLA Modules:
  0.0 42.1 jit_solution(17522303179339473884)
XLA Ops:
  0.0 1.2 %pack.1 = (bf16[2,4,64,128]{3,2,1,0:T(8,128)(2,1)S(1)}, bf16[2,4,64,128]{3,2,1,0:T(8,128)(2,1)S(1)}, bf16[64,32,128]{2,1,0:T(8,128)(2,1)S(1)}) custom-call(bf16[128,4,128]{2,1,0:T(4,128)(2,1)} %keys.1, bf16[128,4,128]{2,1,0:T(4,128)(2,1)} %values.1, bf16[128,32,128]{2,1,0:T(8,128)(2,1)} %refs_0_.1), custom_call_target="tpu_custom_call" | custom-call | tf_op jit(solution)/shard_map/pack/pallas_call | solution.py:281
  1.2 0.7 %collective-permute-start = (bf16[2,4,64,128]{3,2,1,0:T(8,128)(2,1)S(1)}, bf16[2,4,64,128]{3,2,1,0:T(8,128)(2,1)S(1)}, u32[]{:S(2)}, u32[]{:S(2)}) collective-permute-start(bf16[2,4,64,128]{3,2,1,0:T(8,128)(2,1)S(1)} %get-tuple-element.20), channel_id=1, source_target_pairs={{0,1},{1,0},{2,3},{3,2},{4,5},{5,4},{6,7},{7,6},{8,9},{9,8},{10,11... | collective-permute-start | bytes 393224 | tf_op jit(solution)/shard_map/ppermute | solution.py:268
  2.0 1.0 %collective-permute-done = bf16[2,4,64,128]{3,2,1,0:T(8,128)(2,1)S(1)} collective-permute-done((bf16[2,4,64,128]{3,2,1,0:T(8,128)(2,1)S(1)}, bf16[2,4,64,128]{3,2,1,0:T(8,128)(2,1)S(1)}, u32[]{:S(2)}, u32[]{:S(2)}) %collective-permute-start) | collective-permute-done | bytes 131104 | tf_op jit(solution)/shard_map/ppermute | solution.py:268
  2.9 0.0 copy-start
  2.9 0.0 copy-start.1
  3.0 0.4 %collective-permute-start.1 = (bf16[64,32,128]{2,1,0:T(8,128)(2,1)S(1)}, bf16[64,32,128]{2,1,0:T(8,128)(2,1)S(1)}, u32[]{:S(2)}, u32[]{:S(2)}) collective-permute-start(bf16[64,32,128]{2,1,0:T(8,128)(2,1)S(1)} %get-tuple-element.23), channel_id=1, source_target_pairs={{0,1},{1,0},{2,3},{3,2},{4,5},{5,4},{6,7},{7,6},{8,9},{9,8},{10,11... | collective-permute-start | bytes 1572872 | tf_op jit(solution)/shard_map/ppermute | solution.py:268
  3.4 3.0 %collective-permute-start.4 = (bf16[2,8,64,128]{3,2,1,0:T(8,128)(2,1)S(1)}, bf16[2,8,64,128]{3,2,1,0:T(8,128)(2,1)S(1)}, u32[]{:S(2)}, u32[]{:S(2)}) collective-permute-start(bf16[2,8,64,128]{3,2,1,0:T(8,128)(2,1)S(1)} %pad_maximum_fusion.refs_2_.refs_0_), channel_id=1, source_target_pairs={{0,6},{2,8},{4,10},{6,12},{8,14},{10,16},{12,18},{14,20},{16,22},{... | collective-permute-start | bytes 786440 | tf_op jit(solution)/shard_map/ppermute | solution.py:275
  6.4 0.0 collective-permute-done.1.refs_1_
  6.4 2.1 %collective-permute-start.5 = (bf16[2,8,64,128]{3,2,1,0:T(8,128)(2,1)S(1)}, bf16[2,8,64,128]{3,2,1,0:T(8,128)(2,1)S(1)}, u32[]{:S(2)}, u32[]{:S(2)}) collective-permute-start(bf16[2,8,64,128]{3,2,1,0:T(8,128)(2,1)S(1)} %pad_maximum_fusion.refs_2_.refs_0_), channel_id=1, source_target_pairs={{0,8},{2,10},{4,12},{6,14},{8,16},{10,18},{12,20},{14,22},{16,24},... | collective-permute-start | bytes 786440 | tf_op jit(solution)/shard_map/ppermute | solution.py:275
  8.5 2.0 %collective-permute-start.3 = (bf16[2,8,64,128]{3,2,1,0:T(8,128)(2,1)S(1)}, bf16[2,8,64,128]{3,2,1,0:T(8,128)(2,1)S(1)}, u32[]{:S(2)}, u32[]{:S(2)}) collective-permute-start(bf16[2,8,64,128]{3,2,1,0:T(8,128)(2,1)S(1)} %pad_maximum_fusion.refs_2_.refs_0_), channel_id=1, source_target_pairs={{0,4},{2,6},{4,8},{6,10},{8,12},{10,14},{12,16},{14,18},{16,20},{1... | collective-permute-start | bytes 786440 | tf_op jit(solution)/shard_map/ppermute | solution.py:275
  10.5 3.1 %collective-permute-start.2 = (bf16[2,8,64,128]{3,2,1,0:T(8,128)(2,1)S(1)}, bf16[2,8,64,128]{3,2,1,0:T(8,128)(2,1)S(1)}, u32[]{:S(2)}, u32[]{:S(2)}) collective-permute-start(bf16[2,8,64,128]{3,2,1,0:T(8,128)(2,1)S(1)} %pad_maximum_fusion.refs_2_.refs_0_), channel_id=1, source_target_pairs={{0,2},{2,4},{4,6},{6,8},{8,10},{10,12},{12,14},{14,16},{16,18},{18... | collective-permute-start | bytes 786440 | tf_op jit(solution)/shard_map/ppermute | solution.py:275
  13.6 0.1 pad_add_fusion.position
  13.7 0.0 collective-permute-done.4.refs_5_.refs_1_.refs_3_
  13.7 2.4 %collective-permute-done.5.refs_6_.refs_2_.refs_4_ = bf16[2,8,64,128]{3,2,1,0:T(8,128)(2,1)S(1)} collective-permute-done((bf16[2,8,64,128]{3,2,1,0:T(8,128)(2,1)S(1)}, bf16[2,8,64,128]{3,2,1,0:T(8,128)(2,1)S(1)}, u32[]{:S(2)}, u32[]{:S(2)}) %collective-permute-start.5) | collective-permute-done | bytes 262176 | tf_op jit(solution)/shard_map/ppermute | solution.py:275
  16.1 0.6 %early.1 = bf16[2,2,8,64,128]{4,3,2,1,0:T(8,128)(2,1)S(1)} custom-call(s32[2]{0:T(128)S(1)} %pad_add_fusion.position, bf16[2,8,64,128]{3,2,1,0:T(8,128)(2,1)S(1)} %pad_maximum_fusion.refs_2_.refs_0_, bf16[2,8,64,128]{3,2,1,0:T(8,128)(2,1)S(1)} %collective-permute-done.4.refs_5_.refs_1_.refs_3_, ...), custom_call_target="tpu_custom_call" | custom-call | tf_op jit(solution)/shard_map/early/pallas_call | solution.py:308
  16.7 2.1 %collective-permute-start.6 = (bf16[2,2,8,64,128]{4,3,2,1,0:T(8,128)(2,1)S(1)}, bf16[2,2,8,64,128]{4,3,2,1,0:T(8,128)(2,1)S(1)}, u32[]{:S(2)}, u32[]{:S(2)}) collective-permute-start(bf16[2,2,8,64,128]{4,3,2,1,0:T(8,128)(2,1)S(1)} %early.1), channel_id=1, source_target_pairs={{0,8},{2,10},{4,12},{6,14},{8,16},{10,18},{12,20},{14,22},{16,24},... | collective-permute-start | bytes 1572872 | tf_op jit(solution)/shard_map/ppermute | solution.py:275
  18.7 4.3 %collective-permute-done.3.refs_4_.refs_2_ = bf16[2,8,64,128]{3,2,1,0:T(8,128)(2,1)S(1)} collective-permute-done((bf16[2,8,64,128]{3,2,1,0:T(8,128)(2,1)S(1)}, bf16[2,8,64,128]{3,2,1,0:T(8,128)(2,1)S(1)}, u32[]{:S(2)}, u32[]{:S(2)}) %collective-permute-start.3) | collective-permute-done | bytes 262176 | tf_op jit(solution)/shard_map/ppermute | solution.py:275
  23.1 0.0 collective-permute-done.2.refs_3_.refs_1_
  23.1 0.6 %late.1 = bf16[2,2,8,64,128]{4,3,2,1,0:T(8,128)(2,1)S(1)} custom-call(s32[2]{0:T(128)S(1)} %pad_add_fusion.position, bf16[2,8,64,128]{3,2,1,0:T(8,128)(2,1)S(1)} %pad_maximum_fusion.refs_2_.refs_0_, bf16[2,8,64,128]{3,2,1,0:T(8,128)(2,1)S(1)} %collective-permute-done.2.refs_3_.refs_1_, bf16[2,8,64,128]{3,2,1,0:T(8,128)(2,1)S(1)} %collective-permute-done.3.refs_4_.refs_2_, ...), custom_call_target="tpu_custom_call" | custom-call | tf_op jit(solution)/shard_map/late/pallas_call | solution.py:308
  23.7 2.0 %collective-permute-start.7 = (bf16[2,2,8,64,128]{4,3,2,1,0:T(8,128)(2,1)S(1)}, bf16[2,2,8,64,128]{4,3,2,1,0:T(8,128)(2,1)S(1)}, u32[]{:S(2)}, u32[]{:S(2)}) collective-permute-start(bf16[2,2,8,64,128]{4,3,2,1,0:T(8,128)(2,1)S(1)} %late.1), channel_id=1, source_target_pairs={{0,8},{2,10},{4,12},{6,14},{8,16},{10,18},{12,20},{14,22},{16,24},... | collective-permute-start | bytes 1572872 | tf_op jit(solution)/shard_map/ppermute | solution.py:275
  25.7 0.0 copy-done
  25.7 0.0 copy-done.1
  25.7 3.1 %near.1 = (bf16[8,512,128]{2,1,0:T(8,128)(2,1)S(1)}, f32[8,1,512]{2,1,0:T(1,128)S(1)}, f32[8,1,512]{2,1,0:T(1,128)S(1)}, f32[8,128,512]{2,1,0:T(8,128)S(1)}) custom-call(s32[8]{0:T(128)S(1)} %copy-done.1, s32[2]{0:T(128)S(1)} %pad_add_fusion.position, bf16[128,32,128]{2,1,0:T(8,128)(2,1)S(1)} %copy-done, ...), custom_call_target="tpu_custom_call" | custom-call | flops 671088640 | bytes 4194304 | tf_op jit(solution)/shard_map/near/pallas_call | solution.py:231
  28.8 5.1 %collective-permute-done.6.refs_4_ = bf16[2,2,8,64,128]{4,3,2,1,0:T(8,128)(2,1)S(1)} collective-permute-done((bf16[2,2,8,64,128]{4,3,2,1,0:T(8,128)(2,1)S(1)}, bf16[2,2,8,64,128]{4,3,2,1,0:T(8,128)(2,1)S(1)}, u32[]{:S(2)}, u32[]{:S(2)}) %collective-permute-start.6) | collective-permute-done | bytes 524320 | tf_op jit(solution)/shard_map/ppermute | solution.py:275
  34.0 1.7 %middle.1 = (f32[8,1,512]{2,1,0:T(1,128)S(1)}, f32[8,1,512]{2,1,0:T(1,128)S(1)}, f32[8,128,512]{2,1,0:T(8,128)S(1)}) custom-call(s32[8]{0:T(128)S(1)} %copy-done.1, s32[2]{0:T(128)S(1)} %pad_add_fusion.position, bf16[8,512,128]{2,1,0:T(8,128)(2,1)S(1)} %get-tuple-element.26.refs_0_, f32[8,1,512]{2,1,0:T(1,128)S(1)} %get-tuple-element.27.refs_1_, ...), custom_call_target="tpu_custom_call" | custom-call | flops 268435456 | bytes 4194304 | tf_op jit(solution)/shard_map/middle/pallas_call | solution.py:231
  35.7 3.6 %collective-permute-done.7.refs_4_ = bf16[2,2,8,64,128]{4,3,2,1,0:T(8,128)(2,1)S(1)} collective-permute-done((bf16[2,2,8,64,128]{4,3,2,1,0:T(8,128)(2,1)S(1)}, bf16[2,2,8,64,128]{4,3,2,1,0:T(8,128)(2,1)S(1)}, u32[]{:S(2)}, u32[]{:S(2)}) %collective-permute-start.7) | collective-permute-done | bytes 524320 | tf_op jit(solution)/shard_map/ppermute | solution.py:275
  39.3 2.8 %finish.1 = bf16[64,64,128]{2,1,0:T(8,128)(2,1)} custom-call(s32[8]{0:T(128)S(1)} %copy-done.1, s32[2]{0:T(128)S(1)} %pad_add_fusion.position, bf16[8,512,128]{2,1,0:T(8,128)(2,1)S(1)} %get-tuple-element.26.refs_0_, f32[8,1,512]{2,1,0:T(1,128)S(1)} %get-tuple-element.30.refs_1_, f32[8,1,512]{2,1,0:T(1,128)S(1)} %get-tuple-element.31.refs_2_, ...), custom_call_target="tpu_custom_call" | custom-call | flops 268435456 | bytes 4194304 | tf_op jit(solution)/shard_map/finish/pallas_call | solution.py:231
  (2 shorter events, 0.0 us)
Async XLA Ops:
  1.2 1.7 %collective-permute-start = (bf16[2,4,64,128]{3,2,1,0:T(8,128)(2,1)S(1)}, bf16[2,4,64,128]{3,2,1,0:T(8,128)(2,1)S(1)}, u32[]{:S(2)}, u32[]{:S(2)}) collective-permute-start(bf16[2,4,64,128]{3,2,1,0:T(8,128)(2,1)S(1)} %get-tuple-element.20), channel_id=1, source_target_pairs={{0,1},{1,0},{2,3},{3,2},{4,5},{5,4},{6,7},{7,6},{8,9},{9,8},{10,11... | collective-permute-start | bytes 393224 | tf_op jit(solution)/shard_map/ppermute | solution.py:268
  2.9 22.8 %copy-start = (bf16[128,32,128]{2,1,0:T(8,128)(2,1)S(1)}, bf16[128,32,128]{2,1,0:T(8,128)(2,1)}, u32[]{:S(2)}) copy-start(bf16[128,32,128]{2,1,0:T(8,128)(2,1)} %refs_0_.1) | copy-start | bytes 3145732
  2.9 22.8 %copy-start.1 = (s32[8]{0:T(128)S(1)}, s32[8]{0:T(128)}, u32[]{:S(2)}) copy-start(s32[8]{0:T(128)} %doc_lengths.5) | copy-start | bytes 100
  3.0 3.4 %collective-permute-start.1 = (bf16[64,32,128]{2,1,0:T(8,128)(2,1)S(1)}, bf16[64,32,128]{2,1,0:T(8,128)(2,1)S(1)}, u32[]{:S(2)}, u32[]{:S(2)}) collective-permute-start(bf16[64,32,128]{2,1,0:T(8,128)(2,1)S(1)} %get-tuple-element.23), channel_id=1, source_target_pairs={{0,1},{1,0},{2,3},{3,2},{4,5},{5,4},{6,7},{7,6},{8,9},{9,8},{10,11... | collective-permute-start | bytes 1572872 | tf_op jit(solution)/shard_map/ppermute | solution.py:268
  3.4 10.2 %collective-permute-start.4 = (bf16[2,8,64,128]{3,2,1,0:T(8,128)(2,1)S(1)}, bf16[2,8,64,128]{3,2,1,0:T(8,128)(2,1)S(1)}, u32[]{:S(2)}, u32[]{:S(2)}) collective-permute-start(bf16[2,8,64,128]{3,2,1,0:T(8,128)(2,1)S(1)} %pad_maximum_fusion.refs_2_.refs_0_), channel_id=1, source_target_pairs={{0,6},{2,8},{4,10},{6,12},{8,14},{10,16},{12,18},{14,20},{16,22},{... | collective-permute-start | bytes 786440 | tf_op jit(solution)/shard_map/ppermute | solution.py:275
  6.4 9.6 %collective-permute-start.5 = (bf16[2,8,64,128]{3,2,1,0:T(8,128)(2,1)S(1)}, bf16[2,8,64,128]{3,2,1,0:T(8,128)(2,1)S(1)}, u32[]{:S(2)}, u32[]{:S(2)}) collective-permute-start(bf16[2,8,64,128]{3,2,1,0:T(8,128)(2,1)S(1)} %pad_maximum_fusion.refs_2_.refs_0_), channel_id=1, source_target_pairs={{0,8},{2,10},{4,12},{6,14},{8,16},{10,18},{12,20},{14,22},{16,24},... | collective-permute-start | bytes 786440 | tf_op jit(solution)/shard_map/ppermute | solution.py:275
  8.5 14.6 %collective-permute-start.3 = (bf16[2,8,64,128]{3,2,1,0:T(8,128)(2,1)S(1)}, bf16[2,8,64,128]{3,2,1,0:T(8,128)(2,1)S(1)}, u32[]{:S(2)}, u32[]{:S(2)}) collective-permute-start(bf16[2,8,64,128]{3,2,1,0:T(8,128)(2,1)S(1)} %pad_maximum_fusion.refs_2_.refs_0_), channel_id=1, source_target_pairs={{0,4},{2,6},{4,8},{6,10},{8,12},{10,14},{12,16},{14,18},{16,20},{1... | collective-permute-start | bytes 786440 | tf_op jit(solution)/shard_map/ppermute | solution.py:275
  10.5 12.6 %collective-permute-start.2 = (bf16[2,8,64,128]{3,2,1,0:T(8,128)(2,1)S(1)}, bf16[2,8,64,128]{3,2,1,0:T(8,128)(2,1)S(1)}, u32[]{:S(2)}, u32[]{:S(2)}) collective-permute-start(bf16[2,8,64,128]{3,2,1,0:T(8,128)(2,1)S(1)} %pad_maximum_fusion.refs_2_.refs_0_), channel_id=1, source_target_pairs={{0,2},{2,4},{4,6},{6,8},{8,10},{10,12},{12,14},{14,16},{16,18},{18... | collective-permute-start | bytes 786440 | tf_op jit(solution)/shard_map/ppermute | solution.py:275
  16.7 17.3 %collective-permute-start.6 = (bf16[2,2,8,64,128]{4,3,2,1,0:T(8,128)(2,1)S(1)}, bf16[2,2,8,64,128]{4,3,2,1,0:T(8,128)(2,1)S(1)}, u32[]{:S(2)}, u32[]{:S(2)}) collective-permute-start(bf16[2,2,8,64,128]{4,3,2,1,0:T(8,128)(2,1)S(1)} %early.1), channel_id=1, source_target_pairs={{0,8},{2,10},{4,12},{6,14},{8,16},{10,18},{12,20},{14,22},{16,24},... | collective-permute-start | bytes 1572872 | tf_op jit(solution)/shard_map/ppermute | solution.py:275
  23.7 15.6 %collective-permute-start.7 = (bf16[2,2,8,64,128]{4,3,2,1,0:T(8,128)(2,1)S(1)}, bf16[2,2,8,64,128]{4,3,2,1,0:T(8,128)(2,1)S(1)}, u32[]{:S(2)}, u32[]{:S(2)}) collective-permute-start(bf16[2,2,8,64,128]{4,3,2,1,0:T(8,128)(2,1)S(1)} %late.1), channel_id=1, source_target_pairs={{0,8},{2,10},{4,12},{6,14},{8,16},{10,18},{12,20},{14,22},{16,24},... | collective-permute-start | bytes 1572872 | tf_op jit(solution)/shard_map/ppermute | solution.py:275

commit v8 on v5

v8 whole, which is shorter than its diff:
```python
import functools
import math

import jax
import jax.numpy as jnp
from jax import lax
from jax.experimental import pallas as pl
from jax.experimental.pallas import tpu as pltpu
from jax.sharding import PartitionSpec as P

REACH_LOG = 3
MASKED_SCORE = -1e30

EARLY_TARGETS = (0, 2, 3, 1)
LATE_TARGETS = (1, 3, 0, 2)
EARLY_CHOICES = ((1, (1, 1, 1, 1)), (2, (2, 0, 0, 2)))
LATE_CHOICES = ((1, (3, 1, 3, 3)), (2, (2, 0, 4, 4)))
EARLY_DISTANCES = ((7, (7, 5, 8, 8)), (8, (8, 6, 5, 5)))
LATE_DISTANCES = ((5, (5, 8, 6, 7)), (6, (6, 7, 7, 6)))


def query_bounds(first_place, lanes, group, doc_lengths):
    place = first_place + lax.broadcasted_iota(jnp.int32, (1, lanes), 1) // group
    begin = jnp.zeros((1, lanes), jnp.int32)
    end = jnp.int32(0)
    for j in range(doc_lengths.shape[0]):
        end = end + doc_lengths[j]
        begin = jnp.where(place >= end, end, begin)
    return place, begin


def block_bias(stretch, distance, block, group, doc_lengths):
    lanes = block * group
    first = stretch * block
    place, begin = query_bounds(first, lanes, group, doc_lengths)
    key_place = first - distance * block + lax.broadcasted_iota(jnp.int32, (block, lanes), 0)
    allowed = (key_place >= begin) & (key_place <= place)
    return jnp.where(allowed, 0.0, MASKED_SCORE)


def score(q, keys, bias):
    factor = math.log2(math.e) / math.sqrt(q.shape[1])
    scores = lax.dot_general(
        keys, q, (((1,), (1,)), ((), ())), preferred_element_type=jnp.float32
    )
    return scores * factor + bias


def mix(values, weights):
    return lax.dot_general(
        values,
        weights.astype(jnp.bfloat16),
        (((0,), (0,)), ((), ())),
        preferred_element_type=jnp.float32,
    )


def pack_kernel(keys, values, queries, keep, given, given_queries, staged, sems):
    core = lax.axis_index("head")
    block = given_queries.shape[0]
    kept_rows, given_rows = pl.ds(core * block, block), pl.ds((1 - core) * block, block)
    copies = [
        pltpu.make_async_copy(keys, staged.at[0], sems.at[0]),
        pltpu.make_async_copy(values, staged.at[1], sems.at[1]),
        pltpu.make_async_copy(queries.at[given_rows], given_queries, sems.at[2]),
    ]
    for copy in copies:
        copy.start()
    for kind in range(2):
        copies[kind].wait()
        for rows, out in ((given_rows, given), (kept_rows, keep)):
            part = staged[kind, rows].astype(jnp.float32)
            out[kind] = jnp.swapaxes(part, 0, 1).astype(out.dtype)
    copies[2].wait()


def chain_position(devices):
    device, core = lax.axis_index("ctx"), lax.axis_index("head")
    return jnp.where(core == 0, device, 2 * devices - 1 - device)


def bundle_kernel(*refs, devices, choices):
    candidates, out = refs[:-1], refs[-1]
    source = chain_position(devices) - (devices - 4)
    for slot, (usual, special) in enumerate(choices):
        for candidate, ref in enumerate(candidates):
            if candidate != usual and candidate not in special:
                continue
            chosen = jnp.bool_(candidate == usual)
            for row, number in enumerate(special):
                chosen = jnp.where(source == row, number == candidate, chosen)

            @pl.when(chosen)
            def _(slot=slot, ref=ref):
                out[slot] = ref[...]


def near_kernel(doc_lengths, queries, partner_queries, *refs, devices, group):
    blocks, (folded, far_bias, peak, sums, mixes, bias) = refs[:-6], refs[-6:]
    stretch, core = chain_position(devices), lax.axis_index("head")
    kv_count, block, width = blocks[0].shape[1:]
    lanes = block * group
    for distance in range(len(blocks)):
        bias[distance * block : (distance + 1) * block, :] = block_bias(
            stretch, distance, block, group, doc_lengths
        )

    def gather(kind, head):
        return jnp.concatenate([ref[kind, head] for ref in blocks], axis=0)

    for half in range(2):
        side = core if half == 0 else 1 - core
        for begin in range(0, kv_count // 2, 2):
            first_head = side * (kv_count // 2) + begin
            slots = [half * (kv_count // 2) + begin + part for part in range(2)]
            heads = slice(begin * group, (begin + 2) * group)
            if half == 0:
                both = queries[pl.ds(core * block, block), heads, :]
            else:
                both = partner_queries[:, heads, :]
            both = both.astype(jnp.float32)
            qs = [
                both[:, part * group : (part + 1) * group, :]
                .reshape(lanes, width)
                .astype(jnp.bfloat16)
                for part in range(2)
            ]
            scores = [
                score(q, gather(0, first_head + part), bias[...]) for part, q in enumerate(qs)
            ]
            largest = [jnp.max(each, axis=0, keepdims=True) for each in scores]
            weights = [jnp.exp2(each - top) for each, top in zip(scores, largest)]
            for part, slot in enumerate(slots):
                folded[slot] = qs[part]
                peak[slot] = largest[part]
                sums[slot] = jnp.sum(weights[part], axis=0, keepdims=True)
                mixes[slot] = mix(gather(1, first_head + part), weights[part])
    turn = stretch - devices
    for number, table in enumerate((EARLY_DISTANCES, LATE_DISTANCES)):
        for row, (distance, special) in enumerate(table):
            for at, other in enumerate(special):
                distance = jnp.where(turn == at, other, distance)
            far_bias[number, row * block : (row + 1) * block, :] = block_bias(
                stretch, distance, block, group, doc_lengths
            )


def far_kernel(folded, far_bias, peak, sums, mixes, blocks, *refs, number):
    ends = number == 1
    if ends:
        out, staged, sems = refs
    else:
        new_peak, new_sums, new_mixes = refs
    core = lax.axis_index("head")
    _, _, kv_count, block, width = blocks.shape
    group = folded.shape[1] // block
    step = kv_count // 2
    copies = []
    for half in range(2):
        side = core if half == 0 else 1 - core
        first_head = side * step
        slots = [half * step + part for part in range(step)]
        scores = [
            score(
                folded[slot],
                blocks[:, 0, first_head + part].reshape(2 * block, width),
                far_bias[number],
            )
            for part, slot in enumerate(slots)
        ]
        largest = [
            jnp.maximum(jnp.max(each, axis=0, keepdims=True), peak[slot])
            for each, slot in zip(scores, slots)
        ]
        weights = [jnp.exp2(each - top) for each, top in zip(scores, largest)]
        shrinks = [jnp.exp2(peak[slot] - top) for slot, top in zip(slots, largest)]
        totals = [
            jnp.sum(each, axis=0, keepdims=True) + sums[slot] * shrink
            for each, slot, shrink in zip(weights, slots, shrinks)
        ]
        mixed = [
            mix(blocks[:, 1, first_head + part].reshape(2 * block, width), each)
            for part, each in enumerate(weights)
        ]
        if not ends:
            for part, slot in enumerate(slots):
                new_peak[slot] = largest[part]
                new_sums[slot] = totals[part]
                new_mixes[slot] = mixed[part] + mixes[slot] * shrinks[part]
            continue
        for part in range(0, step, 2):
            done = []
            for at in range(part, part + 2):
                scale = 1.0 / totals[at]
                result = mixed[at] * scale + mixes[slots[at]] * (shrinks[at] * scale)
                done.append(result.T.reshape(block, group, width))
            pair = slots[part] // 2
            staged[pair] = jnp.concatenate(done, axis=1).astype(staged.dtype)
            first = pl.multiple_of((first_head + part) * group, 2 * group)
            copy = pltpu.make_async_copy(
                staged.at[pair], out.at[:, pl.ds(first, 2 * group)], sems.at[pair]
            )
            copy.start()
            copies.append(copy)
    for copy in copies:
        copy.wait()


def shards(queries, key_heads, value_head_rows, doc_lengths):
    stride, heads, width = queries.shape
    kv_half = key_heads.shape[1]
    block = stride // 2
    kv_count = 2 * kv_half
    group = heads // kv_half
    lanes = block * group
    devices = lax.axis_size("ctx")
    core = lax.axis_index("head")
    stretches = 2 * devices

    def owner(place):
        return 2 * place if place < devices else 2 * (stretches - 1 - place) + 1

    def swap(array):
        return lax.ppermute(array, "head", [(0, 1), (1, 0)])

    def from_below(array, distance, turned=()):
        target = {at: at + distance for at in range(stretches - distance)}
        for number, to in enumerate(turned):
            target[devices - 4 + number] = devices + to
        pairs = [(owner(at), owner(to)) for at, to in target.items()]
        return lax.ppermute(array, ("ctx", "head"), pairs)

    smem = pl.BlockSpec(memory_space=pltpu.SMEM)
    vmem = pl.BlockSpec(memory_space=pltpu.VMEM)
    inputs = (key_heads, value_head_rows, queries)
    half = jax.ShapeDtypeStruct((2, kv_half, block, width), jnp.bfloat16)
    keep, given, given_queries = pl.pallas_call(
        pack_kernel,
        out_shape=[half, half, jax.ShapeDtypeStruct((block, heads, width), jnp.bfloat16)],
        in_specs=[pl.BlockSpec(memory_space=pltpu.HBM)] * 3,
        out_specs=[vmem] * 3,
        scratch_shapes=[
            pltpu.VMEM((2, stride, kv_half, width), jnp.bfloat16),
            pltpu.SemaphoreType.DMA((3,)),
        ],
        compiler_params=pltpu.CompilerParams(vmem_limit_bytes=6 * 2**20),
        name="pack",
    )(*[pltpu.with_memory_space_constraint(array, pltpu.HBM) for array in inputs])
    given = swap(given)
    own = jnp.concatenate(
        [jnp.where(core == 0, keep, given), jnp.where(core == 0, given, keep)], axis=1
    )
    own, given_queries = lax.optimization_barrier((own, given_queries))
    partner_queries = swap(given_queries)
    by_three = from_below(own, 3)
    own, partner_queries = lax.optimization_barrier((own, partner_queries))
    by_four = from_below(own, 4)
    by_one = from_below(own, 1)
    by_two = from_below(own, 2)

    def bundle(name, candidates, choices):
        return pl.pallas_call(
            functools.partial(bundle_kernel, devices=devices, choices=choices),
            out_shape=jax.ShapeDtypeStruct((2, *own.shape), own.dtype),
            in_specs=[vmem] * len(candidates),
            out_specs=vmem,
            compiler_params=pltpu.CompilerParams(vmem_limit_bytes=6 * 2**20),
            name=name,
        )(*candidates)

    early = from_below(
        bundle("early", (own, by_three, by_four), EARLY_CHOICES), 4, EARLY_TARGETS
    )
    late = from_below(
        bundle("late", (own, by_one, by_two, by_three, by_four), LATE_CHOICES), 4, LATE_TARGETS
    )

    params = pltpu.CompilerParams(vmem_limit_bytes=14 * 2**20)
    row = jax.ShapeDtypeStruct((kv_count, 1, lanes), jnp.float32)
    state = [row, row, jax.ShapeDtypeStruct((kv_count, width, lanes), jnp.float32)]

    def cost(count):
        work = kv_count * count * block * lanes
        return pl.CostEstimate(
            flops=4 * work * width, bytes_accessed=4 * 2**20, transcendentals=work
        )

    near = (own, by_one, by_two, by_three, by_four)
    folded, far_bias, *known = pl.pallas_call(
        functools.partial(near_kernel, devices=devices, group=group),
        out_shape=[
            jax.ShapeDtypeStruct((kv_count, lanes, width), jnp.bfloat16),
            jax.ShapeDtypeStruct((2, 2 * block, lanes), jnp.float32),
            *state,
        ],
        in_specs=[smem] + [vmem] * (2 + len(near)),
        out_specs=[vmem] * 5,
        scratch_shapes=[pltpu.VMEM((len(near) * block, lanes), jnp.float32)],
        compiler_params=params,
        cost_estimate=cost(len(near)),
        name="near",
    )(doc_lengths, queries, partner_queries, *near)
    known = pl.pallas_call(
        functools.partial(far_kernel, number=0),
        out_shape=state,
        in_specs=[vmem] * 6,
        out_specs=[vmem] * 3,
        compiler_params=params,
        cost_estimate=cost(2),
        name="middle",
    )(folded, far_bias, *known, early)
    return pl.pallas_call(
        functools.partial(far_kernel, number=1),
        out_shape=jax.ShapeDtypeStruct((block, 2 * heads, width), jnp.bfloat16),
        in_specs=[vmem] * 6,
        out_specs=pl.BlockSpec(memory_space=pl.ANY),
        scratch_shapes=[
            pltpu.VMEM((kv_count // 2, block, 2 * group, width), jnp.bfloat16),
            pltpu.SemaphoreType.DMA((kv_count // 2,)),
        ],
        compiler_params=params,
        cost_estimate=cost(2),
        name="finish",
    )(folded, far_bias, *known, late)


def solution(mesh):
    in_specs = (P("ctx", "head", None), P("ctx", "head", None), P("ctx", "head", None), P())
    out_specs = P(("ctx", "head"), None, None)
    return jax.shard_map(shards, mesh=mesh, in_specs=in_specs, out_specs=out_specs, check_vma=False)
```

time: 47.1 us -> 41.2 us (0.87)
  local copies, waits for them, and re-layouts: 2.97 us -> 0.01 us
  waiting for transfers between devices: 20.4 us -> 17.5 us
  starting transfers between devices: 14.9 us -> 15.4 us
    ppermute x6, waiting for transfers between devices: 19.1 us -> 16.5 us  [from_below(): return lax.ppermute(array, ('ctx', 'head'), pairs)]
    pallas_call x2 -> x4, Pallas kernels: 6.65 us -> 7.78 us  [the longest x1 3.22 us: shards(): pl.pallas_call(functools.partial(near_kernel, devices=devices, group=grou...]
    pallas_call x2, Pallas kernels: 1.22 us -> 0.1 us  [bundle(): pl.pallas_call(functools.partial(bundle_kernel, devices=devices, choices=...]
    dynamic_slice x1 -> x0, local copies, waits for them, and re-layouts: 1.08 us -> none  [shards(): lax.dynamic_slice_in_dim(queries, (1 - core) * block, block, 0)]
    another operation x1 -> x0, local copies, waits for them, and re-layouts: 0.94 us -> none  [shards(): packed = jnp.stack([key_heads, value_head_rows])]
    unnamed x5 -> x4, local copies, waits for them, and re-layouts: 0.94 us -> 0.01 us
  transfers between devices with their start and end apart: 8 -> 8, of which waited for: 4 -> 5; matrix products, arithmetic and copies ran while one was open for 4% -> 0% of each run, Pallas kernels for 9% -> 11%
where the time goes in v8:
time: 41.2 us; the launch traced here: 40.9 us
  waiting for transfers between devices  17.5 us (42%)
  starting transfers between devices  15.4 us (37%)
  Pallas kernels  7.88 us (19%)
    ppermute x6, waiting for transfers between devices, from_below(): return lax.ppermute(array, ('ctx', 'head'), pairs)  16.5 us
    ppermute x6, starting transfers between devices, from_below(): return lax.ppermute(array, ('ctx', 'head'), pairs)  14.2 us
    pallas_call x1, Pallas kernels, shards(): pl.pallas_call(functools.partial(near_kernel, devices=devices, group=grou...  3.22 us
    pallas_call x1, Pallas kernels, shards(): pl.pallas_call(functools.partial(far_kernel, number=1), out_shape=jax.Sha...  2.14 us
    pallas_call x1, Pallas kernels, shards(): pl.pallas_call(functools.partial(far_kernel, number=0), out_shape=state,...  1.22 us
    pallas_call x1, Pallas kernels, shards(): pl.pallas_call(pack_kernel, out_shape=[half, half, jax.ShapeDtypeStruct((...  1.2 us
    ppermute x2, starting transfers between devices, swap(): return lax.ppermute(array, 'head', [(0, 1), (1, 0)])  1.17 us
    ppermute x2, waiting for transfers between devices, swap(): return lax.ppermute(array, 'head', [(0, 1), (1, 0)])  0.99 us
  transfers between devices with their start and end apart: 8, of which 5 were waited for; matrix products, arithmetic and copies ran while one was open for 0% of the time, Pallas kernels for 11%

profile of v8, /device:TPU:19, one launch (start us, length us, event | category | flops | bytes accessed | tf_op | source)
XLA Modules:
  0.0 40.9 jit_solution(4738781279380896339)
XLA Ops:
  0.0 1.2 %pack.1 = (bf16[2,4,64,128]{3,2,1,0:T(8,128)(2,1)S(1)}, bf16[2,4,64,128]{3,2,1,0:T(8,128)(2,1)S(1)}, bf16[64,32,128]{2,1,0:T(8,128)(2,1)S(1)}) custom-call(bf16[128,4,128]{2,1,0:T(4,128)(2,1)} %keys.1, bf16[128,4,128]{2,1,0:T(4,128)(2,1)} %values.1, bf16[128,32,128]{2,1,0:T(8,128)(2,1)} %queries.3), custom_call_target="tpu_custom_call" | custom-call | tf_op jit(solution)/shard_map/pack/pallas_call | solution.py:237
  1.2 0.7 %collective-permute-start = (bf16[2,4,64,128]{3,2,1,0:T(8,128)(2,1)S(1)}, bf16[2,4,64,128]{3,2,1,0:T(8,128)(2,1)S(1)}, u32[]{:S(2)}, u32[]{:S(2)}) collective-permute-start(bf16[2,4,64,128]{3,2,1,0:T(8,128)(2,1)S(1)} %get-tuple-element.21), channel_id=1, source_target_pairs={{0,1},{1,0},{2,3},{3,2},{4,5},{5,4},{6,7},{7,6},{8,9},{9,8},{10,11... | collective-permute-start | bytes 393224 | tf_op jit(solution)/shard_map/ppermute | solution.py:224
  2.0 1.0 %collective-permute-done = bf16[2,4,64,128]{3,2,1,0:T(8,128)(2,1)S(1)} collective-permute-done((bf16[2,4,64,128]{3,2,1,0:T(8,128)(2,1)S(1)}, bf16[2,4,64,128]{3,2,1,0:T(8,128)(2,1)S(1)}, u32[]{:S(2)}, u32[]{:S(2)}) %collective-permute-start) | collective-permute-done | bytes 131104 | tf_op jit(solution)/shard_map/ppermute | solution.py:224
  2.9 0.0 copy-start
  2.9 0.0 copy-start.1
  3.0 0.4 %collective-permute-start.1 = (bf16[64,32,128]{2,1,0:T(8,128)(2,1)S(1)}, bf16[64,32,128]{2,1,0:T(8,128)(2,1)S(1)}, u32[]{:S(2)}, u32[]{:S(2)}) collective-permute-start(bf16[64,32,128]{2,1,0:T(8,128)(2,1)S(1)} %get-tuple-element.24), channel_id=1, source_target_pairs={{0,1},{1,0},{2,3},{3,2},{4,5},{5,4},{6,7},{7,6},{8,9},{9,8},{10,11... | collective-permute-start | bytes 1572872 | tf_op jit(solution)/shard_map/ppermute | solution.py:224
  3.4 3.0 %collective-permute-start.4 = (bf16[2,8,64,128]{3,2,1,0:T(8,128)(2,1)S(1)}, bf16[2,8,64,128]{3,2,1,0:T(8,128)(2,1)S(1)}, u32[]{:S(2)}, u32[]{:S(2)}) collective-permute-start(bf16[2,8,64,128]{3,2,1,0:T(8,128)(2,1)S(1)} %pad_maximum_fusion.refs_0_), channel_id=1, source_target_pairs={{0,6},{2,8},{4,10},{6,12},{8,14},{10,16},{12,18},{14,20},{16,22},{... | collective-permute-start | bytes 786440 | tf_op jit(solution)/shard_map/ppermute | solution.py:231
  6.4 0.0 collective-permute-done.1.partner_queries
  6.4 2.1 %collective-permute-start.5 = (bf16[2,8,64,128]{3,2,1,0:T(8,128)(2,1)S(1)}, bf16[2,8,64,128]{3,2,1,0:T(8,128)(2,1)S(1)}, u32[]{:S(2)}, u32[]{:S(2)}) collective-permute-start(bf16[2,8,64,128]{3,2,1,0:T(8,128)(2,1)S(1)} %pad_maximum_fusion.refs_0_), channel_id=1, source_target_pairs={{0,8},{2,10},{4,12},{6,14},{8,16},{10,18},{12,20},{14,22},{16,24},... | collective-permute-start | bytes 786440 | tf_op jit(solution)/shard_map/ppermute | solution.py:231
  8.5 2.0 %collective-permute-start.3 = (bf16[2,8,64,128]{3,2,1,0:T(8,128)(2,1)S(1)}, bf16[2,8,64,128]{3,2,1,0:T(8,128)(2,1)S(1)}, u32[]{:S(2)}, u32[]{:S(2)}) collective-permute-start(bf16[2,8,64,128]{3,2,1,0:T(8,128)(2,1)S(1)} %pad_maximum_fusion.refs_0_), channel_id=1, source_target_pairs={{0,4},{2,6},{4,8},{6,10},{8,12},{10,14},{12,16},{14,18},{16,20},{1... | collective-permute-start | bytes 786440 | tf_op jit(solution)/shard_map/ppermute | solution.py:231
  10.5 3.1 %collective-permute-start.2 = (bf16[2,8,64,128]{3,2,1,0:T(8,128)(2,1)S(1)}, bf16[2,8,64,128]{3,2,1,0:T(8,128)(2,1)S(1)}, u32[]{:S(2)}, u32[]{:S(2)}) collective-permute-start(bf16[2,8,64,128]{3,2,1,0:T(8,128)(2,1)S(1)} %pad_maximum_fusion.refs_0_), channel_id=1, source_target_pairs={{0,2},{2,4},{4,6},{6,8},{8,10},{10,12},{12,14},{14,16},{16,18},{18... | collective-permute-start | bytes 786440 | tf_op jit(solution)/shard_map/ppermute | solution.py:231
  13.6 0.0 collective-permute-done.4.refs_3_.refs_1_
  13.6 2.5 %collective-permute-done.5.refs_4_.refs_2_ = bf16[2,8,64,128]{3,2,1,0:T(8,128)(2,1)S(1)} collective-permute-done((bf16[2,8,64,128]{3,2,1,0:T(8,128)(2,1)S(1)}, bf16[2,8,64,128]{3,2,1,0:T(8,128)(2,1)S(1)}, u32[]{:S(2)}, u32[]{:S(2)}) %collective-permute-start.5) | collective-permute-done | bytes 262176 | tf_op jit(solution)/shard_map/ppermute | solution.py:231
  16.1 2.1 %collective-permute-start.6 = (bf16[2,2,8,64,128]{4,3,2,1,0:T(8,128)(2,1)S(1)}, bf16[2,2,8,64,128]{4,3,2,1,0:T(8,128)(2,1)S(1)}, u32[]{:S(2)}, u32[]{:S(2)}) collective-permute-start(bf16[2,2,8,64,128]{4,3,2,1,0:T(8,128)(2,1)S(1)} %early.1), channel_id=1, source_target_pairs={{0,8},{2,10},{4,12},{6,14},{8,16},{10,18},{12,20},{14,22},{16,24},... | collective-permute-start | bytes 1572872 | tf_op jit(solution)/shard_map/ppermute | solution.py:231
  18.2 4.9 %collective-permute-done.3.refs_2_ = bf16[2,8,64,128]{3,2,1,0:T(8,128)(2,1)S(1)} collective-permute-done((bf16[2,8,64,128]{3,2,1,0:T(8,128)(2,1)S(1)}, bf16[2,8,64,128]{3,2,1,0:T(8,128)(2,1)S(1)}, u32[]{:S(2)}, u32[]{:S(2)}) %collective-permute-start.3) | collective-permute-done | bytes 262176 | tf_op jit(solution)/shard_map/ppermute | solution.py:231
  23.1 0.0 collective-permute-done.2.refs_1_
  23.1 0.1 late.1
  23.2 2.0 %collective-permute-start.7 = (bf16[2,2,8,64,128]{4,3,2,1,0:T(8,128)(2,1)S(1)}, bf16[2,2,8,64,128]{4,3,2,1,0:T(8,128)(2,1)S(1)}, u32[]{:S(2)}, u32[]{:S(2)}) collective-permute-start(bf16[2,2,8,64,128]{4,3,2,1,0:T(8,128)(2,1)S(1)} %late.1), channel_id=1, source_target_pairs={{0,8},{2,10},{4,12},{6,14},{8,16},{10,18},{12,20},{14,22},{16,24},... | collective-permute-start | bytes 1572872 | tf_op jit(solution)/shard_map/ppermute | solution.py:231
  25.2 0.0 copy-done
  25.2 0.0 copy-done.1
  25.2 3.2 %near.1 = (bf16[8,512,128]{2,1,0:T(8,128)(2,1)S(1)}, f32[2,128,512]{2,1,0:T(8,128)S(1)}, f32[8,1,512]{2,1,0:T(1,128)S(1)}, f32[8,1,512]{2,1,0:T(1,128)S(1)}, f32[8,128,512]{2,1,0:T(8,128)S(1)}) custom-call(s32[8]{0:T(128)S(1)} %copy-done.1, bf16[128,32,128]{2,1,0:T(8,128)(2,1)S(1)} %copy-done, ...), custom_call_target="tpu_custom_call" | custom-call | flops 671088640 | bytes 4194304 | tf_op jit(solution)/shard_map/near/pallas_call | solution.py:289
  28.4 5.0 %collective-permute-done.6.blocks = bf16[2,2,8,64,128]{4,3,2,1,0:T(8,128)(2,1)S(1)} collective-permute-done((bf16[2,2,8,64,128]{4,3,2,1,0:T(8,128)(2,1)S(1)}, bf16[2,2,8,64,128]{4,3,2,1,0:T(8,128)(2,1)S(1)}, u32[]{:S(2)}, u32[]{:S(2)}) %collective-permute-start.6) | collective-permute-done | bytes 524320 | tf_op jit(solution)/shard_map/ppermute | solution.py:231
  33.4 1.2 %middle.1 = (f32[8,1,512]{2,1,0:T(1,128)S(1)}, f32[8,1,512]{2,1,0:T(1,128)S(1)}, f32[8,128,512]{2,1,0:T(8,128)S(1)}) custom-call(bf16[8,512,128]{2,1,0:T(8,128)(2,1)S(1)} %get-tuple-element.27.folded, f32[2,128,512]{2,1,0:T(8,128)S(1)} %get-tuple-element.28.far_bias, f32[8,1,512]{2,1,0:T(1,128)S(1)} %get-tuple-element.29.peak, ...), custom_call_target="tpu_custom_call" | custom-call | flops 268435456 | bytes 4194304 | tf_op jit(solution)/shard_map/middle/pallas_call | solution.py:303
  34.7 4.1 %collective-permute-done.7.blocks = bf16[2,2,8,64,128]{4,3,2,1,0:T(8,128)(2,1)S(1)} collective-permute-done((bf16[2,2,8,64,128]{4,3,2,1,0:T(8,128)(2,1)S(1)}, bf16[2,2,8,64,128]{4,3,2,1,0:T(8,128)(2,1)S(1)}, u32[]{:S(2)}, u32[]{:S(2)}) %collective-permute-start.7) | collective-permute-done | bytes 524320 | tf_op jit(solution)/shard_map/ppermute | solution.py:231
  38.8 2.1 %finish.1 = bf16[64,64,128]{2,1,0:T(8,128)(2,1)} custom-call(bf16[8,512,128]{2,1,0:T(8,128)(2,1)S(1)} %get-tuple-element.27.folded, f32[2,128,512]{2,1,0:T(8,128)S(1)} %get-tuple-element.28.far_bias, f32[8,1,512]{2,1,0:T(1,128)S(1)} %get-tuple-element.32.peak, f32[8,1,512]{2,1,0:T(1,128)S(1)} %get-tuple-element.33.sums, ...), custom_call_target="tpu_custom_call" | custom-call | flops 268435456 | bytes 4194304 | tf_op jit(solution)/shard_map/finish/pallas_call | solution.py:312
  (3 shorter events, 0.1 us)
Async XLA Ops:
  1.2 1.7 %collective-permute-start = (bf16[2,4,64,128]{3,2,1,0:T(8,128)(2,1)S(1)}, bf16[2,4,64,128]{3,2,1,0:T(8,128)(2,1)S(1)}, u32[]{:S(2)}, u32[]{:S(2)}) collective-permute-start(bf16[2,4,64,128]{3,2,1,0:T(8,128)(2,1)S(1)} %get-tuple-element.21), channel_id=1, source_target_pairs={{0,1},{1,0},{2,3},{3,2},{4,5},{5,4},{6,7},{7,6},{8,9},{9,8},{10,11... | collective-permute-start | bytes 393224 | tf_op jit(solution)/shard_map/ppermute | solution.py:224
  2.9 22.2 %copy-start = (bf16[128,32,128]{2,1,0:T(8,128)(2,1)S(1)}, bf16[128,32,128]{2,1,0:T(8,128)(2,1)}, u32[]{:S(2)}) copy-start(bf16[128,32,128]{2,1,0:T(8,128)(2,1)} %queries.3) | copy-start | bytes 3145732
  2.9 22.2 %copy-start.1 = (s32[8]{0:T(128)S(1)}, s32[8]{0:T(128)}, u32[]{:S(2)}) copy-start(s32[8]{0:T(128)} %doc_lengths.1) | copy-start | bytes 100
  3.0 3.4 %collective-permute-start.1 = (bf16[64,32,128]{2,1,0:T(8,128)(2,1)S(1)}, bf16[64,32,128]{2,1,0:T(8,128)(2,1)S(1)}, u32[]{:S(2)}, u32[]{:S(2)}) collective-permute-start(bf16[64,32,128]{2,1,0:T(8,128)(2,1)S(1)} %get-tuple-element.24), channel_id=1, source_target_pairs={{0,1},{1,0},{2,3},{3,2},{4,5},{5,4},{6,7},{7,6},{8,9},{9,8},{10,11... | collective-permute-start | bytes 1572872 | tf_op jit(solution)/shard_map/ppermute | solution.py:224
  3.4 10.2 %collective-permute-start.4 = (bf16[2,8,64,128]{3,2,1,0:T(8,128)(2,1)S(1)}, bf16[2,8,64,128]{3,2,1,0:T(8,128)(2,1)S(1)}, u32[]{:S(2)}, u32[]{:S(2)}) collective-permute-start(bf16[2,8,64,128]{3,2,1,0:T(8,128)(2,1)S(1)} %pad_maximum_fusion.refs_0_), channel_id=1, source_target_pairs={{0,6},{2,8},{4,10},{6,12},{8,14},{10,16},{12,18},{14,20},{16,22},{... | collective-permute-start | bytes 786440 | tf_op jit(solution)/shard_map/ppermute | solution.py:231
  6.4 9.6 %collective-permute-start.5 = (bf16[2,8,64,128]{3,2,1,0:T(8,128)(2,1)S(1)}, bf16[2,8,64,128]{3,2,1,0:T(8,128)(2,1)S(1)}, u32[]{:S(2)}, u32[]{:S(2)}) collective-permute-start(bf16[2,8,64,128]{3,2,1,0:T(8,128)(2,1)S(1)} %pad_maximum_fusion.refs_0_), channel_id=1, source_target_pairs={{0,8},{2,10},{4,12},{6,14},{8,16},{10,18},{12,20},{14,22},{16,24},... | collective-permute-start | bytes 786440 | tf_op jit(solution)/shard_map/ppermute | solution.py:231
  8.5 14.6 %collective-permute-start.3 = (bf16[2,8,64,128]{3,2,1,0:T(8,128)(2,1)S(1)}, bf16[2,8,64,128]{3,2,1,0:T(8,128)(2,1)S(1)}, u32[]{:S(2)}, u32[]{:S(2)}) collective-permute-start(bf16[2,8,64,128]{3,2,1,0:T(8,128)(2,1)S(1)} %pad_maximum_fusion.refs_0_), channel_id=1, source_target_pairs={{0,4},{2,6},{4,8},{6,10},{8,12},{10,14},{12,16},{14,18},{16,20},{1... | collective-permute-start | bytes 786440 | tf_op jit(solution)/shard_map/ppermute | solution.py:231
  10.5 12.6 %collective-permute-start.2 = (bf16[2,8,64,128]{3,2,1,0:T(8,128)(2,1)S(1)}, bf16[2,8,64,128]{3,2,1,0:T(8,128)(2,1)S(1)}, u32[]{:S(2)}, u32[]{:S(2)}) collective-permute-start(bf16[2,8,64,128]{3,2,1,0:T(8,128)(2,1)S(1)} %pad_maximum_fusion.refs_0_), channel_id=1, source_target_pairs={{0,2},{2,4},{4,6},{6,8},{8,10},{10,12},{12,14},{14,16},{16,18},{18... | collective-permute-start | bytes 786440 | tf_op jit(solution)/shard_map/ppermute | solution.py:231
  16.1 17.3 %collective-permute-start.6 = (bf16[2,2,8,64,128]{4,3,2,1,0:T(8,128)(2,1)S(1)}, bf16[2,2,8,64,128]{4,3,2,1,0:T(8,128)(2,1)S(1)}, u32[]{:S(2)}, u32[]{:S(2)}) collective-permute-start(bf16[2,2,8,64,128]{4,3,2,1,0:T(8,128)(2,1)S(1)} %early.1), channel_id=1, source_target_pairs={{0,8},{2,10},{4,12},{6,14},{8,16},{10,18},{12,20},{14,22},{16,24},... | collective-permute-start | bytes 1572872 | tf_op jit(solution)/shard_map/ppermute | solution.py:231
  23.2 15.6 %collective-permute-start.7 = (bf16[2,2,8,64,128]{4,3,2,1,0:T(8,128)(2,1)S(1)}, bf16[2,2,8,64,128]{4,3,2,1,0:T(8,128)(2,1)S(1)}, u32[]{:S(2)}, u32[]{:S(2)}) collective-permute-start(bf16[2,2,8,64,128]{4,3,2,1,0:T(8,128)(2,1)S(1)} %late.1), channel_id=1, source_target_pairs={{0,8},{2,10},{4,12},{6,14},{8,16},{10,18},{12,20},{14,22},{16,24},... | collective-permute-start | bytes 1572872 | tf_op jit(solution)/shard_map/ppermute | solution.py:231

commit v9 on v8

--- a/solution.py
+++ b/solution.py
@@ -55,23 +55,28 @@
     )
 
 
-def pack_kernel(keys, values, queries, keep, given, given_queries, staged, sems):
+def pack_kernel(*refs, kept):
+    if kept:
+        keys, values, queries, out, given_queries, staged, sems = refs
+    else:
+        keys, values, out, staged, sems = refs
     core = lax.axis_index("head")
-    block = given_queries.shape[0]
-    kept_rows, given_rows = pl.ds(core * block, block), pl.ds((1 - core) * block, block)
+    block = out.shape[2]
+    given_rows = pl.ds((1 - core) * block, block)
+    rows = pl.ds(core * block, block) if kept else given_rows
     copies = [
-        pltpu.make_async_copy(keys, staged.at[0], sems.at[0]),
-        pltpu.make_async_copy(values, staged.at[1], sems.at[1]),
-        pltpu.make_async_copy(queries.at[given_rows], given_queries, sems.at[2]),
+        pltpu.make_async_copy(keys.at[rows], staged.at[0], sems.at[0]),
+        pltpu.make_async_copy(values.at[rows], staged.at[1], sems.at[1]),
     ]
+    if kept:
+        copies.append(pltpu.make_async_copy(queries.at[given_rows], given_queries, sems.at[2]))
     for copy in copies:
         copy.start()
     for kind in range(2):
         copies[kind].wait()
-        for rows, out in ((given_rows, given), (kept_rows, keep)):
-            part = staged[kind, rows].astype(jnp.float32)
-            out[kind] = jnp.swapaxes(part, 0, 1).astype(out.dtype)
-    copies[2].wait()
+        out[kind] = jnp.swapaxes(staged[kind].astype(jnp.float32), 0, 1).astype(out.dtype)
+    for copy in copies[2:]:
+        copy.wait()
 
 
 def chain_position(devices):
@@ -195,13 +200,18 @@
                 result = mixed[at] * scale + mixes[slots[at]] * (shrinks[at] * scale)
                 done.append(result.T.reshape(block, group, width))
             pair = slots[part] // 2
-            staged[pair] = jnp.concatenate(done, axis=1).astype(staged.dtype)
+            done = jnp.concatenate(done, axis=1).astype(staged.dtype)
             first = pl.multiple_of((first_head + part) * group, 2 * group)
-            copy = pltpu.make_async_copy(
-                staged.at[pair], out.at[:, pl.ds(first, 2 * group)], sems.at[pair]
-            )
-            copy.start()
-            copies.append(copy)
+            for piece in range(2):
+                rows = slice(piece * block // 2, (piece + 1) * block // 2)
+                staged[pair, rows] = done[rows]
+                copy = pltpu.make_async_copy(
+                    staged.at[pair, rows],
+                    out.at[rows, pl.ds(first, 2 * group)],
+                    sems.at[pair, piece],
+                )
+                copy.start()
+                copies.append(copy)
     for copy in copies:
         copy.wait()
 
@@ -232,21 +242,30 @@
 
     smem = pl.BlockSpec(memory_space=pltpu.SMEM)
     vmem = pl.BlockSpec(memory_space=pltpu.VMEM)
-    inputs = (key_heads, value_head_rows, queries)
-    half = jax.ShapeDtypeStruct((2, kv_half, block, width), jnp.bfloat16)
-    keep, given, given_queries = pl.pallas_call(
-        pack_kernel,
-        out_shape=[half, half, jax.ShapeDtypeStruct((block, heads, width), jnp.bfloat16)],
-        in_specs=[pl.BlockSpec(memory_space=pltpu.HBM)] * 3,
-        out_specs=[vmem] * 3,
-        scratch_shapes=[
-            pltpu.VMEM((2, stride, kv_half, width), jnp.bfloat16),
-            pltpu.SemaphoreType.DMA((3,)),
-        ],
-        compiler_params=pltpu.CompilerParams(vmem_limit_bytes=6 * 2**20),
-        name="pack",
-    )(*[pltpu.with_memory_space_constraint(array, pltpu.HBM) for array in inputs])
+    def pack(kept):
+        arrays = (key_heads, value_head_rows, queries) if kept else (key_heads, value_head_rows)
+        out_shape = [jax.ShapeDtypeStruct((2, kv_half, block, width), jnp.bfloat16)]
+        if kept:
+            out_shape.append(jax.ShapeDtypeStruct((block, heads, width), jnp.bfloat16))
+        return pl.pallas_call(
+            functools.partial(pack_kernel, kept=kept),
+            out_shape=out_shape,
+            in_specs=[pl.BlockSpec(memory_space=pltpu.HBM)] * len(arrays),
+            out_specs=[vmem] * len(out_shape),
+            scratch_shapes=[
+                pltpu.VMEM((2, block, kv_half, width), jnp.bfloat16),
+                pltpu.SemaphoreType.DMA((len(arrays),)),
+            ],
+            compiler_params=pltpu.CompilerParams(vmem_limit_bytes=6 * 2**20),
+            cost_estimate=pl.CostEstimate(
+                flops=0, bytes_accessed=len(arrays) * 2**20, transcendentals=0
+            ),
+            name="keep" if kept else "give",
+        )(*[pltpu.with_memory_space_constraint(array, pltpu.HBM) for array in arrays])
+
+    (given,) = pack(False)
     given = swap(given)
+    keep, given_queries = pack(True)
     own = jnp.concatenate(
         [jnp.where(core == 0, keep, given), jnp.where(core == 0, given, keep)], axis=1
     )
@@ -316,7 +335,7 @@
         out_specs=pl.BlockSpec(memory_space=pl.ANY),
         scratch_shapes=[
             pltpu.VMEM((kv_count // 2, block, 2 * group, width), jnp.bfloat16),
-            pltpu.SemaphoreType.DMA((kv_count // 2,)),
+            pltpu.SemaphoreType.DMA((kv_count // 2, 2)),
         ],
         compiler_params=params,
         cost_estimate=cost(2),

time: 41.2 us -> 41.2 us (level)
  waiting for transfers between devices: 17.5 us -> 16.5 us
  Pallas kernels: 7.88 us -> 8.84 us
    ppermute x2, waiting for transfers between devices: 0.99 us -> 0.01 us  [swap(): return lax.ppermute(array, 'head', [(0, 1), (1, 0)])]
    pallas_call x1 -> x2, Pallas kernels: 1.2 us -> 2.07 us  [pack(): pl.pallas_call(functools.partial(pack_kernel, kept=kept), out_shape=out_s...]
  transfers between devices with their start and end apart: 8 -> 8, of which waited for: 5 -> 4; matrix products, arithmetic and copies ran while one was open for 0% -> 0% of each run, Pallas kernels for 11% -> 14%
where the time goes in v9:
time: 41.2 us; the launch traced here: 40.9 us
  waiting for transfers between devices  16.5 us (40%)
  starting transfers between devices  15.3 us (37%)
  Pallas kernels  8.84 us (21%)
    ppermute x6, waiting for transfers between devices, from_below(): return lax.ppermute(array, ('ctx', 'head'), pairs)  16.5 us
    ppermute x6, starting transfers between devices, from_below(): return lax.ppermute(array, ('ctx', 'head'), pairs)  14.3 us
    pallas_call x1, Pallas kernels, shards(): pl.pallas_call(functools.partial(near_kernel, devices=devices, group=grou...  3.25 us
    pallas_call x1, Pallas kernels, shards(): pl.pallas_call(functools.partial(far_kernel, number=1), out_shape=jax.Sha...  2.19 us
    pallas_call x2, Pallas kernels, pack(): pl.pallas_call(functools.partial(pack_kernel, kept=kept), out_shape=out_s...  2.07 us
    pallas_call x1, Pallas kernels, shards(): pl.pallas_call(functools.partial(far_kernel, number=0), out_shape=state,...  1.22 us
    ppermute x2, starting transfers between devices, swap(): return lax.ppermute(array, 'head', [(0, 1), (1, 0)])  0.96 us
  transfers between devices with their start and end apart: 8, of which 4 were waited for; matrix products, arithmetic and copies ran while one was open for 0% of the time, Pallas kernels for 14%

profile of v9, /device:TPU:19, one launch (start us, length us, event | category | flops | bytes accessed | tf_op | source)
XLA Modules:
  0.0 40.9 jit_solution(7989866658929357171)
XLA Ops:
  0.0 0.9 %give.1 = bf16[2,4,64,128]{3,2,1,0:T(8,128)(2,1)S(1)} custom-call(bf16[128,4,128]{2,1,0:T(4,128)(2,1)} %refs_0_.3, bf16[128,4,128]{2,1,0:T(4,128)(2,1)} %refs_1_.3), custom_call_target="tpu_custom_call" | custom-call | bytes 2097152 | tf_op jit(solution)/shard_map/give/pallas_call | solution.py:250
  0.9 0.7 %collective-permute-start = (bf16[2,4,64,128]{3,2,1,0:T(8,128)(2,1)S(1)}, bf16[2,4,64,128]{3,2,1,0:T(8,128)(2,1)S(1)}, u32[]{:S(2)}, u32[]{:S(2)}) collective-permute-start(bf16[2,4,64,128]{3,2,1,0:T(8,128)(2,1)S(1)} %give.1), channel_id=1, source_target_pairs={{0,1},{1,0},{2,3},{3,2},{4,5},{5,4},{6,7},{7,6},{8,9},{9,8},{10,11... | collective-permute-start | bytes 393224 | tf_op jit(solution)/shard_map/ppermute | solution.py:234
  1.7 1.1 %keep.1 = (bf16[2,4,64,128]{3,2,1,0:T(8,128)(2,1)S(1)}, bf16[64,32,128]{2,1,0:T(8,128)(2,1)S(1)}) custom-call(bf16[128,4,128]{2,1,0:T(4,128)(2,1)} %refs_0_.3, bf16[128,4,128]{2,1,0:T(4,128)(2,1)} %refs_1_.3, bf16[128,32,128]{2,1,0:T(8,128)(2,1)} %queries.1), custom_call_target="tpu_custom_call" | custom-call | bytes 3145728 | tf_op jit(solution)/shard_map/keep/pallas_call | solution.py:250
  2.8 0.0 collective-permute-done
  2.8 0.0 copy-start
  2.9 0.0 copy-start.1
  2.9 0.2 collective-permute-start.1
  3.2 3.1 %collective-permute-start.4 = (bf16[2,8,64,128]{3,2,1,0:T(8,128)(2,1)S(1)}, bf16[2,8,64,128]{3,2,1,0:T(8,128)(2,1)S(1)}, u32[]{:S(2)}, u32[]{:S(2)}) collective-permute-start(bf16[2,8,64,128]{3,2,1,0:T(8,128)(2,1)S(1)} %pad_maximum_fusion.refs_0_), channel_id=1, source_target_pairs={{0,6},{2,8},{4,10},{6,12},{8,14},{10,16},{12,18},{14,20},{16,22},{... | collective-permute-start | bytes 786440 | tf_op jit(solution)/shard_map/ppermute | solution.py:241
  6.3 0.0 collective-permute-done.1.partner_queries
  6.3 2.1 %collective-permute-start.5 = (bf16[2,8,64,128]{3,2,1,0:T(8,128)(2,1)S(1)}, bf16[2,8,64,128]{3,2,1,0:T(8,128)(2,1)S(1)}, u32[]{:S(2)}, u32[]{:S(2)}) collective-permute-start(bf16[2,8,64,128]{3,2,1,0:T(8,128)(2,1)S(1)} %pad_maximum_fusion.refs_0_), channel_id=1, source_target_pairs={{0,8},{2,10},{4,12},{6,14},{8,16},{10,18},{12,20},{14,22},{16,24},... | collective-permute-start | bytes 786440 | tf_op jit(solution)/shard_map/ppermute | solution.py:241
  8.4 2.0 %collective-permute-start.3 = (bf16[2,8,64,128]{3,2,1,0:T(8,128)(2,1)S(1)}, bf16[2,8,64,128]{3,2,1,0:T(8,128)(2,1)S(1)}, u32[]{:S(2)}, u32[]{:S(2)}) collective-permute-start(bf16[2,8,64,128]{3,2,1,0:T(8,128)(2,1)S(1)} %pad_maximum_fusion.refs_0_), channel_id=1, source_target_pairs={{0,4},{2,6},{4,8},{6,10},{8,12},{10,14},{12,16},{14,18},{16,20},{1... | collective-permute-start | bytes 786440 | tf_op jit(solution)/shard_map/ppermute | solution.py:241
  10.4 3.1 %collective-permute-start.2 = (bf16[2,8,64,128]{3,2,1,0:T(8,128)(2,1)S(1)}, bf16[2,8,64,128]{3,2,1,0:T(8,128)(2,1)S(1)}, u32[]{:S(2)}, u32[]{:S(2)}) collective-permute-start(bf16[2,8,64,128]{3,2,1,0:T(8,128)(2,1)S(1)} %pad_maximum_fusion.refs_0_), channel_id=1, source_target_pairs={{0,2},{2,4},{4,6},{6,8},{8,10},{10,12},{12,14},{14,16},{16,18},{18... | collective-permute-start | bytes 786440 | tf_op jit(solution)/shard_map/ppermute | solution.py:241
  13.4 0.0 collective-permute-done.4.refs_3_.refs_1_
  13.5 2.5 %collective-permute-done.5.refs_4_.refs_2_ = bf16[2,8,64,128]{3,2,1,0:T(8,128)(2,1)S(1)} collective-permute-done((bf16[2,8,64,128]{3,2,1,0:T(8,128)(2,1)S(1)}, bf16[2,8,64,128]{3,2,1,0:T(8,128)(2,1)S(1)}, u32[]{:S(2)}, u32[]{:S(2)}) %collective-permute-start.5) | collective-permute-done | bytes 262176 | tf_op jit(solution)/shard_map/ppermute | solution.py:241
  16.0 2.1 %collective-permute-start.6 = (bf16[2,2,8,64,128]{4,3,2,1,0:T(8,128)(2,1)S(1)}, bf16[2,2,8,64,128]{4,3,2,1,0:T(8,128)(2,1)S(1)}, u32[]{:S(2)}, u32[]{:S(2)}) collective-permute-start(bf16[2,2,8,64,128]{4,3,2,1,0:T(8,128)(2,1)S(1)} %early.1), channel_id=1, source_target_pairs={{0,8},{2,10},{4,12},{6,14},{8,16},{10,18},{12,20},{14,22},{16,24},... | collective-permute-start | bytes 1572872 | tf_op jit(solution)/shard_map/ppermute | solution.py:241
  18.1 4.9 %collective-permute-done.3.refs_2_ = bf16[2,8,64,128]{3,2,1,0:T(8,128)(2,1)S(1)} collective-permute-done((bf16[2,8,64,128]{3,2,1,0:T(8,128)(2,1)S(1)}, bf16[2,8,64,128]{3,2,1,0:T(8,128)(2,1)S(1)}, u32[]{:S(2)}, u32[]{:S(2)}) %collective-permute-start.3) | collective-permute-done | bytes 262176 | tf_op jit(solution)/shard_map/ppermute | solution.py:241
  22.9 0.0 collective-permute-done.2.refs_1_
  22.9 0.1 late.1
  23.0 2.0 %collective-permute-start.7 = (bf16[2,2,8,64,128]{4,3,2,1,0:T(8,128)(2,1)S(1)}, bf16[2,2,8,64,128]{4,3,2,1,0:T(8,128)(2,1)S(1)}, u32[]{:S(2)}, u32[]{:S(2)}) collective-permute-start(bf16[2,2,8,64,128]{4,3,2,1,0:T(8,128)(2,1)S(1)} %late.1), channel_id=1, source_target_pairs={{0,8},{2,10},{4,12},{6,14},{8,16},{10,18},{12,20},{14,22},{16,24},... | collective-permute-start | bytes 1572872 | tf_op jit(solution)/shard_map/ppermute | solution.py:241
  25.0 0.0 copy-done
  25.0 0.0 copy-done.1
  25.0 3.2 %near.1 = (bf16[8,512,128]{2,1,0:T(8,128)(2,1)S(1)}, f32[2,128,512]{2,1,0:T(8,128)S(1)}, f32[8,1,512]{2,1,0:T(1,128)S(1)}, f32[8,1,512]{2,1,0:T(1,128)S(1)}, f32[8,128,512]{2,1,0:T(8,128)S(1)}) custom-call(s32[8]{0:T(128)S(1)} %copy-done.1, bf16[128,32,128]{2,1,0:T(8,128)(2,1)S(1)} %copy-done, ...), custom_call_target="tpu_custom_call" | custom-call | flops 671088640 | bytes 4194304 | tf_op jit(solution)/shard_map/near/pallas_call | solution.py:308
  28.3 5.1 %collective-permute-done.6.blocks = bf16[2,2,8,64,128]{4,3,2,1,0:T(8,128)(2,1)S(1)} collective-permute-done((bf16[2,2,8,64,128]{4,3,2,1,0:T(8,128)(2,1)S(1)}, bf16[2,2,8,64,128]{4,3,2,1,0:T(8,128)(2,1)S(1)}, u32[]{:S(2)}, u32[]{:S(2)}) %collective-permute-start.6) | collective-permute-done | bytes 524320 | tf_op jit(solution)/shard_map/ppermute | solution.py:241
  33.3 1.2 %middle.1 = (f32[8,1,512]{2,1,0:T(1,128)S(1)}, f32[8,1,512]{2,1,0:T(1,128)S(1)}, f32[8,128,512]{2,1,0:T(8,128)S(1)}) custom-call(bf16[8,512,128]{2,1,0:T(8,128)(2,1)S(1)} %get-tuple-element.25.folded, f32[2,128,512]{2,1,0:T(8,128)S(1)} %get-tuple-element.26.far_bias, f32[8,1,512]{2,1,0:T(1,128)S(1)} %get-tuple-element.27.peak, ...), custom_call_target="tpu_custom_call" | custom-call | flops 268435456 | bytes 4194304 | tf_op jit(solution)/shard_map/middle/pallas_call | solution.py:322
  34.6 4.1 %collective-permute-done.7.blocks = bf16[2,2,8,64,128]{4,3,2,1,0:T(8,128)(2,1)S(1)} collective-permute-done((bf16[2,2,8,64,128]{4,3,2,1,0:T(8,128)(2,1)S(1)}, bf16[2,2,8,64,128]{4,3,2,1,0:T(8,128)(2,1)S(1)}, u32[]{:S(2)}, u32[]{:S(2)}) %collective-permute-start.7) | collective-permute-done | bytes 524320 | tf_op jit(solution)/shard_map/ppermute | solution.py:241
  38.7 2.2 %finish.1 = bf16[64,64,128]{2,1,0:T(8,128)(2,1)} custom-call(bf16[8,512,128]{2,1,0:T(8,128)(2,1)S(1)} %get-tuple-element.25.folded, f32[2,128,512]{2,1,0:T(8,128)S(1)} %get-tuple-element.26.far_bias, f32[8,1,512]{2,1,0:T(1,128)S(1)} %get-tuple-element.30.peak, f32[8,1,512]{2,1,0:T(1,128)S(1)} %get-tuple-element.31.sums, ...), custom_call_target="tpu_custom_call" | custom-call | flops 268435456 | bytes 4194304 | tf_op jit(solution)/shard_map/finish/pallas_call | solution.py:331
  (3 shorter events, 0.1 us)
Async XLA Ops:
  0.9 1.9 %collective-permute-start = (bf16[2,4,64,128]{3,2,1,0:T(8,128)(2,1)S(1)}, bf16[2,4,64,128]{3,2,1,0:T(8,128)(2,1)S(1)}, u32[]{:S(2)}, u32[]{:S(2)}) collective-permute-start(bf16[2,4,64,128]{3,2,1,0:T(8,128)(2,1)S(1)} %give.1), channel_id=1, source_target_pairs={{0,1},{1,0},{2,3},{3,2},{4,5},{5,4},{6,7},{7,6},{8,9},{9,8},{10,11... | collective-permute-start | bytes 393224 | tf_op jit(solution)/shard_map/ppermute | solution.py:234
  2.8 22.1 %copy-start = (bf16[128,32,128]{2,1,0:T(8,128)(2,1)S(1)}, bf16[128,32,128]{2,1,0:T(8,128)(2,1)}, u32[]{:S(2)}) copy-start(bf16[128,32,128]{2,1,0:T(8,128)(2,1)} %queries.1) | copy-start | bytes 3145732
  2.9 22.1 %copy-start.1 = (s32[8]{0:T(128)S(1)}, s32[8]{0:T(128)}, u32[]{:S(2)}) copy-start(s32[8]{0:T(128)} %doc_lengths.1) | copy-start | bytes 100
  2.9 3.4 %collective-permute-start.1 = (bf16[64,32,128]{2,1,0:T(8,128)(2,1)S(1)}, bf16[64,32,128]{2,1,0:T(8,128)(2,1)S(1)}, u32[]{:S(2)}, u32[]{:S(2)}) collective-permute-start(bf16[64,32,128]{2,1,0:T(8,128)(2,1)S(1)} %get-tuple-element.22), channel_id=1, source_target_pairs={{0,1},{1,0},{2,3},{3,2},{4,5},{5,4},{6,7},{7,6},{8,9},{9,8},{10,11... | collective-permute-start | bytes 1572872 | tf_op jit(solution)/shard_map/ppermute | solution.py:234
  3.2 10.3 %collective-permute-start.4 = (bf16[2,8,64,128]{3,2,1,0:T(8,128)(2,1)S(1)}, bf16[2,8,64,128]{3,2,1,0:T(8,128)(2,1)S(1)}, u32[]{:S(2)}, u32[]{:S(2)}) collective-permute-start(bf16[2,8,64,128]{3,2,1,0:T(8,128)(2,1)S(1)} %pad_maximum_fusion.refs_0_), channel_id=1, source_target_pairs={{0,6},{2,8},{4,10},{6,12},{8,14},{10,16},{12,18},{14,20},{16,22},{... | collective-permute-start | bytes 786440 | tf_op jit(solution)/shard_map/ppermute | solution.py:241
  6.3 9.6 %collective-permute-start.5 = (bf16[2,8,64,128]{3,2,1,0:T(8,128)(2,1)S(1)}, bf16[2,8,64,128]{3,2,1,0:T(8,128)(2,1)S(1)}, u32[]{:S(2)}, u32[]{:S(2)}) collective-permute-start(bf16[2,8,64,128]{3,2,1,0:T(8,128)(2,1)S(1)} %pad_maximum_fusion.refs_0_), channel_id=1, source_target_pairs={{0,8},{2,10},{4,12},{6,14},{8,16},{10,18},{12,20},{14,22},{16,24},... | collective-permute-start | bytes 786440 | tf_op jit(solution)/shard_map/ppermute | solution.py:241
  8.4 14.5 %collective-permute-start.3 = (bf16[2,8,64,128]{3,2,1,0:T(8,128)(2,1)S(1)}, bf16[2,8,64,128]{3,2,1,0:T(8,128)(2,1)S(1)}, u32[]{:S(2)}, u32[]{:S(2)}) collective-permute-start(bf16[2,8,64,128]{3,2,1,0:T(8,128)(2,1)S(1)} %pad_maximum_fusion.refs_0_), channel_id=1, source_target_pairs={{0,4},{2,6},{4,8},{6,10},{8,12},{10,14},{12,16},{14,18},{16,20},{1... | collective-permute-start | bytes 786440 | tf_op jit(solution)/shard_map/ppermute | solution.py:241
  10.4 12.5 %collective-permute-start.2 = (bf16[2,8,64,128]{3,2,1,0:T(8,128)(2,1)S(1)}, bf16[2,8,64,128]{3,2,1,0:T(8,128)(2,1)S(1)}, u32[]{:S(2)}, u32[]{:S(2)}) collective-permute-start(bf16[2,8,64,128]{3,2,1,0:T(8,128)(2,1)S(1)} %pad_maximum_fusion.refs_0_), channel_id=1, source_target_pairs={{0,2},{2,4},{4,6},{6,8},{8,10},{10,12},{12,14},{14,16},{16,18},{18... | collective-permute-start | bytes 786440 | tf_op jit(solution)/shard_map/ppermute | solution.py:241
  16.0 17.4 %collective-permute-start.6 = (bf16[2,2,8,64,128]{4,3,2,1,0:T(8,128)(2,1)S(1)}, bf16[2,2,8,64,128]{4,3,2,1,0:T(8,128)(2,1)S(1)}, u32[]{:S(2)}, u32[]{:S(2)}) collective-permute-start(bf16[2,2,8,64,128]{4,3,2,1,0:T(8,128)(2,1)S(1)} %early.1), channel_id=1, source_target_pairs={{0,8},{2,10},{4,12},{6,14},{8,16},{10,18},{12,20},{14,22},{16,24},... | collective-permute-start | bytes 1572872 | tf_op jit(solution)/shard_map/ppermute | solution.py:241
  23.0 15.7 %collective-permute-start.7 = (bf16[2,2,8,64,128]{4,3,2,1,0:T(8,128)(2,1)S(1)}, bf16[2,2,8,64,128]{4,3,2,1,0:T(8,128)(2,1)S(1)}, u32[]{:S(2)}, u32[]{:S(2)}) collective-permute-start(bf16[2,2,8,64,128]{4,3,2,1,0:T(8,128)(2,1)S(1)} %late.1), channel_id=1, source_target_pairs={{0,8},{2,10},{4,12},{6,14},{8,16},{10,18},{12,20},{14,22},{16,24},... | collective-permute-start | bytes 1572872 | tf_op jit(solution)/shard_map/ppermute | solution.py:241

commit v10 on v9

--- a/solution.py
+++ b/solution.py
@@ -11,12 +11,13 @@
 REACH_LOG = 3
 MASKED_SCORE = -1e30
 
-EARLY_TARGETS = (0, 2, 3, 1)
-LATE_TARGETS = (1, 3, 0, 2)
-EARLY_CHOICES = ((1, (1, 1, 1, 1)), (2, (2, 0, 0, 2)))
-LATE_CHOICES = ((1, (3, 1, 3, 3)), (2, (2, 0, 4, 4)))
-EARLY_DISTANCES = ((7, (7, 5, 8, 8)), (8, (8, 6, 5, 5)))
-LATE_DISTANCES = ((5, (5, 8, 6, 7)), (6, (6, 7, 7, 6)))
+STEPS = ((3, 1), (4, 4), (1, 3), (2, 2))
+EARLY_TARGETS = (0, 1, 3, 2)
+LATE_TARGETS = (0, 2, 1, 3)
+EARLY_CHOICES = ((1, (1, 1, 1, 1)), (2, (2, 2, 0, 2)))
+LATE_CHOICES = ((3, (3, 1, 3, 1)), (4, (4, 0, 4, 2)))
+EARLY_DISTANCES = ((5, 7, (5, 7, 6, 6)), (8, 8, (8, 8, 7, 5)))
+LATE_DISTANCES = ((7, 5, (7, 6, 8, 7)), (6, 6, (6, 5, 5, 8)))
 
 
 def query_bounds(first_place, lanes, group, doc_lengths):
@@ -85,15 +86,15 @@
 
 
 def bundle_kernel(*refs, devices, choices):
-    candidates, out = refs[:-1], refs[-1]
+    held, out = refs[:-1], refs[-1]
     source = chain_position(devices) - (devices - 4)
     for slot, (usual, special) in enumerate(choices):
-        for candidate, ref in enumerate(candidates):
-            if candidate != usual and candidate not in special:
+        for number, ref in enumerate(held):
+            if number != usual and number not in special:
                 continue
-            chosen = jnp.bool_(candidate == usual)
-            for row, number in enumerate(special):
-                chosen = jnp.where(source == row, number == candidate, chosen)
+            chosen = jnp.bool_(number == usual)
+            for row, other in enumerate(special):
+                chosen = jnp.where(source == row, number == other, chosen)
 
             @pl.when(chosen)
             def _(slot=slot, ref=ref):
@@ -105,8 +106,15 @@
     stretch, core = chain_position(devices), lax.axis_index("head")
     kv_count, block, width = blocks[0].shape[1:]
     lanes = block * group
-    for distance in range(len(blocks)):
-        bias[distance * block : (distance + 1) * block, :] = block_bias(
+    odd = stretch % 2 == 1
+    for row in range(len(blocks)):
+        distance = 0
+        if row > 0:
+            by_even, by_odd = STEPS[row - 1]
+            if by_even % 2 == 1:
+                by_even, by_odd = by_odd, by_even
+            distance = jnp.where(odd, by_odd, by_even)
+        bias[row * block : (row + 1) * block, :] = block_bias(
             stretch, distance, block, group, doc_lengths
         )
 
@@ -142,7 +150,8 @@
                 mixes[slot] = mix(gather(1, first_head + part), weights[part])
     turn = stretch - devices
     for number, table in enumerate((EARLY_DISTANCES, LATE_DISTANCES)):
-        for row, (distance, special) in enumerate(table):
+        for row, (even_distance, odd_distance, special) in enumerate(table):
+            distance = jnp.where(odd, odd_distance, even_distance)
             for at, other in enumerate(special):
                 distance = jnp.where(turn == at, other, distance)
             far_bias[number, row * block : (row + 1) * block, :] = block_bias(
@@ -233,11 +242,11 @@
     def swap(array):
         return lax.ppermute(array, "head", [(0, 1), (1, 0)])
 
-    def from_below(array, distance, turned=()):
-        target = {at: at + distance for at in range(stretches - distance)}
+    def upwards(array, steps, turned=()):
+        target = {at: at + steps[at % 2] for at in range(stretches)}
         for number, to in enumerate(turned):
             target[devices - 4 + number] = devices + to
-        pairs = [(owner(at), owner(to)) for at, to in target.items()]
+        pairs = [(owner(at), owner(to)) for at, to in target.items() if to < stretches]
         return lax.ppermute(array, ("ctx", "head"), pairs)
 
     smem = pl.BlockSpec(memory_space=pltpu.SMEM)
@@ -271,27 +280,23 @@
     )
     own, given_queries = lax.optimization_barrier((own, given_queries))
     partner_queries = swap(given_queries)
-    by_three = from_below(own, 3)
+    first = upwards(own, STEPS[0])
     own, partner_queries = lax.optimization_barrier((own, partner_queries))
-    by_four = from_below(own, 4)
-    by_one = from_below(own, 1)
-    by_two = from_below(own, 2)
-
-    def bundle(name, candidates, choices):
+    second, third, fourth = [upwards(own, steps) for steps in STEPS[1:]]
+
+    def bundle(name, held, choices):
         return pl.pallas_call(
             functools.partial(bundle_kernel, devices=devices, choices=choices),
             out_shape=jax.ShapeDtypeStruct((2, *own.shape), own.dtype),
-            in_specs=[vmem] * len(candidates),
+            in_specs=[vmem] * len(held),
             out_specs=vmem,
             compiler_params=pltpu.CompilerParams(vmem_limit_bytes=6 * 2**20),
             name=name,
-        )(*candidates)
-
-    early = from_below(
-        bundle("early", (own, by_three, by_four), EARLY_CHOICES), 4, EARLY_TARGETS
-    )
-    late = from_below(
-        bundle("late", (own, by_one, by_two, by_three, by_four), LATE_CHOICES), 4, LATE_TARGETS
+        )(*held)
+
+    early = upwards(bundle("early", (own, first, second), EARLY_CHOICES), (4, 4), EARLY_TARGETS)
+    late = upwards(
+        bundle("late", (own, first, second, third, fourth), LATE_CHOICES), (4, 4), LATE_TARGETS
     )
 
     params = pltpu.CompilerParams(vmem_limit_bytes=14 * 2**20)
@@ -304,7 +309,7 @@
             flops=4 * work * width, bytes_accessed=4 * 2**20, transcendentals=work
         )
 
-    near = (own, by_one, by_two, by_three, by_four)
+    near = (own, first, second, third, fourth)
     folded, far_bias, *known = pl.pallas_call(
         functools.partial(near_kernel, devices=devices, group=group),
         out_shape=[

time: 41.2 us -> 37.9 us (0.920)
  waiting for transfers between devices: 16.5 us -> 13.1 us
    ppermute x6, waiting for transfers between devices: 16.5 us -> 13 us  [upwards(): return lax.ppermute(array, ('ctx', 'head'), pairs)]
  transfers between devices with their start and end apart: 8 -> 8, of which waited for: 4 -> 6; matrix products, arithmetic and copies ran while one was open for 0% -> 0% of each run, Pallas kernels for 14% -> 15%
where the time goes in v10:
time: 37.9 us; the launch traced here: 37.6 us
  starting transfers between devices  15.6 us (41%)
  waiting for transfers between devices  13.1 us (35%)
  Pallas kernels  8.76 us (23%)
    ppermute x6, starting transfers between devices, upwards(): return lax.ppermute(array, ('ctx', 'head'), pairs)  14.6 us
    ppermute x6, waiting for transfers between devices, upwards(): return lax.ppermute(array, ('ctx', 'head'), pairs)  13 us
    pallas_call x1, Pallas kernels, shards(): pl.pallas_call(functools.partial(near_kernel, devices=devices, group=grou...  3.2 us
    pallas_call x1, Pallas kernels, shards(): pl.pallas_call(functools.partial(far_kernel, number=1), out_shape=jax.Sha...  2.19 us
    pallas_call x2, Pallas kernels, pack(): pl.pallas_call(functools.partial(pack_kernel, kept=kept), out_shape=out_s...  2.07 us
    pallas_call x1, Pallas kernels, shards(): pl.pallas_call(functools.partial(far_kernel, number=0), out_shape=state,...  1.22 us
    ppermute x2, starting transfers between devices, swap(): return lax.ppermute(array, 'head', [(0, 1), (1, 0)])  0.96 us
  transfers between devices with their start and end apart: 8, of which 6 were waited for; matrix products, arithmetic and copies ran while one was open for 0% of the time, Pallas kernels for 15%

profile of v10, /device:TPU:19, one launch (start us, length us, event | category | flops | bytes accessed | tf_op | source)
XLA Modules:
  0.0 37.6 jit_solution(17065875641880926841)
XLA Ops:
  0.0 0.9 %give.1 = bf16[2,4,64,128]{3,2,1,0:T(8,128)(2,1)S(1)} custom-call(bf16[128,4,128]{2,1,0:T(4,128)(2,1)} %refs_0_.3, bf16[128,4,128]{2,1,0:T(4,128)(2,1)} %refs_1_.3), custom_call_target="tpu_custom_call" | custom-call | bytes 2097152 | tf_op jit(solution)/shard_map/give/pallas_call | solution.py:259
  0.9 0.7 %collective-permute-start = (bf16[2,4,64,128]{3,2,1,0:T(8,128)(2,1)S(1)}, bf16[2,4,64,128]{3,2,1,0:T(8,128)(2,1)S(1)}, u32[]{:S(2)}, u32[]{:S(2)}) collective-permute-start(bf16[2,4,64,128]{3,2,1,0:T(8,128)(2,1)S(1)} %give.1), channel_id=1, source_target_pairs={{0,1},{1,0},{2,3},{3,2},{4,5},{5,4},{6,7},{7,6},{8,9},{9,8},{10,11... | collective-permute-start | bytes 393224 | tf_op jit(solution)/shard_map/ppermute | solution.py:243
  1.7 1.1 %keep.1 = (bf16[2,4,64,128]{3,2,1,0:T(8,128)(2,1)S(1)}, bf16[64,32,128]{2,1,0:T(8,128)(2,1)S(1)}) custom-call(bf16[128,4,128]{2,1,0:T(4,128)(2,1)} %refs_0_.3, bf16[128,4,128]{2,1,0:T(4,128)(2,1)} %refs_1_.3, bf16[128,32,128]{2,1,0:T(8,128)(2,1)} %queries.1), custom_call_target="tpu_custom_call" | custom-call | bytes 3145728 | tf_op jit(solution)/shard_map/keep/pallas_call | solution.py:259
  2.8 0.0 collective-permute-done
  2.8 0.0 copy-start
  2.9 0.0 copy-start.1
  2.9 0.2 collective-permute-start.1
  3.2 3.1 %collective-permute-start.2 = (bf16[2,8,64,128]{3,2,1,0:T(8,128)(2,1)S(1)}, bf16[2,8,64,128]{3,2,1,0:T(8,128)(2,1)S(1)}, u32[]{:S(2)}, u32[]{:S(2)}) collective-permute-start(bf16[2,8,64,128]{3,2,1,0:T(8,128)(2,1)S(1)} %pad_maximum_fusion.refs_0_), channel_id=1, source_target_pairs={{0,6},{2,4},{4,10},{6,8},{8,14},{10,12},{12,18},{14,16},{16,22},{1... | collective-permute-start | bytes 786440 | tf_op jit(solution)/shard_map/ppermute | solution.py:250
  6.3 0.0 collective-permute-done.1.partner_queries
  6.3 2.1 %collective-permute-start.3 = (bf16[2,8,64,128]{3,2,1,0:T(8,128)(2,1)S(1)}, bf16[2,8,64,128]{3,2,1,0:T(8,128)(2,1)S(1)}, u32[]{:S(2)}, u32[]{:S(2)}) collective-permute-start(bf16[2,8,64,128]{3,2,1,0:T(8,128)(2,1)S(1)} %pad_maximum_fusion.refs_0_), channel_id=1, source_target_pairs={{0,8},{2,10},{4,12},{6,14},{8,16},{10,18},{12,20},{14,22},{16,24},... | collective-permute-start | bytes 786440 | tf_op jit(solution)/shard_map/ppermute | solution.py:250
  8.4 2.0 %collective-permute-start.5 = (bf16[2,8,64,128]{3,2,1,0:T(8,128)(2,1)S(1)}, bf16[2,8,64,128]{3,2,1,0:T(8,128)(2,1)S(1)}, u32[]{:S(2)}, u32[]{:S(2)}) collective-permute-start(bf16[2,8,64,128]{3,2,1,0:T(8,128)(2,1)S(1)} %pad_maximum_fusion.refs_0_), channel_id=1, source_target_pairs={{0,4},{2,6},{4,8},{6,10},{8,12},{10,14},{12,16},{14,18},{16,20},{1... | collective-permute-start | bytes 786440 | tf_op jit(solution)/shard_map/ppermute | solution.py:250
  10.4 3.3 %collective-permute-start.4 = (bf16[2,8,64,128]{3,2,1,0:T(8,128)(2,1)S(1)}, bf16[2,8,64,128]{3,2,1,0:T(8,128)(2,1)S(1)}, u32[]{:S(2)}, u32[]{:S(2)}) collective-permute-start(bf16[2,8,64,128]{3,2,1,0:T(8,128)(2,1)S(1)} %pad_maximum_fusion.refs_0_), channel_id=1, source_target_pairs={{0,2},{2,8},{4,6},{6,12},{8,10},{10,16},{12,14},{14,20},{16,18},{1... | collective-permute-start | bytes 786440 | tf_op jit(solution)/shard_map/ppermute | solution.py:250
  13.7 0.5 %collective-permute-done.2.refs_1_ = bf16[2,8,64,128]{3,2,1,0:T(8,128)(2,1)S(1)} collective-permute-done((bf16[2,8,64,128]{3,2,1,0:T(8,128)(2,1)S(1)}, bf16[2,8,64,128]{3,2,1,0:T(8,128)(2,1)S(1)}, u32[]{:S(2)}, u32[]{:S(2)}) %collective-permute-start.2) | collective-permute-done | bytes 262176 | tf_op jit(solution)/shard_map/ppermute | solution.py:250
  14.2 0.3 collective-permute-done.3.refs_2_
  14.5 2.1 %collective-permute-start.6 = (bf16[2,2,8,64,128]{4,3,2,1,0:T(8,128)(2,1)S(1)}, bf16[2,2,8,64,128]{4,3,2,1,0:T(8,128)(2,1)S(1)}, u32[]{:S(2)}, u32[]{:S(2)}) collective-permute-start(bf16[2,2,8,64,128]{4,3,2,1,0:T(8,128)(2,1)S(1)} %early.1), channel_id=1, source_target_pairs={{0,8},{2,10},{4,12},{6,14},{8,16},{10,18},{12,20},{14,22},{16,24},... | collective-permute-start | bytes 1572872 | tf_op jit(solution)/shard_map/ppermute | solution.py:250
  16.6 3.4 %collective-permute-done.5.refs_4_ = bf16[2,8,64,128]{3,2,1,0:T(8,128)(2,1)S(1)} collective-permute-done((bf16[2,8,64,128]{3,2,1,0:T(8,128)(2,1)S(1)}, bf16[2,8,64,128]{3,2,1,0:T(8,128)(2,1)S(1)}, u32[]{:S(2)}, u32[]{:S(2)}) %collective-permute-start.5) | collective-permute-done | bytes 262176 | tf_op jit(solution)/shard_map/ppermute | solution.py:250
  20.0 0.8 %collective-permute-done.4.refs_3_ = bf16[2,8,64,128]{3,2,1,0:T(8,128)(2,1)S(1)} collective-permute-done((bf16[2,8,64,128]{3,2,1,0:T(8,128)(2,1)S(1)}, bf16[2,8,64,128]{3,2,1,0:T(8,128)(2,1)S(1)}, u32[]{:S(2)}, u32[]{:S(2)}) %collective-permute-start.4) | collective-permute-done | bytes 262176 | tf_op jit(solution)/shard_map/ppermute | solution.py:250
  20.9 2.1 %collective-permute-start.7 = (bf16[2,2,8,64,128]{4,3,2,1,0:T(8,128)(2,1)S(1)}, bf16[2,2,8,64,128]{4,3,2,1,0:T(8,128)(2,1)S(1)}, u32[]{:S(2)}, u32[]{:S(2)}) collective-permute-start(bf16[2,2,8,64,128]{4,3,2,1,0:T(8,128)(2,1)S(1)} %late.1), channel_id=1, source_target_pairs={{0,8},{2,10},{4,12},{6,14},{8,16},{10,18},{12,20},{14,22},{16,24},... | collective-permute-start | bytes 1572872 | tf_op jit(solution)/shard_map/ppermute | solution.py:250
  23.0 0.0 copy-done
  23.0 0.0 copy-done.1
  23.0 3.2 %near.1 = (bf16[8,512,128]{2,1,0:T(8,128)(2,1)S(1)}, f32[2,128,512]{2,1,0:T(8,128)S(1)}, f32[8,1,512]{2,1,0:T(1,128)S(1)}, f32[8,1,512]{2,1,0:T(1,128)S(1)}, f32[8,128,512]{2,1,0:T(8,128)S(1)}) custom-call(s32[8]{0:T(128)S(1)} %copy-done.1, bf16[128,32,128]{2,1,0:T(8,128)(2,1)S(1)} %copy-done, ...), custom_call_target="tpu_custom_call" | custom-call | flops 671088640 | bytes 4194304 | tf_op jit(solution)/shard_map/near/pallas_call | solution.py:313
  26.2 2.0 %collective-permute-done.6.blocks = bf16[2,2,8,64,128]{4,3,2,1,0:T(8,128)(2,1)S(1)} collective-permute-done((bf16[2,2,8,64,128]{4,3,2,1,0:T(8,128)(2,1)S(1)}, bf16[2,2,8,64,128]{4,3,2,1,0:T(8,128)(2,1)S(1)}, u32[]{:S(2)}, u32[]{:S(2)}) %collective-permute-start.6) | collective-permute-done | bytes 524320 | tf_op jit(solution)/shard_map/ppermute | solution.py:250
  28.2 1.2 %middle.1 = (f32[8,1,512]{2,1,0:T(1,128)S(1)}, f32[8,1,512]{2,1,0:T(1,128)S(1)}, f32[8,128,512]{2,1,0:T(8,128)S(1)}) custom-call(bf16[8,512,128]{2,1,0:T(8,128)(2,1)S(1)} %get-tuple-element.25.folded, f32[2,128,512]{2,1,0:T(8,128)S(1)} %get-tuple-element.26.far_bias, f32[8,1,512]{2,1,0:T(1,128)S(1)} %get-tuple-element.27.peak, ...), custom_call_target="tpu_custom_call" | custom-call | flops 268435456 | bytes 4194304 | tf_op jit(solution)/shard_map/middle/pallas_call | solution.py:327
  29.5 6.0 %collective-permute-done.7.blocks = bf16[2,2,8,64,128]{4,3,2,1,0:T(8,128)(2,1)S(1)} collective-permute-done((bf16[2,2,8,64,128]{4,3,2,1,0:T(8,128)(2,1)S(1)}, bf16[2,2,8,64,128]{4,3,2,1,0:T(8,128)(2,1)S(1)}, u32[]{:S(2)}, u32[]{:S(2)}) %collective-permute-start.7) | collective-permute-done | bytes 524320 | tf_op jit(solution)/shard_map/ppermute | solution.py:250
  35.4 2.2 %finish.1 = bf16[64,64,128]{2,1,0:T(8,128)(2,1)} custom-call(bf16[8,512,128]{2,1,0:T(8,128)(2,1)S(1)} %get-tuple-element.25.folded, f32[2,128,512]{2,1,0:T(8,128)S(1)} %get-tuple-element.26.far_bias, f32[8,1,512]{2,1,0:T(1,128)S(1)} %get-tuple-element.30.peak, f32[8,1,512]{2,1,0:T(1,128)S(1)} %get-tuple-element.31.sums, ...), custom_call_target="tpu_custom_call" | custom-call | flops 268435456 | bytes 4194304 | tf_op jit(solution)/shard_map/finish/pallas_call | solution.py:336
  (4 shorter events, 0.1 us)
Async XLA Ops:
  0.9 1.9 %collective-permute-start = (bf16[2,4,64,128]{3,2,1,0:T(8,128)(2,1)S(1)}, bf16[2,4,64,128]{3,2,1,0:T(8,128)(2,1)S(1)}, u32[]{:S(2)}, u32[]{:S(2)}) collective-permute-start(bf16[2,4,64,128]{3,2,1,0:T(8,128)(2,1)S(1)} %give.1), channel_id=1, source_target_pairs={{0,1},{1,0},{2,3},{3,2},{4,5},{5,4},{6,7},{7,6},{8,9},{9,8},{10,11... | collective-permute-start | bytes 393224 | tf_op jit(solution)/shard_map/ppermute | solution.py:243
  2.8 20.1 %copy-start = (bf16[128,32,128]{2,1,0:T(8,128)(2,1)S(1)}, bf16[128,32,128]{2,1,0:T(8,128)(2,1)}, u32[]{:S(2)}) copy-start(bf16[128,32,128]{2,1,0:T(8,128)(2,1)} %queries.1) | copy-start | bytes 3145732
  2.9 20.1 %copy-start.1 = (s32[8]{0:T(128)S(1)}, s32[8]{0:T(128)}, u32[]{:S(2)}) copy-start(s32[8]{0:T(128)} %doc_lengths.1) | copy-start | bytes 100
  2.9 3.4 %collective-permute-start.1 = (bf16[64,32,128]{2,1,0:T(8,128)(2,1)S(1)}, bf16[64,32,128]{2,1,0:T(8,128)(2,1)S(1)}, u32[]{:S(2)}, u32[]{:S(2)}) collective-permute-start(bf16[64,32,128]{2,1,0:T(8,128)(2,1)S(1)} %get-tuple-element.22), channel_id=1, source_target_pairs={{0,1},{1,0},{2,3},{3,2},{4,5},{5,4},{6,7},{7,6},{8,9},{9,8},{10,11... | collective-permute-start | bytes 1572872 | tf_op jit(solution)/shard_map/ppermute | solution.py:243
  3.2 11.0 %collective-permute-start.2 = (bf16[2,8,64,128]{3,2,1,0:T(8,128)(2,1)S(1)}, bf16[2,8,64,128]{3,2,1,0:T(8,128)(2,1)S(1)}, u32[]{:S(2)}, u32[]{:S(2)}) collective-permute-start(bf16[2,8,64,128]{3,2,1,0:T(8,128)(2,1)S(1)} %pad_maximum_fusion.refs_0_), channel_id=1, source_target_pairs={{0,6},{2,4},{4,10},{6,8},{8,14},{10,12},{12,18},{14,16},{16,22},{1... | collective-permute-start | bytes 786440 | tf_op jit(solution)/shard_map/ppermute | solution.py:250
  6.3 8.2 %collective-permute-start.3 = (bf16[2,8,64,128]{3,2,1,0:T(8,128)(2,1)S(1)}, bf16[2,8,64,128]{3,2,1,0:T(8,128)(2,1)S(1)}, u32[]{:S(2)}, u32[]{:S(2)}) collective-permute-start(bf16[2,8,64,128]{3,2,1,0:T(8,128)(2,1)S(1)} %pad_maximum_fusion.refs_0_), channel_id=1, source_target_pairs={{0,8},{2,10},{4,12},{6,14},{8,16},{10,18},{12,20},{14,22},{16,24},... | collective-permute-start | bytes 786440 | tf_op jit(solution)/shard_map/ppermute | solution.py:250
  8.4 11.6 %collective-permute-start.5 = (bf16[2,8,64,128]{3,2,1,0:T(8,128)(2,1)S(1)}, bf16[2,8,64,128]{3,2,1,0:T(8,128)(2,1)S(1)}, u32[]{:S(2)}, u32[]{:S(2)}) collective-permute-start(bf16[2,8,64,128]{3,2,1,0:T(8,128)(2,1)S(1)} %pad_maximum_fusion.refs_0_), channel_id=1, source_target_pairs={{0,4},{2,6},{4,8},{6,10},{8,12},{10,14},{12,16},{14,18},{16,20},{1... | collective-permute-start | bytes 786440 | tf_op jit(solution)/shard_map/ppermute | solution.py:250
  10.4 10.5 %collective-permute-start.4 = (bf16[2,8,64,128]{3,2,1,0:T(8,128)(2,1)S(1)}, bf16[2,8,64,128]{3,2,1,0:T(8,128)(2,1)S(1)}, u32[]{:S(2)}, u32[]{:S(2)}) collective-permute-start(bf16[2,8,64,128]{3,2,1,0:T(8,128)(2,1)S(1)} %pad_maximum_fusion.refs_0_), channel_id=1, source_target_pairs={{0,2},{2,8},{4,6},{6,12},{8,10},{10,16},{12,14},{14,20},{16,18},{1... | collective-permute-start | bytes 786440 | tf_op jit(solution)/shard_map/ppermute | solution.py:250
  14.5 13.7 %collective-permute-start.6 = (bf16[2,2,8,64,128]{4,3,2,1,0:T(8,128)(2,1)S(1)}, bf16[2,2,8,64,128]{4,3,2,1,0:T(8,128)(2,1)S(1)}, u32[]{:S(2)}, u32[]{:S(2)}) collective-permute-start(bf16[2,2,8,64,128]{4,3,2,1,0:T(8,128)(2,1)S(1)} %early.1), channel_id=1, source_target_pairs={{0,8},{2,10},{4,12},{6,14},{8,16},{10,18},{12,20},{14,22},{16,24},... | collective-permute-start | bytes 1572872 | tf_op jit(solution)/shard_map/ppermute | solution.py:250
  20.9 14.6 %collective-permute-start.7 = (bf16[2,2,8,64,128]{4,3,2,1,0:T(8,128)(2,1)S(1)}, bf16[2,2,8,64,128]{4,3,2,1,0:T(8,128)(2,1)S(1)}, u32[]{:S(2)}, u32[]{:S(2)}) collective-permute-start(bf16[2,2,8,64,128]{4,3,2,1,0:T(8,128)(2,1)S(1)} %late.1), channel_id=1, source_target_pairs={{0,8},{2,10},{4,12},{6,14},{8,16},{10,18},{12,20},{14,22},{16,24},... | collective-permute-start | bytes 1572872 | tf_op jit(solution)/shard_map/ppermute | solution.py:250

commit v11 on v10

--- a/solution.py
+++ b/solution.py
@@ -40,11 +40,8 @@
 
 
 def score(q, keys, bias):
-    factor = math.log2(math.e) / math.sqrt(q.shape[1])
-    scores = lax.dot_general(
-        keys, q, (((1,), (1,)), ((), ())), preferred_element_type=jnp.float32
-    )
-    return scores * factor + bias
+    factor = math.log2(math.e) / math.sqrt(q.shape[0])
+    return jnp.dot(keys, q, preferred_element_type=jnp.float32) * factor + bias
 
 
 def mix(values, weights):
@@ -135,7 +132,7 @@
             qs = [
                 both[:, part * group : (part + 1) * group, :]
                 .reshape(lanes, width)
-                .astype(jnp.bfloat16)
+                .T.astype(jnp.bfloat16)
                 for part in range(2)
             ]
             scores = [
@@ -167,7 +164,7 @@
         new_peak, new_sums, new_mixes = refs
     core = lax.axis_index("head")
     _, _, kv_count, block, width = blocks.shape
-    group = folded.shape[1] // block
+    group = folded.shape[2] // block
     step = kv_count // 2
     copies = []
     for half in range(2):
@@ -313,7 +310,7 @@
     folded, far_bias, *known = pl.pallas_call(
         functools.partial(near_kernel, devices=devices, group=group),
         out_shape=[
-            jax.ShapeDtypeStruct((kv_count, lanes, width), jnp.bfloat16),
+            jax.ShapeDtypeStruct((kv_count, width, lanes), jnp.bfloat16),
             jax.ShapeDtypeStruct((2, 2 * block, lanes), jnp.float32),
             *state,
         ],

time: 37.9 us -> 37.9 us (level)
  no operation moved by 1% of the time
where the time goes in v11:
time: 37.9 us; the launch traced here: 37.6 us
  starting transfers between devices  15.6 us (41%)
  waiting for transfers between devices  12.9 us (34%)
  Pallas kernels  8.87 us (23%)
    ppermute x6, starting transfers between devices, upwards(): return lax.ppermute(array, ('ctx', 'head'), pairs)  14.6 us
    ppermute x6, waiting for transfers between devices, upwards(): return lax.ppermute(array, ('ctx', 'head'), pairs)  12.9 us
    pallas_call x1, Pallas kernels, shards(): pl.pallas_call(functools.partial(near_kernel, devices=devices, group=grou...  3.35 us
    pallas_call x1, Pallas kernels, shards(): pl.pallas_call(functools.partial(far_kernel, number=1), out_shape=jax.Sha...  2.17 us
    pallas_call x2, Pallas kernels, pack(): pl.pallas_call(functools.partial(pack_kernel, kept=kept), out_shape=out_s...  2.07 us
    pallas_call x1, Pallas kernels, shards(): pl.pallas_call(functools.partial(far_kernel, number=0), out_shape=state,...  1.2 us
    ppermute x2, starting transfers between devices, swap(): return lax.ppermute(array, 'head', [(0, 1), (1, 0)])  0.96 us
  transfers between devices with their start and end apart: 8, of which 6 were waited for; matrix products, arithmetic and copies ran while one was open for 0% of the time, Pallas kernels for 15%

profile of v11, /device:TPU:19, one launch (start us, length us, event | category | flops | bytes accessed | tf_op | source)
XLA Modules:
  0.0 37.6 jit_solution(4761346134304193803)
XLA Ops:
  0.0 0.9 %give.1 = bf16[2,4,64,128]{3,2,1,0:T(8,128)(2,1)S(1)} custom-call(bf16[128,4,128]{2,1,0:T(4,128)(2,1)} %refs_0_.3, bf16[128,4,128]{2,1,0:T(4,128)(2,1)} %refs_1_.3), custom_call_target="tpu_custom_call" | custom-call | bytes 2097152 | tf_op jit(solution)/shard_map/give/pallas_call | solution.py:256
  0.9 0.7 %collective-permute-start = (bf16[2,4,64,128]{3,2,1,0:T(8,128)(2,1)S(1)}, bf16[2,4,64,128]{3,2,1,0:T(8,128)(2,1)S(1)}, u32[]{:S(2)}, u32[]{:S(2)}) collective-permute-start(bf16[2,4,64,128]{3,2,1,0:T(8,128)(2,1)S(1)} %give.1), channel_id=1, source_target_pairs={{0,1},{1,0},{2,3},{3,2},{4,5},{5,4},{6,7},{7,6},{8,9},{9,8},{10,11... | collective-permute-start | bytes 393224 | tf_op jit(solution)/shard_map/ppermute | solution.py:240
  1.7 1.1 %keep.1 = (bf16[2,4,64,128]{3,2,1,0:T(8,128)(2,1)S(1)}, bf16[64,32,128]{2,1,0:T(8,128)(2,1)S(1)}) custom-call(bf16[128,4,128]{2,1,0:T(4,128)(2,1)} %refs_0_.3, bf16[128,4,128]{2,1,0:T(4,128)(2,1)} %refs_1_.3, bf16[128,32,128]{2,1,0:T(8,128)(2,1)} %queries.1), custom_call_target="tpu_custom_call" | custom-call | bytes 3145728 | tf_op jit(solution)/shard_map/keep/pallas_call | solution.py:256
  2.8 0.0 collective-permute-done
  2.8 0.0 copy-start
  2.9 0.0 copy-start.1
  2.9 0.2 collective-permute-start.1
  3.2 3.1 %collective-permute-start.2 = (bf16[2,8,64,128]{3,2,1,0:T(8,128)(2,1)S(1)}, bf16[2,8,64,128]{3,2,1,0:T(8,128)(2,1)S(1)}, u32[]{:S(2)}, u32[]{:S(2)}) collective-permute-start(bf16[2,8,64,128]{3,2,1,0:T(8,128)(2,1)S(1)} %pad_maximum_fusion.refs_0_), channel_id=1, source_target_pairs={{0,6},{2,4},{4,10},{6,8},{8,14},{10,12},{12,18},{14,16},{16,22},{1... | collective-permute-start | bytes 786440 | tf_op jit(solution)/shard_map/ppermute | solution.py:247
  6.3 0.0 collective-permute-done.1.partner_queries
  6.3 2.1 %collective-permute-start.3 = (bf16[2,8,64,128]{3,2,1,0:T(8,128)(2,1)S(1)}, bf16[2,8,64,128]{3,2,1,0:T(8,128)(2,1)S(1)}, u32[]{:S(2)}, u32[]{:S(2)}) collective-permute-start(bf16[2,8,64,128]{3,2,1,0:T(8,128)(2,1)S(1)} %pad_maximum_fusion.refs_0_), channel_id=1, source_target_pairs={{0,8},{2,10},{4,12},{6,14},{8,16},{10,18},{12,20},{14,22},{16,24},... | collective-permute-start | bytes 786440 | tf_op jit(solution)/shard_map/ppermute | solution.py:247
  8.4 2.0 %collective-permute-start.5 = (bf16[2,8,64,128]{3,2,1,0:T(8,128)(2,1)S(1)}, bf16[2,8,64,128]{3,2,1,0:T(8,128)(2,1)S(1)}, u32[]{:S(2)}, u32[]{:S(2)}) collective-permute-start(bf16[2,8,64,128]{3,2,1,0:T(8,128)(2,1)S(1)} %pad_maximum_fusion.refs_0_), channel_id=1, source_target_pairs={{0,4},{2,6},{4,8},{6,10},{8,12},{10,14},{12,16},{14,18},{16,20},{1... | collective-permute-start | bytes 786440 | tf_op jit(solution)/shard_map/ppermute | solution.py:247
  10.4 3.3 %collective-permute-start.4 = (bf16[2,8,64,128]{3,2,1,0:T(8,128)(2,1)S(1)}, bf16[2,8,64,128]{3,2,1,0:T(8,128)(2,1)S(1)}, u32[]{:S(2)}, u32[]{:S(2)}) collective-permute-start(bf16[2,8,64,128]{3,2,1,0:T(8,128)(2,1)S(1)} %pad_maximum_fusion.refs_0_), channel_id=1, source_target_pairs={{0,2},{2,8},{4,6},{6,12},{8,10},{10,16},{12,14},{14,20},{16,18},{1... | collective-permute-start | bytes 786440 | tf_op jit(solution)/shard_map/ppermute | solution.py:247
  13.7 0.5 %collective-permute-done.2.refs_1_ = bf16[2,8,64,128]{3,2,1,0:T(8,128)(2,1)S(1)} collective-permute-done((bf16[2,8,64,128]{3,2,1,0:T(8,128)(2,1)S(1)}, bf16[2,8,64,128]{3,2,1,0:T(8,128)(2,1)S(1)}, u32[]{:S(2)}, u32[]{:S(2)}) %collective-permute-start.2) | collective-permute-done | bytes 262176 | tf_op jit(solution)/shard_map/ppermute | solution.py:247
  14.2 0.3 collective-permute-done.3.refs_2_
  14.5 2.1 %collective-permute-start.6 = (bf16[2,2,8,64,128]{4,3,2,1,0:T(8,128)(2,1)S(1)}, bf16[2,2,8,64,128]{4,3,2,1,0:T(8,128)(2,1)S(1)}, u32[]{:S(2)}, u32[]{:S(2)}) collective-permute-start(bf16[2,2,8,64,128]{4,3,2,1,0:T(8,128)(2,1)S(1)} %early.1), channel_id=1, source_target_pairs={{0,8},{2,10},{4,12},{6,14},{8,16},{10,18},{12,20},{14,22},{16,24},... | collective-permute-start | bytes 1572872 | tf_op jit(solution)/shard_map/ppermute | solution.py:247
  16.6 3.4 %collective-permute-done.5.refs_4_ = bf16[2,8,64,128]{3,2,1,0:T(8,128)(2,1)S(1)} collective-permute-done((bf16[2,8,64,128]{3,2,1,0:T(8,128)(2,1)S(1)}, bf16[2,8,64,128]{3,2,1,0:T(8,128)(2,1)S(1)}, u32[]{:S(2)}, u32[]{:S(2)}) %collective-permute-start.5) | collective-permute-done | bytes 262176 | tf_op jit(solution)/shard_map/ppermute | solution.py:247
  20.0 0.8 %collective-permute-done.4.refs_3_ = bf16[2,8,64,128]{3,2,1,0:T(8,128)(2,1)S(1)} collective-permute-done((bf16[2,8,64,128]{3,2,1,0:T(8,128)(2,1)S(1)}, bf16[2,8,64,128]{3,2,1,0:T(8,128)(2,1)S(1)}, u32[]{:S(2)}, u32[]{:S(2)}) %collective-permute-start.4) | collective-permute-done | bytes 262176 | tf_op jit(solution)/shard_map/ppermute | solution.py:247
  20.9 2.1 %collective-permute-start.7 = (bf16[2,2,8,64,128]{4,3,2,1,0:T(8,128)(2,1)S(1)}, bf16[2,2,8,64,128]{4,3,2,1,0:T(8,128)(2,1)S(1)}, u32[]{:S(2)}, u32[]{:S(2)}) collective-permute-start(bf16[2,2,8,64,128]{4,3,2,1,0:T(8,128)(2,1)S(1)} %late.1), channel_id=1, source_target_pairs={{0,8},{2,10},{4,12},{6,14},{8,16},{10,18},{12,20},{14,22},{16,24},... | collective-permute-start | bytes 1572872 | tf_op jit(solution)/shard_map/ppermute | solution.py:247
  23.0 0.0 copy-done
  23.0 0.0 copy-done.1
  23.0 3.3 %near.1 = (bf16[8,128,512]{2,1,0:T(8,128)(2,1)S(1)}, f32[2,128,512]{2,1,0:T(8,128)S(1)}, f32[8,1,512]{2,1,0:T(1,128)S(1)}, f32[8,1,512]{2,1,0:T(1,128)S(1)}, f32[8,128,512]{2,1,0:T(8,128)S(1)}) custom-call(s32[8]{0:T(128)S(1)} %copy-done.1, bf16[128,32,128]{2,1,0:T(8,128)(2,1)S(1)} %copy-done, ...), custom_call_target="tpu_custom_call" | custom-call | flops 671088640 | bytes 4194304 | tf_op jit(solution)/shard_map/near/pallas_call | solution.py:310
  26.4 1.9 %collective-permute-done.6.blocks = bf16[2,2,8,64,128]{4,3,2,1,0:T(8,128)(2,1)S(1)} collective-permute-done((bf16[2,2,8,64,128]{4,3,2,1,0:T(8,128)(2,1)S(1)}, bf16[2,2,8,64,128]{4,3,2,1,0:T(8,128)(2,1)S(1)}, u32[]{:S(2)}, u32[]{:S(2)}) %collective-permute-start.6) | collective-permute-done | bytes 524320 | tf_op jit(solution)/shard_map/ppermute | solution.py:247
  28.2 1.2 %middle.1 = (f32[8,1,512]{2,1,0:T(1,128)S(1)}, f32[8,1,512]{2,1,0:T(1,128)S(1)}, f32[8,128,512]{2,1,0:T(8,128)S(1)}) custom-call(bf16[8,128,512]{2,1,0:T(8,128)(2,1)S(1)} %get-tuple-element.25.folded, f32[2,128,512]{2,1,0:T(8,128)S(1)} %get-tuple-element.26.far_bias, f32[8,1,512]{2,1,0:T(1,128)S(1)} %get-tuple-element.27.peak, ...), custom_call_target="tpu_custom_call" | custom-call | flops 268435456 | bytes 4194304 | tf_op jit(solution)/shard_map/middle/pallas_call | solution.py:324
  29.4 6.0 %collective-permute-done.7.blocks = bf16[2,2,8,64,128]{4,3,2,1,0:T(8,128)(2,1)S(1)} collective-permute-done((bf16[2,2,8,64,128]{4,3,2,1,0:T(8,128)(2,1)S(1)}, bf16[2,2,8,64,128]{4,3,2,1,0:T(8,128)(2,1)S(1)}, u32[]{:S(2)}, u32[]{:S(2)}) %collective-permute-start.7) | collective-permute-done | bytes 524320 | tf_op jit(solution)/shard_map/ppermute | solution.py:247
  35.4 2.2 %finish.1 = bf16[64,64,128]{2,1,0:T(8,128)(2,1)} custom-call(bf16[8,128,512]{2,1,0:T(8,128)(2,1)S(1)} %get-tuple-element.25.folded, f32[2,128,512]{2,1,0:T(8,128)S(1)} %get-tuple-element.26.far_bias, f32[8,1,512]{2,1,0:T(1,128)S(1)} %get-tuple-element.30.peak, f32[8,1,512]{2,1,0:T(1,128)S(1)} %get-tuple-element.31.sums, ...), custom_call_target="tpu_custom_call" | custom-call | flops 268435456 | bytes 4194304 | tf_op jit(solution)/shard_map/finish/pallas_call | solution.py:333
  (4 shorter events, 0.1 us)
Async XLA Ops:
  0.9 1.9 %collective-permute-start = (bf16[2,4,64,128]{3,2,1,0:T(8,128)(2,1)S(1)}, bf16[2,4,64,128]{3,2,1,0:T(8,128)(2,1)S(1)}, u32[]{:S(2)}, u32[]{:S(2)}) collective-permute-start(bf16[2,4,64,128]{3,2,1,0:T(8,128)(2,1)S(1)} %give.1), channel_id=1, source_target_pairs={{0,1},{1,0},{2,3},{3,2},{4,5},{5,4},{6,7},{7,6},{8,9},{9,8},{10,11... | collective-permute-start | bytes 393224 | tf_op jit(solution)/shard_map/ppermute | solution.py:240
  2.8 20.1 %copy-start = (bf16[128,32,128]{2,1,0:T(8,128)(2,1)S(1)}, bf16[128,32,128]{2,1,0:T(8,128)(2,1)}, u32[]{:S(2)}) copy-start(bf16[128,32,128]{2,1,0:T(8,128)(2,1)} %queries.1) | copy-start | bytes 3145732
  2.9 20.1 %copy-start.1 = (s32[8]{0:T(128)S(1)}, s32[8]{0:T(128)}, u32[]{:S(2)}) copy-start(s32[8]{0:T(128)} %doc_lengths.1) | copy-start | bytes 100
  2.9 3.4 %collective-permute-start.1 = (bf16[64,32,128]{2,1,0:T(8,128)(2,1)S(1)}, bf16[64,32,128]{2,1,0:T(8,128)(2,1)S(1)}, u32[]{:S(2)}, u32[]{:S(2)}) collective-permute-start(bf16[64,32,128]{2,1,0:T(8,128)(2,1)S(1)} %get-tuple-element.22), channel_id=1, source_target_pairs={{0,1},{1,0},{2,3},{3,2},{4,5},{5,4},{6,7},{7,6},{8,9},{9,8},{10,11... | collective-permute-start | bytes 1572872 | tf_op jit(solution)/shard_map/ppermute | solution.py:240
  3.2 11.0 %collective-permute-start.2 = (bf16[2,8,64,128]{3,2,1,0:T(8,128)(2,1)S(1)}, bf16[2,8,64,128]{3,2,1,0:T(8,128)(2,1)S(1)}, u32[]{:S(2)}, u32[]{:S(2)}) collective-permute-start(bf16[2,8,64,128]{3,2,1,0:T(8,128)(2,1)S(1)} %pad_maximum_fusion.refs_0_), channel_id=1, source_target_pairs={{0,6},{2,4},{4,10},{6,8},{8,14},{10,12},{12,18},{14,16},{16,22},{1... | collective-permute-start | bytes 786440 | tf_op jit(solution)/shard_map/ppermute | solution.py:247
  6.3 8.2 %collective-permute-start.3 = (bf16[2,8,64,128]{3,2,1,0:T(8,128)(2,1)S(1)}, bf16[2,8,64,128]{3,2,1,0:T(8,128)(2,1)S(1)}, u32[]{:S(2)}, u32[]{:S(2)}) collective-permute-start(bf16[2,8,64,128]{3,2,1,0:T(8,128)(2,1)S(1)} %pad_maximum_fusion.refs_0_), channel_id=1, source_target_pairs={{0,8},{2,10},{4,12},{6,14},{8,16},{10,18},{12,20},{14,22},{16,24},... | collective-permute-start | bytes 786440 | tf_op jit(solution)/shard_map/ppermute | solution.py:247
  8.4 11.6 %collective-permute-start.5 = (bf16[2,8,64,128]{3,2,1,0:T(8,128)(2,1)S(1)}, bf16[2,8,64,128]{3,2,1,0:T(8,128)(2,1)S(1)}, u32[]{:S(2)}, u32[]{:S(2)}) collective-permute-start(bf16[2,8,64,128]{3,2,1,0:T(8,128)(2,1)S(1)} %pad_maximum_fusion.refs_0_), channel_id=1, source_target_pairs={{0,4},{2,6},{4,8},{6,10},{8,12},{10,14},{12,16},{14,18},{16,20},{1... | collective-permute-start | bytes 786440 | tf_op jit(solution)/shard_map/ppermute | solution.py:247
  10.4 10.5 %collective-permute-start.4 = (bf16[2,8,64,128]{3,2,1,0:T(8,128)(2,1)S(1)}, bf16[2,8,64,128]{3,2,1,0:T(8,128)(2,1)S(1)}, u32[]{:S(2)}, u32[]{:S(2)}) collective-permute-start(bf16[2,8,64,128]{3,2,1,0:T(8,128)(2,1)S(1)} %pad_maximum_fusion.refs_0_), channel_id=1, source_target_pairs={{0,2},{2,8},{4,6},{6,12},{8,10},{10,16},{12,14},{14,20},{16,18},{1... | collective-permute-start | bytes 786440 | tf_op jit(solution)/shard_map/ppermute | solution.py:247
  14.5 13.7 %collective-permute-start.6 = (bf16[2,2,8,64,128]{4,3,2,1,0:T(8,128)(2,1)S(1)}, bf16[2,2,8,64,128]{4,3,2,1,0:T(8,128)(2,1)S(1)}, u32[]{:S(2)}, u32[]{:S(2)}) collective-permute-start(bf16[2,2,8,64,128]{4,3,2,1,0:T(8,128)(2,1)S(1)} %early.1), channel_id=1, source_target_pairs={{0,8},{2,10},{4,12},{6,14},{8,16},{10,18},{12,20},{14,22},{16,24},... | collective-permute-start | bytes 1572872 | tf_op jit(solution)/shard_map/ppermute | solution.py:247
  20.9 14.6 %collective-permute-start.7 = (bf16[2,2,8,64,128]{4,3,2,1,0:T(8,128)(2,1)S(1)}, bf16[2,2,8,64,128]{4,3,2,1,0:T(8,128)(2,1)S(1)}, u32[]{:S(2)}, u32[]{:S(2)}) collective-permute-start(bf16[2,2,8,64,128]{4,3,2,1,0:T(8,128)(2,1)S(1)} %late.1), channel_id=1, source_target_pairs={{0,8},{2,10},{4,12},{6,14},{8,16},{10,18},{12,20},{14,22},{16,24},... | collective-permute-start | bytes 1572872 | tf_op jit(solution)/shard_map/ppermute | solution.py:247

commit v12 on v11

--- a/solution.py
+++ b/solution.py
@@ -165,19 +165,15 @@
     core = lax.axis_index("head")
     _, _, kv_count, block, width = blocks.shape
     group = folded.shape[2] // block
-    step = kv_count // 2
+    half = kv_count // 2
     copies = []
-    for half in range(2):
-        side = core if half == 0 else 1 - core
-        first_head = side * step
-        slots = [half * step + part for part in range(step)]
+
+    def weigh(slots, heads):
         scores = [
             score(
-                folded[slot],
-                blocks[:, 0, first_head + part].reshape(2 * block, width),
-                far_bias[number],
+                folded[slot], blocks[:, 0, head].reshape(2 * block, width), far_bias[number]
             )
-            for part, slot in enumerate(slots)
+            for slot, head in zip(slots, heads)
         ]
         largest = [
             jnp.maximum(jnp.max(each, axis=0, keepdims=True), peak[slot])
@@ -189,35 +185,43 @@
             jnp.sum(each, axis=0, keepdims=True) + sums[slot] * shrink
             for each, slot, shrink in zip(weights, slots, shrinks)
         ]
+        return largest, weights, shrinks, totals
+
+    def merge(slots, heads, largest, weights, shrinks, totals):
         mixed = [
-            mix(blocks[:, 1, first_head + part].reshape(2 * block, width), each)
-            for part, each in enumerate(weights)
+            mix(blocks[:, 1, head].reshape(2 * block, width), each)
+            for head, each in zip(heads, weights)
         ]
         if not ends:
             for part, slot in enumerate(slots):
                 new_peak[slot] = largest[part]
                 new_sums[slot] = totals[part]
                 new_mixes[slot] = mixed[part] + mixes[slot] * shrinks[part]
-            continue
-        for part in range(0, step, 2):
-            done = []
-            for at in range(part, part + 2):
-                scale = 1.0 / totals[at]
-                result = mixed[at] * scale + mixes[slots[at]] * (shrinks[at] * scale)
-                done.append(result.T.reshape(block, group, width))
-            pair = slots[part] // 2
-            done = jnp.concatenate(done, axis=1).astype(staged.dtype)
-            first = pl.multiple_of((first_head + part) * group, 2 * group)
-            for piece in range(2):
-                rows = slice(piece * block // 2, (piece + 1) * block // 2)
-                staged[pair, rows] = done[rows]
-                copy = pltpu.make_async_copy(
-                    staged.at[pair, rows],
-                    out.at[rows, pl.ds(first, 2 * group)],
-                    sems.at[pair, piece],
-                )
-                copy.start()
-                copies.append(copy)
+            return
+        done = []
+        for part, slot in enumerate(slots):
+            scale = 1.0 / totals[part]
+            result = mixed[part] * scale + mixes[slot] * (shrinks[part] * scale)
+            done.append(result.T.reshape(block, group, width))
+        pair = slots[0] // 2
+        staged[pair] = jnp.concatenate(done, axis=1).astype(staged.dtype)
+        first = pl.multiple_of(heads[0] * group, 2 * group)
+        copy = pltpu.make_async_copy(
+            staged.at[pair], out.at[:, pl.ds(first, 2 * group)], sems.at[pair]
+        )
+        copy.start()
+        copies.append(copy)
+
+    waiting = None
+    for begin in range(0, kv_count, 2):
+        side = core if begin < half else 1 - core
+        slots = [begin, begin + 1]
+        heads = [side * half + slot % half for slot in slots]
+        weighed = weigh(slots, heads)
+        if waiting is not None:
+            merge(*waiting)
+        waiting = (slots, heads, *weighed)
+    merge(*waiting)
     for copy in copies:
         copy.wait()
 
@@ -337,7 +341,7 @@
         out_specs=pl.BlockSpec(memory_space=pl.ANY),
         scratch_shapes=[
             pltpu.VMEM((kv_count // 2, block, 2 * group, width), jnp.bfloat16),
-            pltpu.SemaphoreType.DMA((kv_count // 2, 2)),
+            pltpu.SemaphoreType.DMA((kv_count // 2,)),
         ],
         compiler_params=params,
         cost_estimate=cost(2),

time: 37.9 us -> 37.9 us (level)
  no operation moved by 1% of the time
where the time goes in v12:
time: 37.9 us; the launch traced here: 37.6 us
  starting transfers between devices  15.6 us (41%)
  waiting for transfers between devices  13 us (34%)
  Pallas kernels  8.76 us (23%)
    ppermute x6, starting transfers between devices, upwards(): return lax.ppermute(array, ('ctx', 'head'), pairs)  14.6 us
    ppermute x6, waiting for transfers between devices, upwards(): return lax.ppermute(array, ('ctx', 'head'), pairs)  13 us
    pallas_call x1, Pallas kernels, shards(): pl.pallas_call(functools.partial(near_kernel, devices=devices, group=grou...  3.35 us
    pallas_call x1, Pallas kernels, shards(): pl.pallas_call(functools.partial(far_kernel, number=1), out_shape=jax.Sha...  2.13 us
    pallas_call x2, Pallas kernels, pack(): pl.pallas_call(functools.partial(pack_kernel, kept=kept), out_shape=out_s...  2.07 us
    pallas_call x1, Pallas kernels, shards(): pl.pallas_call(functools.partial(far_kernel, number=0), out_shape=state,...  1.13 us
    ppermute x2, starting transfers between devices, swap(): return lax.ppermute(array, 'head', [(0, 1), (1, 0)])  0.96 us
  transfers between devices with their start and end apart: 8, of which 6 were waited for; matrix products, arithmetic and copies ran while one was open for 0% of the time, Pallas kernels for 15%

profile of v12, /device:TPU:19, one launch (start us, length us, event | category | flops | bytes accessed | tf_op | source)
XLA Modules:
  0.0 37.6 jit_solution(10046959559948365448)
XLA Ops:
  0.0 0.9 %give.1 = bf16[2,4,64,128]{3,2,1,0:T(8,128)(2,1)S(1)} custom-call(bf16[128,4,128]{2,1,0:T(4,128)(2,1)} %refs_0_.3, bf16[128,4,128]{2,1,0:T(4,128)(2,1)} %refs_1_.3), custom_call_target="tpu_custom_call" | custom-call | bytes 2097152 | tf_op jit(solution)/shard_map/give/pallas_call | solution.py:260
  0.9 0.7 %collective-permute-start = (bf16[2,4,64,128]{3,2,1,0:T(8,128)(2,1)S(1)}, bf16[2,4,64,128]{3,2,1,0:T(8,128)(2,1)S(1)}, u32[]{:S(2)}, u32[]{:S(2)}) collective-permute-start(bf16[2,4,64,128]{3,2,1,0:T(8,128)(2,1)S(1)} %give.1), channel_id=1, source_target_pairs={{0,1},{1,0},{2,3},{3,2},{4,5},{5,4},{6,7},{7,6},{8,9},{9,8},{10,11... | collective-permute-start | bytes 393224 | tf_op jit(solution)/shard_map/ppermute | solution.py:244
  1.7 1.1 %keep.1 = (bf16[2,4,64,128]{3,2,1,0:T(8,128)(2,1)S(1)}, bf16[64,32,128]{2,1,0:T(8,128)(2,1)S(1)}) custom-call(bf16[128,4,128]{2,1,0:T(4,128)(2,1)} %refs_0_.3, bf16[128,4,128]{2,1,0:T(4,128)(2,1)} %refs_1_.3, bf16[128,32,128]{2,1,0:T(8,128)(2,1)} %queries.1), custom_call_target="tpu_custom_call" | custom-call | bytes 3145728 | tf_op jit(solution)/shard_map/keep/pallas_call | solution.py:260
  2.8 0.0 collective-permute-done
  2.8 0.0 copy-start
  2.9 0.0 copy-start.1
  2.9 0.2 collective-permute-start.1
  3.2 3.1 %collective-permute-start.2 = (bf16[2,8,64,128]{3,2,1,0:T(8,128)(2,1)S(1)}, bf16[2,8,64,128]{3,2,1,0:T(8,128)(2,1)S(1)}, u32[]{:S(2)}, u32[]{:S(2)}) collective-permute-start(bf16[2,8,64,128]{3,2,1,0:T(8,128)(2,1)S(1)} %pad_maximum_fusion.refs_0_), channel_id=1, source_target_pairs={{0,6},{2,4},{4,10},{6,8},{8,14},{10,12},{12,18},{14,16},{16,22},{1... | collective-permute-start | bytes 786440 | tf_op jit(solution)/shard_map/ppermute | solution.py:251
  6.3 0.0 collective-permute-done.1.partner_queries
  6.3 2.1 %collective-permute-start.3 = (bf16[2,8,64,128]{3,2,1,0:T(8,128)(2,1)S(1)}, bf16[2,8,64,128]{3,2,1,0:T(8,128)(2,1)S(1)}, u32[]{:S(2)}, u32[]{:S(2)}) collective-permute-start(bf16[2,8,64,128]{3,2,1,0:T(8,128)(2,1)S(1)} %pad_maximum_fusion.refs_0_), channel_id=1, source_target_pairs={{0,8},{2,10},{4,12},{6,14},{8,16},{10,18},{12,20},{14,22},{16,24},... | collective-permute-start | bytes 786440 | tf_op jit(solution)/shard_map/ppermute | solution.py:251
  8.4 2.0 %collective-permute-start.5 = (bf16[2,8,64,128]{3,2,1,0:T(8,128)(2,1)S(1)}, bf16[2,8,64,128]{3,2,1,0:T(8,128)(2,1)S(1)}, u32[]{:S(2)}, u32[]{:S(2)}) collective-permute-start(bf16[2,8,64,128]{3,2,1,0:T(8,128)(2,1)S(1)} %pad_maximum_fusion.refs_0_), channel_id=1, source_target_pairs={{0,4},{2,6},{4,8},{6,10},{8,12},{10,14},{12,16},{14,18},{16,20},{1... | collective-permute-start | bytes 786440 | tf_op jit(solution)/shard_map/ppermute | solution.py:251
  10.4 3.3 %collective-permute-start.4 = (bf16[2,8,64,128]{3,2,1,0:T(8,128)(2,1)S(1)}, bf16[2,8,64,128]{3,2,1,0:T(8,128)(2,1)S(1)}, u32[]{:S(2)}, u32[]{:S(2)}) collective-permute-start(bf16[2,8,64,128]{3,2,1,0:T(8,128)(2,1)S(1)} %pad_maximum_fusion.refs_0_), channel_id=1, source_target_pairs={{0,2},{2,8},{4,6},{6,12},{8,10},{10,16},{12,14},{14,20},{16,18},{1... | collective-permute-start | bytes 786440 | tf_op jit(solution)/shard_map/ppermute | solution.py:251
  13.7 0.5 %collective-permute-done.2.refs_1_ = bf16[2,8,64,128]{3,2,1,0:T(8,128)(2,1)S(1)} collective-permute-done((bf16[2,8,64,128]{3,2,1,0:T(8,128)(2,1)S(1)}, bf16[2,8,64,128]{3,2,1,0:T(8,128)(2,1)S(1)}, u32[]{:S(2)}, u32[]{:S(2)}) %collective-permute-start.2) | collective-permute-done | bytes 262176 | tf_op jit(solution)/shard_map/ppermute | solution.py:251
  14.2 0.3 collective-permute-done.3.refs_2_
  14.5 2.1 %collective-permute-start.6 = (bf16[2,2,8,64,128]{4,3,2,1,0:T(8,128)(2,1)S(1)}, bf16[2,2,8,64,128]{4,3,2,1,0:T(8,128)(2,1)S(1)}, u32[]{:S(2)}, u32[]{:S(2)}) collective-permute-start(bf16[2,2,8,64,128]{4,3,2,1,0:T(8,128)(2,1)S(1)} %early.1), channel_id=1, source_target_pairs={{0,8},{2,10},{4,12},{6,14},{8,16},{10,18},{12,20},{14,22},{16,24},... | collective-permute-start | bytes 1572872 | tf_op jit(solution)/shard_map/ppermute | solution.py:251
  16.6 3.4 %collective-permute-done.5.refs_4_ = bf16[2,8,64,128]{3,2,1,0:T(8,128)(2,1)S(1)} collective-permute-done((bf16[2,8,64,128]{3,2,1,0:T(8,128)(2,1)S(1)}, bf16[2,8,64,128]{3,2,1,0:T(8,128)(2,1)S(1)}, u32[]{:S(2)}, u32[]{:S(2)}) %collective-permute-start.5) | collective-permute-done | bytes 262176 | tf_op jit(solution)/shard_map/ppermute | solution.py:251
  20.0 0.8 %collective-permute-done.4.refs_3_ = bf16[2,8,64,128]{3,2,1,0:T(8,128)(2,1)S(1)} collective-permute-done((bf16[2,8,64,128]{3,2,1,0:T(8,128)(2,1)S(1)}, bf16[2,8,64,128]{3,2,1,0:T(8,128)(2,1)S(1)}, u32[]{:S(2)}, u32[]{:S(2)}) %collective-permute-start.4) | collective-permute-done | bytes 262176 | tf_op jit(solution)/shard_map/ppermute | solution.py:251
  20.9 2.1 %collective-permute-start.7 = (bf16[2,2,8,64,128]{4,3,2,1,0:T(8,128)(2,1)S(1)}, bf16[2,2,8,64,128]{4,3,2,1,0:T(8,128)(2,1)S(1)}, u32[]{:S(2)}, u32[]{:S(2)}) collective-permute-start(bf16[2,2,8,64,128]{4,3,2,1,0:T(8,128)(2,1)S(1)} %late.1), channel_id=1, source_target_pairs={{0,8},{2,10},{4,12},{6,14},{8,16},{10,18},{12,20},{14,22},{16,24},... | collective-permute-start | bytes 1572872 | tf_op jit(solution)/shard_map/ppermute | solution.py:251
  23.0 0.0 copy-done
  23.0 0.0 copy-done.1
  23.0 3.3 %near.1 = (bf16[8,128,512]{2,1,0:T(8,128)(2,1)S(1)}, f32[2,128,512]{2,1,0:T(8,128)S(1)}, f32[8,1,512]{2,1,0:T(1,128)S(1)}, f32[8,1,512]{2,1,0:T(1,128)S(1)}, f32[8,128,512]{2,1,0:T(8,128)S(1)}) custom-call(s32[8]{0:T(128)S(1)} %copy-done.1, bf16[128,32,128]{2,1,0:T(8,128)(2,1)S(1)} %copy-done, ...), custom_call_target="tpu_custom_call" | custom-call | flops 671088640 | bytes 4194304 | tf_op jit(solution)/shard_map/near/pallas_call | solution.py:314
  26.4 1.9 %collective-permute-done.6.blocks = bf16[2,2,8,64,128]{4,3,2,1,0:T(8,128)(2,1)S(1)} collective-permute-done((bf16[2,2,8,64,128]{4,3,2,1,0:T(8,128)(2,1)S(1)}, bf16[2,2,8,64,128]{4,3,2,1,0:T(8,128)(2,1)S(1)}, u32[]{:S(2)}, u32[]{:S(2)}) %collective-permute-start.6) | collective-permute-done | bytes 524320 | tf_op jit(solution)/shard_map/ppermute | solution.py:251
  28.2 1.1 %middle.1 = (f32[8,1,512]{2,1,0:T(1,128)S(1)}, f32[8,1,512]{2,1,0:T(1,128)S(1)}, f32[8,128,512]{2,1,0:T(8,128)S(1)}) custom-call(bf16[8,128,512]{2,1,0:T(8,128)(2,1)S(1)} %get-tuple-element.25.folded, f32[2,128,512]{2,1,0:T(8,128)S(1)} %get-tuple-element.26.far_bias, f32[8,1,512]{2,1,0:T(1,128)S(1)} %get-tuple-element.27.peak, ...), custom_call_target="tpu_custom_call" | custom-call | flops 268435456 | bytes 4194304 | tf_op jit(solution)/shard_map/middle/pallas_call | solution.py:328
  29.4 6.1 %collective-permute-done.7.blocks = bf16[2,2,8,64,128]{4,3,2,1,0:T(8,128)(2,1)S(1)} collective-permute-done((bf16[2,2,8,64,128]{4,3,2,1,0:T(8,128)(2,1)S(1)}, bf16[2,2,8,64,128]{4,3,2,1,0:T(8,128)(2,1)S(1)}, u32[]{:S(2)}, u32[]{:S(2)}) %collective-permute-start.7) | collective-permute-done | bytes 524320 | tf_op jit(solution)/shard_map/ppermute | solution.py:251
  35.4 2.1 %finish.1 = bf16[64,64,128]{2,1,0:T(8,128)(2,1)} custom-call(bf16[8,128,512]{2,1,0:T(8,128)(2,1)S(1)} %get-tuple-element.25.folded, f32[2,128,512]{2,1,0:T(8,128)S(1)} %get-tuple-element.26.far_bias, f32[8,1,512]{2,1,0:T(1,128)S(1)} %get-tuple-element.30.peak, f32[8,1,512]{2,1,0:T(1,128)S(1)} %get-tuple-element.31.sums, ...), custom_call_target="tpu_custom_call" | custom-call | flops 268435456 | bytes 4194304 | tf_op jit(solution)/shard_map/finish/pallas_call | solution.py:337
  (4 shorter events, 0.1 us)
Async XLA Ops:
  0.9 1.9 %collective-permute-start = (bf16[2,4,64,128]{3,2,1,0:T(8,128)(2,1)S(1)}, bf16[2,4,64,128]{3,2,1,0:T(8,128)(2,1)S(1)}, u32[]{:S(2)}, u32[]{:S(2)}) collective-permute-start(bf16[2,4,64,128]{3,2,1,0:T(8,128)(2,1)S(1)} %give.1), channel_id=1, source_target_pairs={{0,1},{1,0},{2,3},{3,2},{4,5},{5,4},{6,7},{7,6},{8,9},{9,8},{10,11... | collective-permute-start | bytes 393224 | tf_op jit(solution)/shard_map/ppermute | solution.py:244
  2.8 20.1 %copy-start = (bf16[128,32,128]{2,1,0:T(8,128)(2,1)S(1)}, bf16[128,32,128]{2,1,0:T(8,128)(2,1)}, u32[]{:S(2)}) copy-start(bf16[128,32,128]{2,1,0:T(8,128)(2,1)} %queries.1) | copy-start | bytes 3145732
  2.9 20.1 %copy-start.1 = (s32[8]{0:T(128)S(1)}, s32[8]{0:T(128)}, u32[]{:S(2)}) copy-start(s32[8]{0:T(128)} %doc_lengths.1) | copy-start | bytes 100
  2.9 3.4 %collective-permute-start.1 = (bf16[64,32,128]{2,1,0:T(8,128)(2,1)S(1)}, bf16[64,32,128]{2,1,0:T(8,128)(2,1)S(1)}, u32[]{:S(2)}, u32[]{:S(2)}) collective-permute-start(bf16[64,32,128]{2,1,0:T(8,128)(2,1)S(1)} %get-tuple-element.22), channel_id=1, source_target_pairs={{0,1},{1,0},{2,3},{3,2},{4,5},{5,4},{6,7},{7,6},{8,9},{9,8},{10,11... | collective-permute-start | bytes 1572872 | tf_op jit(solution)/shard_map/ppermute | solution.py:244
  3.2 11.0 %collective-permute-start.2 = (bf16[2,8,64,128]{3,2,1,0:T(8,128)(2,1)S(1)}, bf16[2,8,64,128]{3,2,1,0:T(8,128)(2,1)S(1)}, u32[]{:S(2)}, u32[]{:S(2)}) collective-permute-start(bf16[2,8,64,128]{3,2,1,0:T(8,128)(2,1)S(1)} %pad_maximum_fusion.refs_0_), channel_id=1, source_target_pairs={{0,6},{2,4},{4,10},{6,8},{8,14},{10,12},{12,18},{14,16},{16,22},{1... | collective-permute-start | bytes 786440 | tf_op jit(solution)/shard_map/ppermute | solution.py:251
  6.3 8.2 %collective-permute-start.3 = (bf16[2,8,64,128]{3,2,1,0:T(8,128)(2,1)S(1)}, bf16[2,8,64,128]{3,2,1,0:T(8,128)(2,1)S(1)}, u32[]{:S(2)}, u32[]{:S(2)}) collective-permute-start(bf16[2,8,64,128]{3,2,1,0:T(8,128)(2,1)S(1)} %pad_maximum_fusion.refs_0_), channel_id=1, source_target_pairs={{0,8},{2,10},{4,12},{6,14},{8,16},{10,18},{12,20},{14,22},{16,24},... | collective-permute-start | bytes 786440 | tf_op jit(solution)/shard_map/ppermute | solution.py:251
  8.4 11.6 %collective-permute-start.5 = (bf16[2,8,64,128]{3,2,1,0:T(8,128)(2,1)S(1)}, bf16[2,8,64,128]{3,2,1,0:T(8,128)(2,1)S(1)}, u32[]{:S(2)}, u32[]{:S(2)}) collective-permute-start(bf16[2,8,64,128]{3,2,1,0:T(8,128)(2,1)S(1)} %pad_maximum_fusion.refs_0_), channel_id=1, source_target_pairs={{0,4},{2,6},{4,8},{6,10},{8,12},{10,14},{12,16},{14,18},{16,20},{1... | collective-permute-start | bytes 786440 | tf_op jit(solution)/shard_map/ppermute | solution.py:251
  10.4 10.5 %collective-permute-start.4 = (bf16[2,8,64,128]{3,2,1,0:T(8,128)(2,1)S(1)}, bf16[2,8,64,128]{3,2,1,0:T(8,128)(2,1)S(1)}, u32[]{:S(2)}, u32[]{:S(2)}) collective-permute-start(bf16[2,8,64,128]{3,2,1,0:T(8,128)(2,1)S(1)} %pad_maximum_fusion.refs_0_), channel_id=1, source_target_pairs={{0,2},{2,8},{4,6},{6,12},{8,10},{10,16},{12,14},{14,20},{16,18},{1... | collective-permute-start | bytes 786440 | tf_op jit(solution)/shard_map/ppermute | solution.py:251
  14.5 13.7 %collective-permute-start.6 = (bf16[2,2,8,64,128]{4,3,2,1,0:T(8,128)(2,1)S(1)}, bf16[2,2,8,64,128]{4,3,2,1,0:T(8,128)(2,1)S(1)}, u32[]{:S(2)}, u32[]{:S(2)}) collective-permute-start(bf16[2,2,8,64,128]{4,3,2,1,0:T(8,128)(2,1)S(1)} %early.1), channel_id=1, source_target_pairs={{0,8},{2,10},{4,12},{6,14},{8,16},{10,18},{12,20},{14,22},{16,24},... | collective-permute-start | bytes 1572872 | tf_op jit(solution)/shard_map/ppermute | solution.py:251
  20.9 14.6 %collective-permute-start.7 = (bf16[2,2,8,64,128]{4,3,2,1,0:T(8,128)(2,1)S(1)}, bf16[2,2,8,64,128]{4,3,2,1,0:T(8,128)(2,1)S(1)}, u32[]{:S(2)}, u32[]{:S(2)}) collective-permute-start(bf16[2,2,8,64,128]{4,3,2,1,0:T(8,128)(2,1)S(1)} %late.1), channel_id=1, source_target_pairs={{0,8},{2,10},{4,12},{6,14},{8,16},{10,18},{12,20},{14,22},{16,24},... | collective-permute-start | bytes 1572872 | tf_op jit(solution)/shard_map/ppermute | solution.py:251

commit v13 on v12

--- a/solution.py
+++ b/solution.py
@@ -11,13 +11,47 @@
 REACH_LOG = 3
 MASKED_SCORE = -1e30
 
-STEPS = ((3, 1), (4, 4), (1, 3), (2, 2))
+ORDERS = (
+    ((3, 4, 1, 2), (1, 4, 3, 2), (3, 4, 1, 2), (1, 4, 3, 2)),
+    ((3, 4, 1, 2), (1, 3, 4, 2), (4, 3, 1, 2), (1, 4, 3, 2)),
+)
 EARLY_TARGETS = (0, 1, 3, 2)
-LATE_TARGETS = (0, 2, 1, 3)
+LATE_TARGETS = (0, 2, 3, 1)
 EARLY_CHOICES = ((1, (1, 1, 1, 1)), (2, (2, 2, 0, 2)))
 LATE_CHOICES = ((3, (3, 1, 3, 1)), (4, (4, 0, 4, 2)))
-EARLY_DISTANCES = ((5, 7, (5, 7, 6, 6)), (8, 8, (8, 8, 7, 5)))
-LATE_DISTANCES = ((7, 5, (7, 6, 8, 7)), (6, 6, (6, 5, 5, 8)))
+
+
+def schedule(stretches):
+    middle = stretches // 2
+    near_steps = [{} for _ in range(4)]
+    held = [{0: at} for at in range(stretches)]
+    for at in range(stretches):
+        for distance, step in enumerate(ORDERS[at >= middle][at % 4], 1):
+            if at + distance < stretches:
+                near_steps[step - 1][at] = at + distance
+                held[at + distance][step] = at
+    nothing = stretches
+    distances = [
+        [to - held[to].get(step, to - nothing) for step in range(1, 5)] + [nothing] * 4
+        for to in range(stretches)
+    ]
+    far_steps = []
+    for number, (targets, choices) in enumerate(
+        ((EARLY_TARGETS, EARLY_CHOICES), (LATE_TARGETS, LATE_CHOICES))
+    ):
+        far_steps.append({})
+        for at in range(stretches - 4):
+            turning = middle - 4 <= at < middle
+            row = at - (middle - 4)
+            to = middle + targets[row] if turning else at + 4
+            sent = [special[row] if turning else usual for usual, special in choices]
+            if not any(what in held[at] for what in sent):
+                continue
+            far_steps[-1][at] = to
+            for slot, what in enumerate(sent):
+                if what in held[at]:
+                    distances[to][4 + 2 * number + slot] = to - held[at][what]
+    return near_steps, far_steps, distances
 
 
 def query_bounds(first_place, lanes, group, doc_lengths):
@@ -98,19 +132,13 @@
                 out[slot] = ref[...]
 
 
-def near_kernel(doc_lengths, queries, partner_queries, *refs, devices, group):
+def near_kernel(doc_lengths, distances, queries, partner_queries, *refs, devices, group):
     blocks, (folded, far_bias, peak, sums, mixes, bias) = refs[:-6], refs[-6:]
     stretch, core = chain_position(devices), lax.axis_index("head")
     kv_count, block, width = blocks[0].shape[1:]
     lanes = block * group
-    odd = stretch % 2 == 1
     for row in range(len(blocks)):
-        distance = 0
-        if row > 0:
-            by_even, by_odd = STEPS[row - 1]
-            if by_even % 2 == 1:
-                by_even, by_odd = by_odd, by_even
-            distance = jnp.where(odd, by_odd, by_even)
+        distance = 0 if row == 0 else distances[stretch, row - 1]
         bias[row * block : (row + 1) * block, :] = block_bias(
             stretch, distance, block, group, doc_lengths
         )
@@ -145,14 +173,10 @@
                 peak[slot] = largest[part]
                 sums[slot] = jnp.sum(weights[part], axis=0, keepdims=True)
                 mixes[slot] = mix(gather(1, first_head + part), weights[part])
-    turn = stretch - devices
-    for number, table in enumerate((EARLY_DISTANCES, LATE_DISTANCES)):
-        for row, (even_distance, odd_distance, special) in enumerate(table):
-            distance = jnp.where(odd, odd_distance, even_distance)
-            for at, other in enumerate(special):
-                distance = jnp.where(turn == at, other, distance)
+    for number in range(2):
+        for row in range(2):
             far_bias[number, row * block : (row + 1) * block, :] = block_bias(
-                stretch, distance, block, group, doc_lengths
+                stretch, distances[stretch, 4 + 2 * number + row], block, group, doc_lengths
             )
 
 
@@ -243,13 +267,11 @@
     def swap(array):
         return lax.ppermute(array, "head", [(0, 1), (1, 0)])
 
-    def upwards(array, steps, turned=()):
-        target = {at: at + steps[at % 2] for at in range(stretches)}
-        for number, to in enumerate(turned):
-            target[devices - 4 + number] = devices + to
-        pairs = [(owner(at), owner(to)) for at, to in target.items() if to < stretches]
+    def upwards(array, step):
+        pairs = [(owner(at), owner(to)) for at, to in step.items()]
         return lax.ppermute(array, ("ctx", "head"), pairs)
 
+    near_steps, far_steps, distances = schedule(stretches)
     smem = pl.BlockSpec(memory_space=pltpu.SMEM)
     vmem = pl.BlockSpec(memory_space=pltpu.VMEM)
     def pack(kept):
@@ -281,9 +303,9 @@
     )
     own, given_queries = lax.optimization_barrier((own, given_queries))
     partner_queries = swap(given_queries)
-    first = upwards(own, STEPS[0])
+    first = upwards(own, near_steps[0])
     own, partner_queries = lax.optimization_barrier((own, partner_queries))
-    second, third, fourth = [upwards(own, steps) for steps in STEPS[1:]]
+    second, third, fourth = [upwards(own, step) for step in near_steps[1:]]
 
     def bundle(name, held, choices):
         return pl.pallas_call(
@@ -295,9 +317,9 @@
             name=name,
         )(*held)
 
-    early = upwards(bundle("early", (own, first, second), EARLY_CHOICES), (4, 4), EARLY_TARGETS)
+    early = upwards(bundle("early", (own, first, second), EARLY_CHOICES), far_steps[0])
     late = upwards(
-        bundle("late", (own, first, second, third, fourth), LATE_CHOICES), (4, 4), LATE_TARGETS
+        bundle("late", (own, first, second, third, fourth), LATE_CHOICES), far_steps[1]
     )
 
     params = pltpu.CompilerParams(vmem_limit_bytes=14 * 2**20)
@@ -318,13 +340,13 @@
             jax.ShapeDtypeStruct((2, 2 * block, lanes), jnp.float32),
             *state,
         ],
-        in_specs=[smem] + [vmem] * (2 + len(near)),
+        in_specs=[smem] * 2 + [vmem] * (2 + len(near)),
         out_specs=[vmem] * 5,
         scratch_shapes=[pltpu.VMEM((len(near) * block, lanes), jnp.float32)],
         compiler_params=params,
         cost_estimate=cost(len(near)),
         name="near",
-    )(doc_lengths, queries, partner_queries, *near)
+    )(doc_lengths, jnp.array(distances, jnp.int32), queries, partner_queries, *near)
     known = pl.pallas_call(
         functools.partial(far_kernel, number=0),
         out_shape=state,

time: 37.9 us -> 37.9 us (level)
  transfers between devices with their start and end apart: 8 -> 8, of which waited for: 6 -> 6; matrix products, arithmetic and copies ran while one was open for 0% -> 0% of each run, Pallas kernels for 15% -> 16%
where the time goes in v13:
time: 37.9 us; the launch traced here: 37.6 us
  starting transfers between devices  15.4 us (41%)
  waiting for transfers between devices  12.9 us (34%)
  Pallas kernels  9.02 us (24%)
    ppermute x6, starting transfers between devices, upwards(): return lax.ppermute(array, ('ctx', 'head'), pairs)  14.5 us
    ppermute x6, waiting for transfers between devices, upwards(): return lax.ppermute(array, ('ctx', 'head'), pairs)  12.9 us
    pallas_call x1, Pallas kernels, shards(): pl.pallas_call(functools.partial(near_kernel, devices=devices, group=grou...  3.61 us
    pallas_call x1, Pallas kernels, shards(): pl.pallas_call(functools.partial(far_kernel, number=1), out_shape=jax.Sha...  2.13 us
    pallas_call x2, Pallas kernels, pack(): pl.pallas_call(functools.partial(pack_kernel, kept=kept), out_shape=out_s...  2.07 us
    pallas_call x1, Pallas kernels, shards(): pl.pallas_call(functools.partial(far_kernel, number=0), out_shape=state,...  1.13 us
    ppermute x2, starting transfers between devices, swap(): return lax.ppermute(array, 'head', [(0, 1), (1, 0)])  0.95 us
  transfers between devices with their start and end apart: 8, of which 6 were waited for; matrix products, arithmetic and copies ran while one was open for 0% of the time, Pallas kernels for 16%

profile of v13, /device:TPU:19, one launch (start us, length us, event | category | flops | bytes accessed | tf_op | source)
XLA Modules:
  0.0 37.6 jit_solution(895327641687223719)
XLA Ops:
  0.0 0.9 %give.1 = bf16[2,4,64,128]{3,2,1,0:T(8,128)(2,1)S(1)} custom-call(bf16[128,4,128]{2,1,0:T(4,128)(2,1)} %refs_0_.3, bf16[128,4,128]{2,1,0:T(4,128)(2,1)} %refs_1_.3), custom_call_target="tpu_custom_call" | custom-call | bytes 2097152 | tf_op jit(solution)/shard_map/give/pallas_call | solution.py:282
  0.9 0.7 %collective-permute-start = (bf16[2,4,64,128]{3,2,1,0:T(8,128)(2,1)S(1)}, bf16[2,4,64,128]{3,2,1,0:T(8,128)(2,1)S(1)}, u32[]{:S(2)}, u32[]{:S(2)}) collective-permute-start(bf16[2,4,64,128]{3,2,1,0:T(8,128)(2,1)S(1)} %give.1), channel_id=1, source_target_pairs={{0,1},{1,0},{2,3},{3,2},{4,5},{5,4},{6,7},{7,6},{8,9},{9,8},{10,11... | collective-permute-start | bytes 393224 | tf_op jit(solution)/shard_map/ppermute | solution.py:268
  1.7 1.1 %keep.1 = (bf16[2,4,64,128]{3,2,1,0:T(8,128)(2,1)S(1)}, bf16[64,32,128]{2,1,0:T(8,128)(2,1)S(1)}) custom-call(bf16[128,4,128]{2,1,0:T(4,128)(2,1)} %refs_0_.3, bf16[128,4,128]{2,1,0:T(4,128)(2,1)} %refs_1_.3, bf16[128,32,128]{2,1,0:T(8,128)(2,1)} %queries.1), custom_call_target="tpu_custom_call" | custom-call | bytes 3145728 | tf_op jit(solution)/shard_map/keep/pallas_call | solution.py:282
  2.8 0.0 collective-permute-done
  2.8 0.0 copy-start
  2.9 0.0 copy-start.1
  2.9 0.0 copy-start.2
  2.9 0.2 collective-permute-start.1
  3.2 3.1 %collective-permute-start.2 = (bf16[2,8,64,128]{3,2,1,0:T(8,128)(2,1)S(1)}, bf16[2,8,64,128]{3,2,1,0:T(8,128)(2,1)S(1)}, u32[]{:S(2)}, u32[]{:S(2)}) collective-permute-start(bf16[2,8,64,128]{3,2,1,0:T(8,128)(2,1)S(1)} %pad_maximum_fusion.refs_0_), channel_id=1, source_target_pairs={{0,6},{2,4},{4,10},{6,8},{8,14},{10,12},{12,18},{14,16},{16,22},{1... | collective-permute-start | bytes 786440 | tf_op jit(solution)/shard_map/ppermute | solution.py:272
  6.3 0.0 collective-permute-done.1.partner_queries
  6.3 2.1 %collective-permute-start.3 = (bf16[2,8,64,128]{3,2,1,0:T(8,128)(2,1)S(1)}, bf16[2,8,64,128]{3,2,1,0:T(8,128)(2,1)S(1)}, u32[]{:S(2)}, u32[]{:S(2)}) collective-permute-start(bf16[2,8,64,128]{3,2,1,0:T(8,128)(2,1)S(1)} %pad_maximum_fusion.refs_0_), channel_id=1, source_target_pairs={{0,8},{2,10},{4,12},{6,14},{8,16},{10,18},{12,20},{14,22},{16,24},... | collective-permute-start | bytes 786440 | tf_op jit(solution)/shard_map/ppermute | solution.py:272
  8.4 3.1 %collective-permute-start.5 = (bf16[2,8,64,128]{3,2,1,0:T(8,128)(2,1)S(1)}, bf16[2,8,64,128]{3,2,1,0:T(8,128)(2,1)S(1)}, u32[]{:S(2)}, u32[]{:S(2)}) collective-permute-start(bf16[2,8,64,128]{3,2,1,0:T(8,128)(2,1)S(1)} %pad_maximum_fusion.refs_0_), channel_id=1, source_target_pairs={{0,4},{2,6},{4,8},{6,10},{8,12},{10,14},{12,16},{14,18},{16,20},{1... | collective-permute-start | bytes 786440 | tf_op jit(solution)/shard_map/ppermute | solution.py:272
  11.5 1.9 %collective-permute-start.4 = (bf16[2,8,64,128]{3,2,1,0:T(8,128)(2,1)S(1)}, bf16[2,8,64,128]{3,2,1,0:T(8,128)(2,1)S(1)}, u32[]{:S(2)}, u32[]{:S(2)}) collective-permute-start(bf16[2,8,64,128]{3,2,1,0:T(8,128)(2,1)S(1)} %pad_maximum_fusion.refs_0_), channel_id=1, source_target_pairs={{0,2},{2,8},{4,6},{6,12},{8,10},{10,16},{12,14},{14,20},{16,18},{1... | collective-permute-start | bytes 786440 | tf_op jit(solution)/shard_map/ppermute | solution.py:272
  13.4 0.8 %collective-permute-done.2.refs_1_ = bf16[2,8,64,128]{3,2,1,0:T(8,128)(2,1)S(1)} collective-permute-done((bf16[2,8,64,128]{3,2,1,0:T(8,128)(2,1)S(1)}, bf16[2,8,64,128]{3,2,1,0:T(8,128)(2,1)S(1)}, u32[]{:S(2)}, u32[]{:S(2)}) %collective-permute-start.2) | collective-permute-done | bytes 262176 | tf_op jit(solution)/shard_map/ppermute | solution.py:272
  14.2 0.3 collective-permute-done.3.refs_2_
  14.5 2.1 %collective-permute-start.6 = (bf16[2,2,8,64,128]{4,3,2,1,0:T(8,128)(2,1)S(1)}, bf16[2,2,8,64,128]{4,3,2,1,0:T(8,128)(2,1)S(1)}, u32[]{:S(2)}, u32[]{:S(2)}) collective-permute-start(bf16[2,2,8,64,128]{4,3,2,1,0:T(8,128)(2,1)S(1)} %early.1), channel_id=1, source_target_pairs={{4,12},{6,14},{8,16},{10,18},{12,20},{14,22},{16,24},{18,26},{20,2... | collective-permute-start | bytes 1572872 | tf_op jit(solution)/shard_map/ppermute | solution.py:272
  16.6 3.4 %collective-permute-done.5.refs_4_ = bf16[2,8,64,128]{3,2,1,0:T(8,128)(2,1)S(1)} collective-permute-done((bf16[2,8,64,128]{3,2,1,0:T(8,128)(2,1)S(1)}, bf16[2,8,64,128]{3,2,1,0:T(8,128)(2,1)S(1)}, u32[]{:S(2)}, u32[]{:S(2)}) %collective-permute-start.5) | collective-permute-done | bytes 262176 | tf_op jit(solution)/shard_map/ppermute | solution.py:272
  20.0 1.3 %collective-permute-done.4.refs_3_ = bf16[2,8,64,128]{3,2,1,0:T(8,128)(2,1)S(1)} collective-permute-done((bf16[2,8,64,128]{3,2,1,0:T(8,128)(2,1)S(1)}, bf16[2,8,64,128]{3,2,1,0:T(8,128)(2,1)S(1)}, u32[]{:S(2)}, u32[]{:S(2)}) %collective-permute-start.4) | collective-permute-done | bytes 262176 | tf_op jit(solution)/shard_map/ppermute | solution.py:272
  21.4 2.2 %collective-permute-start.7 = (bf16[2,2,8,64,128]{4,3,2,1,0:T(8,128)(2,1)S(1)}, bf16[2,2,8,64,128]{4,3,2,1,0:T(8,128)(2,1)S(1)}, u32[]{:S(2)}, u32[]{:S(2)}) collective-permute-start(bf16[2,2,8,64,128]{4,3,2,1,0:T(8,128)(2,1)S(1)} %late.1), channel_id=1, source_target_pairs={{2,10},{4,12},{6,14},{8,16},{10,18},{12,20},{14,22},{16,24},{18,26... | collective-permute-start | bytes 1572872 | tf_op jit(solution)/shard_map/ppermute | solution.py:272
  23.5 0.0 copy-done
  23.5 0.0 copy-done.1
  23.5 0.0 copy-done.2
  23.5 3.6 %near.1 = (bf16[8,128,512]{2,1,0:T(8,128)(2,1)S(1)}, f32[2,128,512]{2,1,0:T(8,128)S(1)}, f32[8,1,512]{2,1,0:T(1,128)S(1)}, f32[8,1,512]{2,1,0:T(1,128)S(1)}, f32[8,128,512]{2,1,0:T(8,128)S(1)}) custom-call(s32[8]{0:T(128)S(1)} %copy-done.2, s32[32,8]{1,0:T(8,128)S(1)} %copy-done.1, bf16[128,32,128]{2,1,0:T(8,128)(2,1)S(1)} %copy-done, ...), custom_call_target="tpu_custom_call" | custom-call | flops 671088640 | bytes 4194304 | tf_op jit(solution)/shard_map/near/pallas_call | solution.py:336
  27.2 1.1 %collective-permute-done.6.blocks = bf16[2,2,8,64,128]{4,3,2,1,0:T(8,128)(2,1)S(1)} collective-permute-done((bf16[2,2,8,64,128]{4,3,2,1,0:T(8,128)(2,1)S(1)}, bf16[2,2,8,64,128]{4,3,2,1,0:T(8,128)(2,1)S(1)}, u32[]{:S(2)}, u32[]{:S(2)}) %collective-permute-start.6) | collective-permute-done | bytes 524320 | tf_op jit(solution)/shard_map/ppermute | solution.py:272
  28.2 1.1 %middle.1 = (f32[8,1,512]{2,1,0:T(1,128)S(1)}, f32[8,1,512]{2,1,0:T(1,128)S(1)}, f32[8,128,512]{2,1,0:T(8,128)S(1)}) custom-call(bf16[8,128,512]{2,1,0:T(8,128)(2,1)S(1)} %get-tuple-element.25.folded, f32[2,128,512]{2,1,0:T(8,128)S(1)} %get-tuple-element.26.far_bias, f32[8,1,512]{2,1,0:T(1,128)S(1)} %get-tuple-element.27.peak, ...), custom_call_target="tpu_custom_call" | custom-call | flops 268435456 | bytes 4194304 | tf_op jit(solution)/shard_map/middle/pallas_call | solution.py:350
  29.4 6.1 %collective-permute-done.7.blocks = bf16[2,2,8,64,128]{4,3,2,1,0:T(8,128)(2,1)S(1)} collective-permute-done((bf16[2,2,8,64,128]{4,3,2,1,0:T(8,128)(2,1)S(1)}, bf16[2,2,8,64,128]{4,3,2,1,0:T(8,128)(2,1)S(1)}, u32[]{:S(2)}, u32[]{:S(2)}) %collective-permute-start.7) | collective-permute-done | bytes 524320 | tf_op jit(solution)/shard_map/ppermute | solution.py:272
  35.5 2.1 %finish.1 = bf16[64,64,128]{2,1,0:T(8,128)(2,1)} custom-call(bf16[8,128,512]{2,1,0:T(8,128)(2,1)S(1)} %get-tuple-element.25.folded, f32[2,128,512]{2,1,0:T(8,128)S(1)} %get-tuple-element.26.far_bias, f32[8,1,512]{2,1,0:T(1,128)S(1)} %get-tuple-element.30.peak, f32[8,1,512]{2,1,0:T(1,128)S(1)} %get-tuple-element.31.sums, ...), custom_call_target="tpu_custom_call" | custom-call | flops 268435456 | bytes 4194304 | tf_op jit(solution)/shard_map/finish/pallas_call | solution.py:359
  (4 shorter events, 0.1 us)
Async XLA Ops:
  0.9 1.9 %collective-permute-start = (bf16[2,4,64,128]{3,2,1,0:T(8,128)(2,1)S(1)}, bf16[2,4,64,128]{3,2,1,0:T(8,128)(2,1)S(1)}, u32[]{:S(2)}, u32[]{:S(2)}) collective-permute-start(bf16[2,4,64,128]{3,2,1,0:T(8,128)(2,1)S(1)} %give.1), channel_id=1, source_target_pairs={{0,1},{1,0},{2,3},{3,2},{4,5},{5,4},{6,7},{7,6},{8,9},{9,8},{10,11... | collective-permute-start | bytes 393224 | tf_op jit(solution)/shard_map/ppermute | solution.py:268
  2.8 20.7 %copy-start = (bf16[128,32,128]{2,1,0:T(8,128)(2,1)S(1)}, bf16[128,32,128]{2,1,0:T(8,128)(2,1)}, u32[]{:S(2)}) copy-start(bf16[128,32,128]{2,1,0:T(8,128)(2,1)} %queries.1) | copy-start | bytes 3145732
  2.9 20.7 %copy-start.1 = (s32[32,8]{1,0:T(8,128)S(1)}, s32[32,8]{1,0:T(8,128)}, u32[]{:S(2)}) copy-start(s32[32,8]{1,0:T(8,128)} %constant.8.clone.distances) | copy-start | bytes 3076
  2.9 20.7 %copy-start.2 = (s32[8]{0:T(128)S(1)}, s32[8]{0:T(128)}, u32[]{:S(2)}) copy-start(s32[8]{0:T(128)} %doc_lengths.1) | copy-start | bytes 100
  2.9 3.3 %collective-permute-start.1 = (bf16[64,32,128]{2,1,0:T(8,128)(2,1)S(1)}, bf16[64,32,128]{2,1,0:T(8,128)(2,1)S(1)}, u32[]{:S(2)}, u32[]{:S(2)}) collective-permute-start(bf16[64,32,128]{2,1,0:T(8,128)(2,1)S(1)} %get-tuple-element.22), channel_id=1, source_target_pairs={{0,1},{1,0},{2,3},{3,2},{4,5},{5,4},{6,7},{7,6},{8,9},{9,8},{10,11... | collective-permute-start | bytes 1572872 | tf_op jit(solution)/shard_map/ppermute | solution.py:268
  3.2 11.0 %collective-permute-start.2 = (bf16[2,8,64,128]{3,2,1,0:T(8,128)(2,1)S(1)}, bf16[2,8,64,128]{3,2,1,0:T(8,128)(2,1)S(1)}, u32[]{:S(2)}, u32[]{:S(2)}) collective-permute-start(bf16[2,8,64,128]{3,2,1,0:T(8,128)(2,1)S(1)} %pad_maximum_fusion.refs_0_), channel_id=1, source_target_pairs={{0,6},{2,4},{4,10},{6,8},{8,14},{10,12},{12,18},{14,16},{16,22},{1... | collective-permute-start | bytes 786440 | tf_op jit(solution)/shard_map/ppermute | solution.py:272
  6.3 8.2 %collective-permute-start.3 = (bf16[2,8,64,128]{3,2,1,0:T(8,128)(2,1)S(1)}, bf16[2,8,64,128]{3,2,1,0:T(8,128)(2,1)S(1)}, u32[]{:S(2)}, u32[]{:S(2)}) collective-permute-start(bf16[2,8,64,128]{3,2,1,0:T(8,128)(2,1)S(1)} %pad_maximum_fusion.refs_0_), channel_id=1, source_target_pairs={{0,8},{2,10},{4,12},{6,14},{8,16},{10,18},{12,20},{14,22},{16,24},... | collective-permute-start | bytes 786440 | tf_op jit(solution)/shard_map/ppermute | solution.py:272
  8.4 11.6 %collective-permute-start.5 = (bf16[2,8,64,128]{3,2,1,0:T(8,128)(2,1)S(1)}, bf16[2,8,64,128]{3,2,1,0:T(8,128)(2,1)S(1)}, u32[]{:S(2)}, u32[]{:S(2)}) collective-permute-start(bf16[2,8,64,128]{3,2,1,0:T(8,128)(2,1)S(1)} %pad_maximum_fusion.refs_0_), channel_id=1, source_target_pairs={{0,4},{2,6},{4,8},{6,10},{8,12},{10,14},{12,16},{14,18},{16,20},{1... | collective-permute-start | bytes 786440 | tf_op jit(solution)/shard_map/ppermute | solution.py:272
  11.5 9.8 %collective-permute-start.4 = (bf16[2,8,64,128]{3,2,1,0:T(8,128)(2,1)S(1)}, bf16[2,8,64,128]{3,2,1,0:T(8,128)(2,1)S(1)}, u32[]{:S(2)}, u32[]{:S(2)}) collective-permute-start(bf16[2,8,64,128]{3,2,1,0:T(8,128)(2,1)S(1)} %pad_maximum_fusion.refs_0_), channel_id=1, source_target_pairs={{0,2},{2,8},{4,6},{6,12},{8,10},{10,16},{12,14},{14,20},{16,18},{1... | collective-permute-start | bytes 786440 | tf_op jit(solution)/shard_map/ppermute | solution.py:272
  14.5 13.7 %collective-permute-start.6 = (bf16[2,2,8,64,128]{4,3,2,1,0:T(8,128)(2,1)S(1)}, bf16[2,2,8,64,128]{4,3,2,1,0:T(8,128)(2,1)S(1)}, u32[]{:S(2)}, u32[]{:S(2)}) collective-permute-start(bf16[2,2,8,64,128]{4,3,2,1,0:T(8,128)(2,1)S(1)} %early.1), channel_id=1, source_target_pairs={{4,12},{6,14},{8,16},{10,18},{12,20},{14,22},{16,24},{18,26},{20,2... | collective-permute-start | bytes 1572872 | tf_op jit(solution)/shard_map/ppermute | solution.py:272
  21.4 14.1 %collective-permute-start.7 = (bf16[2,2,8,64,128]{4,3,2,1,0:T(8,128)(2,1)S(1)}, bf16[2,2,8,64,128]{4,3,2,1,0:T(8,128)(2,1)S(1)}, u32[]{:S(2)}, u32[]{:S(2)}) collective-permute-start(bf16[2,2,8,64,128]{4,3,2,1,0:T(8,128)(2,1)S(1)} %late.1), channel_id=1, source_target_pairs={{2,10},{4,12},{6,14},{8,16},{10,18},{12,20},{14,22},{16,24},{18,26... | collective-permute-start | bytes 1572872 | tf_op jit(solution)/shard_map/ppermute | solution.py:272

commit v14 on v13

--- a/solution.py
+++ b/solution.py
@@ -11,12 +11,9 @@
 REACH_LOG = 3
 MASKED_SCORE = -1e30
 
-ORDERS = (
-    ((3, 4, 1, 2), (1, 4, 3, 2), (3, 4, 1, 2), (1, 4, 3, 2)),
-    ((3, 4, 1, 2), (1, 3, 4, 2), (4, 3, 1, 2), (1, 4, 3, 2)),
-)
+ORDERS = ((3, 4, 1, 2), (1, 4, 3, 2))
 EARLY_TARGETS = (0, 1, 3, 2)
-LATE_TARGETS = (0, 2, 3, 1)
+LATE_TARGETS = (0, 2, 1, 3)
 EARLY_CHOICES = ((1, (1, 1, 1, 1)), (2, (2, 2, 0, 2)))
 LATE_CHOICES = ((3, (3, 1, 3, 1)), (4, (4, 0, 4, 2)))
 
@@ -26,7 +23,7 @@
     near_steps = [{} for _ in range(4)]
     held = [{0: at} for at in range(stretches)]
     for at in range(stretches):
-        for distance, step in enumerate(ORDERS[at >= middle][at % 4], 1):
+        for distance, step in enumerate(ORDERS[at % 2], 1):
             if at + distance < stretches:
                 near_steps[step - 1][at] = at + distance
                 held[at + distance][step] = at

time: 37.9 us -> 37.9 us (level)
  no operation moved by 1% of the time
where the time goes in v14:
time: 37.9 us; the launch traced here: 37.6 us
  starting transfers between devices  15.6 us (41%)
  waiting for transfers between devices  12.7 us (34%)
  Pallas kernels  9.04 us (24%)
    ppermute x6, starting transfers between devices, upwards(): return lax.ppermute(array, ('ctx', 'head'), pairs)  14.6 us
    ppermute x6, waiting for transfers between devices, upwards(): return lax.ppermute(array, ('ctx', 'head'), pairs)  12.7 us
    pallas_call x1, Pallas kernels, shards(): pl.pallas_call(functools.partial(near_kernel, devices=devices, group=grou...  3.62 us
    pallas_call x1, Pallas kernels, shards(): pl.pallas_call(functools.partial(far_kernel, number=1), out_shape=jax.Sha...  2.13 us
    pallas_call x2, Pallas kernels, pack(): pl.pallas_call(functools.partial(pack_kernel, kept=kept), out_shape=out_s...  2.07 us
    pallas_call x1, Pallas kernels, shards(): pl.pallas_call(functools.partial(far_kernel, number=0), out_shape=state,...  1.13 us
    ppermute x2, starting transfers between devices, swap(): return lax.ppermute(array, 'head', [(0, 1), (1, 0)])  0.95 us
  transfers between devices with their start and end apart: 8, of which 6 were waited for; matrix products, arithmetic and copies ran while one was open for 0% of the time, Pallas kernels for 16%

profile of v14, /device:TPU:19, one launch (start us, length us, event | category | flops | bytes accessed | tf_op | source)
XLA Modules:
  0.0 37.6 jit_solution(13547603662283736431)
XLA Ops:
  0.0 0.9 %give.1 = bf16[2,4,64,128]{3,2,1,0:T(8,128)(2,1)S(1)} custom-call(bf16[128,4,128]{2,1,0:T(4,128)(2,1)} %refs_0_.3, bf16[128,4,128]{2,1,0:T(4,128)(2,1)} %refs_1_.3), custom_call_target="tpu_custom_call" | custom-call | bytes 2097152 | tf_op jit(solution)/shard_map/give/pallas_call | solution.py:279
  0.9 0.7 %collective-permute-start = (bf16[2,4,64,128]{3,2,1,0:T(8,128)(2,1)S(1)}, bf16[2,4,64,128]{3,2,1,0:T(8,128)(2,1)S(1)}, u32[]{:S(2)}, u32[]{:S(2)}) collective-permute-start(bf16[2,4,64,128]{3,2,1,0:T(8,128)(2,1)S(1)} %give.1), channel_id=1, source_target_pairs={{0,1},{1,0},{2,3},{3,2},{4,5},{5,4},{6,7},{7,6},{8,9},{9,8},{10,11... | collective-permute-start | bytes 393224 | tf_op jit(solution)/shard_map/ppermute | solution.py:265
  1.7 1.1 %keep.1 = (bf16[2,4,64,128]{3,2,1,0:T(8,128)(2,1)S(1)}, bf16[64,32,128]{2,1,0:T(8,128)(2,1)S(1)}) custom-call(bf16[128,4,128]{2,1,0:T(4,128)(2,1)} %refs_0_.3, bf16[128,4,128]{2,1,0:T(4,128)(2,1)} %refs_1_.3, bf16[128,32,128]{2,1,0:T(8,128)(2,1)} %queries.1), custom_call_target="tpu_custom_call" | custom-call | bytes 3145728 | tf_op jit(solution)/shard_map/keep/pallas_call | solution.py:279
  2.8 0.0 collective-permute-done
  2.8 0.0 copy-start
  2.9 0.0 copy-start.1
  2.9 0.0 copy-start.2
  2.9 0.2 collective-permute-start.1
  3.2 3.1 %collective-permute-start.2 = (bf16[2,8,64,128]{3,2,1,0:T(8,128)(2,1)S(1)}, bf16[2,8,64,128]{3,2,1,0:T(8,128)(2,1)S(1)}, u32[]{:S(2)}, u32[]{:S(2)}) collective-permute-start(bf16[2,8,64,128]{3,2,1,0:T(8,128)(2,1)S(1)} %pad_maximum_fusion.refs_0_), channel_id=1, source_target_pairs={{0,6},{2,4},{4,10},{6,8},{8,14},{10,12},{12,18},{14,16},{16,22},{1... | collective-permute-start | bytes 786440 | tf_op jit(solution)/shard_map/ppermute | solution.py:269
  6.3 0.0 collective-permute-done.1.partner_queries
  6.3 2.1 %collective-permute-start.3 = (bf16[2,8,64,128]{3,2,1,0:T(8,128)(2,1)S(1)}, bf16[2,8,64,128]{3,2,1,0:T(8,128)(2,1)S(1)}, u32[]{:S(2)}, u32[]{:S(2)}) collective-permute-start(bf16[2,8,64,128]{3,2,1,0:T(8,128)(2,1)S(1)} %pad_maximum_fusion.refs_0_), channel_id=1, source_target_pairs={{0,8},{2,10},{4,12},{6,14},{8,16},{10,18},{12,20},{14,22},{16,24},... | collective-permute-start | bytes 786440 | tf_op jit(solution)/shard_map/ppermute | solution.py:269
  8.4 2.0 %collective-permute-start.5 = (bf16[2,8,64,128]{3,2,1,0:T(8,128)(2,1)S(1)}, bf16[2,8,64,128]{3,2,1,0:T(8,128)(2,1)S(1)}, u32[]{:S(2)}, u32[]{:S(2)}) collective-permute-start(bf16[2,8,64,128]{3,2,1,0:T(8,128)(2,1)S(1)} %pad_maximum_fusion.refs_0_), channel_id=1, source_target_pairs={{0,4},{2,6},{4,8},{6,10},{8,12},{10,14},{12,16},{14,18},{16,20},{1... | collective-permute-start | bytes 786440 | tf_op jit(solution)/shard_map/ppermute | solution.py:269
  10.4 3.3 %collective-permute-start.4 = (bf16[2,8,64,128]{3,2,1,0:T(8,128)(2,1)S(1)}, bf16[2,8,64,128]{3,2,1,0:T(8,128)(2,1)S(1)}, u32[]{:S(2)}, u32[]{:S(2)}) collective-permute-start(bf16[2,8,64,128]{3,2,1,0:T(8,128)(2,1)S(1)} %pad_maximum_fusion.refs_0_), channel_id=1, source_target_pairs={{0,2},{2,8},{4,6},{6,12},{8,10},{10,16},{12,14},{14,20},{16,18},{1... | collective-permute-start | bytes 786440 | tf_op jit(solution)/shard_map/ppermute | solution.py:269
  13.7 0.5 %collective-permute-done.2.refs_1_ = bf16[2,8,64,128]{3,2,1,0:T(8,128)(2,1)S(1)} collective-permute-done((bf16[2,8,64,128]{3,2,1,0:T(8,128)(2,1)S(1)}, bf16[2,8,64,128]{3,2,1,0:T(8,128)(2,1)S(1)}, u32[]{:S(2)}, u32[]{:S(2)}) %collective-permute-start.2) | collective-permute-done | bytes 262176 | tf_op jit(solution)/shard_map/ppermute | solution.py:269
  14.2 0.3 collective-permute-done.3.refs_2_
  14.5 2.1 %collective-permute-start.6 = (bf16[2,2,8,64,128]{4,3,2,1,0:T(8,128)(2,1)S(1)}, bf16[2,2,8,64,128]{4,3,2,1,0:T(8,128)(2,1)S(1)}, u32[]{:S(2)}, u32[]{:S(2)}) collective-permute-start(bf16[2,2,8,64,128]{4,3,2,1,0:T(8,128)(2,1)S(1)} %early.1), channel_id=1, source_target_pairs={{4,12},{6,14},{8,16},{10,18},{12,20},{14,22},{16,24},{18,26},{20,2... | collective-permute-start | bytes 1572872 | tf_op jit(solution)/shard_map/ppermute | solution.py:269
  16.6 3.4 %collective-permute-done.5.refs_4_ = bf16[2,8,64,128]{3,2,1,0:T(8,128)(2,1)S(1)} collective-permute-done((bf16[2,8,64,128]{3,2,1,0:T(8,128)(2,1)S(1)}, bf16[2,8,64,128]{3,2,1,0:T(8,128)(2,1)S(1)}, u32[]{:S(2)}, u32[]{:S(2)}) %collective-permute-start.5) | collective-permute-done | bytes 262176 | tf_op jit(solution)/shard_map/ppermute | solution.py:269
  20.0 0.8 %collective-permute-done.4.refs_3_ = bf16[2,8,64,128]{3,2,1,0:T(8,128)(2,1)S(1)} collective-permute-done((bf16[2,8,64,128]{3,2,1,0:T(8,128)(2,1)S(1)}, bf16[2,8,64,128]{3,2,1,0:T(8,128)(2,1)S(1)}, u32[]{:S(2)}, u32[]{:S(2)}) %collective-permute-start.4) | collective-permute-done | bytes 262176 | tf_op jit(solution)/shard_map/ppermute | solution.py:269
  20.9 2.1 %collective-permute-start.7 = (bf16[2,2,8,64,128]{4,3,2,1,0:T(8,128)(2,1)S(1)}, bf16[2,2,8,64,128]{4,3,2,1,0:T(8,128)(2,1)S(1)}, u32[]{:S(2)}, u32[]{:S(2)}) collective-permute-start(bf16[2,2,8,64,128]{4,3,2,1,0:T(8,128)(2,1)S(1)} %late.1), channel_id=1, source_target_pairs={{2,10},{4,12},{6,14},{8,16},{10,18},{12,20},{14,22},{16,24},{18,26... | collective-permute-start | bytes 1572872 | tf_op jit(solution)/shard_map/ppermute | solution.py:269
  23.0 0.0 copy-done
  23.0 0.0 copy-done.1
  23.0 0.0 copy-done.2
  23.0 3.6 %near.1 = (bf16[8,128,512]{2,1,0:T(8,128)(2,1)S(1)}, f32[2,128,512]{2,1,0:T(8,128)S(1)}, f32[8,1,512]{2,1,0:T(1,128)S(1)}, f32[8,1,512]{2,1,0:T(1,128)S(1)}, f32[8,128,512]{2,1,0:T(8,128)S(1)}) custom-call(s32[8]{0:T(128)S(1)} %copy-done.2, s32[32,8]{1,0:T(8,128)S(1)} %copy-done.1, bf16[128,32,128]{2,1,0:T(8,128)(2,1)S(1)} %copy-done, ...), custom_call_target="tpu_custom_call" | custom-call | flops 671088640 | bytes 4194304 | tf_op jit(solution)/shard_map/near/pallas_call | solution.py:333
  26.7 1.6 %collective-permute-done.6.blocks = bf16[2,2,8,64,128]{4,3,2,1,0:T(8,128)(2,1)S(1)} collective-permute-done((bf16[2,2,8,64,128]{4,3,2,1,0:T(8,128)(2,1)S(1)}, bf16[2,2,8,64,128]{4,3,2,1,0:T(8,128)(2,1)S(1)}, u32[]{:S(2)}, u32[]{:S(2)}) %collective-permute-start.6) | collective-permute-done | bytes 524320 | tf_op jit(solution)/shard_map/ppermute | solution.py:269
  28.2 1.1 %middle.1 = (f32[8,1,512]{2,1,0:T(1,128)S(1)}, f32[8,1,512]{2,1,0:T(1,128)S(1)}, f32[8,128,512]{2,1,0:T(8,128)S(1)}) custom-call(bf16[8,128,512]{2,1,0:T(8,128)(2,1)S(1)} %get-tuple-element.25.folded, f32[2,128,512]{2,1,0:T(8,128)S(1)} %get-tuple-element.26.far_bias, f32[8,1,512]{2,1,0:T(1,128)S(1)} %get-tuple-element.27.peak, ...), custom_call_target="tpu_custom_call" | custom-call | flops 268435456 | bytes 4194304 | tf_op jit(solution)/shard_map/middle/pallas_call | solution.py:347
  29.4 6.1 %collective-permute-done.7.blocks = bf16[2,2,8,64,128]{4,3,2,1,0:T(8,128)(2,1)S(1)} collective-permute-done((bf16[2,2,8,64,128]{4,3,2,1,0:T(8,128)(2,1)S(1)}, bf16[2,2,8,64,128]{4,3,2,1,0:T(8,128)(2,1)S(1)}, u32[]{:S(2)}, u32[]{:S(2)}) %collective-permute-start.7) | collective-permute-done | bytes 524320 | tf_op jit(solution)/shard_map/ppermute | solution.py:269
  35.5 2.1 %finish.1 = bf16[64,64,128]{2,1,0:T(8,128)(2,1)} custom-call(bf16[8,128,512]{2,1,0:T(8,128)(2,1)S(1)} %get-tuple-element.25.folded, f32[2,128,512]{2,1,0:T(8,128)S(1)} %get-tuple-element.26.far_bias, f32[8,1,512]{2,1,0:T(1,128)S(1)} %get-tuple-element.30.peak, f32[8,1,512]{2,1,0:T(1,128)S(1)} %get-tuple-element.31.sums, ...), custom_call_target="tpu_custom_call" | custom-call | flops 268435456 | bytes 4194304 | tf_op jit(solution)/shard_map/finish/pallas_call | solution.py:356
  (4 shorter events, 0.1 us)
Async XLA Ops:
  0.9 1.9 %collective-permute-start = (bf16[2,4,64,128]{3,2,1,0:T(8,128)(2,1)S(1)}, bf16[2,4,64,128]{3,2,1,0:T(8,128)(2,1)S(1)}, u32[]{:S(2)}, u32[]{:S(2)}) collective-permute-start(bf16[2,4,64,128]{3,2,1,0:T(8,128)(2,1)S(1)} %give.1), channel_id=1, source_target_pairs={{0,1},{1,0},{2,3},{3,2},{4,5},{5,4},{6,7},{7,6},{8,9},{9,8},{10,11... | collective-permute-start | bytes 393224 | tf_op jit(solution)/shard_map/ppermute | solution.py:265
  2.8 20.1 %copy-start = (bf16[128,32,128]{2,1,0:T(8,128)(2,1)S(1)}, bf16[128,32,128]{2,1,0:T(8,128)(2,1)}, u32[]{:S(2)}) copy-start(bf16[128,32,128]{2,1,0:T(8,128)(2,1)} %queries.1) | copy-start | bytes 3145732
  2.9 20.1 %copy-start.1 = (s32[32,8]{1,0:T(8,128)S(1)}, s32[32,8]{1,0:T(8,128)}, u32[]{:S(2)}) copy-start(s32[32,8]{1,0:T(8,128)} %constant.8.clone.distances) | copy-start | bytes 3076
  2.9 20.1 %copy-start.2 = (s32[8]{0:T(128)S(1)}, s32[8]{0:T(128)}, u32[]{:S(2)}) copy-start(s32[8]{0:T(128)} %doc_lengths.1) | copy-start | bytes 100
  2.9 3.3 %collective-permute-start.1 = (bf16[64,32,128]{2,1,0:T(8,128)(2,1)S(1)}, bf16[64,32,128]{2,1,0:T(8,128)(2,1)S(1)}, u32[]{:S(2)}, u32[]{:S(2)}) collective-permute-start(bf16[64,32,128]{2,1,0:T(8,128)(2,1)S(1)} %get-tuple-element.22), channel_id=1, source_target_pairs={{0,1},{1,0},{2,3},{3,2},{4,5},{5,4},{6,7},{7,6},{8,9},{9,8},{10,11... | collective-permute-start | bytes 1572872 | tf_op jit(solution)/shard_map/ppermute | solution.py:265
  3.2 11.0 %collective-permute-start.2 = (bf16[2,8,64,128]{3,2,1,0:T(8,128)(2,1)S(1)}, bf16[2,8,64,128]{3,2,1,0:T(8,128)(2,1)S(1)}, u32[]{:S(2)}, u32[]{:S(2)}) collective-permute-start(bf16[2,8,64,128]{3,2,1,0:T(8,128)(2,1)S(1)} %pad_maximum_fusion.refs_0_), channel_id=1, source_target_pairs={{0,6},{2,4},{4,10},{6,8},{8,14},{10,12},{12,18},{14,16},{16,22},{1... | collective-permute-start | bytes 786440 | tf_op jit(solution)/shard_map/ppermute | solution.py:269
  6.3 8.2 %collective-permute-start.3 = (bf16[2,8,64,128]{3,2,1,0:T(8,128)(2,1)S(1)}, bf16[2,8,64,128]{3,2,1,0:T(8,128)(2,1)S(1)}, u32[]{:S(2)}, u32[]{:S(2)}) collective-permute-start(bf16[2,8,64,128]{3,2,1,0:T(8,128)(2,1)S(1)} %pad_maximum_fusion.refs_0_), channel_id=1, source_target_pairs={{0,8},{2,10},{4,12},{6,14},{8,16},{10,18},{12,20},{14,22},{16,24},... | collective-permute-start | bytes 786440 | tf_op jit(solution)/shard_map/ppermute | solution.py:269
  8.4 11.6 %collective-permute-start.5 = (bf16[2,8,64,128]{3,2,1,0:T(8,128)(2,1)S(1)}, bf16[2,8,64,128]{3,2,1,0:T(8,128)(2,1)S(1)}, u32[]{:S(2)}, u32[]{:S(2)}) collective-permute-start(bf16[2,8,64,128]{3,2,1,0:T(8,128)(2,1)S(1)} %pad_maximum_fusion.refs_0_), channel_id=1, source_target_pairs={{0,4},{2,6},{4,8},{6,10},{8,12},{10,14},{12,16},{14,18},{16,20},{1... | collective-permute-start | bytes 786440 | tf_op jit(solution)/shard_map/ppermute | solution.py:269
  10.4 10.5 %collective-permute-start.4 = (bf16[2,8,64,128]{3,2,1,0:T(8,128)(2,1)S(1)}, bf16[2,8,64,128]{3,2,1,0:T(8,128)(2,1)S(1)}, u32[]{:S(2)}, u32[]{:S(2)}) collective-permute-start(bf16[2,8,64,128]{3,2,1,0:T(8,128)(2,1)S(1)} %pad_maximum_fusion.refs_0_), channel_id=1, source_target_pairs={{0,2},{2,8},{4,6},{6,12},{8,10},{10,16},{12,14},{14,20},{16,18},{1... | collective-permute-start | bytes 786440 | tf_op jit(solution)/shard_map/ppermute | solution.py:269
  14.5 13.7 %collective-permute-start.6 = (bf16[2,2,8,64,128]{4,3,2,1,0:T(8,128)(2,1)S(1)}, bf16[2,2,8,64,128]{4,3,2,1,0:T(8,128)(2,1)S(1)}, u32[]{:S(2)}, u32[]{:S(2)}) collective-permute-start(bf16[2,2,8,64,128]{4,3,2,1,0:T(8,128)(2,1)S(1)} %early.1), channel_id=1, source_target_pairs={{4,12},{6,14},{8,16},{10,18},{12,20},{14,22},{16,24},{18,26},{20,2... | collective-permute-start | bytes 1572872 | tf_op jit(solution)/shard_map/ppermute | solution.py:269
  20.9 14.6 %collective-permute-start.7 = (bf16[2,2,8,64,128]{4,3,2,1,0:T(8,128)(2,1)S(1)}, bf16[2,2,8,64,128]{4,3,2,1,0:T(8,128)(2,1)S(1)}, u32[]{:S(2)}, u32[]{:S(2)}) collective-permute-start(bf16[2,2,8,64,128]{4,3,2,1,0:T(8,128)(2,1)S(1)} %late.1), channel_id=1, source_target_pairs={{2,10},{4,12},{6,14},{8,16},{10,18},{12,20},{14,22},{16,24},{18,26... | collective-permute-start | bytes 1572872 | tf_op jit(solution)/shard_map/ppermute | solution.py:269

commit v15 on v12

--- a/solution.py
+++ b/solution.py
@@ -72,7 +72,8 @@
         copy.start()
     for kind in range(2):
         copies[kind].wait()
-        out[kind] = jnp.swapaxes(staged[kind].astype(jnp.float32), 0, 1).astype(out.dtype)
+        for head in range(out.shape[1]):
+            out[kind, head] = staged[kind, :, head, :]
     for copy in copies[2:]:
         copy.wait()
 

time: 37.9 us -> 38 us (level)
  no operation moved by 1% of the time
where the time goes in v15:
time: 38 us; the launch traced here: 37.7 us
  starting transfers between devices  15.6 us (41%)
  waiting for transfers between devices  13 us (34%)
  Pallas kernels  8.94 us (24%)
    ppermute x6, starting transfers between devices, upwards(): return lax.ppermute(array, ('ctx', 'head'), pairs)  14.6 us
    ppermute x6, waiting for transfers between devices, upwards(): return lax.ppermute(array, ('ctx', 'head'), pairs)  13 us
    pallas_call x1, Pallas kernels, shards(): pl.pallas_call(functools.partial(near_kernel, devices=devices, group=grou...  3.35 us
    pallas_call x2, Pallas kernels, pack(): pl.pallas_call(functools.partial(pack_kernel, kept=kept), out_shape=out_s...  2.24 us
    pallas_call x1, Pallas kernels, shards(): pl.pallas_call(functools.partial(far_kernel, number=1), out_shape=jax.Sha...  2.13 us
    pallas_call x1, Pallas kernels, shards(): pl.pallas_call(functools.partial(far_kernel, number=0), out_shape=state,...  1.13 us
    ppermute x2, starting transfers between devices, swap(): return lax.ppermute(array, 'head', [(0, 1), (1, 0)])  0.96 us
  transfers between devices with their start and end apart: 8, of which 6 were waited for; matrix products, arithmetic and copies ran while one was open for 0% of the time, Pallas kernels for 15%

profile of v15, /device:TPU:19, one launch (start us, length us, event | category | flops | bytes accessed | tf_op | source)
XLA Modules:
  0.0 37.7 jit_solution(15705746355051232469)
XLA Ops:
  0.0 1.1 %give.1 = bf16[2,4,64,128]{3,2,1,0:T(8,128)(2,1)S(1)} custom-call(bf16[128,4,128]{2,1,0:T(4,128)(2,1)} %refs_0_.3, bf16[128,4,128]{2,1,0:T(4,128)(2,1)} %refs_1_.3), custom_call_target="tpu_custom_call" | custom-call | bytes 2097152 | tf_op jit(solution)/shard_map/give/pallas_call | solution.py:261
  1.1 0.7 %collective-permute-start = (bf16[2,4,64,128]{3,2,1,0:T(8,128)(2,1)S(1)}, bf16[2,4,64,128]{3,2,1,0:T(8,128)(2,1)S(1)}, u32[]{:S(2)}, u32[]{:S(2)}) collective-permute-start(bf16[2,4,64,128]{3,2,1,0:T(8,128)(2,1)S(1)} %give.1), channel_id=1, source_target_pairs={{0,1},{1,0},{2,3},{3,2},{4,5},{5,4},{6,7},{7,6},{8,9},{9,8},{10,11... | collective-permute-start | bytes 393224 | tf_op jit(solution)/shard_map/ppermute | solution.py:245
  1.8 1.1 %keep.1 = (bf16[2,4,64,128]{3,2,1,0:T(8,128)(2,1)S(1)}, bf16[64,32,128]{2,1,0:T(8,128)(2,1)S(1)}) custom-call(bf16[128,4,128]{2,1,0:T(4,128)(2,1)} %refs_0_.3, bf16[128,4,128]{2,1,0:T(4,128)(2,1)} %refs_1_.3, bf16[128,32,128]{2,1,0:T(8,128)(2,1)} %queries.1), custom_call_target="tpu_custom_call" | custom-call | bytes 3145728 | tf_op jit(solution)/shard_map/keep/pallas_call | solution.py:261
  3.0 0.0 collective-permute-done
  3.0 0.0 copy-start
  3.0 0.0 copy-start.1
  3.1 0.2 collective-permute-start.1
  3.3 3.1 %collective-permute-start.2 = (bf16[2,8,64,128]{3,2,1,0:T(8,128)(2,1)S(1)}, bf16[2,8,64,128]{3,2,1,0:T(8,128)(2,1)S(1)}, u32[]{:S(2)}, u32[]{:S(2)}) collective-permute-start(bf16[2,8,64,128]{3,2,1,0:T(8,128)(2,1)S(1)} %pad_maximum_fusion.refs_0_), channel_id=1, source_target_pairs={{0,6},{2,4},{4,10},{6,8},{8,14},{10,12},{12,18},{14,16},{16,22},{1... | collective-permute-start | bytes 786440 | tf_op jit(solution)/shard_map/ppermute | solution.py:252
  6.5 0.0 collective-permute-done.1.partner_queries
  6.5 2.1 %collective-permute-start.3 = (bf16[2,8,64,128]{3,2,1,0:T(8,128)(2,1)S(1)}, bf16[2,8,64,128]{3,2,1,0:T(8,128)(2,1)S(1)}, u32[]{:S(2)}, u32[]{:S(2)}) collective-permute-start(bf16[2,8,64,128]{3,2,1,0:T(8,128)(2,1)S(1)} %pad_maximum_fusion.refs_0_), channel_id=1, source_target_pairs={{0,8},{2,10},{4,12},{6,14},{8,16},{10,18},{12,20},{14,22},{16,24},... | collective-permute-start | bytes 786440 | tf_op jit(solution)/shard_map/ppermute | solution.py:252
  8.6 2.0 %collective-permute-start.5 = (bf16[2,8,64,128]{3,2,1,0:T(8,128)(2,1)S(1)}, bf16[2,8,64,128]{3,2,1,0:T(8,128)(2,1)S(1)}, u32[]{:S(2)}, u32[]{:S(2)}) collective-permute-start(bf16[2,8,64,128]{3,2,1,0:T(8,128)(2,1)S(1)} %pad_maximum_fusion.refs_0_), channel_id=1, source_target_pairs={{0,4},{2,6},{4,8},{6,10},{8,12},{10,14},{12,16},{14,18},{16,20},{1... | collective-permute-start | bytes 786440 | tf_op jit(solution)/shard_map/ppermute | solution.py:252
  10.5 3.3 %collective-permute-start.4 = (bf16[2,8,64,128]{3,2,1,0:T(8,128)(2,1)S(1)}, bf16[2,8,64,128]{3,2,1,0:T(8,128)(2,1)S(1)}, u32[]{:S(2)}, u32[]{:S(2)}) collective-permute-start(bf16[2,8,64,128]{3,2,1,0:T(8,128)(2,1)S(1)} %pad_maximum_fusion.refs_0_), channel_id=1, source_target_pairs={{0,2},{2,8},{4,6},{6,12},{8,10},{10,16},{12,14},{14,20},{16,18},{1... | collective-permute-start | bytes 786440 | tf_op jit(solution)/shard_map/ppermute | solution.py:252
  13.8 0.5 %collective-permute-done.2.refs_1_ = bf16[2,8,64,128]{3,2,1,0:T(8,128)(2,1)S(1)} collective-permute-done((bf16[2,8,64,128]{3,2,1,0:T(8,128)(2,1)S(1)}, bf16[2,8,64,128]{3,2,1,0:T(8,128)(2,1)S(1)}, u32[]{:S(2)}, u32[]{:S(2)}) %collective-permute-start.2) | collective-permute-done | bytes 262176 | tf_op jit(solution)/shard_map/ppermute | solution.py:252
  14.4 0.3 collective-permute-done.3.refs_2_
  14.7 2.1 %collective-permute-start.6 = (bf16[2,2,8,64,128]{4,3,2,1,0:T(8,128)(2,1)S(1)}, bf16[2,2,8,64,128]{4,3,2,1,0:T(8,128)(2,1)S(1)}, u32[]{:S(2)}, u32[]{:S(2)}) collective-permute-start(bf16[2,2,8,64,128]{4,3,2,1,0:T(8,128)(2,1)S(1)} %early.1), channel_id=1, source_target_pairs={{0,8},{2,10},{4,12},{6,14},{8,16},{10,18},{12,20},{14,22},{16,24},... | collective-permute-start | bytes 1572872 | tf_op jit(solution)/shard_map/ppermute | solution.py:252
  16.8 3.4 %collective-permute-done.5.refs_4_ = bf16[2,8,64,128]{3,2,1,0:T(8,128)(2,1)S(1)} collective-permute-done((bf16[2,8,64,128]{3,2,1,0:T(8,128)(2,1)S(1)}, bf16[2,8,64,128]{3,2,1,0:T(8,128)(2,1)S(1)}, u32[]{:S(2)}, u32[]{:S(2)}) %collective-permute-start.5) | collective-permute-done | bytes 262176 | tf_op jit(solution)/shard_map/ppermute | solution.py:252
  20.2 0.8 %collective-permute-done.4.refs_3_ = bf16[2,8,64,128]{3,2,1,0:T(8,128)(2,1)S(1)} collective-permute-done((bf16[2,8,64,128]{3,2,1,0:T(8,128)(2,1)S(1)}, bf16[2,8,64,128]{3,2,1,0:T(8,128)(2,1)S(1)}, u32[]{:S(2)}, u32[]{:S(2)}) %collective-permute-start.4) | collective-permute-done | bytes 262176 | tf_op jit(solution)/shard_map/ppermute | solution.py:252
  21.0 2.1 %collective-permute-start.7 = (bf16[2,2,8,64,128]{4,3,2,1,0:T(8,128)(2,1)S(1)}, bf16[2,2,8,64,128]{4,3,2,1,0:T(8,128)(2,1)S(1)}, u32[]{:S(2)}, u32[]{:S(2)}) collective-permute-start(bf16[2,2,8,64,128]{4,3,2,1,0:T(8,128)(2,1)S(1)} %late.1), channel_id=1, source_target_pairs={{0,8},{2,10},{4,12},{6,14},{8,16},{10,18},{12,20},{14,22},{16,24},... | collective-permute-start | bytes 1572872 | tf_op jit(solution)/shard_map/ppermute | solution.py:252
  23.2 0.0 copy-done
  23.2 0.0 copy-done.1
  23.2 3.4 %near.1 = (bf16[8,128,512]{2,1,0:T(8,128)(2,1)S(1)}, f32[2,128,512]{2,1,0:T(8,128)S(1)}, f32[8,1,512]{2,1,0:T(1,128)S(1)}, f32[8,1,512]{2,1,0:T(1,128)S(1)}, f32[8,128,512]{2,1,0:T(8,128)S(1)}) custom-call(s32[8]{0:T(128)S(1)} %copy-done.1, bf16[128,32,128]{2,1,0:T(8,128)(2,1)S(1)} %copy-done, ...), custom_call_target="tpu_custom_call" | custom-call | flops 671088640 | bytes 4194304 | tf_op jit(solution)/shard_map/near/pallas_call | solution.py:315
  26.5 1.9 %collective-permute-done.6.blocks = bf16[2,2,8,64,128]{4,3,2,1,0:T(8,128)(2,1)S(1)} collective-permute-done((bf16[2,2,8,64,128]{4,3,2,1,0:T(8,128)(2,1)S(1)}, bf16[2,2,8,64,128]{4,3,2,1,0:T(8,128)(2,1)S(1)}, u32[]{:S(2)}, u32[]{:S(2)}) %collective-permute-start.6) | collective-permute-done | bytes 524320 | tf_op jit(solution)/shard_map/ppermute | solution.py:252
  28.4 1.1 %middle.1 = (f32[8,1,512]{2,1,0:T(1,128)S(1)}, f32[8,1,512]{2,1,0:T(1,128)S(1)}, f32[8,128,512]{2,1,0:T(8,128)S(1)}) custom-call(bf16[8,128,512]{2,1,0:T(8,128)(2,1)S(1)} %get-tuple-element.25.folded, f32[2,128,512]{2,1,0:T(8,128)S(1)} %get-tuple-element.26.far_bias, f32[8,1,512]{2,1,0:T(1,128)S(1)} %get-tuple-element.27.peak, ...), custom_call_target="tpu_custom_call" | custom-call | flops 268435456 | bytes 4194304 | tf_op jit(solution)/shard_map/middle/pallas_call | solution.py:329
  29.5 6.1 %collective-permute-done.7.blocks = bf16[2,2,8,64,128]{4,3,2,1,0:T(8,128)(2,1)S(1)} collective-permute-done((bf16[2,2,8,64,128]{4,3,2,1,0:T(8,128)(2,1)S(1)}, bf16[2,2,8,64,128]{4,3,2,1,0:T(8,128)(2,1)S(1)}, u32[]{:S(2)}, u32[]{:S(2)}) %collective-permute-start.7) | collective-permute-done | bytes 524320 | tf_op jit(solution)/shard_map/ppermute | solution.py:252
  35.6 2.1 %finish.1 = bf16[64,64,128]{2,1,0:T(8,128)(2,1)} custom-call(bf16[8,128,512]{2,1,0:T(8,128)(2,1)S(1)} %get-tuple-element.25.folded, f32[2,128,512]{2,1,0:T(8,128)S(1)} %get-tuple-element.26.far_bias, f32[8,1,512]{2,1,0:T(1,128)S(1)} %get-tuple-element.30.peak, f32[8,1,512]{2,1,0:T(1,128)S(1)} %get-tuple-element.31.sums, ...), custom_call_target="tpu_custom_call" | custom-call | flops 268435456 | bytes 4194304 | tf_op jit(solution)/shard_map/finish/pallas_call | solution.py:338
  (4 shorter events, 0.1 us)
Async XLA Ops:
  1.1 1.9 %collective-permute-start = (bf16[2,4,64,128]{3,2,1,0:T(8,128)(2,1)S(1)}, bf16[2,4,64,128]{3,2,1,0:T(8,128)(2,1)S(1)}, u32[]{:S(2)}, u32[]{:S(2)}) collective-permute-start(bf16[2,4,64,128]{3,2,1,0:T(8,128)(2,1)S(1)} %give.1), channel_id=1, source_target_pairs={{0,1},{1,0},{2,3},{3,2},{4,5},{5,4},{6,7},{7,6},{8,9},{9,8},{10,11... | collective-permute-start | bytes 393224 | tf_op jit(solution)/shard_map/ppermute | solution.py:245
  3.0 20.1 %copy-start = (bf16[128,32,128]{2,1,0:T(8,128)(2,1)S(1)}, bf16[128,32,128]{2,1,0:T(8,128)(2,1)}, u32[]{:S(2)}) copy-start(bf16[128,32,128]{2,1,0:T(8,128)(2,1)} %queries.1) | copy-start | bytes 3145732
  3.0 20.1 %copy-start.1 = (s32[8]{0:T(128)S(1)}, s32[8]{0:T(128)}, u32[]{:S(2)}) copy-start(s32[8]{0:T(128)} %doc_lengths.1) | copy-start | bytes 100
  3.1 3.4 %collective-permute-start.1 = (bf16[64,32,128]{2,1,0:T(8,128)(2,1)S(1)}, bf16[64,32,128]{2,1,0:T(8,128)(2,1)S(1)}, u32[]{:S(2)}, u32[]{:S(2)}) collective-permute-start(bf16[64,32,128]{2,1,0:T(8,128)(2,1)S(1)} %get-tuple-element.22), channel_id=1, source_target_pairs={{0,1},{1,0},{2,3},{3,2},{4,5},{5,4},{6,7},{7,6},{8,9},{9,8},{10,11... | collective-permute-start | bytes 1572872 | tf_op jit(solution)/shard_map/ppermute | solution.py:245
  3.3 11.0 %collective-permute-start.2 = (bf16[2,8,64,128]{3,2,1,0:T(8,128)(2,1)S(1)}, bf16[2,8,64,128]{3,2,1,0:T(8,128)(2,1)S(1)}, u32[]{:S(2)}, u32[]{:S(2)}) collective-permute-start(bf16[2,8,64,128]{3,2,1,0:T(8,128)(2,1)S(1)} %pad_maximum_fusion.refs_0_), channel_id=1, source_target_pairs={{0,6},{2,4},{4,10},{6,8},{8,14},{10,12},{12,18},{14,16},{16,22},{1... | collective-permute-start | bytes 786440 | tf_op jit(solution)/shard_map/ppermute | solution.py:252
  6.5 8.2 %collective-permute-start.3 = (bf16[2,8,64,128]{3,2,1,0:T(8,128)(2,1)S(1)}, bf16[2,8,64,128]{3,2,1,0:T(8,128)(2,1)S(1)}, u32[]{:S(2)}, u32[]{:S(2)}) collective-permute-start(bf16[2,8,64,128]{3,2,1,0:T(8,128)(2,1)S(1)} %pad_maximum_fusion.refs_0_), channel_id=1, source_target_pairs={{0,8},{2,10},{4,12},{6,14},{8,16},{10,18},{12,20},{14,22},{16,24},... | collective-permute-start | bytes 786440 | tf_op jit(solution)/shard_map/ppermute | solution.py:252
  8.6 11.6 %collective-permute-start.5 = (bf16[2,8,64,128]{3,2,1,0:T(8,128)(2,1)S(1)}, bf16[2,8,64,128]{3,2,1,0:T(8,128)(2,1)S(1)}, u32[]{:S(2)}, u32[]{:S(2)}) collective-permute-start(bf16[2,8,64,128]{3,2,1,0:T(8,128)(2,1)S(1)} %pad_maximum_fusion.refs_0_), channel_id=1, source_target_pairs={{0,4},{2,6},{4,8},{6,10},{8,12},{10,14},{12,16},{14,18},{16,20},{1... | collective-permute-start | bytes 786440 | tf_op jit(solution)/shard_map/ppermute | solution.py:252
  10.5 10.5 %collective-permute-start.4 = (bf16[2,8,64,128]{3,2,1,0:T(8,128)(2,1)S(1)}, bf16[2,8,64,128]{3,2,1,0:T(8,128)(2,1)S(1)}, u32[]{:S(2)}, u32[]{:S(2)}) collective-permute-start(bf16[2,8,64,128]{3,2,1,0:T(8,128)(2,1)S(1)} %pad_maximum_fusion.refs_0_), channel_id=1, source_target_pairs={{0,2},{2,8},{4,6},{6,12},{8,10},{10,16},{12,14},{14,20},{16,18},{1... | collective-permute-start | bytes 786440 | tf_op jit(solution)/shard_map/ppermute | solution.py:252
  14.7 13.7 %collective-permute-start.6 = (bf16[2,2,8,64,128]{4,3,2,1,0:T(8,128)(2,1)S(1)}, bf16[2,2,8,64,128]{4,3,2,1,0:T(8,128)(2,1)S(1)}, u32[]{:S(2)}, u32[]{:S(2)}) collective-permute-start(bf16[2,2,8,64,128]{4,3,2,1,0:T(8,128)(2,1)S(1)} %early.1), channel_id=1, source_target_pairs={{0,8},{2,10},{4,12},{6,14},{8,16},{10,18},{12,20},{14,22},{16,24},... | collective-permute-start | bytes 1572872 | tf_op jit(solution)/shard_map/ppermute | solution.py:252
  21.0 14.6 %collective-permute-start.7 = (bf16[2,2,8,64,128]{4,3,2,1,0:T(8,128)(2,1)S(1)}, bf16[2,2,8,64,128]{4,3,2,1,0:T(8,128)(2,1)S(1)}, u32[]{:S(2)}, u32[]{:S(2)}) collective-permute-start(bf16[2,2,8,64,128]{4,3,2,1,0:T(8,128)(2,1)S(1)} %late.1), channel_id=1, source_target_pairs={{0,8},{2,10},{4,12},{6,14},{8,16},{10,18},{12,20},{14,22},{16,24},... | collective-permute-start | bytes 1572872 | tf_op jit(solution)/shard_map/ppermute | solution.py:252

commit v16 on v12

--- a/solution.py
+++ b/solution.py
@@ -68,8 +68,8 @@
     ]
     if kept:
         copies.append(pltpu.make_async_copy(queries.at[given_rows], given_queries, sems.at[2]))
-    for copy in copies:
-        copy.start()
+    for number, copy in enumerate(copies):
+        copy.start(priority=number % 2)
     for kind in range(2):
         copies[kind].wait()
         out[kind] = jnp.swapaxes(staged[kind].astype(jnp.float32), 0, 1).astype(out.dtype)
@@ -209,7 +209,7 @@
         copy = pltpu.make_async_copy(
             staged.at[pair], out.at[:, pl.ds(first, 2 * group)], sems.at[pair]
         )
-        copy.start()
+        copy.start(priority=pair % 2)
         copies.append(copy)
 
     waiting = None

time: 37.9 us -> 37.8 us (level)
  no operation moved by 1% of the time
where the time goes in v16:
time: 37.8 us; the launch traced here: 37.5 us
  starting transfers between devices  15.5 us (41%)
  waiting for transfers between devices  13 us (34%)
  Pallas kernels  8.74 us (23%)
    ppermute x6, starting transfers between devices, upwards(): return lax.ppermute(array, ('ctx', 'head'), pairs)  14.5 us
    ppermute x6, waiting for transfers between devices, upwards(): return lax.ppermute(array, ('ctx', 'head'), pairs)  13 us
    pallas_call x1, Pallas kernels, shards(): pl.pallas_call(functools.partial(near_kernel, devices=devices, group=grou...  3.35 us
    pallas_call x1, Pallas kernels, shards(): pl.pallas_call(functools.partial(far_kernel, number=1), out_shape=jax.Sha...  2.14 us
    pallas_call x2, Pallas kernels, pack(): pl.pallas_call(functools.partial(pack_kernel, kept=kept), out_shape=out_s...  2.04 us
    pallas_call x1, Pallas kernels, shards(): pl.pallas_call(functools.partial(far_kernel, number=0), out_shape=state,...  1.14 us
    ppermute x2, starting transfers between devices, swap(): return lax.ppermute(array, 'head', [(0, 1), (1, 0)])  1 us
  transfers between devices with their start and end apart: 8, of which 6 were waited for; matrix products, arithmetic and copies ran while one was open for 0% of the time, Pallas kernels for 15%

profile of v16, /device:TPU:19, one launch (start us, length us, event | category | flops | bytes accessed | tf_op | source)
XLA Modules:
  0.0 37.5 jit_solution(18374872661253138899)
XLA Ops:
  0.0 0.9 %give.1 = bf16[2,4,64,128]{3,2,1,0:T(8,128)(2,1)S(1)} custom-call(bf16[128,4,128]{2,1,0:T(4,128)(2,1)} %refs_0_.3, bf16[128,4,128]{2,1,0:T(4,128)(2,1)} %refs_1_.3), custom_call_target="tpu_custom_call" | custom-call | bytes 2097152 | tf_op jit(solution)/shard_map/give/pallas_call | solution.py:260
  0.9 0.7 %collective-permute-start = (bf16[2,4,64,128]{3,2,1,0:T(8,128)(2,1)S(1)}, bf16[2,4,64,128]{3,2,1,0:T(8,128)(2,1)S(1)}, u32[]{:S(2)}, u32[]{:S(2)}) collective-permute-start(bf16[2,4,64,128]{3,2,1,0:T(8,128)(2,1)S(1)} %give.1), channel_id=1, source_target_pairs={{0,1},{1,0},{2,3},{3,2},{4,5},{5,4},{6,7},{7,6},{8,9},{9,8},{10,11... | collective-permute-start | bytes 393224 | tf_op jit(solution)/shard_map/ppermute | solution.py:244
  1.7 1.1 %keep.1 = (bf16[2,4,64,128]{3,2,1,0:T(8,128)(2,1)S(1)}, bf16[64,32,128]{2,1,0:T(8,128)(2,1)S(1)}) custom-call(bf16[128,4,128]{2,1,0:T(4,128)(2,1)} %refs_0_.3, bf16[128,4,128]{2,1,0:T(4,128)(2,1)} %refs_1_.3, bf16[128,32,128]{2,1,0:T(8,128)(2,1)} %queries.1), custom_call_target="tpu_custom_call" | custom-call | bytes 3145728 | tf_op jit(solution)/shard_map/keep/pallas_call | solution.py:260
  2.8 0.0 collective-permute-done
  2.8 0.0 copy-start
  2.8 0.0 copy-start.1
  2.9 0.3 collective-permute-start.1
  3.2 3.0 %collective-permute-start.2 = (bf16[2,8,64,128]{3,2,1,0:T(8,128)(2,1)S(1)}, bf16[2,8,64,128]{3,2,1,0:T(8,128)(2,1)S(1)}, u32[]{:S(2)}, u32[]{:S(2)}) collective-permute-start(bf16[2,8,64,128]{3,2,1,0:T(8,128)(2,1)S(1)} %pad_maximum_fusion.refs_0_), channel_id=1, source_target_pairs={{0,6},{2,4},{4,10},{6,8},{8,14},{10,12},{12,18},{14,16},{16,22},{1... | collective-permute-start | bytes 786440 | tf_op jit(solution)/shard_map/ppermute | solution.py:251
  6.2 0.0 collective-permute-done.1.partner_queries
  6.2 2.1 %collective-permute-start.3 = (bf16[2,8,64,128]{3,2,1,0:T(8,128)(2,1)S(1)}, bf16[2,8,64,128]{3,2,1,0:T(8,128)(2,1)S(1)}, u32[]{:S(2)}, u32[]{:S(2)}) collective-permute-start(bf16[2,8,64,128]{3,2,1,0:T(8,128)(2,1)S(1)} %pad_maximum_fusion.refs_0_), channel_id=1, source_target_pairs={{0,8},{2,10},{4,12},{6,14},{8,16},{10,18},{12,20},{14,22},{16,24},... | collective-permute-start | bytes 786440 | tf_op jit(solution)/shard_map/ppermute | solution.py:251
  8.3 2.0 %collective-permute-start.5 = (bf16[2,8,64,128]{3,2,1,0:T(8,128)(2,1)S(1)}, bf16[2,8,64,128]{3,2,1,0:T(8,128)(2,1)S(1)}, u32[]{:S(2)}, u32[]{:S(2)}) collective-permute-start(bf16[2,8,64,128]{3,2,1,0:T(8,128)(2,1)S(1)} %pad_maximum_fusion.refs_0_), channel_id=1, source_target_pairs={{0,4},{2,6},{4,8},{6,10},{8,12},{10,14},{12,16},{14,18},{16,20},{1... | collective-permute-start | bytes 786440 | tf_op jit(solution)/shard_map/ppermute | solution.py:251
  10.2 3.3 %collective-permute-start.4 = (bf16[2,8,64,128]{3,2,1,0:T(8,128)(2,1)S(1)}, bf16[2,8,64,128]{3,2,1,0:T(8,128)(2,1)S(1)}, u32[]{:S(2)}, u32[]{:S(2)}) collective-permute-start(bf16[2,8,64,128]{3,2,1,0:T(8,128)(2,1)S(1)} %pad_maximum_fusion.refs_0_), channel_id=1, source_target_pairs={{0,2},{2,8},{4,6},{6,12},{8,10},{10,16},{12,14},{14,20},{16,18},{1... | collective-permute-start | bytes 786440 | tf_op jit(solution)/shard_map/ppermute | solution.py:251
  13.5 0.5 %collective-permute-done.2.refs_1_ = bf16[2,8,64,128]{3,2,1,0:T(8,128)(2,1)S(1)} collective-permute-done((bf16[2,8,64,128]{3,2,1,0:T(8,128)(2,1)S(1)}, bf16[2,8,64,128]{3,2,1,0:T(8,128)(2,1)S(1)}, u32[]{:S(2)}, u32[]{:S(2)}) %collective-permute-start.2) | collective-permute-done | bytes 262176 | tf_op jit(solution)/shard_map/ppermute | solution.py:251
  14.1 0.3 collective-permute-done.3.refs_2_
  14.4 2.1 %collective-permute-start.6 = (bf16[2,2,8,64,128]{4,3,2,1,0:T(8,128)(2,1)S(1)}, bf16[2,2,8,64,128]{4,3,2,1,0:T(8,128)(2,1)S(1)}, u32[]{:S(2)}, u32[]{:S(2)}) collective-permute-start(bf16[2,2,8,64,128]{4,3,2,1,0:T(8,128)(2,1)S(1)} %early.1), channel_id=1, source_target_pairs={{0,8},{2,10},{4,12},{6,14},{8,16},{10,18},{12,20},{14,22},{16,24},... | collective-permute-start | bytes 1572872 | tf_op jit(solution)/shard_map/ppermute | solution.py:251
  16.5 3.4 %collective-permute-done.5.refs_4_ = bf16[2,8,64,128]{3,2,1,0:T(8,128)(2,1)S(1)} collective-permute-done((bf16[2,8,64,128]{3,2,1,0:T(8,128)(2,1)S(1)}, bf16[2,8,64,128]{3,2,1,0:T(8,128)(2,1)S(1)}, u32[]{:S(2)}, u32[]{:S(2)}) %collective-permute-start.5) | collective-permute-done | bytes 262176 | tf_op jit(solution)/shard_map/ppermute | solution.py:251
  19.9 0.8 %collective-permute-done.4.refs_3_ = bf16[2,8,64,128]{3,2,1,0:T(8,128)(2,1)S(1)} collective-permute-done((bf16[2,8,64,128]{3,2,1,0:T(8,128)(2,1)S(1)}, bf16[2,8,64,128]{3,2,1,0:T(8,128)(2,1)S(1)}, u32[]{:S(2)}, u32[]{:S(2)}) %collective-permute-start.4) | collective-permute-done | bytes 262176 | tf_op jit(solution)/shard_map/ppermute | solution.py:251
  20.7 2.1 %collective-permute-start.7 = (bf16[2,2,8,64,128]{4,3,2,1,0:T(8,128)(2,1)S(1)}, bf16[2,2,8,64,128]{4,3,2,1,0:T(8,128)(2,1)S(1)}, u32[]{:S(2)}, u32[]{:S(2)}) collective-permute-start(bf16[2,2,8,64,128]{4,3,2,1,0:T(8,128)(2,1)S(1)} %late.1), channel_id=1, source_target_pairs={{0,8},{2,10},{4,12},{6,14},{8,16},{10,18},{12,20},{14,22},{16,24},... | collective-permute-start | bytes 1572872 | tf_op jit(solution)/shard_map/ppermute | solution.py:251
  22.8 0.0 copy-done
  22.9 0.0 copy-done.1
  22.9 3.4 %near.1 = (bf16[8,128,512]{2,1,0:T(8,128)(2,1)S(1)}, f32[2,128,512]{2,1,0:T(8,128)S(1)}, f32[8,1,512]{2,1,0:T(1,128)S(1)}, f32[8,1,512]{2,1,0:T(1,128)S(1)}, f32[8,128,512]{2,1,0:T(8,128)S(1)}) custom-call(s32[8]{0:T(128)S(1)} %copy-done.1, bf16[128,32,128]{2,1,0:T(8,128)(2,1)S(1)} %copy-done, ...), custom_call_target="tpu_custom_call" | custom-call | flops 671088640 | bytes 4194304 | tf_op jit(solution)/shard_map/near/pallas_call | solution.py:314
  26.2 1.9 %collective-permute-done.6.blocks = bf16[2,2,8,64,128]{4,3,2,1,0:T(8,128)(2,1)S(1)} collective-permute-done((bf16[2,2,8,64,128]{4,3,2,1,0:T(8,128)(2,1)S(1)}, bf16[2,2,8,64,128]{4,3,2,1,0:T(8,128)(2,1)S(1)}, u32[]{:S(2)}, u32[]{:S(2)}) %collective-permute-start.6) | collective-permute-done | bytes 524320 | tf_op jit(solution)/shard_map/ppermute | solution.py:251
  28.1 1.1 %middle.1 = (f32[8,1,512]{2,1,0:T(1,128)S(1)}, f32[8,1,512]{2,1,0:T(1,128)S(1)}, f32[8,128,512]{2,1,0:T(8,128)S(1)}) custom-call(bf16[8,128,512]{2,1,0:T(8,128)(2,1)S(1)} %get-tuple-element.25.folded, f32[2,128,512]{2,1,0:T(8,128)S(1)} %get-tuple-element.26.far_bias, f32[8,1,512]{2,1,0:T(1,128)S(1)} %get-tuple-element.27.peak, ...), custom_call_target="tpu_custom_call" | custom-call | flops 268435456 | bytes 4194304 | tf_op jit(solution)/shard_map/middle/pallas_call | solution.py:328
  29.2 6.1 %collective-permute-done.7.blocks = bf16[2,2,8,64,128]{4,3,2,1,0:T(8,128)(2,1)S(1)} collective-permute-done((bf16[2,2,8,64,128]{4,3,2,1,0:T(8,128)(2,1)S(1)}, bf16[2,2,8,64,128]{4,3,2,1,0:T(8,128)(2,1)S(1)}, u32[]{:S(2)}, u32[]{:S(2)}) %collective-permute-start.7) | collective-permute-done | bytes 524320 | tf_op jit(solution)/shard_map/ppermute | solution.py:251
  35.3 2.1 %finish.1 = bf16[64,64,128]{2,1,0:T(8,128)(2,1)} custom-call(bf16[8,128,512]{2,1,0:T(8,128)(2,1)S(1)} %get-tuple-element.25.folded, f32[2,128,512]{2,1,0:T(8,128)S(1)} %get-tuple-element.26.far_bias, f32[8,1,512]{2,1,0:T(1,128)S(1)} %get-tuple-element.30.peak, f32[8,1,512]{2,1,0:T(1,128)S(1)} %get-tuple-element.31.sums, ...), custom_call_target="tpu_custom_call" | custom-call | flops 268435456 | bytes 4194304 | tf_op jit(solution)/shard_map/finish/pallas_call | solution.py:337
  (4 shorter events, 0.1 us)
Async XLA Ops:
  0.9 1.9 %collective-permute-start = (bf16[2,4,64,128]{3,2,1,0:T(8,128)(2,1)S(1)}, bf16[2,4,64,128]{3,2,1,0:T(8,128)(2,1)S(1)}, u32[]{:S(2)}, u32[]{:S(2)}) collective-permute-start(bf16[2,4,64,128]{3,2,1,0:T(8,128)(2,1)S(1)} %give.1), channel_id=1, source_target_pairs={{0,1},{1,0},{2,3},{3,2},{4,5},{5,4},{6,7},{7,6},{8,9},{9,8},{10,11... | collective-permute-start | bytes 393224 | tf_op jit(solution)/shard_map/ppermute | solution.py:244
  2.8 20.0 %copy-start = (bf16[128,32,128]{2,1,0:T(8,128)(2,1)S(1)}, bf16[128,32,128]{2,1,0:T(8,128)(2,1)}, u32[]{:S(2)}) copy-start(bf16[128,32,128]{2,1,0:T(8,128)(2,1)} %queries.1) | copy-start | bytes 3145732
  2.8 20.0 %copy-start.1 = (s32[8]{0:T(128)S(1)}, s32[8]{0:T(128)}, u32[]{:S(2)}) copy-start(s32[8]{0:T(128)} %doc_lengths.1) | copy-start | bytes 100
  2.9 3.3 %collective-permute-start.1 = (bf16[64,32,128]{2,1,0:T(8,128)(2,1)S(1)}, bf16[64,32,128]{2,1,0:T(8,128)(2,1)S(1)}, u32[]{:S(2)}, u32[]{:S(2)}) collective-permute-start(bf16[64,32,128]{2,1,0:T(8,128)(2,1)S(1)} %get-tuple-element.22), channel_id=1, source_target_pairs={{0,1},{1,0},{2,3},{3,2},{4,5},{5,4},{6,7},{7,6},{8,9},{9,8},{10,11... | collective-permute-start | bytes 1572872 | tf_op jit(solution)/shard_map/ppermute | solution.py:244
  3.2 10.9 %collective-permute-start.2 = (bf16[2,8,64,128]{3,2,1,0:T(8,128)(2,1)S(1)}, bf16[2,8,64,128]{3,2,1,0:T(8,128)(2,1)S(1)}, u32[]{:S(2)}, u32[]{:S(2)}) collective-permute-start(bf16[2,8,64,128]{3,2,1,0:T(8,128)(2,1)S(1)} %pad_maximum_fusion.refs_0_), channel_id=1, source_target_pairs={{0,6},{2,4},{4,10},{6,8},{8,14},{10,12},{12,18},{14,16},{16,22},{1... | collective-permute-start | bytes 786440 | tf_op jit(solution)/shard_map/ppermute | solution.py:251
  6.2 8.2 %collective-permute-start.3 = (bf16[2,8,64,128]{3,2,1,0:T(8,128)(2,1)S(1)}, bf16[2,8,64,128]{3,2,1,0:T(8,128)(2,1)S(1)}, u32[]{:S(2)}, u32[]{:S(2)}) collective-permute-start(bf16[2,8,64,128]{3,2,1,0:T(8,128)(2,1)S(1)} %pad_maximum_fusion.refs_0_), channel_id=1, source_target_pairs={{0,8},{2,10},{4,12},{6,14},{8,16},{10,18},{12,20},{14,22},{16,24},... | collective-permute-start | bytes 786440 | tf_op jit(solution)/shard_map/ppermute | solution.py:251
  8.3 11.6 %collective-permute-start.5 = (bf16[2,8,64,128]{3,2,1,0:T(8,128)(2,1)S(1)}, bf16[2,8,64,128]{3,2,1,0:T(8,128)(2,1)S(1)}, u32[]{:S(2)}, u32[]{:S(2)}) collective-permute-start(bf16[2,8,64,128]{3,2,1,0:T(8,128)(2,1)S(1)} %pad_maximum_fusion.refs_0_), channel_id=1, source_target_pairs={{0,4},{2,6},{4,8},{6,10},{8,12},{10,14},{12,16},{14,18},{16,20},{1... | collective-permute-start | bytes 786440 | tf_op jit(solution)/shard_map/ppermute | solution.py:251
  10.2 10.5 %collective-permute-start.4 = (bf16[2,8,64,128]{3,2,1,0:T(8,128)(2,1)S(1)}, bf16[2,8,64,128]{3,2,1,0:T(8,128)(2,1)S(1)}, u32[]{:S(2)}, u32[]{:S(2)}) collective-permute-start(bf16[2,8,64,128]{3,2,1,0:T(8,128)(2,1)S(1)} %pad_maximum_fusion.refs_0_), channel_id=1, source_target_pairs={{0,2},{2,8},{4,6},{6,12},{8,10},{10,16},{12,14},{14,20},{16,18},{1... | collective-permute-start | bytes 786440 | tf_op jit(solution)/shard_map/ppermute | solution.py:251
  14.4 13.7 %collective-permute-start.6 = (bf16[2,2,8,64,128]{4,3,2,1,0:T(8,128)(2,1)S(1)}, bf16[2,2,8,64,128]{4,3,2,1,0:T(8,128)(2,1)S(1)}, u32[]{:S(2)}, u32[]{:S(2)}) collective-permute-start(bf16[2,2,8,64,128]{4,3,2,1,0:T(8,128)(2,1)S(1)} %early.1), channel_id=1, source_target_pairs={{0,8},{2,10},{4,12},{6,14},{8,16},{10,18},{12,20},{14,22},{16,24},... | collective-permute-start | bytes 1572872 | tf_op jit(solution)/shard_map/ppermute | solution.py:251
  20.7 14.6 %collective-permute-start.7 = (bf16[2,2,8,64,128]{4,3,2,1,0:T(8,128)(2,1)S(1)}, bf16[2,2,8,64,128]{4,3,2,1,0:T(8,128)(2,1)S(1)}, u32[]{:S(2)}, u32[]{:S(2)}) collective-permute-start(bf16[2,2,8,64,128]{4,3,2,1,0:T(8,128)(2,1)S(1)} %late.1), channel_id=1, source_target_pairs={{0,8},{2,10},{4,12},{6,14},{8,16},{10,18},{12,20},{14,22},{16,24},... | collective-permute-start | bytes 1572872 | tf_op jit(solution)/shard_map/ppermute | solution.py:251

commit v17 on v12

--- a/solution.py
+++ b/solution.py
@@ -276,10 +276,10 @@
     (given,) = pack(False)
     given = swap(given)
     keep, given_queries = pack(True)
+    given, given_queries = lax.optimization_barrier((given, given_queries))
     own = jnp.concatenate(
         [jnp.where(core == 0, keep, given), jnp.where(core == 0, given, keep)], axis=1
     )
-    own, given_queries = lax.optimization_barrier((own, given_queries))
     partner_queries = swap(given_queries)
     first = upwards(own, STEPS[0])
     own, partner_queries = lax.optimization_barrier((own, partner_queries))

time: 37.9 us -> 37.8 us (level)
  no operation moved by 1% of the time
where the time goes in v17:
time: 37.8 us; the launch traced here: 37.5 us
  starting transfers between devices  15.6 us (41%)
  waiting for transfers between devices  13 us (34%)
  Pallas kernels  8.74 us (23%)
    ppermute x6, starting transfers between devices, upwards(): return lax.ppermute(array, ('ctx', 'head'), pairs)  14.6 us
    ppermute x6, waiting for transfers between devices, upwards(): return lax.ppermute(array, ('ctx', 'head'), pairs)  13 us
    pallas_call x1, Pallas kernels, shards(): pl.pallas_call(functools.partial(near_kernel, devices=devices, group=grou...  3.34 us
    pallas_call x1, Pallas kernels, shards(): pl.pallas_call(functools.partial(far_kernel, number=1), out_shape=jax.Sha...  2.13 us
    pallas_call x2, Pallas kernels, pack(): pl.pallas_call(functools.partial(pack_kernel, kept=kept), out_shape=out_s...  2.07 us
    pallas_call x1, Pallas kernels, shards(): pl.pallas_call(functools.partial(far_kernel, number=0), out_shape=state,...  1.13 us
    ppermute x2, starting transfers between devices, swap(): return lax.ppermute(array, 'head', [(0, 1), (1, 0)])  0.93 us
  transfers between devices with their start and end apart: 8, of which 6 were waited for; matrix products, arithmetic and copies ran while one was open for 0% of the time, Pallas kernels for 15%

profile of v17, /device:TPU:19, one launch (start us, length us, event | category | flops | bytes accessed | tf_op | source)
XLA Modules:
  0.0 37.5 jit_solution(17920214823356959224)
XLA Ops:
  0.0 0.9 %give.1 = bf16[2,4,64,128]{3,2,1,0:T(8,128)(2,1)S(1)} custom-call(bf16[128,4,128]{2,1,0:T(4,128)(2,1)} %refs_0_.3, bf16[128,4,128]{2,1,0:T(4,128)(2,1)} %refs_1_.3), custom_call_target="tpu_custom_call" | custom-call | bytes 2097152 | tf_op jit(solution)/shard_map/give/pallas_call | solution.py:260
  0.9 0.7 %collective-permute-start = (bf16[2,4,64,128]{3,2,1,0:T(8,128)(2,1)S(1)}, bf16[2,4,64,128]{3,2,1,0:T(8,128)(2,1)S(1)}, u32[]{:S(2)}, u32[]{:S(2)}) collective-permute-start(bf16[2,4,64,128]{3,2,1,0:T(8,128)(2,1)S(1)} %give.1), channel_id=1, source_target_pairs={{0,1},{1,0},{2,3},{3,2},{4,5},{5,4},{6,7},{7,6},{8,9},{9,8},{10,11... | collective-permute-start | bytes 393224 | tf_op jit(solution)/shard_map/ppermute | solution.py:244
  1.7 1.1 %keep.1 = (bf16[2,4,64,128]{3,2,1,0:T(8,128)(2,1)S(1)}, bf16[64,32,128]{2,1,0:T(8,128)(2,1)S(1)}) custom-call(bf16[128,4,128]{2,1,0:T(4,128)(2,1)} %refs_0_.3, bf16[128,4,128]{2,1,0:T(4,128)(2,1)} %refs_1_.3, bf16[128,32,128]{2,1,0:T(8,128)(2,1)} %queries.1), custom_call_target="tpu_custom_call" | custom-call | bytes 3145728 | tf_op jit(solution)/shard_map/keep/pallas_call | solution.py:260
  2.8 0.0 collective-permute-done
  2.8 0.2 collective-permute-start.1
  3.0 0.0 copy-start
  3.0 0.0 copy-start.1
  3.1 3.1 %collective-permute-start.2 = (bf16[2,8,64,128]{3,2,1,0:T(8,128)(2,1)S(1)}, bf16[2,8,64,128]{3,2,1,0:T(8,128)(2,1)S(1)}, u32[]{:S(2)}, u32[]{:S(2)}) collective-permute-start(bf16[2,8,64,128]{3,2,1,0:T(8,128)(2,1)S(1)} %pad_maximum_fusion.refs_0_), channel_id=1, source_target_pairs={{0,6},{2,4},{4,10},{6,8},{8,14},{10,12},{12,18},{14,16},{16,22},{1... | collective-permute-start | bytes 786440 | tf_op jit(solution)/shard_map/ppermute | solution.py:251
  6.2 0.0 collective-permute-done.1.partner_queries
  6.2 2.1 %collective-permute-start.3 = (bf16[2,8,64,128]{3,2,1,0:T(8,128)(2,1)S(1)}, bf16[2,8,64,128]{3,2,1,0:T(8,128)(2,1)S(1)}, u32[]{:S(2)}, u32[]{:S(2)}) collective-permute-start(bf16[2,8,64,128]{3,2,1,0:T(8,128)(2,1)S(1)} %pad_maximum_fusion.refs_0_), channel_id=1, source_target_pairs={{0,8},{2,10},{4,12},{6,14},{8,16},{10,18},{12,20},{14,22},{16,24},... | collective-permute-start | bytes 786440 | tf_op jit(solution)/shard_map/ppermute | solution.py:251
  8.3 2.0 %collective-permute-start.5 = (bf16[2,8,64,128]{3,2,1,0:T(8,128)(2,1)S(1)}, bf16[2,8,64,128]{3,2,1,0:T(8,128)(2,1)S(1)}, u32[]{:S(2)}, u32[]{:S(2)}) collective-permute-start(bf16[2,8,64,128]{3,2,1,0:T(8,128)(2,1)S(1)} %pad_maximum_fusion.refs_0_), channel_id=1, source_target_pairs={{0,4},{2,6},{4,8},{6,10},{8,12},{10,14},{12,16},{14,18},{16,20},{1... | collective-permute-start | bytes 786440 | tf_op jit(solution)/shard_map/ppermute | solution.py:251
  10.3 3.3 %collective-permute-start.4 = (bf16[2,8,64,128]{3,2,1,0:T(8,128)(2,1)S(1)}, bf16[2,8,64,128]{3,2,1,0:T(8,128)(2,1)S(1)}, u32[]{:S(2)}, u32[]{:S(2)}) collective-permute-start(bf16[2,8,64,128]{3,2,1,0:T(8,128)(2,1)S(1)} %pad_maximum_fusion.refs_0_), channel_id=1, source_target_pairs={{0,2},{2,8},{4,6},{6,12},{8,10},{10,16},{12,14},{14,20},{16,18},{1... | collective-permute-start | bytes 786440 | tf_op jit(solution)/shard_map/ppermute | solution.py:251
  13.6 0.5 %collective-permute-done.2.refs_1_ = bf16[2,8,64,128]{3,2,1,0:T(8,128)(2,1)S(1)} collective-permute-done((bf16[2,8,64,128]{3,2,1,0:T(8,128)(2,1)S(1)}, bf16[2,8,64,128]{3,2,1,0:T(8,128)(2,1)S(1)}, u32[]{:S(2)}, u32[]{:S(2)}) %collective-permute-start.2) | collective-permute-done | bytes 262176 | tf_op jit(solution)/shard_map/ppermute | solution.py:251
  14.2 0.3 collective-permute-done.3.refs_2_
  14.5 2.1 %collective-permute-start.6 = (bf16[2,2,8,64,128]{4,3,2,1,0:T(8,128)(2,1)S(1)}, bf16[2,2,8,64,128]{4,3,2,1,0:T(8,128)(2,1)S(1)}, u32[]{:S(2)}, u32[]{:S(2)}) collective-permute-start(bf16[2,2,8,64,128]{4,3,2,1,0:T(8,128)(2,1)S(1)} %early.1), channel_id=1, source_target_pairs={{0,8},{2,10},{4,12},{6,14},{8,16},{10,18},{12,20},{14,22},{16,24},... | collective-permute-start | bytes 1572872 | tf_op jit(solution)/shard_map/ppermute | solution.py:251
  16.5 3.4 %collective-permute-done.5.refs_4_ = bf16[2,8,64,128]{3,2,1,0:T(8,128)(2,1)S(1)} collective-permute-done((bf16[2,8,64,128]{3,2,1,0:T(8,128)(2,1)S(1)}, bf16[2,8,64,128]{3,2,1,0:T(8,128)(2,1)S(1)}, u32[]{:S(2)}, u32[]{:S(2)}) %collective-permute-start.5) | collective-permute-done | bytes 262176 | tf_op jit(solution)/shard_map/ppermute | solution.py:251
  20.0 0.8 %collective-permute-done.4.refs_3_ = bf16[2,8,64,128]{3,2,1,0:T(8,128)(2,1)S(1)} collective-permute-done((bf16[2,8,64,128]{3,2,1,0:T(8,128)(2,1)S(1)}, bf16[2,8,64,128]{3,2,1,0:T(8,128)(2,1)S(1)}, u32[]{:S(2)}, u32[]{:S(2)}) %collective-permute-start.4) | collective-permute-done | bytes 262176 | tf_op jit(solution)/shard_map/ppermute | solution.py:251
  20.8 2.1 %collective-permute-start.7 = (bf16[2,2,8,64,128]{4,3,2,1,0:T(8,128)(2,1)S(1)}, bf16[2,2,8,64,128]{4,3,2,1,0:T(8,128)(2,1)S(1)}, u32[]{:S(2)}, u32[]{:S(2)}) collective-permute-start(bf16[2,2,8,64,128]{4,3,2,1,0:T(8,128)(2,1)S(1)} %late.1), channel_id=1, source_target_pairs={{0,8},{2,10},{4,12},{6,14},{8,16},{10,18},{12,20},{14,22},{16,24},... | collective-permute-start | bytes 1572872 | tf_op jit(solution)/shard_map/ppermute | solution.py:251
  22.9 0.0 copy-done
  22.9 0.0 copy-done.1
  22.9 3.3 %near.1 = (bf16[8,128,512]{2,1,0:T(8,128)(2,1)S(1)}, f32[2,128,512]{2,1,0:T(8,128)S(1)}, f32[8,1,512]{2,1,0:T(1,128)S(1)}, f32[8,1,512]{2,1,0:T(1,128)S(1)}, f32[8,128,512]{2,1,0:T(8,128)S(1)}) custom-call(s32[8]{0:T(128)S(1)} %copy-done.1, bf16[128,32,128]{2,1,0:T(8,128)(2,1)S(1)} %copy-done, ...), custom_call_target="tpu_custom_call" | custom-call | flops 671088640 | bytes 4194304 | tf_op jit(solution)/shard_map/near/pallas_call | solution.py:314
  26.3 1.9 %collective-permute-done.6.blocks = bf16[2,2,8,64,128]{4,3,2,1,0:T(8,128)(2,1)S(1)} collective-permute-done((bf16[2,2,8,64,128]{4,3,2,1,0:T(8,128)(2,1)S(1)}, bf16[2,2,8,64,128]{4,3,2,1,0:T(8,128)(2,1)S(1)}, u32[]{:S(2)}, u32[]{:S(2)}) %collective-permute-start.6) | collective-permute-done | bytes 524320 | tf_op jit(solution)/shard_map/ppermute | solution.py:251
  28.2 1.1 %middle.1 = (f32[8,1,512]{2,1,0:T(1,128)S(1)}, f32[8,1,512]{2,1,0:T(1,128)S(1)}, f32[8,128,512]{2,1,0:T(8,128)S(1)}) custom-call(bf16[8,128,512]{2,1,0:T(8,128)(2,1)S(1)} %get-tuple-element.25.folded, f32[2,128,512]{2,1,0:T(8,128)S(1)} %get-tuple-element.26.far_bias, f32[8,1,512]{2,1,0:T(1,128)S(1)} %get-tuple-element.27.peak, ...), custom_call_target="tpu_custom_call" | custom-call | flops 268435456 | bytes 4194304 | tf_op jit(solution)/shard_map/middle/pallas_call | solution.py:328
  29.3 6.1 %collective-permute-done.7.blocks = bf16[2,2,8,64,128]{4,3,2,1,0:T(8,128)(2,1)S(1)} collective-permute-done((bf16[2,2,8,64,128]{4,3,2,1,0:T(8,128)(2,1)S(1)}, bf16[2,2,8,64,128]{4,3,2,1,0:T(8,128)(2,1)S(1)}, u32[]{:S(2)}, u32[]{:S(2)}) %collective-permute-start.7) | collective-permute-done | bytes 524320 | tf_op jit(solution)/shard_map/ppermute | solution.py:251
  35.4 2.1 %finish.1 = bf16[64,64,128]{2,1,0:T(8,128)(2,1)} custom-call(bf16[8,128,512]{2,1,0:T(8,128)(2,1)S(1)} %get-tuple-element.25.folded, f32[2,128,512]{2,1,0:T(8,128)S(1)} %get-tuple-element.26.far_bias, f32[8,1,512]{2,1,0:T(1,128)S(1)} %get-tuple-element.30.peak, f32[8,1,512]{2,1,0:T(1,128)S(1)} %get-tuple-element.31.sums, ...), custom_call_target="tpu_custom_call" | custom-call | flops 268435456 | bytes 4194304 | tf_op jit(solution)/shard_map/finish/pallas_call | solution.py:337
  (4 shorter events, 0.1 us)
Async XLA Ops:
  0.9 1.9 %collective-permute-start = (bf16[2,4,64,128]{3,2,1,0:T(8,128)(2,1)S(1)}, bf16[2,4,64,128]{3,2,1,0:T(8,128)(2,1)S(1)}, u32[]{:S(2)}, u32[]{:S(2)}) collective-permute-start(bf16[2,4,64,128]{3,2,1,0:T(8,128)(2,1)S(1)} %give.1), channel_id=1, source_target_pairs={{0,1},{1,0},{2,3},{3,2},{4,5},{5,4},{6,7},{7,6},{8,9},{9,8},{10,11... | collective-permute-start | bytes 393224 | tf_op jit(solution)/shard_map/ppermute | solution.py:244
  2.8 3.4 %collective-permute-start.1 = (bf16[64,32,128]{2,1,0:T(8,128)(2,1)S(1)}, bf16[64,32,128]{2,1,0:T(8,128)(2,1)S(1)}, u32[]{:S(2)}, u32[]{:S(2)}) collective-permute-start(bf16[64,32,128]{2,1,0:T(8,128)(2,1)S(1)} %get-tuple-element.22), channel_id=1, source_target_pairs={{0,1},{1,0},{2,3},{3,2},{4,5},{5,4},{6,7},{7,6},{8,9},{9,8},{10,11... | collective-permute-start | bytes 1572872 | tf_op jit(solution)/shard_map/ppermute | solution.py:244
  3.0 19.9 %copy-start = (bf16[128,32,128]{2,1,0:T(8,128)(2,1)S(1)}, bf16[128,32,128]{2,1,0:T(8,128)(2,1)}, u32[]{:S(2)}) copy-start(bf16[128,32,128]{2,1,0:T(8,128)(2,1)} %queries.1) | copy-start | bytes 3145732
  3.0 19.9 %copy-start.1 = (s32[8]{0:T(128)S(1)}, s32[8]{0:T(128)}, u32[]{:S(2)}) copy-start(s32[8]{0:T(128)} %doc_lengths.1) | copy-start | bytes 100
  3.1 11.1 %collective-permute-start.2 = (bf16[2,8,64,128]{3,2,1,0:T(8,128)(2,1)S(1)}, bf16[2,8,64,128]{3,2,1,0:T(8,128)(2,1)S(1)}, u32[]{:S(2)}, u32[]{:S(2)}) collective-permute-start(bf16[2,8,64,128]{3,2,1,0:T(8,128)(2,1)S(1)} %pad_maximum_fusion.refs_0_), channel_id=1, source_target_pairs={{0,6},{2,4},{4,10},{6,8},{8,14},{10,12},{12,18},{14,16},{16,22},{1... | collective-permute-start | bytes 786440 | tf_op jit(solution)/shard_map/ppermute | solution.py:251
  6.2 8.2 %collective-permute-start.3 = (bf16[2,8,64,128]{3,2,1,0:T(8,128)(2,1)S(1)}, bf16[2,8,64,128]{3,2,1,0:T(8,128)(2,1)S(1)}, u32[]{:S(2)}, u32[]{:S(2)}) collective-permute-start(bf16[2,8,64,128]{3,2,1,0:T(8,128)(2,1)S(1)} %pad_maximum_fusion.refs_0_), channel_id=1, source_target_pairs={{0,8},{2,10},{4,12},{6,14},{8,16},{10,18},{12,20},{14,22},{16,24},... | collective-permute-start | bytes 786440 | tf_op jit(solution)/shard_map/ppermute | solution.py:251
  8.3 11.6 %collective-permute-start.5 = (bf16[2,8,64,128]{3,2,1,0:T(8,128)(2,1)S(1)}, bf16[2,8,64,128]{3,2,1,0:T(8,128)(2,1)S(1)}, u32[]{:S(2)}, u32[]{:S(2)}) collective-permute-start(bf16[2,8,64,128]{3,2,1,0:T(8,128)(2,1)S(1)} %pad_maximum_fusion.refs_0_), channel_id=1, source_target_pairs={{0,4},{2,6},{4,8},{6,10},{8,12},{10,14},{12,16},{14,18},{16,20},{1... | collective-permute-start | bytes 786440 | tf_op jit(solution)/shard_map/ppermute | solution.py:251
  10.3 10.5 %collective-permute-start.4 = (bf16[2,8,64,128]{3,2,1,0:T(8,128)(2,1)S(1)}, bf16[2,8,64,128]{3,2,1,0:T(8,128)(2,1)S(1)}, u32[]{:S(2)}, u32[]{:S(2)}) collective-permute-start(bf16[2,8,64,128]{3,2,1,0:T(8,128)(2,1)S(1)} %pad_maximum_fusion.refs_0_), channel_id=1, source_target_pairs={{0,2},{2,8},{4,6},{6,12},{8,10},{10,16},{12,14},{14,20},{16,18},{1... | collective-permute-start | bytes 786440 | tf_op jit(solution)/shard_map/ppermute | solution.py:251
  14.5 13.7 %collective-permute-start.6 = (bf16[2,2,8,64,128]{4,3,2,1,0:T(8,128)(2,1)S(1)}, bf16[2,2,8,64,128]{4,3,2,1,0:T(8,128)(2,1)S(1)}, u32[]{:S(2)}, u32[]{:S(2)}) collective-permute-start(bf16[2,2,8,64,128]{4,3,2,1,0:T(8,128)(2,1)S(1)} %early.1), channel_id=1, source_target_pairs={{0,8},{2,10},{4,12},{6,14},{8,16},{10,18},{12,20},{14,22},{16,24},... | collective-permute-start | bytes 1572872 | tf_op jit(solution)/shard_map/ppermute | solution.py:251
  20.8 14.6 %collective-permute-start.7 = (bf16[2,2,8,64,128]{4,3,2,1,0:T(8,128)(2,1)S(1)}, bf16[2,2,8,64,128]{4,3,2,1,0:T(8,128)(2,1)S(1)}, u32[]{:S(2)}, u32[]{:S(2)}) collective-permute-start(bf16[2,2,8,64,128]{4,3,2,1,0:T(8,128)(2,1)S(1)} %late.1), channel_id=1, source_target_pairs={{0,8},{2,10},{4,12},{6,14},{8,16},{10,18},{12,20},{14,22},{16,24},... | collective-permute-start | bytes 1572872 | tf_op jit(solution)/shard_map/ppermute | solution.py:251
